TPU v7x, 32 devices: a whole 2x2x4 slice. The times are simulated.
32 devices in a mesh: fsdp: 32 (over z, y, x, core).
Axes of the slice: x: 2, y: 2, z: 4, core: 2. Of those that a mesh axis runs over, the one named last changes fastest.
Arguments:
- tokens: bfloat16 [8192, 2048], P('fsdp'), may hold values from -6 to 6
- block_of: int32 [8192], P('fsdp'), may hold values from 0 to 7, as said below
- clip_limit: int32 [], replicated, may hold values from 4 to 9
- norm_attn: bfloat16 [2048], P('fsdp'), may hold values from 0.5 to 1.5
- w_query: bfloat16 [2048, 2048], P('fsdp'), may hold values from -0.3314563 to 0.3314563
- w_key: bfloat16 [2048, 2048], P('fsdp'), may hold values from -0.125 to 0.125
- w_value: bfloat16 [2048, 2048], P('fsdp'), may hold values from -0.125 to 0.125
- w_out: bfloat16 [2048, 2048], P('fsdp'), may hold values from -0.5 to 0.5
- norm_ffn: bfloat16 [2048], P('fsdp'), may hold values from 0.5 to 1.5
- w_gate: bfloat16 [2048, 8192], P('fsdp'), may hold values from -0.125 to 0.125
- w_up: bfloat16 [2048, 8192], P('fsdp'), may hold values from -0.125 to 0.125
- w_down: bfloat16 [8192, 2048], P('fsdp'), may hold values from -0.0625 to 0.0625
- cotangent: bfloat16 [8192, 2048], P('fsdp'), may hold values from -6 to 6
Outputs:
- mixed: bfloat16 [8192, 2048], P('fsdp')
- d_tokens: float32 [8192, 2048], P('fsdp')
- d_norm_attn: float32 [2048], P('fsdp')
- d_query: float32 [2048, 2048], P('fsdp')
- d_key: float32 [2048, 2048], P('fsdp')
- d_value: float32 [2048, 2048], P('fsdp')
- d_out: float32 [2048, 2048], P('fsdp')
- d_norm_ffn: float32 [2048], P('fsdp')
- d_gate: float32 [2048, 8192], P('fsdp')
- d_up: float32 [2048, 8192], P('fsdp')
- d_down: float32 [8192, 2048], P('fsdp')
- head_peak: float32 [32], replicated
- clipped_query: bfloat16 [2048, 2048], P('fsdp')
- clipped_key: bfloat16 [2048, 2048], P('fsdp')
Inputs may be any that keep to these rules, and one draw needn't show every extreme that they name: `block_of`: within each sequence of 2048 tokens the block number starts at 0 and never falls; block j begins at a position between j * 256 - 256 // 2 + 1 and j * 256.
All inputs are finite; a program needn't handle non-finite values.
Results may differ from a plain program's by a relative error of at most 0.015.
Values may be sent and summed in bfloat16 or wider, within the bound.
A program may use at most 832 MiB of HBM per device.

v0:
```python
import jax
import jax.numpy as jnp
from jax import lax
from jax.sharding import PartitionSpec as P

HEAD_DIM = 64
SEQ = 2048


epsilon = 1e-05
rope_base = 130000.0
group_width = 4


def shifted(block, axis, distance):
    devices = range(lax.axis_size(axis))
    route = [(i - distance, i) for i in devices if i - distance in devices]
    return lax.ppermute(block, axis, route)


def rope_tables(positions, head_size):
    half_dim = head_size // 2
    inverse = rope_base ** (-jnp.arange(half_dim, dtype=jnp.float32) * 2.0 / head_size)
    angles = positions.astype(jnp.float32)[:, None] * inverse[None, :]
    return (jnp.cos(angles), jnp.sin(angles))


def rotate(stacked, cosine_table, sine_table):
    half_dim = stacked.shape[-1] // 2
    first_half = stacked[..., :half_dim]
    second_half = stacked[..., half_dim:]
    cos_rows = cosine_table[:, None, :]
    sin_rows = sine_table[:, None, :]
    return jnp.concatenate(
        [
            first_half * cos_rows - second_half * sin_rows,
            second_half * cos_rows + first_half * sin_rows,
        ],
        -1,
    )


def norm_scale(hidden_in):
    return lax.rsqrt(jnp.mean(hidden_in * hidden_in, -1, keepdims=True) + epsilon)


def norm_back(hidden_in, scale_in, gain_in, upstream):
    scaled = upstream * gain_in
    inner = jnp.mean(scaled * hidden_in, -1, keepdims=True)
    back_grad = scale_in * scaled - scale_in * scale_in * scale_in * hidden_in * inner
    gain_grad = jnp.sum(upstream * hidden_in * scale_in, 0)
    return (back_grad, gain_grad)


def split_heads(stacked):
    return jnp.moveaxis(
        stacked.reshape(
            stacked.shape[0], stacked.shape[1] // group_width, group_width, stacked.shape[2]
        ),
        1,
        0,
    )


def join_heads(stacked):
    moved = jnp.moveaxis(stacked, 0, 1)
    return moved.reshape(moved.shape[0], -1)


def contract_last(left, right):
    return lax.dot_general(
        left, right, (((1,), (1,)), ((), ())), preferred_element_type=jnp.float32
    )


def contract_rows(left, right):
    return lax.dot_general(
        left, right, (((0,), (0,)), ((), ())), preferred_element_type=jnp.float32
    )


def body(
    tokens,
    block_of,
    clip_limit,
    norm_attn,
    w_query,
    w_key,
    w_value,
    w_out,
    norm_ffn,
    w_gate,
    w_up,
    w_down,
    cotangent,
):
    tok_rows, model_width = tokens.shape
    head_size = HEAD_DIM
    head_total = model_width // head_size
    ff_width = w_gate.shape[1]
    ff_ratio = ff_width // model_width
    score_scale = head_size ** (-0.5)
    devices_all = lax.axis_size("fsdp")
    device_index = lax.axis_index("fsdp")
    group_size = SEQ // tok_rows
    first_token = device_index * tok_rows
    positions = (first_token + jnp.arange(tok_rows, dtype=jnp.int32)) % SEQ
    cosine_table, sine_table = rope_tables(positions, head_size)
    hidden_in = tokens.astype(jnp.float32)
    gain_attn, gain_ffn, query_full, key_full, value_full, out_full = (
        lax.all_gather(norm_attn, "fsdp", axis=0, tiled=True),
        lax.all_gather(norm_ffn, "fsdp", axis=0, tiled=True),
        lax.all_gather(w_query, "fsdp", axis=0, tiled=True),
        lax.all_gather(w_key, "fsdp", axis=0, tiled=True),
        lax.all_gather(w_value, "fsdp", axis=0, tiled=True),
        lax.all_gather(w_out, "fsdp", axis=0, tiled=True),
    )
    gain_attn = gain_attn.astype(jnp.float32)
    gain_ffn = gain_ffn.astype(jnp.float32)
    scale_attn = norm_scale(hidden_in)
    normed_attn = (hidden_in * scale_attn * gain_attn).astype(jnp.bfloat16)

    def as_heads(matrix):
        return matrix.reshape(matrix.shape[0], head_total, head_size)

    def project(weight_full):
        return jnp.dot(normed_attn, weight_full, preferred_element_type=jnp.float32)

    query_heads = rotate(as_heads(project(query_full)), cosine_table, sine_table).astype(
        jnp.bfloat16
    )
    key_heads = rotate(as_heads(project(key_full)), cosine_table, sine_table).astype(jnp.bfloat16)
    value_heads = as_heads(project(value_full)).astype(jnp.bfloat16)
    local_set = (key_heads, value_heads, block_of.astype(jnp.bfloat16))
    earlier_sets = []
    for distance in range(1, group_size):
        earlier_sets.append(shifted((local_set[0], local_set[1], local_set[2]), "fsdp", distance))
    later_set = shifted((local_set[0], local_set[1], local_set[2]), "fsdp", -1)
    all_sets = [local_set] + earlier_sets + [later_set]
    sources = (
        [device_index]
        + [device_index - distance for distance in range(1, group_size)]
        + [device_index + 1]
    )
    my_group = device_index // group_size
    key_valid = jnp.concatenate(
        [
            jnp.broadcast_to(
                (source >= 0) & (source < devices_all) & (source // group_size == my_group),
                (tok_rows,),
            )
            for source in sources
        ]
    )
    keys_all = jnp.concatenate([member_set[0] for member_set in all_sets], 0)
    values_all = jnp.concatenate([member_set[1] for member_set in all_sets], 0)
    key_blocks = jnp.concatenate([member_set[2].astype(jnp.float32) for member_set in all_sets], 0)
    query_blocks = block_of.astype(jnp.float32)
    visible = key_valid[None, :] & (key_blocks[None, :] <= query_blocks[:, None])

    def masked_scores(query_group, key_group):
        scores = (
            jnp.einsum("qhd,khd->hqk", query_group, key_group, preferred_element_type=jnp.float32)
            * score_scale
        )
        return jnp.where(visible[None], scores, -jnp.inf)

    def attend_forward(operands):
        query_group, key_group, value_group = operands
        masked = masked_scores(query_group, key_group)
        row_max = jnp.max(masked, -1, keepdims=True)
        numerators = jnp.exp(masked - row_max)
        totals = jnp.sum(numerators, -1, keepdims=True)
        attention = (numerators / totals).astype(jnp.bfloat16)
        mixed_group = jnp.einsum(
            "hqk,khd->qhd", attention, value_group, preferred_element_type=jnp.float32
        )
        return (
            mixed_group,
            row_max[..., 0] + jnp.log(totals[..., 0]),
            jnp.max(row_max, axis=(1, 2)),
        )

    query_split = split_heads(query_heads)
    keys_split = split_heads(keys_all)
    values_split = split_heads(values_all)
    mixed_groups, log_totals, peak_groups = lax.map(
        attend_forward, (query_split, keys_split, values_split)
    )
    head_peak = lax.pmax(peak_groups.reshape(head_total), "fsdp")
    attended = join_heads(mixed_groups).astype(jnp.bfloat16)
    after_attn = hidden_in + jnp.dot(attended, out_full, preferred_element_type=jnp.float32)
    scale_ffn = norm_scale(after_attn)
    normed_ffn = (after_attn * scale_ffn * gain_ffn).astype(jnp.bfloat16)
    pieces = (
        lax.all_gather(w_gate, "fsdp", axis=0, tiled=True),
        lax.all_gather(w_up, "fsdp", axis=0, tiled=True),
    )
    columns = normed_ffn
    gate_pre = jnp.dot(columns, pieces[0], preferred_element_type=jnp.float32)
    up_pre = jnp.dot(columns, pieces[1], preferred_element_type=jnp.float32)
    hidden = (jax.nn.silu(gate_pre) * up_pre).astype(jnp.bfloat16)
    columns = hidden
    ffn_out = jnp.dot(
        columns,
        lax.all_gather(w_down, "fsdp", axis=0, tiled=True),
        preferred_element_type=jnp.float32,
    )
    mixed = (after_attn + ffn_out).astype(jnp.bfloat16)
    cot_grad = cotangent.astype(jnp.float32)
    d_hidden = contract_last(cotangent, lax.all_gather(w_down, "fsdp", axis=0, tiled=True))
    sigmoid_gate = jax.nn.sigmoid(gate_pre)
    grad_gate = (d_hidden * up_pre * sigmoid_gate * (1.0 + gate_pre * (1.0 - sigmoid_gate))).astype(
        jnp.bfloat16
    )
    grad_up = (d_hidden * jax.nn.silu(gate_pre)).astype(jnp.bfloat16)
    gate_up_upstream = jnp.concatenate([grad_gate, grad_up], 1)
    pieces = (
        lax.all_gather(w_gate, "fsdp", axis=0, tiled=True),
        lax.all_gather(w_up, "fsdp", axis=0, tiled=True),
    )
    d_normed_ffn = contract_last(grad_gate, pieces[0]) + contract_last(grad_up, pieces[1])
    d_after_norm, d_gain_ffn = norm_back(after_attn, scale_ffn, gain_ffn, d_normed_ffn)
    d_residual = cot_grad + d_after_norm
    branch_grad = d_residual.astype(jnp.bfloat16)
    query_full, key_full, value_full, out_full = (
        lax.all_gather(w_query, "fsdp", axis=0, tiled=True),
        lax.all_gather(w_key, "fsdp", axis=0, tiled=True),
        lax.all_gather(w_value, "fsdp", axis=0, tiled=True),
        lax.all_gather(w_out, "fsdp", axis=0, tiled=True),
    )
    grad_attended = contract_last(branch_grad, out_full).astype(jnp.bfloat16)

    def attend_backward(operands):
        query_group, key_group, value_group, grad_group, log_group = operands
        masked = masked_scores(query_group, key_group)
        attention = jnp.exp(masked - log_group[..., None])
        grad_attention = jnp.einsum(
            "qhd,khd->hqk", grad_group, value_group, preferred_element_type=jnp.float32
        )
        centre = jnp.sum(attention * grad_attention, -1, keepdims=True)
        grad_scores = (attention * (grad_attention - centre)).astype(jnp.bfloat16)
        grad_query = (
            jnp.einsum("hqk,khd->qhd", grad_scores, key_group, preferred_element_type=jnp.float32)
            * score_scale
        )
        grad_key = (
            jnp.einsum("hqk,qhd->khd", grad_scores, query_group, preferred_element_type=jnp.float32)
            * score_scale
        )
        grad_value = jnp.einsum(
            "hqk,qhd->khd",
            attention.astype(jnp.bfloat16),
            grad_group,
            preferred_element_type=jnp.float32,
        )
        return (grad_query, grad_key, grad_value)

    grad_query_groups, grad_key_groups, grad_value_groups = lax.map(
        attend_backward,
        (query_split, keys_split, values_split, split_heads(as_heads(grad_attended)), log_totals),
    )
    grad_query_rot = join_heads(grad_query_groups)
    grad_key_all = join_heads(grad_key_groups)
    grad_value_all = join_heads(grad_value_groups)

    def set_rows(matrix, position):
        return matrix[position * tok_rows : (position + 1) * tok_rows]

    key_total = set_rows(grad_key_all, 0)
    value_total = set_rows(grad_value_all, 0)
    for distance in range(1, group_size):
        arrived = shifted(
            (set_rows(grad_key_all, distance), set_rows(grad_value_all, distance)),
            "fsdp",
            -distance,
        )
        key_total = key_total + arrived[0]
        value_total = value_total + arrived[1]
    arrived_later = (
        shifted(set_rows(grad_key_all, group_size).astype(jnp.bfloat16), "fsdp", 1).astype(
            jnp.float32
        ),
        shifted(set_rows(grad_value_all, group_size).astype(jnp.bfloat16), "fsdp", 1).astype(
            jnp.float32
        ),
    )
    key_total = key_total + arrived_later[0]
    value_total = value_total + arrived_later[1]
    grad_query_lin = (
        rotate(as_heads(grad_query_rot), cosine_table, -sine_table)
        .reshape(tok_rows, model_width)
        .astype(jnp.bfloat16)
    )
    grad_key_lin = (
        rotate(as_heads(key_total), cosine_table, -sine_table)
        .reshape(tok_rows, model_width)
        .astype(jnp.bfloat16)
    )
    grad_value_lin = value_total.astype(jnp.bfloat16)
    d_normed_attn = (
        contract_last(grad_query_lin, query_full)
        + contract_last(grad_key_lin, key_full)
        + contract_last(grad_value_lin, value_full)
    )
    d_first_norm, d_gain_attn = norm_back(hidden_in, scale_attn, gain_attn, d_normed_attn)
    d_tokens = d_residual + d_first_norm
    attn_upstream = jnp.concatenate([grad_query_lin, grad_key_lin, grad_value_lin], 1)
    normed_cols = normed_attn
    attn_shares = lax.psum_scatter(
        jnp.concatenate(
            [contract_rows(normed_cols, attn_upstream), contract_rows(attended, branch_grad)], 1
        ),
        "fsdp",
        scatter_dimension=0,
        tiled=True,
    )
    normed_cols = normed_ffn
    down_term = contract_rows(hidden, cotangent).reshape(
        w_gate.shape[0] * lax.axis_size("fsdp"), ff_ratio * model_width
    )
    ffn_shares = lax.psum_scatter(
        jnp.concatenate([contract_rows(normed_cols, gate_up_upstream), down_term], 1),
        "fsdp",
        scatter_dimension=0,
        tiled=True,
    )
    d_gate = ffn_shares[:, :ff_width]
    d_up = ffn_shares[:, ff_width : 2 * ff_width]
    d_down = ffn_shares[:, 2 * ff_width :].reshape(-1, model_width)
    d_norm_attn, d_norm_ffn = (
        lax.psum_scatter(d_gain_attn, "fsdp", scatter_dimension=0, tiled=True),
        lax.psum_scatter(d_gain_ffn, "fsdp", scatter_dimension=0, tiled=True),
    )
    clip_value = clip_limit.astype(jnp.float32)
    factor = jnp.sqrt(clip_value / jnp.maximum(head_peak, clip_value))
    columns = jnp.repeat(factor, head_size)
    clipped_query = (w_query.astype(jnp.float32) * columns[None, :]).astype(jnp.bfloat16)
    clipped_key = (w_key.astype(jnp.float32) * columns[None, :]).astype(jnp.bfloat16)
    return (
        mixed,
        d_tokens,
        d_norm_attn,
        attn_shares[:, :model_width],
        attn_shares[:, model_width : 2 * model_width],
        attn_shares[:, 2 * model_width : 3 * model_width],
        attn_shares[:, 3 * model_width :],
        d_norm_ffn,
        d_gate,
        d_up,
        d_down,
        head_peak,
        clipped_query,
        clipped_key,
    )


def solution(mesh):
    return jax.shard_map(
        body,
        mesh=mesh,
        in_specs=(
            P("fsdp", None),
            P("fsdp"),
            P(),
            P("fsdp"),
            P("fsdp", None),
            P("fsdp", None),
            P("fsdp", None),
            P("fsdp", None),
            P("fsdp"),
            P("fsdp", None),
            P("fsdp", None),
            P("fsdp", None),
            P("fsdp", None),
        ),
        out_specs=(
            P("fsdp", None),
            P("fsdp", None),
            P("fsdp"),
            P("fsdp", None),
            P("fsdp", None),
            P("fsdp", None),
            P("fsdp", None),
            P("fsdp"),
            P("fsdp", None),
            P("fsdp", None),
            P("fsdp", None),
            P(),
            P("fsdp", None),
            P("fsdp", None),
        ),
        check_vma=False,
    )
```

profile of v0, /device:TPU:0, one launch (start us, length us, event | category | flops | bytes accessed | tf_op | source)
XLA Modules:
  0.0 4503.9 jit_solution(6720176308736544276)
XLA Ops:
  27.2 40.9 all-reduce.5
  71.3 20.4 all-gather.8.cloned.1.call-done
  129.9 93.0 %all-gather.12.cloned.1.call-done = bf16[2048,2048]{1,0:T(8,128)(2,1)} async-done(((bf16[64,2048]{1,0:T(8,128)(2,1)}), bf16[2048,2048]{1,0:T(8,128)(2,1)}) %all-gather.12.cloned.1.call-update) | async-done | bytes 8388624 | tf_op jit(solution)/shard_map/all_gather | solution.py:114
  235.6 98.7 %all-gather.10.cloned.1.call-done = bf16[2048,2048]{1,0:T(8,128)(2,1)} async-done(((bf16[64,2048]{1,0:T(8,128)(2,1)}), bf16[2048,2048]{1,0:T(8,128)(2,1)}) %all-gather.10.cloned.1.call-update) | async-done | bytes 8388624 | tf_op jit(solution)/shard_map/all_gather | solution.py:113
  361.9 20.8 collective-permute-done.6
  389.5 9.5 collective-permute-start.21
  409.0 55.0 %collective-permute-start.22 = (bf16[256,32,64]{0,2,1:T(8,128)(2,1)S(1)}, bf16[256,32,64]{0,2,1:T(8,128)(2,1)S(1)}, u32[]{:S(2)}, u32[]{:S(2)}) collective-permute-start(bf16[256,32,64]{0,2,1:T(8,128)(2,1)S(1)} %get-tuple-element.264), channel_id=1, source_target_pairs={{0,7},{1,8},{2,9},{3,10},{4,11},{5,12},{6,13},{7,14},{8,15},{9,16}... | collective-permute-start | bytes 3145736 | tf_op jit(solution)/shard_map/ppermute | solution.py:18
  466.5 14.9 collective-permute-done.22
  485.1 81.2 %while.32 = (s32[]{:T(128)}, bf16[8,256,4,64]{1,3,2,0:T(8,128)(2,1)S(1)}, f32[8,4,256]{2,1,0:T(4,128)S(1)}, f32[8,4]{1,0:T(8,128)}, bf16[8,2304,4,64]{1,3,2,0:T(...) while((s32[]{:T(128)}, ...), condition=%wide.region_5.6_spmd.clone.clone, body=%wide.region_1.5_spmd.clone.sunk.clone | while | flops 626392064 | bytes 32291236 | solution.py:187
  574.0 190.4 %all-gather.16.cloned.1.call-done = bf16[2048,8192]{1,0:T(8,128)(2,1)} async-done(((bf16[64,8192]{1,0:T(8,128)(2,1)}), bf16[2048,8192]{1,0:T(8,128)(2,1)}) %all-gather.16.cloned.1.call-update) | async-done | bytes 33554448 | tf_op jit(solution)/shard_map/all_gather | solution.py:196
  764.5 17.9 fusion.117
  782.4 177.8 %all-gather.18.cloned.1.call-done = bf16[2048,8192]{1,0:T(8,128)(2,1)} async-done(((bf16[64,8192]{1,0:T(8,128)(2,1)}), bf16[2048,8192]{1,0:T(8,128)(2,1)}) %all-gather.18.cloned.1.call-update) | async-done | bytes 33554448 | tf_op jit(solution)/shard_map/all_gather | solution.py:197
  960.2 18.6 fusion.118
  978.7 177.3 %all-gather.20.cloned.1.call-done = bf16[8192,2048]{1,0:T(8,128)(2,1)} async-done(((bf16[256,2048]{1,0:T(8,128)(2,1)}), bf16[8192,2048]{1,0:T(8,128)(2,1)}) %all-gather.20.cloned.1.call-update) | async-done | bytes 33554448 | tf_op jit(solution)/shard_map/all_gather | solution.py:206
  1156.0 23.1 multiply_convert_fusion.1
  1179.2 16.9 fusion.119
  1196.0 18.4 multiply_reduce_fusion.1
  1221.6 272.9 %while.33 = (s32[]{:T(128)}, f32[8,256,4,64]{1,3,2,0:T(8,128)}, f32[8,2304,4,64]{1,3,2,0:T(8,128)}, f32[8,2304,4,64]{1,3,2,0:T(8,128)}, bf16[8,2304,4,64]{1,3,2,...) while((s32[]{:T(128)}, f32[8,256,4,64]{1,3,2,0:T(8,128)}, ...), condition=%wide.region_10.11_spmd.clone.clone, body=%wide.region_8.10_spmd.clone.sunk.clone | while | flops 1533017088 | bytes 175412688 | solution.py:259
  1224.8 9.5 multiply_reduce_fusion.6
  1234.3 9.4 multiply_convert_fusion.9
  1258.9 9.5 multiply_reduce_fusion.6
  1268.4 9.4 multiply_convert_fusion.9
  1293.0 9.5 multiply_reduce_fusion.6
  1327.1 9.5 multiply_reduce_fusion.6
  1361.3 9.5 multiply_reduce_fusion.6
  1395.4 9.5 multiply_reduce_fusion.6
  1429.5 9.5 multiply_reduce_fusion.6
  1463.6 9.5 multiply_reduce_fusion.6
  1500.0 13.0 fusion.113
  1531.9 30.4 collective-permute-done.30
  1567.5 86.5 %collective-permute-done.28 = f32[256,2048]{0,1:T(8,128)} collective-permute-done((f32[256,2048]{0,1:T(8,128)}, f32[256,2048]{0,1:T(8,128)}, u32[]{:S(2)}, u32[]{:S(2)}) %collective-permute-start.28) | collective-permute-done | bytes 2097184 | tf_op jit(solution)/shard_map/ppermute | solution.py:18
  1666.2 11.1 collective-permute-done.25
  1680.0 57.5 %collective-permute-done.38 = f32[256,2048]{0,1:T(8,128)S(1)} collective-permute-done((f32[256,2048]{0,1:T(8,128)}, f32[256,2048]{0,1:T(8,128)S(1)}, u32[]{:S(2)}, u32[]{:S(2)}) %collective-permute-start.38) | collective-permute-done | bytes 2097184 | tf_op jit(solution)/shard_map/ppermute | solution.py:18
  1738.8 11.5 collective-permute-done.37
  1767.8 66.2 %collective-permute-done.36 = f32[256,2048]{0,1:T(8,128)} collective-permute-done((f32[256,2048]{0,1:T(8,128)}, f32[256,2048]{0,1:T(8,128)}, u32[]{:S(2)}, u32[]{:S(2)}) %collective-permute-start.36) | collective-permute-done | bytes 2097184 | tf_op jit(solution)/shard_map/ppermute | solution.py:18
  1833.9 39.1 collective-permute-done.34
  1873.0 23.2 collective-permute-done.33
  1902.7 19.7 fusion.65
  1922.4 43.3 pad_maximum_fusion.1
  1966.9 25.3 fusion.121
  1992.3 79.5 %reshape.249 = f32[2048,8192]{1,0:T(8,128)} reshape(f32[8192,2048]{1,0:T(8,128)} %fusion.121) | data formatting | bytes 134217728 | tf_op jit(solution)/shard_map/reshape | solution.py:319
  2071.7 46.7 %fusion.60 = f32[2048,16384]{1,0:T(8,128)} fusion(bf16[256,2048]{1,0:T(8,128)(2,1)S(1)} %copy-done.20, bf16[256,8192]{1,0:T(8,128)(2,1)} %get-tuple-element.246, bf16[256,8192]{1,0:T(8,128)(2,1)} %get-tuple-element.247), kind=kOutput, calls=%fused_computation.57 | convolution fusion | flops 17196646400 | bytes 143654912 | tf_op jit(solution)/shard_map/dot_general | solution.py:77
  2118.4 131.5 %pad_maximum_fusion = f32[2048,24576]{1,0:T(8,128)} fusion(f32[2048,8192]{1,0:T(8,128)} %reshape.249, f32[2048,16384]{1,0:T(8,128)} %fusion.60), kind=kLoop, calls=%fused_computation.55 | loop fusion | flops 50331648 | bytes 402653184 | tf_op jit(solution)/shard_map/concatenate | solution.py:323
  2250.9 253.5 %pmax.7 = f32[32]{0:T(128)S(1)} all-reduce(f32[32]{0:T(128)S(1)} %reshape.251), channel_id=1, replica_groups=mesh['fsdp'=32] {'fsdp'}, use_global_device_ids=true, to_apply=%region_18.19 | all-reduce | flops 32 | bytes 256 | tf_op jit(solution)/shard_map/pmax | solution.py:190
  2505.5 17.4 fusion.71
  2539.6 46.0 %all-reduce.4 = (f32[2048]{0:T(1024)S(1)}, f32[2048]{0:T(1024)S(1)}) all-reduce(f32[2048]{0:T(1024)S(1)} %get-tuple-element.176, f32[2048]{0:T(1024)S(1)} %copy-done.47), channel_id=2, replica_groups=mesh['fsdp'=32] {'fsdp'}, use_global_device_ids=true, to_apply=%region_13.14.clone | all-reduce | flops 4096 | bytes 32768
  2590.3 287.6 %reduce-scatter.3.cloned.1.call-done = f32[64,8192]{1,0:T(8,128)} async-done(((f32[2048,8192]{1,0:T(8,128)}), f32[64,8192]{1,0:T(8,128)}) %reduce-scatter.3.cloned.1.call-update) | async-done | bytes 2097168 | tf_op jit(solution)/shard_map/reduce_scatter | solution.py:310
  2880.8 1609.2 %reduce-scatter.5.cloned.1.call-done = f32[64,24576]{1,0:T(8,128)} async-done(((f32[2048,24576]{1,0:T(8,128)}), f32[64,24576]{1,0:T(8,128)}) %reduce-scatter.5.cloned.1.call-update) | async-done | bytes 6291472 | tf_op jit(solution)/shard_map/reduce_scatter | solution.py:322
  (461 shorter events, 500.3 us)
Async XLA Ops:
  7.2 84.4 %all-gather.8.cloned.1.call-start = ((), (), s32[]{:S(2)}) async-start(), calls=%async_computation.2 | async-start | bytes 8650752 | tf_op jit(solution)/shard_map/all_gather | solution.py:115
  8.0 214.9 %all-gather.12.cloned.1.call-start = ((), (), s32[]{:S(2)}) async-start(), calls=%async_computation.4 | async-start | bytes 8650752 | tf_op jit(solution)/shard_map/all_gather | solution.py:114
  8.7 325.6 %all-gather.10.cloned.1.call-start = ((), (), s32[]{:S(2)}) async-start(), calls=%async_computation.3 | async-start | bytes 8650752 | tf_op jit(solution)/shard_map/all_gather | solution.py:113
  9.4 556.8 %all-gather.14.cloned.1.call-start = ((), (), s32[]{:S(2)}) async-start(), calls=%async_computation.5 | async-start | bytes 8650752 | tf_op jit(solution)/shard_map/all_gather | solution.py:116
  10.0 754.5 %all-gather.16.cloned.1.call-start = ((), (), s32[]{:S(2)}) async-start(), calls=%async_computation.6 | async-start | bytes 34603008 | tf_op jit(solution)/shard_map/all_gather | solution.py:196
  10.6 949.6 %all-gather.18.cloned.1.call-start = ((), (), s32[]{:S(2)}) async-start(), calls=%async_computation.7 | async-start | bytes 34603008 | tf_op jit(solution)/shard_map/all_gather | solution.py:197
  11.2 1144.8 %all-gather.20.cloned.1.call-start = ((), (), s32[]{:S(2)}) async-start(), calls=%async_computation.8 | async-start | bytes 34603008 | tf_op jit(solution)/shard_map/all_gather | solution.py:206
  11.9 2866.0 %reduce-scatter.3.cloned.1.call-start = ((), (), s32[]{:S(2)}) async-start(), calls=%async_computation.9 | async-start | bytes 69206016 | tf_op jit(solution)/shard_map/reduce_scatter | solution.py:310
  12.0 90.0 %collective-permute-start.8 = (bf16[256]{0:T(256)(128)(2,1)S(1)}, bf16[256]{0:T(256)(128)(2,1)S(1)}, u32[]{:S(2)}, u32[]{:S(2)}) collective-permute-start(bf16[256]{0:T(256)(128)(2,1)S(1)} %get-tuple-element.279), channel_id=1, source_target_pairs={{0,1},{1,2},{2,3},{3,4},{4,5},{5,6},{6,7},{7,8},{8,9},{9,10},{10,1... | collective-permute-start | bytes 1544 | tf_op jit(solution)/shard_map/ppermute | solution.py:18
  14.4 91.0 %collective-permute-start.9 = (bf16[256]{0:T(256)(128)(2,1)S(1)}, bf16[256]{0:T(256)(128)(2,1)S(1)}, u32[]{:S(2)}, u32[]{:S(2)}) collective-permute-start(bf16[256]{0:T(256)(128)(2,1)S(1)} %get-tuple-element.279), channel_id=1, source_target_pairs={{0,2},{1,3},{2,4},{3,5},{4,6},{5,7},{6,8},{7,9},{8,10},{9,11},{10,... | collective-permute-start | bytes 1544 | tf_op jit(solution)/shard_map/ppermute | solution.py:18
  18.8 91.7 %collective-permute-start.10 = (bf16[256]{0:T(256)(128)(2,1)S(1)}, bf16[256]{0:T(256)(128)(2,1)S(1)}, u32[]{:S(2)}, u32[]{:S(2)}) collective-permute-start(bf16[256]{0:T(256)(128)(2,1)S(1)} %get-tuple-element.279), channel_id=1, source_target_pairs={{0,3},{1,4},{2,5},{3,6},{4,7},{5,8},{6,9},{7,10},{8,11},{9,12},{10... | collective-permute-start | bytes 1544 | tf_op jit(solution)/shard_map/ppermute | solution.py:18
  23.1 90.3 %collective-permute-start.11 = (bf16[256]{0:T(256)(128)(2,1)S(1)}, bf16[256]{0:T(256)(128)(2,1)S(1)}, u32[]{:S(2)}, u32[]{:S(2)}) collective-permute-start(bf16[256]{0:T(256)(128)(2,1)S(1)} %get-tuple-element.279), channel_id=1, source_target_pairs={{0,4},{1,5},{2,6},{3,7},{4,8},{5,9},{6,10},{7,11},{8,12},{9,13},{1... | collective-permute-start | bytes 1544 | tf_op jit(solution)/shard_map/ppermute | solution.py:18
  98.7 134.6 %collective-permute-start = (bf16[256,32,64]{0,2,1:T(8,128)(2,1)}, bf16[256,32,64]{0,2,1:T(8,128)(2,1)S(1)}, u32[]{:S(2)}, u32[]{:S(2)}) collective-permute-start(bf16[256,32,64]{0,2,1:T(8,128)(2,1)} %bitcast), channel_id=1, source_target_pairs={{0,1},{1,2},{2,3},{3,4},{4,5},{5,6},{6,7},{7,8},{8,9},{9,10},{10,1... | collective-permute-start | bytes 3145736 | tf_op jit(solution)/shard_map/ppermute | solution.py:18
  102.0 12.9 collective-permute-start.12
  105.4 9.8 collective-permute-start.13
  113.4 117.6 %collective-permute-start.15 = (bf16[256]{0:T(256)(128)(2,1)S(1)}, bf16[256]{0:T(256)(128)(2,1)S(1)}, u32[]{:S(2)}, u32[]{:S(2)}) collective-permute-start(bf16[256]{0:T(256)(128)(2,1)S(1)} %get-tuple-element.279), channel_id=1, source_target_pairs={{1,0},{2,1},{3,2},{4,3},{5,4},{6,5},{7,6},{8,7},{9,8},{10,9},{11,1... | collective-permute-start | bytes 1544 | tf_op jit(solution)/shard_map/ppermute | solution.py:18
  115.6 225.7 %collective-permute-start.1 = (bf16[256,32,64]{0,2,1:T(8,128)(2,1)}, bf16[256,32,64]{0,2,1:T(8,128)(2,1)}, u32[]{:S(2)}, u32[]{:S(2)}) collective-permute-start(bf16[256,32,64]{0,2,1:T(8,128)(2,1)} %bitcast), channel_id=1, source_target_pairs={{0,2},{1,3},{2,4},{3,5},{4,6},{5,7},{6,8},{7,9},{8,10},{9,11},{10,... | collective-permute-start | bytes 3145736 | tf_op jit(solution)/shard_map/ppermute | solution.py:18
  121.5 223.9 %collective-permute-start.2 = (bf16[256,32,64]{0,2,1:T(8,128)(2,1)}, bf16[256,32,64]{0,2,1:T(8,128)(2,1)}, u32[]{:S(2)}, u32[]{:S(2)}) collective-permute-start(bf16[256,32,64]{0,2,1:T(8,128)(2,1)} %bitcast), channel_id=1, source_target_pairs={{0,3},{1,4},{2,5},{3,6},{4,7},{5,8},{6,9},{7,10},{8,11},{9,12},{10... | collective-permute-start | bytes 3145736 | tf_op jit(solution)/shard_map/ppermute | solution.py:18
  123.8 223.3 %collective-permute-start.3 = (bf16[256,32,64]{0,2,1:T(8,128)(2,1)}, bf16[256,32,64]{0,2,1:T(8,128)(2,1)}, u32[]{:S(2)}, u32[]{:S(2)}) collective-permute-start(bf16[256,32,64]{0,2,1:T(8,128)(2,1)} %bitcast), channel_id=1, source_target_pairs={{0,4},{1,5},{2,6},{3,7},{4,8},{5,9},{6,10},{7,11},{8,12},{9,13},{1... | collective-permute-start | bytes 3145736 | tf_op jit(solution)/shard_map/ppermute | solution.py:18
  231.0 119.2 %collective-permute-start.4 = (bf16[256,32,64]{0,2,1:T(8,128)(2,1)}, bf16[256,32,64]{0,2,1:T(8,128)(2,1)}, u32[]{:S(2)}, u32[]{:S(2)}) collective-permute-start(bf16[256,32,64]{0,2,1:T(8,128)(2,1)} %bitcast), channel_id=1, source_target_pairs={{0,5},{1,6},{2,7},{3,8},{4,9},{5,10},{6,11},{7,12},{8,13},{9,14},{... | collective-permute-start | bytes 3145736 | tf_op jit(solution)/shard_map/ppermute | solution.py:18
  233.3 121.6 %collective-permute-start.5 = (bf16[256,32,64]{0,2,1:T(8,128)(2,1)}, bf16[256,32,64]{0,2,1:T(8,128)(2,1)}, u32[]{:S(2)}, u32[]{:S(2)}) collective-permute-start(bf16[256,32,64]{0,2,1:T(8,128)(2,1)} %bitcast), channel_id=1, source_target_pairs={{0,6},{1,7},{2,8},{3,9},{4,10},{5,11},{6,12},{7,13},{8,14},{9,15},... | collective-permute-start | bytes 3145736 | tf_op jit(solution)/shard_map/ppermute | solution.py:18
  341.3 41.4 collective-permute-start.6
  345.4 40.0 collective-permute-start.7
  347.1 42.4 collective-permute-start.16
  350.2 58.8 %collective-permute-start.17 = (bf16[256,32,64]{0,2,1:T(8,128)(2,1)S(1)}, bf16[256,32,64]{0,2,1:T(8,128)(2,1)S(1)}, u32[]{:S(2)}, u32[]{:S(2)}) collective-permute-start(bf16[256,32,64]{0,2,1:T(8,128)(2,1)S(1)} %get-tuple-element.264), channel_id=1, source_target_pairs={{0,2},{1,3},{2,4},{3,5},{4,6},{5,7},{6,8},{7,9},{8,10},{9,11},{10,... | collective-permute-start | bytes 3145736 | tf_op jit(solution)/shard_map/ppermute | solution.py:18
  354.9 109.2 %collective-permute-start.18 = (bf16[256,32,64]{0,2,1:T(8,128)(2,1)S(1)}, bf16[256,32,64]{0,2,1:T(8,128)(2,1)S(1)}, u32[]{:S(2)}, u32[]{:S(2)}) collective-permute-start(bf16[256,32,64]{0,2,1:T(8,128)(2,1)S(1)} %get-tuple-element.264), channel_id=1, source_target_pairs={{0,3},{1,4},{2,5},{3,6},{4,7},{5,8},{6,9},{7,10},{8,11},{9,12},{10... | collective-permute-start | bytes 3145736 | tf_op jit(solution)/shard_map/ppermute | solution.py:18
  382.7 83.5 %collective-permute-start.19 = (bf16[256,32,64]{0,2,1:T(8,128)(2,1)S(1)}, bf16[256,32,64]{0,2,1:T(8,128)(2,1)S(1)}, u32[]{:S(2)}, u32[]{:S(2)}) collective-permute-start(bf16[256,32,64]{0,2,1:T(8,128)(2,1)S(1)} %get-tuple-element.264), channel_id=1, source_target_pairs={{0,4},{1,5},{2,6},{3,7},{4,8},{5,9},{6,10},{7,11},{8,12},{9,13},{1... | collective-permute-start | bytes 3145736 | tf_op jit(solution)/shard_map/ppermute | solution.py:18
  385.4 80.9 %collective-permute-start.20 = (bf16[256,32,64]{0,2,1:T(8,128)(2,1)S(1)}, bf16[256,32,64]{0,2,1:T(8,128)(2,1)S(1)}, u32[]{:S(2)}, u32[]{:S(2)}) collective-permute-start(bf16[256,32,64]{0,2,1:T(8,128)(2,1)S(1)} %get-tuple-element.264), channel_id=1, source_target_pairs={{0,5},{1,6},{2,7},{3,8},{4,9},{5,10},{6,11},{7,12},{8,13},{9,14},{... | collective-permute-start | bytes 3145736 | tf_op jit(solution)/shard_map/ppermute | solution.py:18
  389.5 76.9 %collective-permute-start.21 = (bf16[256,32,64]{0,2,1:T(8,128)(2,1)S(1)}, bf16[256,32,64]{0,2,1:T(8,128)(2,1)S(1)}, u32[]{:S(2)}, u32[]{:S(2)}) collective-permute-start(bf16[256,32,64]{0,2,1:T(8,128)(2,1)S(1)} %get-tuple-element.264), channel_id=1, source_target_pairs={{0,6},{1,7},{2,8},{3,9},{4,10},{5,11},{6,12},{7,13},{8,14},{9,15},... | collective-permute-start | bytes 3145736 | tf_op jit(solution)/shard_map/ppermute | solution.py:18
  409.0 72.3 %collective-permute-start.22 = (bf16[256,32,64]{0,2,1:T(8,128)(2,1)S(1)}, bf16[256,32,64]{0,2,1:T(8,128)(2,1)S(1)}, u32[]{:S(2)}, u32[]{:S(2)}) collective-permute-start(bf16[256,32,64]{0,2,1:T(8,128)(2,1)S(1)} %get-tuple-element.264), channel_id=1, source_target_pairs={{0,7},{1,8},{2,9},{3,10},{4,11},{5,12},{6,13},{7,14},{8,15},{9,16}... | collective-permute-start | bytes 3145736 | tf_op jit(solution)/shard_map/ppermute | solution.py:18
  464.1 17.3 collective-permute-start.23
  1497.4 22.3 collective-permute-start.31
  1513.1 49.2 %collective-permute-start.30 = (f32[256,2048]{0,1:T(8,128)}, f32[256,2048]{0,1:T(8,128)}, u32[]{:S(2)}, u32[]{:S(2)}) collective-permute-start(f32[256,2048]{0,1:T(8,128)} %bitcast.271), channel_id=1, source_target_pairs={{7,0},{8,1},{9,2},{10,3},{11,4},{12,5},{13,6},{14,7},{15,8},{16,9}... | collective-permute-start | bytes 6291464 | tf_op jit(solution)/shard_map/ppermute | solution.py:18
  1514.4 51.8 %collective-permute-start.29 = (f32[256,2048]{0,1:T(8,128)}, f32[256,2048]{0,1:T(8,128)}, u32[]{:S(2)}, u32[]{:S(2)}) collective-permute-start(f32[256,2048]{0,1:T(8,128)} %bitcast.270), channel_id=1, source_target_pairs={{6,0},{7,1},{8,2},{9,3},{10,4},{11,5},{12,6},{13,7},{14,8},{15,9},... | collective-permute-start | bytes 6291464 | tf_op jit(solution)/shard_map/ppermute | solution.py:18
  1515.7 138.2 %collective-permute-start.28 = (f32[256,2048]{0,1:T(8,128)}, f32[256,2048]{0,1:T(8,128)}, u32[]{:S(2)}, u32[]{:S(2)}) collective-permute-start(f32[256,2048]{0,1:T(8,128)} %bitcast.269), channel_id=1, source_target_pairs={{5,0},{6,1},{7,2},{8,3},{9,4},{10,5},{11,6},{12,7},{13,8},{14,9},{... | collective-permute-start | bytes 6291464 | tf_op jit(solution)/shard_map/ppermute | solution.py:18
  1517.0 138.2 %collective-permute-start.27 = (f32[256,2048]{0,1:T(8,128)}, f32[256,2048]{0,1:T(8,128)}, u32[]{:S(2)}, u32[]{:S(2)}) collective-permute-start(f32[256,2048]{0,1:T(8,128)} %bitcast.267), channel_id=1, source_target_pairs={{4,0},{5,1},{6,2},{7,3},{8,4},{9,5},{10,6},{11,7},{12,8},{13,9},{1... | collective-permute-start | bytes 6291464 | tf_op jit(solution)/shard_map/ppermute | solution.py:18
  1520.7 9.9 collective-permute-start.39
  1530.6 134.3 %collective-permute-start.26 = (f32[256,2048]{0,1:T(8,128)}, f32[256,2048]{0,1:T(8,128)S(1)}, u32[]{:S(2)}, u32[]{:S(2)}) collective-permute-start(f32[256,2048]{0,1:T(8,128)} %bitcast.265), channel_id=1, source_target_pairs={{3,0},{4,1},{5,2},{6,3},{7,4},{8,5},{9,6},{10,7},{11,8},{12,9},{13... | collective-permute-start | bytes 6291464 | tf_op jit(solution)/shard_map/ppermute | solution.py:18
  1562.3 115.1 %collective-permute-start.25 = (f32[256,2048]{0,1:T(8,128)}, f32[256,2048]{0,1:T(8,128)S(1)}, u32[]{:S(2)}, u32[]{:S(2)}) collective-permute-start(f32[256,2048]{0,1:T(8,128)} %bitcast.264), channel_id=1, source_target_pairs={{2,0},{3,1},{4,2},{5,3},{6,4},{7,5},{8,6},{9,7},{10,8},{11,9},{12,... | collective-permute-start | bytes 6291464 | tf_op jit(solution)/shard_map/ppermute | solution.py:18
  1566.2 112.5 %collective-permute-start.24 = (f32[256,2048]{0,1:T(8,128)}, f32[256,2048]{0,1:T(8,128)S(1)}, u32[]{:S(2)}, u32[]{:S(2)}) collective-permute-start(f32[256,2048]{0,1:T(8,128)} %bitcast.263), channel_id=1, source_target_pairs={{1,0},{2,1},{3,2},{4,3},{5,4},{6,5},{7,6},{8,7},{9,8},{10,9},{11,1... | collective-permute-start | bytes 6291464 | tf_op jit(solution)/shard_map/ppermute | solution.py:18
  1653.9 83.6 %collective-permute-start.38 = (f32[256,2048]{0,1:T(8,128)}, f32[256,2048]{0,1:T(8,128)S(1)}, u32[]{:S(2)}, u32[]{:S(2)}) collective-permute-start(f32[256,2048]{0,1:T(8,128)} %bitcast.268), channel_id=1, source_target_pairs={{7,0},{8,1},{9,2},{10,3},{11,4},{12,5},{13,6},{14,7},{15,8},{16,9}... | collective-permute-start | bytes 6291464 | tf_op jit(solution)/shard_map/ppermute | solution.py:18
  1655.2 95.1 %collective-permute-start.37 = (f32[256,2048]{0,1:T(8,128)}, f32[256,2048]{0,1:T(8,128)S(1)}, u32[]{:S(2)}, u32[]{:S(2)}) collective-permute-start(f32[256,2048]{0,1:T(8,128)} %bitcast.266), channel_id=1, source_target_pairs={{6,0},{7,1},{8,2},{9,3},{10,4},{11,5},{12,6},{13,7},{14,8},{15,9},... | collective-permute-start | bytes 6291464 | tf_op jit(solution)/shard_map/ppermute | solution.py:18
  1665.0 169.0 %collective-permute-start.36 = (f32[256,2048]{0,1:T(8,128)}, f32[256,2048]{0,1:T(8,128)}, u32[]{:S(2)}, u32[]{:S(2)}) collective-permute-start(f32[256,2048]{0,1:T(8,128)} %bitcast.262), channel_id=1, source_target_pairs={{5,0},{6,1},{7,2},{8,3},{9,4},{10,5},{11,6},{12,7},{13,8},{14,9},{... | collective-permute-start | bytes 6291464 | tf_op jit(solution)/shard_map/ppermute | solution.py:18
  1677.4 156.5 %collective-permute-start.35 = (f32[256,2048]{0,1:T(8,128)}, f32[256,2048]{0,1:T(8,128)}, u32[]{:S(2)}, u32[]{:S(2)}) collective-permute-start(f32[256,2048]{0,1:T(8,128)} %bitcast.261), channel_id=1, source_target_pairs={{4,0},{5,1},{6,2},{7,3},{8,4},{9,5},{10,6},{11,7},{12,8},{13,9},{1... | collective-permute-start | bytes 6291464 | tf_op jit(solution)/shard_map/ppermute | solution.py:18
  1678.7 194.3 %collective-permute-start.34 = (f32[256,2048]{0,1:T(8,128)}, f32[256,2048]{0,1:T(8,128)}, u32[]{:S(2)}, u32[]{:S(2)}) collective-permute-start(f32[256,2048]{0,1:T(8,128)} %bitcast.260), channel_id=1, source_target_pairs={{3,0},{4,1},{5,2},{6,3},{7,4},{8,5},{9,6},{10,7},{11,8},{12,9},{13... | collective-permute-start | bytes 6291464 | tf_op jit(solution)/shard_map/ppermute | solution.py:18
  1737.5 158.6 %collective-permute-start.33 = (f32[256,2048]{0,1:T(8,128)}, f32[256,2048]{0,1:T(8,128)}, u32[]{:S(2)}, u32[]{:S(2)}) collective-permute-start(f32[256,2048]{0,1:T(8,128)} %bitcast.259), channel_id=1, source_target_pairs={{2,0},{3,1},{4,2},{5,3},{6,4},{7,5},{8,6},{9,7},{10,8},{11,9},{12,... | collective-permute-start | bytes 6291464 | tf_op jit(solution)/shard_map/ppermute | solution.py:18
  1750.4 145.8 %collective-permute-start.32 = (f32[256,2048]{0,1:T(8,128)}, f32[256,2048]{0,1:T(8,128)}, u32[]{:S(2)}, u32[]{:S(2)}) collective-permute-start(f32[256,2048]{0,1:T(8,128)} %bitcast.258), channel_id=1, source_target_pairs={{1,0},{2,1},{3,2},{4,3},{5,4},{6,5},{7,6},{8,7},{9,8},{10,9},{11,1... | collective-permute-start | bytes 6291464 | tf_op jit(solution)/shard_map/ppermute | solution.py:18
  1965.7 2524.2 %reduce-scatter.5.cloned.1.call-start = ((), (), s32[]{:S(2)}) async-start(), calls=%async_computation.10 | async-start | bytes 207618048 | tf_op jit(solution)/shard_map/reduce_scatter | solution.py:322
  (85 other events, 5024.6 us)
Sparse Core Ops, SparseCore 0:
  10.9 80.6 all-gather.7
  94.5 128.3 all-gather.11
  225.7 108.5 all-gather.9
  337.0 161.2 all-gather.13
  501.1 263.3 all-gather.15
  767.2 192.9 all-gather.17
  963.0 192.9 all-gather.19
  1965.9 911.9 reduce-scatter.2
  2884.3 1605.6 reduce-scatter.4
where the time goes:
time: 4520 us; the launch traced here: 4500 us
  waiting for transfers between devices  3040 us (67%)
  matrix products  494 us (11%)
  blocking collectives  340 us (8%)
  other arithmetic  297 us (7%)
  starting transfers between devices  159 us (4%)
  local copies, waits for them, and re-layouts  158 us (3%)
    reduce_scatter x1, waiting for transfers between devices, body(): lax.psum_scatter(jnp.concatenate([contract_rows(normed_cols, gate_up_upst...  1610 us
    ppermute x40, waiting for transfers between devices, shifted(): return lax.ppermute(block, axis, route)  381 us
    reduce_scatter x1, waiting for transfers between devices, body(): lax.psum_scatter(jnp.concatenate([contract_rows(normed_cols, attn_upstrea...  288 us
    pmax x1, blocking collectives, body(): head_peak = lax.pmax(peak_groups.reshape(head_total), 'fsdp')  254 us
    all_gather x1, waiting for transfers between devices, body(): lax.all_gather(w_gate, 'fsdp', axis=0, tiled=True)  190 us
    all_gather x1, waiting for transfers between devices, body(): lax.all_gather(w_up, 'fsdp', axis=0, tiled=True)  178 us
    all_gather x1, waiting for transfers between devices, body(): lax.all_gather(w_down, 'fsdp', axis=0, tiled=True)  177 us
    ppermute x40, starting transfers between devices, shifted(): return lax.ppermute(block, axis, route)  158 us
  transfers between devices with their start and end apart: 49, of which 21 were waited for; matrix products, arithmetic and copies ran while one was open for 12% of the time, Pallas kernels for 0%

commit v1 on v0

v1 whole, which is shorter than its diff:
```python
import functools

import jax
import jax.numpy as jnp
from jax import lax
from jax.experimental import pallas as pl
from jax.experimental.pallas import tpu as pltpu
from jax.sharding import PartitionSpec as P

HEAD_DIM = 64
SEQ = 2048
BLOCK = 256
AXIS = "fsdp"
MESH = pl.DeviceIdType.MESH

epsilon = 1e-05
rope_base = 130000.0
bf16 = jnp.bfloat16
f32 = jnp.float32


def contract(left, right, left_dim, right_dim):
    return lax.dot_general(
        left, right, (((left_dim,), (right_dim,)), ((), ())), preferred_element_type=f32
    )


def rope_tables(length, width):
    half_dim = HEAD_DIM // 2
    inverse = rope_base ** (-jnp.arange(half_dim, dtype=f32) * 2.0 / HEAD_DIM)
    angles = jnp.arange(length, dtype=f32)[:, None] * inverse[None, :]
    cosine, sine = jnp.cos(angles), jnp.sin(angles)
    repeats = width // HEAD_DIM
    return (
        jnp.tile(jnp.concatenate([cosine, cosine], 1), (1, repeats)),
        jnp.tile(jnp.concatenate([-sine, sine], 1), (1, repeats)),
    )


def swap_halves(rows):
    width = rows.shape[1]
    half = HEAD_DIM // 2
    lane = lax.broadcasted_iota(jnp.int32, rows.shape, 1)
    return jnp.where(
        lane % HEAD_DIM < half, pltpu.roll(rows, width - half, 1), pltpu.roll(rows, half, 1)
    )


def head_mask(shape, head):
    lane = lax.broadcasted_iota(jnp.int32, shape, 1)
    return (lane >= head * HEAD_DIM) & (lane < (head + 1) * HEAD_DIM)


def visible_tail(row_ref, col_ref, q0, cols):
    tail = min(2 * BLOCK, cols)
    q_blocks = col_ref[pl.ds(q0, BLOCK), :]
    k_blocks = row_ref[:, pl.ds(cols - tail, tail)]
    return k_blocks <= q_blocks


def attend_forward_kernel(
    heads, qkv_ref, cos_ref, sin_ref, row_ref, col_ref, q_ref, k_ref, v_ref, out_ref, lse_ref, peak_ref
):
    length = qkv_ref.shape[0]
    width = heads * HEAD_DIM
    for t in range(length // BLOCK):
        rows = pl.ds(t * BLOCK, BLOCK)
        cosine, sine = cos_ref[rows, :], sin_ref[rows, :]
        query = qkv_ref[rows, 0:width]
        q_ref[rows, :] = ((query * cosine + swap_halves(query) * sine).astype(bf16).astype(f32)
                          * HEAD_DIM ** (-0.5)).astype(bf16)
        key = qkv_ref[rows, width : 2 * width]
        k_ref[rows, :] = (key * cosine + swap_halves(key) * sine).astype(bf16)
        v_ref[rows, :] = qkv_ref[rows, 2 * width : 3 * width].astype(bf16)
    peak_ref[...] = jnp.full(peak_ref.shape, -jnp.inf, f32)
    for t in range(length // BLOCK):
        q0 = t * BLOCK
        rows = pl.ds(q0, BLOCK)
        cols = min(q0 + 2 * BLOCK, length)
        tail = min(2 * BLOCK, cols)

        def one_head(head, total):
            query = jnp.where(head_mask((BLOCK, width), head), q_ref[rows, :], 0).astype(bf16)
            scores = contract(query, k_ref[0:cols, :], 1, 1)
            hidden = jnp.where(visible_tail(row_ref, col_ref, q0, cols), scores[:, cols - tail :], -jnp.inf)
            if tail < cols:
                scores = jnp.concatenate([scores[:, : cols - tail], hidden], 1)
            else:
                scores = hidden
            row_max = jnp.max(scores, 1, keepdims=True)
            numerators = jnp.exp(scores - row_max)
            totals = jnp.sum(numerators, 1, keepdims=True)
            mixed = contract(numerators.astype(bf16), v_ref[0:cols, :], 1, 0) / totals
            lse_ref[rows, pl.ds(0, 128)] = jnp.where(
                lax.broadcasted_iota(jnp.int32, (BLOCK, 128), 1) == head,
                row_max + jnp.log(totals),
                lse_ref[rows, pl.ds(0, 128)],
            )
            peak_ref[...] = jnp.where(
                lax.broadcasted_iota(jnp.int32, peak_ref.shape, 1) == head,
                jnp.maximum(peak_ref[...], jnp.max(row_max)),
                peak_ref[...],
            )
            return jnp.where(head_mask((BLOCK, width), head), mixed, total)

        total = lax.fori_loop(0, heads, one_head, jnp.zeros((BLOCK, width), f32))
        out_ref[rows, :] = total.astype(bf16)


def attend_forward(qkv, cosine, sine, blocks, heads):
    length = qkv.shape[0]
    width = heads * HEAD_DIM
    shape = jax.ShapeDtypeStruct
    return pl.pallas_call(
        functools.partial(attend_forward_kernel, heads),
        out_shape=(
            shape((length, width), bf16),
            shape((length, width), bf16),
            shape((length, width), bf16),
            shape((length, width), bf16),
            shape((length, 128), f32),
            shape((8, 128), f32),
        ),
        in_specs=[pl.BlockSpec(memory_space=pltpu.VMEM)] * 5,
        out_specs=tuple([pl.BlockSpec(memory_space=pltpu.VMEM)] * 6),
        compiler_params=pltpu.CompilerParams(vmem_limit_bytes=56 * 1024 * 1024),
        cost_estimate=pl.CostEstimate(
            flops=8 * heads * length * length * HEAD_DIM, bytes_accessed=length * width * 24,
            transcendentals=heads * length * length,
        ),
        name="attend_forward",
    )(qkv, cosine, sine, blocks.reshape(1, length), blocks.reshape(length, 1))


def attend_backward_kernel(
    heads, q_ref, k_ref, v_ref, grad_ref, lse_ref, cos_ref, sin_ref, row_ref, col_ref, out_ref, dk_ref, dv_ref
):
    length = q_ref.shape[0]
    width = heads * HEAD_DIM
    dk_ref[...] = jnp.zeros_like(dk_ref)
    dv_ref[...] = jnp.zeros_like(dv_ref)
    for t in range(length // BLOCK):
        q0 = t * BLOCK
        rows = pl.ds(q0, BLOCK)
        cols = min(q0 + 2 * BLOCK, length)
        tail = min(2 * BLOCK, cols)

        def one_head(head, dq):
            mask = head_mask((BLOCK, width), head)
            query = jnp.where(mask, q_ref[rows, :], 0).astype(bf16)
            grad = jnp.where(mask, grad_ref[rows, :], 0).astype(bf16)
            lse = jnp.sum(
                jnp.where(
                    lax.broadcasted_iota(jnp.int32, (BLOCK, 128), 1) == head, lse_ref[rows, :], 0.0
                ),
                1,
                keepdims=True,
            )
            scores = contract(query, k_ref[0:cols, :], 1, 1)
            hidden = jnp.where(visible_tail(row_ref, col_ref, q0, cols), scores[:, cols - tail :], -jnp.inf)
            if tail < cols:
                scores = jnp.concatenate([scores[:, : cols - tail], hidden], 1)
            else:
                scores = hidden
            attention = jnp.exp(scores - lse)
            grad_attention = contract(grad, v_ref[0:cols, :], 1, 1)
            weighted = attention * grad_attention
            centre = jnp.sum(weighted, 1, keepdims=True)
            grad_scores = (weighted - attention * centre).astype(bf16)
            dv_ref[0:cols, :] += contract(attention.astype(bf16), grad, 0, 0)
            dk_ref[0:cols, :] += contract(grad_scores, query, 0, 0)
            return jnp.where(mask, contract(grad_scores, k_ref[0:cols, :], 1, 0), dq)

        dq = lax.fori_loop(0, heads, one_head, jnp.zeros((BLOCK, width), f32)) * HEAD_DIM ** (-0.5)
        out_ref[rows, 0:width] = (
            dq * cos_ref[rows, :] - swap_halves(dq) * sin_ref[rows, :]
        ).astype(bf16)
    for t in range(length // BLOCK):
        rows = pl.ds(t * BLOCK, BLOCK)
        dk = dk_ref[rows, :]
        out_ref[rows, width : 2 * width] = (
            dk * cos_ref[rows, :] - swap_halves(dk) * sin_ref[rows, :]
        ).astype(bf16)
        out_ref[rows, 2 * width : 3 * width] = dv_ref[rows, :].astype(bf16)


def attend_backward(query, key, value, grad, lse, cosine, sine, blocks, heads):
    length = query.shape[0]
    width = heads * HEAD_DIM
    return pl.pallas_call(
        functools.partial(attend_backward_kernel, heads),
        out_shape=jax.ShapeDtypeStruct((length, 3 * width), bf16),
        in_specs=[pl.BlockSpec(memory_space=pltpu.VMEM)] * 9,
        out_specs=pl.BlockSpec(memory_space=pltpu.VMEM),
        scratch_shapes=[pltpu.VMEM((length, width), f32), pltpu.VMEM((length, width), f32)],
        compiler_params=pltpu.CompilerParams(vmem_limit_bytes=56 * 1024 * 1024),
        cost_estimate=pl.CostEstimate(
            flops=20 * heads * length * length * HEAD_DIM, bytes_accessed=length * width * 24,
            transcendentals=heads * length * length,
        ),
        name="attend_backward",
    )(query, key, value, grad, lse, cosine, sine, blocks.reshape(1, length), blocks.reshape(length, 1))


def bit_of(index, bit):
    return lax.rem(lax.div(index, bit), 2)


def flip_bit(index, bit):
    return index + bit - 2 * bit * bit_of(index, bit)


class Links:

    def __init__(self, send_sems, recv_sems):
        self.send_sems, self.recv_sems = send_sems, recv_sems

    def copy(self, slot, src, dst, device):
        return pltpu.make_async_remote_copy(
            src_ref=src, dst_ref=dst, send_sem=self.send_sems.at[slot],
            recv_sem=self.recv_sems.at[slot], device_id=(device,), device_id_type=MESH,
        )


def greet(partners):
    barrier = pltpu.get_barrier_semaphore()
    for partner in partners:
        pl.semaphore_signal(barrier, inc=1, device_id=(partner,), device_id_type=MESH)
    pl.semaphore_wait(barrier, len(partners))


def spread_block(bits, own_ref, out_ref, links, local_sem):
    core, first, second = bits
    me = lax.axis_index(AXIS)
    sibling, next_a, next_b = (flip_bit(me, bit) for bit in bits)
    block = own_ref.shape[0]
    half = block // 2
    in_a, in_b = bit_of(me, first), bit_of(me, second)

    def rows(flip_a, flip_b, part):
        place = bit_of(me, core)
        place = place + 2 * lax.rem(in_a + flip_a, 2) + 4 * lax.rem(in_b + flip_b, 2)
        start, size = (0, block) if part is None else (part * half, half)
        return pl.ds(pl.multiple_of(place * block + start, half), size)

    def passed(slot, where, device):
        return links.copy(slot, out_ref.at[where], out_ref.at[where], device)

    def first_hand(slot, part, device):
        return links.copy(
            slot, own_ref.at[pl.ds(part * half, half)], out_ref.at[rows(0, 0, part)], device
        )

    copies = {
        0: first_hand(0, 0, next_a),
        1: first_hand(1, 1, next_b),
        2: first_hand(2, 1, next_a),
        3: first_hand(3, 0, next_b),
        4: links.copy(4, own_ref, out_ref.at[rows(0, 0, None)], sibling),
        5: passed(5, rows(1, 0, 0), next_b),
        6: passed(6, rows(1, 0, 0), sibling),
        7: passed(7, rows(0, 1, 1), next_a),
        8: passed(8, rows(0, 1, 1), sibling),
        9: passed(9, rows(1, 0, 1), sibling),
        10: passed(10, rows(0, 1, 0), sibling),
        11: passed(11, rows(1, 1, 0), sibling),
        12: passed(12, rows(1, 1, 1), sibling),
    }
    for slot in range(5):
        copies[slot].start()
    keep = pltpu.make_async_copy(own_ref, out_ref.at[rows(0, 0, None)], local_sem)
    keep.start()
    copies[0].wait_recv()
    copies[5].start()
    copies[6].start()
    copies[1].wait_recv()
    copies[7].start()
    copies[8].start()
    copies[2].wait_recv()
    copies[9].start()
    copies[3].wait_recv()
    copies[10].start()
    copies[5].wait_recv()
    copies[11].start()
    copies[7].wait_recv()
    copies[12].start()
    for slot in (4, 6, 8, 9, 10, 11, 12):
        copies[slot].wait_recv()
    keep.wait()
    for slot in copies:
        copies[slot].wait_send()


SPREAD_COPIES = 13
SUM_COPIES = 10


def sum_block(bits, product, total, to_core, from_core, chip_sum, arrived, links):
    core, first, second = bits
    me = lax.axis_index(AXIS)
    sibling, next_a, next_b = (flip_bit(me, bit) for bit in bits)
    block, width = total.shape
    half = block // 2
    tile = 512

    def place(step, other_core):
        flip_a, flip_b = 1 - step // 2, 1 - step % 2
        return (
            lax.rem(bit_of(me, core) + other_core, 2)
            + 2 * lax.rem(bit_of(me, first) + flip_a, 2)
            + 4 * lax.rem(bit_of(me, second) + flip_b, 2)
        )

    def part(index):
        return pl.ds(index * half, half)

    diag_a = links.copy(4, chip_sum.at[0, part(0)], arrived.at[0], next_a)
    diag_b = links.copy(5, chip_sum.at[0, part(1)], arrived.at[1], next_b)
    plain_a = links.copy(6, chip_sum.at[1, part(0)], arrived.at[2], next_a)
    plain_b = links.copy(7, chip_sum.at[2, part(1)], arrived.at[3], next_b)
    last_a = links.copy(8, chip_sum.at[1, part(1)], arrived.at[4], next_a)
    last_b = links.copy(9, chip_sum.at[2, part(0)], arrived.at[5], next_b)

    def core_copy(step):
        return links.copy(step, to_core.at[step], from_core.at[step], sibling)

    @pl.loop(0, 4)
    def _(step):
        @pl.loop(0, width // tile)
        def _(column):
            columns = pl.ds(pl.multiple_of(column * tile, tile), tile)
            to_core[step, :, columns] = product(place(step, 1), columns).astype(bf16)

        core_copy(step).start()

    @pl.loop(0, 4)
    def _(step):
        core_copy(step).wait_recv()

        @pl.loop(0, width // tile)
        def _(column):
            columns = pl.ds(pl.multiple_of(column * tile, tile), tile)
            summed = product(place(step, 0), columns) + from_core[step, :, columns].astype(f32)
            total[:, columns] = summed
            chip_sum[step, :, columns] = summed.astype(bf16)

        @pl.when(step == 0)
        def _():
            diag_a.start()
            diag_b.start()

        @pl.when(step == 1)
        def _():
            plain_a.start()

        @pl.when(step == 2)
        def _():
            plain_b.start()

    diag_a.wait_recv()
    chip_sum[2, 0:half, :] = (chip_sum[2, 0:half, :].astype(f32) + arrived[0].astype(f32)).astype(bf16)
    last_b.start()
    diag_b.wait_recv()
    chip_sum[1, half:block, :] = (
        chip_sum[1, half:block, :].astype(f32) + arrived[1].astype(f32)
    ).astype(bf16)
    last_a.start()
    plain_a.wait_recv()
    total[0:half, :] += arrived[2].astype(f32)
    plain_b.wait_recv()
    total[half:block, :] += arrived[3].astype(f32)
    last_b.wait_recv()
    total[0:half, :] += arrived[5].astype(f32)
    last_a.wait_recv()
    total[half:block, :] += arrived[4].astype(f32)

    @pl.loop(0, 4)
    def _(step):
        core_copy(step).wait_send()

    for copy in (diag_a, diag_b, plain_a, plain_b, last_a, last_b):
        copy.wait_send()


def sum_scratch(block, width):
    return [
        pltpu.VMEM((block, width), f32),
        pltpu.VMEM((4, block, width), bf16),
        pltpu.VMEM((4, block, width), bf16),
        pltpu.VMEM((4, block, width), bf16),
        pltpu.VMEM((6, block // 2, width), bf16),
        pltpu.SemaphoreType.DMA((SUM_COPIES,)),
        pltpu.SemaphoreType.DMA((SUM_COPIES,)),
    ]


def spread_scratch(block, width):
    return [
        pltpu.VMEM((block, width), bf16),
        pltpu.SemaphoreType.DMA((SPREAD_COPIES,)),
        pltpu.SemaphoreType.DMA((SPREAD_COPIES,)),
        pltpu.SemaphoreType.DMA,
    ]


vmem = pl.BlockSpec(memory_space=pltpu.VMEM)
anywhere = pl.BlockSpec(memory_space=pl.ANY)


def link_params(collective_id):
    return pltpu.CompilerParams(
        collective_id=collective_id, has_side_effects=True, vmem_limit_bytes=60 * 1024 * 1024
    )


def cost(flops, size):
    return pl.CostEstimate(flops=int(flops), bytes_accessed=int(size), transcendentals=0)


def tokens_kernel(bits, own_ref, out_ref, send_sems, recv_sems, local_sem):
    me = lax.axis_index(AXIS)
    greet([flip_bit(me, bit) for bit in bits])
    spread_block(bits, own_ref, out_ref, Links(send_sems, recv_sems), local_sem)


def gather_tokens(tokens, bits):
    block, width = tokens.shape
    return pl.pallas_call(
        functools.partial(tokens_kernel, bits),
        out_shape=jax.ShapeDtypeStruct((8 * block, width), bf16),
        in_specs=[vmem],
        out_specs=anywhere,
        scratch_shapes=spread_scratch(block, width)[1:],
        compiler_params=link_params(1),
        cost_estimate=cost(0, 100e6),
        name="gather_tokens",
    )(tokens)


def row_scale(values):
    return lax.rsqrt(jnp.mean(values * values, -1, keepdims=True) + epsilon)


def branch_kernel(
    sum_bits, spread_bits, left_ref, right_ref, residual_ref, gain_ref, h2_ref, out_ref,
    total, to_core, from_core, chip_sum, arrived, sum_send, sum_recv, own, send_sems, recv_sems, local_sem,
):
    me = lax.axis_index(AXIS)
    block = total.shape[0]
    greet([flip_bit(me, bit) for bit in sorted(set(sum_bits) | set(spread_bits))])

    def product(place, columns):
        rows = pl.ds(pl.multiple_of(place * block, block), block)
        return contract(left_ref[rows, :], right_ref[:, columns], 1, 0)

    sum_block(
        sum_bits, product, total, to_core, from_core, chip_sum, arrived, Links(sum_send, sum_recv)
    )
    h2 = residual_ref[...].astype(f32) + total[...]
    h2_ref[...] = h2
    own[...] = (h2 * row_scale(h2) * gain_ref[...]).astype(bf16)
    spread_block(spread_bits, own, out_ref, Links(send_sems, recv_sems), local_sem)


def branch(left, right, residual, gain, sum_bits, spread_bits):
    block, width = residual.shape
    return pl.pallas_call(
        functools.partial(branch_kernel, sum_bits, spread_bits),
        out_shape=(
            jax.ShapeDtypeStruct((block, width), f32),
            jax.ShapeDtypeStruct((8 * block, width), bf16),
        ),
        in_specs=[vmem] * 4,
        out_specs=(vmem, anywhere),
        scratch_shapes=sum_scratch(block, width) + spread_scratch(block, width),
        compiler_params=link_params(2),
        cost_estimate=cost(16 * block * left.shape[1] * width, 250e6),
        name="attention_branch",
    )(left, right, residual, gain)


def norm_back(values, gain, upstream):
    scaled = upstream * gain
    scale = row_scale(values)
    inner = jnp.mean(scaled * values, -1, keepdims=True)
    return scale * scaled - scale * scale * scale * values * inner


def ffn_back_kernel(
    sum_bits, spread_bits, gate_ref, up_ref, gate_w_ref, up_w_ref, h2_ref, cot_ref, gain_ref, residual_ref, out_ref,
    total, to_core, from_core, chip_sum, arrived, sum_send, sum_recv, own, send_sems, recv_sems, local_sem,
):
    me = lax.axis_index(AXIS)
    block = total.shape[0]
    greet([flip_bit(me, bit) for bit in sorted(set(sum_bits) | set(spread_bits))])

    def product(place, columns):
        rows = pl.ds(pl.multiple_of(place * block, block), block)
        return contract(gate_ref[rows, :], gate_w_ref[columns, :], 1, 1) + contract(
            up_ref[rows, :], up_w_ref[columns, :], 1, 1
        )

    sum_block(
        sum_bits, product, total, to_core, from_core, chip_sum, arrived, Links(sum_send, sum_recv)
    )
    residual = cot_ref[...].astype(f32) + norm_back(h2_ref[...], gain_ref[...], total[...])
    residual_ref[...] = residual
    own[...] = residual.astype(bf16)
    spread_block(spread_bits, own, out_ref, Links(send_sems, recv_sems), local_sem)


def ffn_back(gate, up, gate_w, up_w, h2, cot, gain, sum_bits, spread_bits):
    block, width = h2.shape
    return pl.pallas_call(
        functools.partial(ffn_back_kernel, sum_bits, spread_bits),
        out_shape=(
            jax.ShapeDtypeStruct((block, width), f32),
            jax.ShapeDtypeStruct((8 * block, width), bf16),
        ),
        in_specs=[vmem] * 7,
        out_specs=(vmem, anywhere),
        scratch_shapes=sum_scratch(block, width) + spread_scratch(block, width),
        compiler_params=link_params(3),
        cost_estimate=cost(32 * block * gate.shape[1] * width, 250e6),
        name="ffn_back",
    )(gate, up, gate_w, up_w, h2, cot, gain)


def first_back_kernel(
    sum_bits, left_ref, right_ref, tokens_ref, gain_ref, residual_ref, out_ref,
    total, to_core, from_core, chip_sum, arrived, sum_send, sum_recv,
):
    me = lax.axis_index(AXIS)
    block = total.shape[0]
    greet([flip_bit(me, bit) for bit in sum_bits])

    def product(place, columns):
        rows = pl.ds(pl.multiple_of(place * block, block), block)
        return contract(left_ref[rows, :], right_ref[columns, :], 1, 1)

    sum_block(
        sum_bits, product, total, to_core, from_core, chip_sum, arrived, Links(sum_send, sum_recv)
    )
    out_ref[...] = residual_ref[...] + norm_back(
        tokens_ref[...].astype(f32), gain_ref[...], total[...]
    )


def first_back(left, right, tokens, gain, residual, sum_bits):
    block, width = tokens.shape
    return pl.pallas_call(
        functools.partial(first_back_kernel, sum_bits),
        out_shape=jax.ShapeDtypeStruct((block, width), f32),
        in_specs=[vmem] * 5,
        out_specs=vmem,
        scratch_shapes=sum_scratch(block, width),
        compiler_params=link_params(4),
        cost_estimate=cost(16 * block * left.shape[1] * width, 150e6),
        name="first_back",
    )(left, right, tokens, gain, residual)


def body(
    tokens, block_of, clip_limit, norm_attn, w_query, w_key, w_value, w_out,
    norm_ffn, w_gate, w_up, w_down, cotangent,
):
    tok_rows, width = tokens.shape
    devices = lax.axis_size(AXIS)
    team = SEQ // tok_rows
    teams = devices // team
    head_total = width // HEAD_DIM
    heads = head_total // team
    head_cols = heads * HEAD_DIM
    ff_rows = w_down.shape[0]
    weight_rows = w_gate.shape[0]
    ff_cols = w_gate.shape[1] // team
    device = lax.axis_index(AXIS)
    mate = device % team
    bit_count = devices.bit_length() - 1
    attn_bits, ffn_bits = (1, 2, 4), (1, 2, 8)
    data_bits = [4] + [1 << k for k in range(4, bit_count)]
    in_team = [[g * team + b for b in range(team)] for g in range(teams)]
    across = [[g * team + b for g in range(teams)] for b in range(team)]
    ffn_team = [
        [g * 16 + z * 8 + y * 4 + c for z in range(2) for c in range(4)]
        for g in range(devices // 16)
        for y in range(2)
    ]

    def flip(x, bit):
        return lax.ppermute(x, AXIS, [(i, i ^ bit) for i in range(devices)])

    def gather_across(x):
        return lax.all_gather(x, AXIS, axis=0, tiled=True, axis_index_groups=across)

    def scatter_across(x):
        return lax.psum_scatter(
            x.astype(bf16), AXIS, scatter_dimension=0, tiled=True, axis_index_groups=across
        )

    def swap(x, groups):
        return lax.all_to_all(x, AXIS, 0, 0, tiled=True, axis_index_groups=groups)

    def dim_of(bit):
        return bit_count - bit.bit_length()

    def data_pieces(x):
        pieces = {0: x}
        for bit in reversed(data_bits):
            for key in list(pieces):
                pieces[key | bit] = flip(pieces[key], bit)
        return pieces

    def place_pieces(pieces, dims, shape):
        total = jnp.zeros(shape, bf16)
        for key, piece in pieces.items():
            start = [0] * len(shape)
            size = list(shape)
            for bit in data_bits:
                start[dims[bit]] = ((device // bit) + (1 if key & bit else 0)) % 2
                size[dims[bit]] = 1
            total = lax.dynamic_update_slice(total, piece.reshape(size), start)
        return total

    def data_sum(x, dims):
        alive = dict(dims)
        for bit in data_bits:
            dim = alive.pop(bit)
            alive = {b: d - (d > dim) for b, d in alive.items()}
            mine = (device // bit) % 2
            keep = lax.dynamic_index_in_dim(x, mine, dim, False)
            sent = flip(lax.dynamic_index_in_dim(x, 1 - mine, dim, False), bit)
            x = (keep.astype(f32) + sent.astype(f32)).astype(bf16)
        return x

    def columns_out(weight, piece):
        rows, cols = weight.shape
        split = weight.reshape(rows, cols // (team * piece), team, piece)
        return split.transpose(2, 0, 1, 3).reshape(team, rows, cols // team)

    def columns_back(weight, piece):
        rows, cols = weight.shape[1:]
        split = weight.reshape(team, rows, cols // piece, piece)
        return split.transpose(1, 2, 0, 3).reshape(rows, team * cols)

    def ffn_out(weight):
        split = weight.reshape(weight_rows, devices // 16, 2, 2, 4, ff_rows)
        return split.transpose(2, 4, 0, 1, 3, 5).reshape(team, weight_rows, ff_cols)

    def ffn_home(grad):
        split = grad.reshape(2, 4, weight_rows, devices // 16, 2, ff_rows)
        return split.transpose(2, 3, 0, 4, 1, 5).reshape(weight_rows, team * ff_cols)

    row_dims = {bit: dim_of(bit) for bit in data_bits}
    row_shape = (2,) * bit_count
    unit_dims = {bit: i for i, bit in enumerate(reversed(data_bits))}
    unit_shape = (2,) * len(data_bits)

    def gather_small(x):
        for k in range(bit_count):
            other = flip(x, 1 << k)
            high = (device // (1 << k)) % 2 == 1
            x = jnp.concatenate([jnp.where(high, other, x), jnp.where(high, x, other)], 1)
        return x

    gains = gather_small(jnp.stack([norm_attn, norm_ffn])).astype(f32)
    gain_attn, gain_ffn = gains[0:1], gains[1:2]
    blocks = block_of.reshape(1, tok_rows)
    for k in range(3):
        other = flip(blocks, 1 << k)
        high = (device // (1 << k)) % 2 == 1
        blocks = jnp.concatenate([jnp.where(high, other, blocks), jnp.where(high, blocks, other)], 1)

    qkv_mine = jnp.concatenate([columns_out(w, HEAD_DIM) for w in (w_query, w_key, w_value)], 2)
    qkv_w = gather_across(swap(qkv_mine, in_team).reshape(team * weight_rows, 3 * head_cols))
    if weight_rows == HEAD_DIM:
        out_w = gather_across(w_out)
    else:
        out_all = lax.all_gather(w_out, AXIS, axis=0, tiled=True)
        out_w = lax.dynamic_index_in_dim(
            out_all.reshape(heads, team, HEAD_DIM, width), mate, 1, False
        ).reshape(head_cols, width)
    gate_up = swap(jnp.concatenate([ffn_out(w_gate), ffn_out(w_up)], 2), ffn_team)
    gate_up, down_mine, qkv_w = lax.optimization_barrier((gate_up, w_down, qkv_w))

    def whole_rows(mine):
        shape = row_shape + (weight_rows, ff_cols)
        return place_pieces(data_pieces(mine), row_dims, shape).reshape(width, ff_cols)

    gate_w = whole_rows(gate_up[:, :, :ff_cols])
    up_w = whole_rows(gate_up[:, :, ff_cols:])
    down_w = place_pieces(
        data_pieces(down_mine), unit_dims, unit_shape + (ff_rows, width)
    ).reshape(ff_cols, width)

    team_tokens = gather_tokens(tokens, attn_bits).astype(f32)
    normed_attn = (team_tokens * row_scale(team_tokens) * gain_attn).astype(bf16)
    qkv = contract(normed_attn, qkv_w, 1, 0)
    cosine, sine = rope_tables(SEQ, head_cols)
    query, key, value, attended, lse, peak = attend_forward(qkv, cosine, sine, blocks, heads)
    head_peak = jnp.where(
        (jnp.arange(head_total) % team) == mate, jnp.repeat(peak[0, :heads], team), -jnp.inf
    )
    for k in range(bit_count):
        head_peak = jnp.maximum(head_peak, flip(head_peak, 1 << k))
    after_attn, normed_ffn = branch(attended, out_w, tokens, gain_ffn, attn_bits, ffn_bits)
    gate_pre = contract(normed_ffn, gate_w, 1, 0)
    up_pre = contract(normed_ffn, up_w, 1, 0)
    sigmoid_gate = jax.nn.sigmoid(gate_pre)
    silu_gate = gate_pre * sigmoid_gate
    hidden = (silu_gate * up_pre).astype(bf16)
    down_part = contract(hidden, down_w, 1, 0).astype(bf16)
    mixed = (
        after_attn
        + lax.psum_scatter(
            down_part, AXIS, scatter_dimension=0, tiled=True, axis_index_groups=ffn_team
        ).astype(f32)
    ).astype(bf16)

    team_cot = lax.all_gather(cotangent, AXIS, axis=0, tiled=True, axis_index_groups=ffn_team)
    d_down = data_sum(
        contract(hidden, team_cot, 0, 0).astype(bf16).reshape(unit_shape + (ff_rows, width)), unit_dims
    ).astype(f32)
    d_hidden = contract(team_cot, down_w, 1, 1)
    grad_gate = (d_hidden * up_pre * sigmoid_gate * (1.0 + gate_pre * (1.0 - sigmoid_gate))).astype(bf16)
    grad_up = (d_hidden * silu_gate).astype(bf16)
    d_residual, branch_grad = ffn_back(
        grad_gate, grad_up, gate_w, up_w, after_attn, cotangent, gain_ffn, ffn_bits, attn_bits
    )

    def row_sums(part):
        part = data_sum(part.astype(bf16).reshape(row_shape + (weight_rows, ff_cols)), row_dims)
        return part.reshape(team, weight_rows, ff_cols)

    d_gate_up = swap(
        jnp.concatenate(
            [row_sums(contract(normed_ffn, g, 0, 0)) for g in (grad_gate, grad_up)], 2
        ),
        ffn_team,
    )
    d_gate = ffn_home(d_gate_up[:, :, :ff_cols]).astype(f32)
    d_up = ffn_home(d_gate_up[:, :, ff_cols:]).astype(f32)
    grad_attended = contract(branch_grad, out_w, 1, 1).astype(bf16)
    grad_qkv = attend_backward(
        query, key, value, grad_attended, lse, cosine, sine, blocks, heads
    )
    out_part = contract(attended, branch_grad, 0, 0)
    if weight_rows == HEAD_DIM:
        d_out = scatter_across(out_part).astype(f32)
    else:
        spread = jnp.where(
            (jnp.arange(team) == mate)[None, :, None, None],
            out_part.reshape(heads, 1, HEAD_DIM, width), 0.0,
        ).reshape(width, width)
        d_out = lax.psum_scatter(spread, AXIS, scatter_dimension=0, tiled=True)
    d_qkv = scatter_across(contract(normed_attn, grad_qkv, 0, 0))
    d_qkv = swap(d_qkv.reshape(team, weight_rows, 3 * head_cols), in_team)
    d_query, d_key, d_value = (
        columns_back(d_qkv[:, :, i * head_cols : (i + 1) * head_cols], HEAD_DIM).astype(f32)
        for i in range(3)
    )
    d_tokens = first_back(grad_qkv, qkv_w, tokens, gain_attn, d_residual, attn_bits)

    def gain_grad(pairs, gain):
        return sum(jnp.sum(w.astype(f32) * g, 1) for w, g in pairs) / gain.astype(f32)

    d_norm_attn = gain_grad(((w_query, d_query), (w_key, d_key), (w_value, d_value)), norm_attn)
    d_norm_ffn = gain_grad(((w_gate, d_gate), (w_up, d_up)), norm_ffn)
    clip_value = clip_limit.astype(f32)
    factor = jnp.sqrt(clip_value / jnp.maximum(head_peak, clip_value))
    factors = jnp.repeat(factor, HEAD_DIM)[None, :]
    clipped_query = (w_query.astype(f32) * factors).astype(bf16)
    clipped_key = (w_key.astype(f32) * factors).astype(bf16)
    return (
        mixed, d_tokens, d_norm_attn, d_query, d_key, d_value, d_out, d_norm_ffn,
        d_gate, d_up, d_down, head_peak, clipped_query, clipped_key,
    )


def solution(mesh):
    rows, whole = P(AXIS, None), P(AXIS)
    return jax.shard_map(
        body,
        mesh=mesh,
        in_specs=(rows, whole, P(), whole, rows, rows, rows, rows, whole, rows, rows, rows, rows),
        out_specs=(
            rows, rows, whole, rows, rows, rows, rows, whole, rows, rows, rows, P(), rows, rows,
        ),
        check_vma=False,
    )
```

time: 4520 us -> 1030 us (0.23)
  waiting for transfers between devices: 3040 us -> 249 us
  Pallas kernels: 0 us -> 444 us
  matrix products: 494 us -> 131 us
  blocking collectives: 340 us -> 17.8 us
  other arithmetic: 297 us -> 35.6 us
  starting transfers between devices: 159 us -> 51.1 us
  local copies, waits for them, and re-layouts: 158 us -> 74.3 us
    reduce_scatter x2 -> x3, waiting for transfers between devices: 1900 us -> 0.02 us  [the longest x2 0.02 us: scatter_across(): lax.psum_scatter(x.astype(bf16), AXIS, scatter_dimension=0, tiled=True, a...]
    all_gather x7 -> x3, waiting for transfers between devices: 758 us -> 23.1 us  [the longest x2 23.1 us: gather_across(): return lax.all_gather(x, AXIS, axis=0, tiled=True, axis_index_groups=across)]
    pallas_call x0 -> x6, Pallas kernels: none -> 444 us  [the longest x1 133 us: branch(): pl.pallas_call(functools.partial(branch_kernel, sum_bits, spread_bits), o...]
    dot_general x74 -> x11, matrix products: 494 us -> 131 us  [contract(): lax.dot_general(left, right, (((left_dim,), (right_dim,)), ((), ())), pre...]
    pmax x1 -> x0, blocking collectives: 254 us -> none  [body(): head_peak = lax.pmax(peak_groups.reshape(head_total), 'fsdp')]
    concatenate x5 -> x11, other arithmetic: 175 us -> 3.88 us  [the longest x1 1.51 us: body(): jnp.concatenate([ffn_out(w_gate), ffn_out(w_up)], 2)]
    ppermute x40 -> x28, waiting for transfers between devices: 381 us -> 225 us  [flip(): return lax.ppermute(x, AXIS, [(i, i ^ bit) for i in range(devices)])]
    ppermute x40 -> x28, starting transfers between devices: 158 us -> 37.9 us  [flip(): return lax.ppermute(x, AXIS, [(i, i ^ bit) for i in range(devices)])]
  transfers between devices with their start and end apart: 49 -> 37, of which waited for: 21 -> 16; matrix products, arithmetic and copies ran while one was open for 12% -> 19% of each run, Pallas kernels for 0% -> 34%
where the time goes in v1:
time: 1030 us; the launch traced here: 1020 us
  Pallas kernels  444 us (43%)
  waiting for transfers between devices  249 us (24%)
  matrix products  131 us (13%)
  local copies, waits for them, and re-layouts  74.3 us (7%)
  starting transfers between devices  51.1 us (5%)
  other arithmetic  35.6 us (3%)
  blocking collectives  17.8 us (2%)
  between operations  16 us (2%)
    ppermute x28, waiting for transfers between devices, flip(): return lax.ppermute(x, AXIS, [(i, i ^ bit) for i in range(devices)])  225 us
    pallas_call x1, Pallas kernels, branch(): pl.pallas_call(functools.partial(branch_kernel, sum_bits, spread_bits), o...  133 us
    dot_general x11, matrix products, contract(): lax.dot_general(left, right, (((left_dim,), (right_dim,)), ((), ())), pre...  131 us
    pallas_call x1, Pallas kernels, ffn_back(): pl.pallas_call(functools.partial(ffn_back_kernel, sum_bits, spread_bits),...  98.9 us
    pallas_call x1, Pallas kernels, gather_tokens(): pl.pallas_call(functools.partial(tokens_kernel, bits), out_shape=jax.Shap...  60.4 us
    pallas_call x1, Pallas kernels, attend_backward(): pl.pallas_call(functools.partial(attend_backward_kernel, heads), out_shap...  53.6 us
    pallas_call x1, Pallas kernels, first_back(): pl.pallas_call(functools.partial(first_back_kernel, sum_bits), out_shape=...  50.9 us
    pallas_call x1, Pallas kernels, attend_forward(): pl.pallas_call(functools.partial(attend_forward_kernel, heads), out_shape...  47.1 us
  transfers between devices with their start and end apart: 37, of which 16 were waited for; matrix products, arithmetic and copies ran while one was open for 19% of the time, Pallas kernels for 34%

profile of v1, /device:TPU:0, one launch (start us, length us, event | category | flops | bytes accessed | tf_op | source)
XLA Modules:
  0.0 1017.9 jit_solution(5368567920579982705)
XLA Ops:
  12.5 17.8 %all_to_all.20 = bf16[8,64,768]{2,1,0:T(8,128)(2,1)} all-to-all(bf16[8,64,768]{2,1,0:T(8,128)(2,1)S(1)} %pad_maximum_fusion.2), channel_id=1, replica_groups={{0,1,2,3,4,5,6,7},{8,9,10,11,12,13,14,15},{16,17,18,19,20,21,22,23},{24..., dimensions={0} | all-to-all | bytes 1572864 | tf_op jit(solution)/shard_map/all_to_all | solution.py:602
  37.4 4.4 all-to-all-start
  42.5 60.4 %gather_tokens.1 = bf16[2048,2048]{1,0:T(8,128)(2,1)} custom-call(bf16[256,2048]{1,0:T(8,128)(2,1)} %tokens_ref.1), custom_call_target="tpu_custom_call" | custom-call | bytes 100000000 | tf_op jit(solution)/shard_map/gather_tokens/pallas_call | solution.py:428
  103.0 5.1 fusion
  121.5 3.0 collective-permute-start.4
  129.1 2.8 collective-permute-start.8
  134.1 2.7 collective-permute-start.14
  136.8 10.9 %fusion.12.qkv_ref = f32[2048,768]{1,0:T(8,128)} fusion(bf16[2048,768]{1,0:T(8,128)(2,1)S(1)} %copy-done.25, bf16[2048,2048]{1,0:T(8,128)(2,1)} %gather_tokens.1, f32[2048]{0:T(1024)S(1)} %bitcast.171, f32[2048]{0:T(1024)S(1)} %add_rsqrt_fusion), kind=kOutput, calls=%fused_computation.27 | convolution fusion | flops 6459228160 | bytes 17842176 | tf_op jit(solution)/shard_map/dot_general | solution.py:23
  147.7 47.1 %attend_forward.1 = (bf16[2048,256]{1,0:T(8,128)(2,1)}, bf16[2048,256]{1,0:T(8,128)(2,1)}, bf16[2048,256]{1,0:T(8,128)(2,1)}, bf16[2048,256]{1,0:T(8,128)(2,1)}, f32[2048,128]{1,0:T(8,128)}, /*index=5*/f32[8,128]{1,0:T(8,128)}) custom-call(f32[2048,768]{1,0:T(8,128)} %fusion.12.qkv_ref, f32[2048,256]{1,0:T(8,128)} %copy.64.cos_ref, ...), custom_call_target="tpu_custom_call" | custom-call | flops 8589934592 | bytes 12582912 | tf_op jit(solution)/shard_map/attend_forward/pallas_call | solution.py:114
  194.8 23.1 %all-gather.6.cloned.1.call-done.right_ref = bf16[256,2048]{1,0:T(8,128)(2,1)} async-done(((bf16[64,2048]{1,0:T(8,128)(2,1)}), bf16[256,2048]{1,0:T(8,128)(2,1)}) %all-gather.6.cloned.1.call-update) | async-done | bytes 1048592 | tf_op jit(solution)/shard_map/all_gather | solution.py:594
  217.9 132.5 %attention_branch.1 = (f32[256,2048]{1,0:T(8,128)}, bf16[2048,2048]{1,0:T(8,128)(2,1)}) custom-call(bf16[2048,256]{1,0:T(8,128)(2,1)} %get-tuple-element.28.left_ref, bf16[256,2048]{1,0:T(8,128)(2,1)} %all-gather.6.cloned.1.call-done.right_ref, bf16[256,2048]{1,0:T(8,128)(2,1)} %tokens_ref.1, f32[1,2048]{1,0:T(1,128)} %get-tuple-element.56.gain_ref), custom_call_target="tpu_custom_call" | custom-call | flops 2147483648 | bytes 250000000 | tf_op jit(solution)/shard_map/attention_branch/pallas_call | solution.py:467
  367.4 14.0 %collective-permute-done.15 = bf16[256,2048]{1,0:T(8,128)(2,1)S(1)} collective-permute-done((bf16[256,2048]{1,0:T(8,128)(2,1)S(1)}, bf16[256,2048]{1,0:T(8,128)(2,1)S(1)}, u32[]{:S(2)}, u32[]{:S(2)}) %collective-permute-start.15) | collective-permute-done | bytes 1048608 | tf_op jit(solution)/shard_map/ppermute | solution.py:591
  382.4 21.4 %collective-permute-done.10 = bf16[8,64,1024]{2,1,0:T(8,128)(2,1)S(1)} collective-permute-done((bf16[8,64,1024]{2,1,0:T(8,128)(2,1)}, bf16[8,64,1024]{2,1,0:T(8,128)(2,1)S(1)}, u32[]{:S(2)}, u32[]{:S(2)}) %collective-permute-start.10) | collective-permute-done | bytes 1048608 | tf_op jit(solution)/shard_map/ppermute | solution.py:591
  404.0 22.4 %collective-permute-done.13 = bf16[8,64,1024]{2,1,0:T(8,128)(2,1)S(1)} collective-permute-done((bf16[8,64,1024]{2,1,0:T(8,128)(2,1)}, bf16[8,64,1024]{2,1,0:T(8,128)(2,1)S(1)}, u32[]{:S(2)}, u32[]{:S(2)}) %collective-permute-start.13) | collective-permute-done | bytes 1048608 | tf_op jit(solution)/shard_map/ppermute | solution.py:591
  426.4 21.8 %collective-permute-done.16 = bf16[256,2048]{1,0:T(8,128)(2,1)S(1)} collective-permute-done((bf16[256,2048]{1,0:T(8,128)(2,1)}, bf16[256,2048]{1,0:T(8,128)(2,1)S(1)}, u32[]{:S(2)}, u32[]{:S(2)}) %collective-permute-start.16) | collective-permute-done | bytes 1048608 | tf_op jit(solution)/shard_map/ppermute | solution.py:591
  449.3 10.9 %fusion.27 = f32[2048,1024]{1,0:T(8,128)} fusion(bf16[2048,2048]{1,0:T(8,128)(2,1)S(1)} %bitcast.180, bf16[2048,1024]{1,0:T(8,128)(2,1)S(1)} %bitcast.153), kind=kOutput, calls=%fused_computation.119 | convolution fusion | flops 8589934592 | bytes 20971520 | tf_op jit(solution)/shard_map/dot_general | solution.py:23
  460.2 11.1 %fusion.28 = f32[2048,1024]{1,0:T(8,128)} fusion(bf16[2048,2048]{1,0:T(8,128)(2,1)S(1)} %bitcast.180, bf16[2048,1024]{1,0:T(8,128)(2,1)S(1)} %bitcast.151), kind=kOutput, calls=%fused_computation.120 | convolution fusion | flops 8589934592 | bytes 20971520 | tf_op jit(solution)/shard_map/dot_general | solution.py:23
  471.4 21.9 %fusion.6 = (bf16[2048,1024]{1,0:T(8,128)(2,1)}, bf16[2048,1024]{1,0:T(8,128)(2,1)}, bf16[2048,1024]{1,0:T(8,128)(2,1)}) fusion(f32[2048,1024]{1,0:T(8,128)} %fusion.27, f32[2048,1024]{1,0:T(8,128)} %fusion.28, bf16[1024,2048]{1,0:T(8,128)(2,1)} %bitcast.35, bf16[2048,2048]{1,0:T(8,128)(2,1)} %all-gather.8.cloned.1.call-done), kind=kOutput, calls=%fused_computation.10 | convolution fusion | flops 8621391872 | bytes 41943040 | tf_op jit(solution)/shard_map/dot_general | solution.py:23
  493.3 98.9 %ffn_back.1 = (f32[256,2048]{1,0:T(8,128)}, bf16[2048,2048]{1,0:T(8,128)(2,1)}) custom-call(bf16[2048,1024]{1,0:T(8,128)(2,1)} %get-tuple-element.43.gate_ref, bf16[2048,1024]{1,0:T(8,128)(2,1)} %get-tuple-element.42.up_ref, bf16[2048,1024]{1,0:T(8,128)(2,1)} %bitcast.154, bf16[2048,1024]{1,0:T(8,128)(2,1)} %bitcast.152, ...), custom_call_target="tpu_custom_call" | custom-call | flops 17179869184 | bytes 250000000 | tf_op jit(solution)/shard_map/ffn_back/pallas_call | solution.py:514
  592.2 6.8 convolution_convert_fusion.5
  599.2 6.7 convolution_convert_fusion.6.grad_ref
  605.9 53.6 %attend_backward.1.left_ref = bf16[2048,768]{1,0:T(8,128)(2,1)} custom-call(bf16[2048,256]{1,0:T(8,128)(2,1)} %get-tuple-element.33.q_ref, bf16[2048,256]{1,0:T(8,128)(2,1)} %get-tuple-element.34.k_ref, bf16[2048,256]{1,0:T(8,128)(2,1)} %get-tuple-element.35.v_ref, bf16[2048,256]{1,0:T(8,128)(2,1)} %convolution_convert_fusion.6.grad_ref, ...), custom_call_target="tpu_custom_call" | custom-call | flops 21474836480 | bytes 12582912 | tf_op jit(solution)/shard_map/attend_backward/pallas_call | solution.py:190
  659.5 12.0 %convolution_convert_fusion.4 = bf16[2048,768]{1,0:T(8,128)(2,1)} fusion(bf16[2048,768]{1,0:T(8,128)(2,1)} %attend_backward.1.left_ref, bf16[2048,2048]{1,0:T(8,128)(2,1)} %gather_tokens.1, f32[2048]{0:T(1024)S(1)} %bitcast.172, f32[2048]{0:T(1024)S(1)} %add_rsqrt_fusion), kind=kOutput, calls=%fused_computation.24 | convolution fusion | flops 6460801024 | bytes 14696448 | tf_op jit(solution)/shard_map/dot_general | solution.py:23
  671.6 13.9 %convolution_convert_fusion = bf16[2048,2048]{1,0:T(8,128)(2,1)} fusion(bf16[2048,1024]{1,0:T(8,128)(2,1)} %get-tuple-element.44, bf16[1024,2048]{1,0:T(8,128)(2,1)} %bitcast.35), kind=kOutput, calls=%fused_computation.14 | convolution fusion | flops 8594128896 | bytes 16777216 | tf_op jit(solution)/shard_map/dot_general | solution.py:23
  685.5 12.8 %convolution_convert_fusion.2 = bf16[2048,1024]{1,0:T(8,128)(2,1)S(1)} fusion(bf16[2048,2048]{1,0:T(8,128)(2,1)} %get-tuple-element.30, bf16[2048,1024]{1,0:T(8,128)(2,1)} %get-tuple-element.42.up_ref), kind=kOutput, calls=%fused_computation.22 | convolution fusion | flops 8592031744 | bytes 16777216 | tf_op jit(solution)/shard_map/dot_general | solution.py:23
  702.7 11.9 %convolution_convert_fusion.3 = bf16[2048,1024]{1,0:T(8,128)(2,1)S(1)} fusion(bf16[2048,2048]{1,0:T(8,128)(2,1)} %get-tuple-element.30, bf16[2048,1024]{1,0:T(8,128)(2,1)S(1)} %copy-done.28), kind=kOutput, calls=%fused_computation.23 | convolution fusion | flops 8592031744 | bytes 16777216 | tf_op jit(solution)/shard_map/dot_general | solution.py:23
  718.9 31.3 %collective-permute-done.19 = bf16[2,2,2,2,64,1024]{5,4,3,2,1,0:T(8,128)(2,1)} collective-permute-done((bf16[2,2,2,2,64,1024]{5,4,3,2,1,0:T(8,128)(2,1)}, bf16[2,2,2,2,64,1024]{5,4,3,2,1,0:T(8,128)(2,1)}, u32[]{:S(2)}, u32[]{:S(2)}) %collective-permute-start.19) | collective-permute-done | bytes 2097184 | tf_op jit(solution)/shard_map/ppermute | solution.py:591
  750.2 3.2 fusion.9
  753.6 40.9 %collective-permute-done.17 = bf16[2,2,2,2,64,1024]{5,4,3,2,1,0:T(8,128)(2,1)S(1)} collective-permute-done((bf16[2,2,2,2,64,1024]{5,4,3,2,1,0:T(8,128)(2,1)}, bf16[2,2,2,2,64,1024]{5,4,3,2,1,0:T(8,128)(2,1)S(1)}, u32[]{:S(2)}, u32[]{:S(2)}) %collective-permute-start.17) | collective-permute-done | bytes 2097184 | tf_op jit(solution)/shard_map/ppermute | solution.py:591
  795.7 11.9 %convolution_convert_fusion.1 = bf16[1024,2048]{1,0:T(8,128)(2,1)S(1)} fusion(bf16[2048,1024]{1,0:T(8,128)(2,1)S(1)} %copy-done.27, bf16[2048,2048]{1,0:T(8,128)(2,1)} %all-gather.8.cloned.1.call-done), kind=kOutput, calls=%fused_computation.21 | convolution fusion | flops 8592031744 | bytes 16777216 | tf_op jit(solution)/shard_map/dot_general | solution.py:23
  809.1 2.7 collective-permute-done.20
  812.2 33.6 %collective-permute-done.18 = bf16[2,2,2,64,1024]{4,3,2,1,0:T(8,128)(2,1)S(1)} collective-permute-done((bf16[2,2,2,64,1024]{4,3,2,1,0:T(8,128)(2,1)S(1)}, bf16[2,2,2,64,1024]{4,3,2,1,0:T(8,128)(2,1)S(1)}, u32[]{:S(2)}, u32[]{:S(2)}) %collective-permute-start.18) | collective-permute-done | bytes 1048608 | tf_op jit(solution)/shard_map/ppermute | solution.py:591
  847.7 4.4 all-to-all-start.3
  855.2 3.0 fusion.8
  862.2 8.2 collective-permute-done.24
  871.1 2.8 collective-permute-done.25
  874.0 8.9 collective-permute-start.26
  882.8 15.4 %collective-permute-done.26 = f32[32]{0:T(128)S(1)} collective-permute-done((f32[32]{0:T(128)S(1)}, f32[32]{0:T(128)S(1)}, u32[]{:S(2)}, u32[]{:S(2)}) %collective-permute-start.26) | collective-permute-done | bytes 160 | tf_op jit(solution)/shard_map/ppermute | solution.py:591
  900.7 6.2 collective-permute-done.27
  907.5 50.9 %first_back.1 = f32[256,2048]{1,0:T(8,128)} custom-call(bf16[2048,768]{1,0:T(8,128)(2,1)} %attend_backward.1.left_ref, bf16[2048,768]{1,0:T(8,128)(2,1)} %all-gather.4.cloned.1.call-done.right_ref, bf16[256,2048]{1,0:T(8,128)(2,1)} %tokens_ref.1, f32[1,2048]{1,0:T(1,128)} %copy-done.19, f32[256,2048]{1,0:T(8,128)} %get-tuple-element.38.residual_ref), custom_call_target="tpu_custom_call" | custom-call | flops 6442450944 | bytes 150000000 | tf_op jit(solution)/shard_map/first_back/pallas_call | solution.py:551
  961.9 4.2 all-to-all-start.2
  966.1 3.3 slice_convert_fusion
  969.5 4.0 reshape.248
  973.4 4.3 copy.82
  977.7 3.3 reshape.241
  981.0 2.8 reshape.249
  983.8 4.4 copy.83
  988.2 3.5 reshape.242
  (225 shorter events, 98.7 us)
Async XLA Ops:
  7.2 119.9 %all-gather.4.cloned.1.call-start = ((), (), s32[]{:S(2)}) async-start(), calls=%async_computation.7 | async-start | bytes 3932160 | tf_op jit(solution)/shard_map/all_gather | solution.py:594
  12.5 21.0 %copy-start.8 = (bf16[64,8192]{1,0:T(8,128)(2,1)S(1)}, bf16[64,8192]{1,0:T(8,128)(2,1)}, u32[]{:S(2)}) copy-start(bf16[64,8192]{1,0:T(8,128)(2,1)} %param.22) | copy-start | bytes 3145732
  30.3 187.6 %all-gather.6.cloned.1.call-start = ((), (), s32[]{:S(2)}) async-start(), calls=%async_computation.8 | async-start | bytes 1310720 | tf_op jit(solution)/shard_map/all_gather | solution.py:594
  37.4 89.7 %all-to-all-start = ((bf16[8,64,2048]{2,1,0:T(8,128)(2,1)}), bf16[8,64,2048]{2,1,0:T(8,128)(2,1)}, u32[]{:S(2)}, u32[]{:S(2)}) async-start(bf16[8,64,2048]{2,1,0:T(8,128)(2,1)} %pad_maximum_fusion), calls=%async_computation | async-start | bytes 4194304 | tf_op jit(solution)/shard_map/all_to_all | solution.py:602
  41.7 429.6 %all-gather.8.cloned.1.call-start = ((), (), s32[]{:S(2)}) async-start(), calls=%async_computation.10 | async-start | bytes 9437184 | tf_op jit(solution)/shard_map/all_gather | solution.py:720
  41.8 67.5 %collective-permute-start = (bf16[2,64]{1,0:T(2,128)(2,1)S(1)}, bf16[2,64]{1,0:T(2,128)(2,1)S(1)}, u32[]{:S(2)}, u32[]{:S(2)}) collective-permute-start(bf16[2,64]{1,0:T(2,128)(2,1)S(1)} %pad_maximum_fusion.8), channel_id=1, source_target_pairs={{0,1},{1,0},{2,3},{3,2},{4,5},{5,4},{6,7},{7,6},{8,9},{9,8},{10,11... | collective-permute-start | bytes 776 | tf_op jit(solution)/shard_map/ppermute | solution.py:591
  42.2 72.6 %collective-permute-start.5 = (s32[1,256]{1,0:T(1,128)S(1)}, s32[1,256]{1,0:T(1,128)S(1)}, u32[]{:S(2)}, u32[]{:S(2)}) collective-permute-start(s32[1,256]{1,0:T(1,128)S(1)} %bitcast.177), channel_id=1, source_target_pairs={{0,1},{1,0},{2,3},{3,2},{4,5},{5,4},{6,7},{7,6},{8,9},{9,8},{10,11... | collective-permute-start | bytes 3080 | tf_op jit(solution)/shard_map/ppermute | solution.py:591
  42.5 915.9 %reduce-scatter.8.cloned.1.call-start = ((), (), s32[]{:S(2)}) async-start(), calls=%async_computation.12 | async-start | bytes 1310720 | tf_op jit(solution)/shard_map/reduce_scatter | solution.py:597
  109.5 4.7 collective-permute-start.1
  112.3 21.8 %copy-start.17 = (bf16[256,2048]{1,0:T(8,128)(2,1)S(1)}, bf16[256,2048]{1,0:T(8,128)(2,1)}, u32[]{:S(2)}) copy-start(bf16[256,2048]{1,0:T(8,128)(2,1)} %param.24) | copy-start | bytes 3145732
  114.2 3.6 collective-permute-start.2
  114.8 5.1 collective-permute-start.6
  117.8 3.7 collective-permute-start.3
  119.9 4.6 collective-permute-start.7
  121.5 5.0 collective-permute-start.4
  127.1 532.4 %copy-start.19 = (f32[1,2048]{1,0:T(1,128)}, f32[1,2048]{1,0:T(1,128)S(1)}, u32[]{:S(2)}) copy-start(f32[1,2048]{1,0:T(1,128)S(1)} %get-tuple-element.57.gain_ref) | copy-start | bytes 24580
  129.1 226.2 %collective-permute-start.8 = (bf16[8,64,1024]{2,1,0:T(8,128)(2,1)S(1)}, bf16[8,64,1024]{2,1,0:T(8,128)(2,1)}, u32[]{:S(2)}, u32[]{:S(2)}) collective-permute-start(bf16[8,64,1024]{2,1,0:T(8,128)(2,1)S(1)} %get-tuple-element.47), channel_id=1, source_target_pairs={{0,16},{1,17},{2,18},{3,19},{4,20},{5,21},{6,22},{7,23},{8,24},{9,... | collective-permute-start | bytes 3145736 | tf_op jit(solution)/shard_map/ppermute | solution.py:591
  131.9 232.2 %collective-permute-start.9 = (bf16[8,64,1024]{2,1,0:T(8,128)(2,1)S(1)}, bf16[8,64,1024]{2,1,0:T(8,128)(2,1)}, u32[]{:S(2)}, u32[]{:S(2)}) collective-permute-start(bf16[8,64,1024]{2,1,0:T(8,128)(2,1)S(1)} %get-tuple-element.47), channel_id=1, source_target_pairs={{0,4},{1,5},{2,6},{3,7},{4,0},{5,1},{6,2},{7,3},{8,12},{9,13},{10,... | collective-permute-start | bytes 3145736 | tf_op jit(solution)/shard_map/ppermute | solution.py:591
  132.3 224.6 %collective-permute-start.11 = (bf16[8,64,1024]{2,1,0:T(8,128)(2,1)S(1)}, bf16[8,64,1024]{2,1,0:T(8,128)(2,1)}, u32[]{:S(2)}, u32[]{:S(2)}) collective-permute-start(bf16[8,64,1024]{2,1,0:T(8,128)(2,1)S(1)} %get-tuple-element.48), channel_id=1, source_target_pairs={{0,16},{1,17},{2,18},{3,19},{4,20},{5,21},{6,22},{7,23},{8,24},{9,... | collective-permute-start | bytes 3145736 | tf_op jit(solution)/shard_map/ppermute | solution.py:591
  132.6 233.4 %collective-permute-start.12 = (bf16[8,64,1024]{2,1,0:T(8,128)(2,1)S(1)}, bf16[8,64,1024]{2,1,0:T(8,128)(2,1)}, u32[]{:S(2)}, u32[]{:S(2)}) collective-permute-start(bf16[8,64,1024]{2,1,0:T(8,128)(2,1)S(1)} %get-tuple-element.48), channel_id=1, source_target_pairs={{0,4},{1,5},{2,6},{3,7},{4,0},{5,1},{6,2},{7,3},{8,12},{9,13},{10,... | collective-permute-start | bytes 3145736 | tf_op jit(solution)/shard_map/ppermute | solution.py:591
  134.1 223.3 %collective-permute-start.14 = (bf16[256,2048]{1,0:T(8,128)(2,1)S(1)}, bf16[256,2048]{1,0:T(8,128)(2,1)}, u32[]{:S(2)}, u32[]{:S(2)}) collective-permute-start(bf16[256,2048]{1,0:T(8,128)(2,1)S(1)} %copy-done.17), channel_id=1, source_target_pairs={{0,16},{1,17},{2,18},{3,19},{4,20},{5,21},{6,22},{7,23},{8,24},{9,... | collective-permute-start | bytes 3145736 | tf_op jit(solution)/shard_map/ppermute | solution.py:591
  355.3 26.1 %collective-permute-start.15 = (bf16[256,2048]{1,0:T(8,128)(2,1)S(1)}, bf16[256,2048]{1,0:T(8,128)(2,1)S(1)}, u32[]{:S(2)}, u32[]{:S(2)}) collective-permute-start(bf16[256,2048]{1,0:T(8,128)(2,1)S(1)} %copy-done.17), channel_id=1, source_target_pairs={{0,4},{1,5},{2,6},{3,7},{4,0},{5,1},{6,2},{7,3},{8,12},{9,13},{10,... | collective-permute-start | bytes 3145736 | tf_op jit(solution)/shard_map/ppermute | solution.py:591
  356.8 47.0 %collective-permute-start.10 = (bf16[8,64,1024]{2,1,0:T(8,128)(2,1)}, bf16[8,64,1024]{2,1,0:T(8,128)(2,1)S(1)}, u32[]{:S(2)}, u32[]{:S(2)}) collective-permute-start(bf16[8,64,1024]{2,1,0:T(8,128)(2,1)} %collective-permute-done.8), channel_id=1, source_target_pairs={{0,4},{1,5},{2,6},{3,7},{4,0},{5,1},{6,2},{7,3},{8,12},{9,13},{10,... | collective-permute-start | bytes 3145736 | tf_op jit(solution)/shard_map/ppermute | solution.py:591
  357.4 68.9 %collective-permute-start.13 = (bf16[8,64,1024]{2,1,0:T(8,128)(2,1)}, bf16[8,64,1024]{2,1,0:T(8,128)(2,1)S(1)}, u32[]{:S(2)}, u32[]{:S(2)}) collective-permute-start(bf16[8,64,1024]{2,1,0:T(8,128)(2,1)} %collective-permute-done.11), channel_id=1, source_target_pairs={{0,4},{1,5},{2,6},{3,7},{4,0},{5,1},{6,2},{7,3},{8,12},{9,13},{10,... | collective-permute-start | bytes 3145736 | tf_op jit(solution)/shard_map/ppermute | solution.py:591
  361.2 88.1 %slice-start = ((s8[8388608]{0:T(1024)(128)(4,1)}), s8[4194304]{0:T(1024)(128)(4,1)S(1)}, s32[]{:S(2)}) async-start(s8[8388608]{0:T(1024)(128)(4,1)} %bitcast.179), calls=%async_computation.13 | async-start | bytes 8388608
  364.1 84.2 %collective-permute-start.16 = (bf16[256,2048]{1,0:T(8,128)(2,1)}, bf16[256,2048]{1,0:T(8,128)(2,1)S(1)}, u32[]{:S(2)}, u32[]{:S(2)}) collective-permute-start(bf16[256,2048]{1,0:T(8,128)(2,1)} %collective-permute-done.14), channel_id=1, source_target_pairs={{0,4},{1,5},{2,6},{3,7},{4,0},{5,1},{6,2},{7,3},{8,12},{9,13},{10,... | collective-permute-start | bytes 3145736 | tf_op jit(solution)/shard_map/ppermute | solution.py:591
  367.4 81.9 %slice-start.1 = ((s8[8388608]{0:T(1024)(128)(4,1)}), s8[4194304]{0:T(1024)(128)(4,1)S(1)}, s32[]{:S(2)}) async-start(s8[8388608]{0:T(1024)(128)(4,1)} %bitcast.179), calls=%async_computation.14 | async-start | bytes 8388608
  404.0 56.3 %copy-start.7 = (bf16[2,2,2,2,2,64,1024]{6,5,4,3,2,1,0:T(8,128)(2,1)}, bf16[2,2,2,2,2,64,1024]{6,5,4,3,2,1,0:T(8,128)(2,1)S(1)}, u32[]{:S(2)}) copy-start(bf16[2,2,2,2,2,64,1024]{6,5,4,3,2,1,0:T(8,128)(2,1)S(1)} %constant_dynamic-update-slice_fusion.4) | copy-start | bytes 12582916
  426.4 33.8 %copy-start.6 = (bf16[2,2,2,2,2,64,1024]{6,5,4,3,2,1,0:T(8,128)(2,1)}, bf16[2,2,2,2,2,64,1024]{6,5,4,3,2,1,0:T(8,128)(2,1)S(1)}, u32[]{:S(2)}) copy-start(bf16[2,2,2,2,2,64,1024]{6,5,4,3,2,1,0:T(8,128)(2,1)S(1)} %constant_dynamic-update-slice_fusion) | copy-start | bytes 12582916
  493.2 99.0 %copy-start.11 = (bf16[2048,256]{1,0:T(8,128)(2,1)S(1)}, bf16[2048,256]{1,0:T(8,128)(2,1)}, u32[]{:S(2)}) copy-start(bf16[2048,256]{1,0:T(8,128)(2,1)} %get-tuple-element.28.left_ref) | copy-start | bytes 3145732
  599.1 362.8 %reduce-scatter.6.cloned.1.call-start = ((), (), s32[]{:S(2)}) async-start(), calls=%async_computation.11 | async-start | bytes 3932160 | tf_op jit(solution)/shard_map/reduce_scatter | solution.py:597
  671.5 335.4 %reduce-scatter.4.cloned.1.call-start = ((), (), s32[]{:S(2)}) async-start(), calls=%async_computation.9 | async-start | bytes 9437184 | tf_op jit(solution)/shard_map/reduce_scatter | solution.py:715
  701.4 48.8 %collective-permute-start.19 = (bf16[2,2,2,2,64,1024]{5,4,3,2,1,0:T(8,128)(2,1)}, bf16[2,2,2,2,64,1024]{5,4,3,2,1,0:T(8,128)(2,1)}, u32[]{:S(2)}, u32[]{:S(2)}) collective-permute-start(bf16[2,2,2,2,64,1024]{5,4,3,2,1,0:T(8,128)(2,1)} %dynamic-slice_bitcast_fusion.1), channel_id=1, source_target_pairs={{0,4},{1,5},{2,6},{3,7},{4,0},{5,1},{6,2},{7,3},{8,12},{9,13},{10,... | collective-permute-start | bytes 6291464 | tf_op jit(solution)/shard_map/ppermute | solution.py:591
  718.1 76.4 %collective-permute-start.17 = (bf16[2,2,2,2,64,1024]{5,4,3,2,1,0:T(8,128)(2,1)}, bf16[2,2,2,2,64,1024]{5,4,3,2,1,0:T(8,128)(2,1)S(1)}, u32[]{:S(2)}, u32[]{:S(2)}) collective-permute-start(bf16[2,2,2,2,64,1024]{5,4,3,2,1,0:T(8,128)(2,1)} %dynamic-slice_bitcast_fusion.2), channel_id=1, source_target_pairs={{0,4},{1,5},{2,6},{3,7},{4,0},{5,1},{6,2},{7,3},{8,12},{9,13},{10,... | collective-permute-start | bytes 6291464 | tf_op jit(solution)/shard_map/ppermute | solution.py:591
  718.9 75.6 %copy-start.4 = (bf16[2048,1024]{1,0:T(8,128)(2,1)S(1)}, bf16[2048,1024]{1,0:T(8,128)(2,1)}, u32[]{:S(2)}) copy-start(bf16[2048,1024]{1,0:T(8,128)(2,1)} %copy-done.3) | copy-start | bytes 12582916
  753.5 42.2 %copy-start.27 = (bf16[2048,1024]{1,0:T(8,128)(2,1)S(1)}, bf16[2048,1024]{1,0:T(8,128)(2,1)}, u32[]{:S(2)}) copy-start(bf16[2048,1024]{1,0:T(8,128)(2,1)} %get-tuple-element.44) | copy-start | bytes 12582916
  753.5 58.3 %collective-permute-start.20 = (bf16[2,2,2,64,1024]{4,3,2,1,0:T(8,128)(2,1)S(1)}, bf16[2,2,2,64,1024]{4,3,2,1,0:T(8,128)(2,1)S(1)}, u32[]{:S(2)}, u32[]{:S(2)}) collective-permute-start(bf16[2,2,2,64,1024]{4,3,2,1,0:T(8,128)(2,1)S(1)} %dynamic-slice_bitcast_fusion.4), channel_id=1, source_target_pairs={{0,16},{1,17},{2,18},{3,19},{4,20},{5,21},{6,22},{7,23},{8,24},{9,... | collective-permute-start | bytes 3145736 | tf_op jit(solution)/shard_map/ppermute | solution.py:591
  795.6 50.2 %collective-permute-start.18 = (bf16[2,2,2,64,1024]{4,3,2,1,0:T(8,128)(2,1)S(1)}, bf16[2,2,2,64,1024]{4,3,2,1,0:T(8,128)(2,1)S(1)}, u32[]{:S(2)}, u32[]{:S(2)}) collective-permute-start(bf16[2,2,2,64,1024]{4,3,2,1,0:T(8,128)(2,1)S(1)} %dynamic-slice_bitcast_fusion.5), channel_id=1, source_target_pairs={{0,16},{1,17},{2,18},{3,19},{4,20},{5,21},{6,22},{7,23},{8,24},{9,... | collective-permute-start | bytes 3145736 | tf_op jit(solution)/shard_map/ppermute | solution.py:591
  807.6 38.6 %copy-start.2 = (bf16[1024,2048]{1,0:T(8,128)(2,1)}, bf16[1024,2048]{1,0:T(8,128)(2,1)S(1)}, u32[]{:S(2)}) copy-start(bf16[1024,2048]{1,0:T(8,128)(2,1)S(1)} %convolution_convert_fusion.1) | copy-start | bytes 12582916
  807.8 47.4 %collective-permute-start.21 = (bf16[2,256,2048]{2,1,0:T(8,128)(2,1)S(1)}, bf16[2,256,2048]{2,1,0:T(8,128)(2,1)}, u32[]{:S(2)}, u32[]{:S(2)}) collective-permute-start(bf16[2,256,2048]{2,1,0:T(8,128)(2,1)S(1)} %dynamic-slice_bitcast_fusion), channel_id=1, source_target_pairs={{0,4},{1,5},{2,6},{3,7},{4,0},{5,1},{6,2},{7,3},{8,12},{9,13},{10,... | collective-permute-start | bytes 6291464 | tf_op jit(solution)/shard_map/ppermute | solution.py:591
  847.7 114.2 %all-to-all-start.3 = ((bf16[8,64,2048]{2,1,0:T(8,128)(2,1)}), bf16[8,64,2048]{2,1,0:T(8,128)(2,1)}, u32[]{:S(2)}, u32[]{:S(2)}) async-start(bf16[8,64,2048]{2,1,0:T(8,128)(2,1)} %pad_maximum_fusion.1), calls=%async_computation.6 | async-start | bytes 4194304 | tf_op jit(solution)/shard_map/all_to_all | solution.py:602
  853.0 8.8 collective-permute-start.23
  859.3 101.0 %collective-permute-start.22 = (bf16[256,2048]{1,0:T(8,128)(2,1)}, bf16[256,2048]{1,0:T(8,128)(2,1)S(1)}, u32[]{:S(2)}, u32[]{:S(2)}) collective-permute-start(bf16[256,2048]{1,0:T(8,128)(2,1)} %dynamic-slice_bitcast_fusion.3), channel_id=1, source_target_pairs={{0,16},{1,17},{2,18},{3,19},{4,20},{5,21},{6,22},{7,23},{8,24},{9,... | collective-permute-start | bytes 3145736 | tf_op jit(solution)/shard_map/ppermute | solution.py:591
  861.8 8.6 collective-permute-start.24
  870.4 3.5 collective-permute-start.25
  874.0 24.3 %collective-permute-start.26 = (f32[32]{0:T(128)S(1)}, f32[32]{0:T(128)S(1)}, u32[]{:S(2)}, u32[]{:S(2)}) collective-permute-start(f32[32]{0:T(128)S(1)} %max.21), channel_id=1, source_target_pairs={{0,8},{1,9},{2,10},{3,11},{4,12},{5,13},{6,14},{7,15},{8,0},{9,1},... | collective-permute-start | bytes 392 | tf_op jit(solution)/shard_map/ppermute | solution.py:591
  898.2 8.6 collective-permute-start.27
  961.9 33.5 %all-to-all-start.2 = ((bf16[8,64,768]{2,1,0:T(8,128)(2,1)}), bf16[8,64,768]{2,1,0:T(8,128)(2,1)}, u32[]{:S(2)}, u32[]{:S(2)}) async-start(bf16[8,64,768]{2,1,0:T(8,128)(2,1)} %bitcast.170), calls=%async_computation.4 | async-start | bytes 1572864 | tf_op jit(solution)/shard_map/all_to_all | solution.py:602
  (20 other events, 119.7 us)
Sparse Core Ops, SparseCore 0:
  30.4 82.8 all-gather.3
  114.9 102.9 all-gather.5
  219.5 117.8 all-gather.7
  599.2 24.5 reduce-scatter.7
  671.6 57.7 reduce-scatter.5
  731.7 96.0 reduce-scatter.3

commit v2 on v1

v2 whole, which is shorter than its diff:
```python
import functools

import jax
import jax.numpy as jnp
from jax import lax
from jax.experimental import pallas as pl
from jax.experimental.pallas import tpu as pltpu
from jax.sharding import PartitionSpec as P

HEAD_DIM = 64
SEQ = 2048
BLOCK = 256
AXIS = "fsdp"
MESH = pl.DeviceIdType.MESH

epsilon = 1e-05
rope_base = 130000.0
bf16 = jnp.bfloat16
f32 = jnp.float32
vmem = pl.BlockSpec(memory_space=pltpu.VMEM)
anywhere = pl.BlockSpec(memory_space=pl.ANY)


def contract(left, right, left_dim, right_dim):
    return lax.dot_general(
        left, right, (((left_dim,), (right_dim,)), ((), ())), preferred_element_type=f32
    )


def rope_tables(length, width):
    half_dim = HEAD_DIM // 2
    inverse = rope_base ** (-jnp.arange(half_dim, dtype=f32) * 2.0 / HEAD_DIM)
    angles = jnp.arange(length, dtype=f32)[:, None] * inverse[None, :]
    cosine, sine = jnp.cos(angles), jnp.sin(angles)
    repeats = width // HEAD_DIM
    return (
        jnp.tile(jnp.concatenate([cosine, cosine], 1), (1, repeats)),
        jnp.tile(jnp.concatenate([-sine, sine], 1), (1, repeats)),
    )


def swap_halves(rows):
    width = rows.shape[1]
    half = HEAD_DIM // 2
    lane = lax.broadcasted_iota(jnp.int32, rows.shape, 1)
    return jnp.where(
        lane % HEAD_DIM < half, pltpu.roll(rows, width - half, 1), pltpu.roll(rows, half, 1)
    )


PAIR = 2 * HEAD_DIM


def head_mask(shape, head):
    lane = lax.broadcasted_iota(jnp.int32, shape, 1)
    return (lane >= head * HEAD_DIM) & (lane < (head + 1) * HEAD_DIM)


def masked_scores(query, key_ref, row_ref, col_ref, q0, cols):
    tail = min(2 * BLOCK, cols)
    scores = contract(query, key_ref[0:cols, :], 1, 1)
    shown = row_ref[:, pl.ds(cols - tail, tail)] <= col_ref[pl.ds(q0, BLOCK), :]
    hidden = jnp.where(shown, scores[:, cols - tail :], -jnp.inf)
    return jnp.concatenate([scores[:, : cols - tail], hidden], 1) if tail < cols else hidden


def attend_forward_kernel(
    qkv_ref, cos_ref, sin_ref, row_ref, col_ref, q_ref, k_ref, v_ref, out_ref, lse_ref, peak_ref
):
    pairs, length, _ = q_ref.shape
    for t in range(length // BLOCK):
        rows = pl.ds(t * BLOCK, BLOCK)
        cosine, sine = cos_ref[rows, :], sin_ref[rows, :]
        for pair in range(pairs):
            first = 3 * pair * PAIR
            query = qkv_ref[rows, first : first + PAIR]
            query = (query * cosine + swap_halves(query) * sine).astype(bf16)
            q_ref[pair, rows, :] = (query.astype(f32) * HEAD_DIM ** (-0.5)).astype(bf16)
            key = qkv_ref[rows, first + PAIR : first + 2 * PAIR]
            k_ref[pair, rows, :] = (key * cosine + swap_halves(key) * sine).astype(bf16)
            v_ref[pair, rows, :] = qkv_ref[rows, first + 2 * PAIR : first + 3 * PAIR].astype(bf16)
    peak_ref[...] = jnp.full(peak_ref.shape, -jnp.inf, f32)
    lane = lax.broadcasted_iota(jnp.int32, (BLOCK, 128), 1)
    for t in range(length // BLOCK):
        q0 = t * BLOCK
        rows = pl.ds(q0, BLOCK)
        cols = min(q0 + 2 * BLOCK, length)

        @pl.loop(0, pairs)
        def _(pair):
            total = jnp.zeros((BLOCK, PAIR), f32)
            for sub in range(2):
                head = 2 * pair + sub
                mask = head_mask((BLOCK, PAIR), sub)
                query = jnp.where(mask, q_ref[pair, rows, :], 0).astype(bf16)
                scores = masked_scores(query, k_ref.at[pair], row_ref, col_ref, q0, cols)
                row_max = jnp.max(scores, 1, keepdims=True)
                numerators = jnp.exp(scores - row_max)
                totals = jnp.sum(numerators, 1, keepdims=True)
                mixed = contract(numerators.astype(bf16), v_ref[pair, 0:cols, :], 1, 0) / totals
                total = jnp.where(mask, mixed, total)
                lse_ref[rows, :] = jnp.where(lane == head, row_max + jnp.log(totals), lse_ref[rows, :])
                peak_ref[...] = jnp.where(
                    lax.broadcasted_iota(jnp.int32, peak_ref.shape, 1) == head,
                    jnp.maximum(peak_ref[...], jnp.max(row_max)),
                    peak_ref[...],
                )
            out_ref[rows, pl.ds(pl.multiple_of(pair * PAIR, PAIR), PAIR)] = total.astype(bf16)


def attend_forward(qkv, cosine, sine, row_blocks, col_blocks):
    length = qkv.shape[0]
    pairs = qkv.shape[1] // (3 * PAIR)
    shape = jax.ShapeDtypeStruct
    return pl.pallas_call(
        attend_forward_kernel,
        out_shape=(
            shape((pairs, length, PAIR), bf16),
            shape((pairs, length, PAIR), bf16),
            shape((pairs, length, PAIR), bf16),
            shape((length, pairs * PAIR), bf16),
            shape((length, 128), f32),
            shape((8, 128), f32),
        ),
        in_specs=[vmem] * 5,
        out_specs=tuple([vmem] * 6),
        compiler_params=pltpu.CompilerParams(vmem_limit_bytes=56 * 1024 * 1024),
        cost_estimate=pl.CostEstimate(
            flops=16 * pairs * length * length * PAIR, bytes_accessed=length * PAIR * pairs * 24,
            transcendentals=2 * pairs * length * length,
        ),
        name="attend_forward",
    )(qkv, cosine, sine, row_blocks, col_blocks)


def attend_backward_kernel(
    first_head, q_ref, k_ref, v_ref, grad_ref, lse_ref, cos_ref, sin_ref, row_ref, col_ref, out_ref, dk_ref, dv_ref
):
    length = q_ref.shape[0]
    dk_ref[...] = jnp.zeros_like(dk_ref)
    dv_ref[...] = jnp.zeros_like(dv_ref)
    lane = lax.broadcasted_iota(jnp.int32, (BLOCK, 128), 1)
    for t in range(length // BLOCK):
        q0 = t * BLOCK
        rows = pl.ds(q0, BLOCK)
        cols = min(q0 + 2 * BLOCK, length)

        def one_head(sub, dq):
            mask = head_mask((BLOCK, PAIR), sub)
            query = jnp.where(mask, q_ref[rows, :], 0).astype(bf16)
            grad = jnp.where(mask, grad_ref[rows, :], 0).astype(bf16)
            lse = jnp.sum(
                jnp.where(lane == first_head + sub, lse_ref[rows, :], 0.0), 1, keepdims=True
            )
            scores = masked_scores(query, k_ref, row_ref, col_ref, q0, cols)
            attention = jnp.exp(scores - lse)
            grad_attention = contract(grad, v_ref[0:cols, :], 1, 1)
            weighted = attention * grad_attention
            centre = jnp.sum(weighted, 1, keepdims=True)
            grad_scores = (weighted - attention * centre).astype(bf16)
            dv_ref[0:cols, :] += contract(attention.astype(bf16), grad, 0, 0)
            dk_ref[0:cols, :] += contract(grad_scores, query, 0, 0)
            return jnp.where(mask, contract(grad_scores, k_ref[0:cols, :], 1, 0), dq)

        dq = lax.fori_loop(0, 2, one_head, jnp.zeros((BLOCK, PAIR), f32)) * HEAD_DIM ** (-0.5)
        out_ref[rows, 0:PAIR] = (dq * cos_ref[rows, :] - swap_halves(dq) * sin_ref[rows, :]).astype(bf16)
    for t in range(length // BLOCK):
        rows = pl.ds(t * BLOCK, BLOCK)
        dk = dk_ref[rows, :]
        out_ref[rows, PAIR : 2 * PAIR] = (
            dk * cos_ref[rows, :] - swap_halves(dk) * sin_ref[rows, :]
        ).astype(bf16)
        out_ref[rows, 2 * PAIR : 3 * PAIR] = dv_ref[rows, :].astype(bf16)


def attend_backward(pair, query, key, value, grad, lse, cosine, sine, row_blocks, col_blocks):
    length = query.shape[1]
    heads = pl.BlockSpec((None, length, PAIR), lambda _: (pair, 0, 0))
    return pl.pallas_call(
        functools.partial(attend_backward_kernel, 2 * pair),
        grid=(1,),
        out_shape=jax.ShapeDtypeStruct((length, 3 * PAIR), bf16),
        in_specs=[heads] * 3 + [pl.BlockSpec((length, PAIR), lambda _: (0, pair))] + [vmem] * 5,
        out_specs=vmem,
        scratch_shapes=[pltpu.VMEM((length, PAIR), f32), pltpu.VMEM((length, PAIR), f32)],
        compiler_params=pltpu.CompilerParams(vmem_limit_bytes=56 * 1024 * 1024),
        cost_estimate=pl.CostEstimate(
            flops=40 * length * length * PAIR, bytes_accessed=length * PAIR * 24,
            transcendentals=2 * length * length,
        ),
        name="attend_backward",
    )(query, key, value, grad, lse, cosine, sine, row_blocks, col_blocks)


def bit_of(index, bit):
    return lax.rem(lax.div(index, bit), 2)


def flip_bit(index, bit):
    return index + bit - 2 * bit * bit_of(index, bit)


class Links:

    def __init__(self, send_sems, recv_sems):
        self.send_sems, self.recv_sems = send_sems, recv_sems

    def copy(self, slot, src, dst, device):
        return pltpu.make_async_remote_copy(
            src_ref=src, dst_ref=dst, send_sem=self.send_sems.at[slot],
            recv_sem=self.recv_sems.at[slot], device_id=(device,), device_id_type=MESH,
        )


def greet(partners):
    barrier = pltpu.get_barrier_semaphore()
    for partner in partners:
        pl.semaphore_signal(barrier, inc=1, device_id=(partner,), device_id_type=MESH)
    pl.semaphore_wait(barrier, len(partners))


def spread_block(bits, own_ref, out_ref, links, local_sem):
    core, first, second = bits
    me = lax.axis_index(AXIS)
    sibling, next_a, next_b = (flip_bit(me, bit) for bit in bits)
    block = own_ref.shape[0]
    half = block // 2
    in_a, in_b = bit_of(me, first), bit_of(me, second)

    def rows(flip_a, flip_b, part):
        place = bit_of(me, core)
        place = place + 2 * lax.rem(in_a + flip_a, 2) + 4 * lax.rem(in_b + flip_b, 2)
        start, size = (0, block) if part is None else (part * half, half)
        return pl.ds(pl.multiple_of(place * block + start, half), size)

    def passed(slot, where, device):
        return links.copy(slot, out_ref.at[where], out_ref.at[where], device)

    def first_hand(slot, part, device):
        return links.copy(
            slot, own_ref.at[pl.ds(part * half, half)], out_ref.at[rows(0, 0, part)], device
        )

    copies = {
        0: first_hand(0, 0, next_a),
        1: first_hand(1, 1, next_b),
        2: first_hand(2, 1, next_a),
        3: first_hand(3, 0, next_b),
        4: links.copy(4, own_ref, out_ref.at[rows(0, 0, None)], sibling),
        5: passed(5, rows(1, 0, 0), next_b),
        6: passed(6, rows(1, 0, 0), sibling),
        7: passed(7, rows(0, 1, 1), next_a),
        8: passed(8, rows(0, 1, 1), sibling),
        9: passed(9, rows(1, 0, 1), sibling),
        10: passed(10, rows(0, 1, 0), sibling),
        11: passed(11, rows(1, 1, 0), sibling),
        12: passed(12, rows(1, 1, 1), sibling),
    }
    keep = pltpu.make_async_copy(own_ref, out_ref.at[rows(0, 0, None)], local_sem)

    def begin():
        for slot in range(5):
            copies[slot].start()
        keep.start()

    def hand_on(arrived, *sent):
        def phase():
            copies[arrived].wait_recv()
            for slot in sent:
                copies[slot].start()

        return phase

    def finish():
        for slot in (4, 6, 8, 9, 10, 11, 12):
            copies[slot].wait_recv()
        keep.wait()
        for slot in copies:
            copies[slot].wait_send()

    return [
        begin, hand_on(0, 5, 6), hand_on(1, 7, 8), hand_on(2, 9), hand_on(3, 10),
        hand_on(5, 11), hand_on(7, 12), finish,
    ]


def run(phases):
    for phase in phases:
        phase()


SPREAD_COPIES = 13
SUM_COPIES = 10


def sum_block(bits, product, total, to_core, from_core, chip_sum, arrived, links):
    core, first, second = bits
    me = lax.axis_index(AXIS)
    sibling, next_a, next_b = (flip_bit(me, bit) for bit in bits)
    block, width = total.shape
    half = block // 2
    tile = 512

    def place(step, other_core):
        flip_a, flip_b = 1 - step // 2, 1 - step % 2
        return (
            lax.rem(bit_of(me, core) + other_core, 2)
            + 2 * lax.rem(bit_of(me, first) + flip_a, 2)
            + 4 * lax.rem(bit_of(me, second) + flip_b, 2)
        )

    def part(index):
        return pl.ds(index * half, half)

    diag_a = links.copy(4, chip_sum.at[0, part(0)], arrived.at[0], next_a)
    diag_b = links.copy(5, chip_sum.at[0, part(1)], arrived.at[1], next_b)
    plain_a = links.copy(6, chip_sum.at[1, part(0)], arrived.at[2], next_a)
    plain_b = links.copy(7, chip_sum.at[2, part(1)], arrived.at[3], next_b)
    last_a = links.copy(8, chip_sum.at[1, part(1)], arrived.at[4], next_a)
    last_b = links.copy(9, chip_sum.at[2, part(0)], arrived.at[5], next_b)

    def core_copy(step):
        return links.copy(step, to_core.at[step], from_core.at[step], sibling)

    def for_sibling():
        @pl.loop(0, 4)
        def _(step):
            @pl.loop(0, width // tile)
            def _(column):
                columns = pl.ds(pl.multiple_of(column * tile, tile), tile)
                to_core[step, :, columns] = product(place(step, 1), columns).astype(bf16)

            core_copy(step).start()

    def for_chip():
        @pl.loop(0, 4)
        def _(step):
            core_copy(step).wait_recv()

            @pl.loop(0, width // tile)
            def _(column):
                columns = pl.ds(pl.multiple_of(column * tile, tile), tile)
                summed = product(place(step, 0), columns) + from_core[step, :, columns].astype(f32)
                total[:, columns] = summed

                @pl.when(step < 3)
                def _():
                    chip_sum[step, :, columns] = summed.astype(bf16)

            @pl.when(step == 0)
            def _():
                diag_a.start()
                diag_b.start()

            @pl.when(step == 1)
            def _():
                plain_a.start()

            @pl.when(step == 2)
            def _():
                plain_b.start()

    def hand_on():
        diag_a.wait_recv()
        chip_sum[2, 0:half, :] = (
            chip_sum[2, 0:half, :].astype(f32) + arrived[0].astype(f32)
        ).astype(bf16)
        last_b.start()
        diag_b.wait_recv()
        chip_sum[1, half:block, :] = (
            chip_sum[1, half:block, :].astype(f32) + arrived[1].astype(f32)
        ).astype(bf16)
        last_a.start()

    def finish():
        plain_a.wait_recv()
        total[0:half, :] += arrived[2].astype(f32)
        plain_b.wait_recv()
        total[half:block, :] += arrived[3].astype(f32)
        last_b.wait_recv()
        total[0:half, :] += arrived[5].astype(f32)
        last_a.wait_recv()
        total[half:block, :] += arrived[4].astype(f32)

        @pl.loop(0, 4)
        def _(step):
            core_copy(step).wait_send()

        for copy in (diag_a, diag_b, plain_a, plain_b, last_a, last_b):
            copy.wait_send()

    return for_sibling, for_chip, hand_on, finish


def sum_scratch(block, width):
    return [
        pltpu.VMEM((block, width), f32),
        pltpu.VMEM((4, block, width), bf16),
        pltpu.VMEM((4, block, width), bf16),
        pltpu.VMEM((3, block, width), bf16),
        pltpu.VMEM((6, block // 2, width), bf16),
        pltpu.SemaphoreType.DMA((SUM_COPIES,)),
        pltpu.SemaphoreType.DMA((SUM_COPIES,)),
    ]


def spread_scratch(block, width):
    return [
        pltpu.VMEM((block, width), bf16),
        pltpu.SemaphoreType.DMA((SPREAD_COPIES,)),
        pltpu.SemaphoreType.DMA((SPREAD_COPIES,)),
        pltpu.SemaphoreType.DMA,
    ]


def link_params(collective_id):
    return pltpu.CompilerParams(
        collective_id=collective_id, has_side_effects=True, vmem_limit_bytes=60 * 1024 * 1024
    )


def cost(flops, size):
    return pl.CostEstimate(flops=int(flops), bytes_accessed=int(size), transcendentals=0)


def front_kernel(
    team, teams, tokens_ref, mine_ref, small_ref, tokens_out, weights_out, small_out,
    send_sems, recv_sems, local_sem, swap_send, swap_recv, swap_local, line_send, line_recv, small_send, small_recv, small_local,
):
    me = lax.axis_index(AXIS)
    mate, group = lax.rem(me, team), lax.div(me, team)
    devices = team * teams
    bits = [1 << k for k in range(devices.bit_length() - 1)]
    mates = [group * team + lax.rem(mate + k, team) for k in range(1, team)]
    above, below = lax.rem(me + team, devices), lax.rem(me + devices - team, devices)
    greet(mates + [above, below] + [flip_bit(me, bit) for bit in bits if bit >= team])
    rows = mine_ref.shape[1]
    swaps, line, small = Links(swap_send, swap_recv), Links(line_send, line_recv), Links(small_send, small_recv)

    def share(place):
        return pl.ds(pl.multiple_of(place * rows, rows), rows)

    swap_copies = [
        swaps.copy(k, mine_ref.at[lax.rem(mate + k + 1, team)], weights_out.at[group, share(mate)], mates[k])
        for k in range(team - 1)
    ]
    for copy in swap_copies:
        copy.start()
    keep = pltpu.make_async_copy(mine_ref.at[mate], weights_out.at[group, share(mate)], swap_local)
    keep.start()
    spread = spread_block(
        (1, 2, 4), tokens_ref, tokens_out, Links(send_sems, recv_sems), local_sem
    )
    spread[0]()
    small_keep = pltpu.make_async_copy(small_ref, small_out.at[me], small_local)
    small_keep.start()
    small_keep.wait()

    def small_copy(k):
        block = pl.ds(pl.multiple_of(me - lax.rem(me, bits[k]), bits[k]), bits[k])
        return small.copy(k, small_out.at[block], small_out.at[block], flip_bit(me, bits[k]))

    def small_step(k):
        if k:
            small_copy(k - 1).wait_recv()
        if k < len(bits):
            small_copy(k).start()

    small_step(0)

    def passed(slot, shard, device):
        return line.copy(slot, weights_out.at[shard], weights_out.at[shard], device)

    steps = teams - 1

    def up(step):
        return passed(step - 1, group - (step - 1), above)

    def down(step):
        return passed(steps + step - 1, group + (step - 1), below)

    def line_start(step):
        pl.when((group < teams - 1) & (group >= step - 1))(lambda: up(step).start())
        pl.when((group > 0) & (group + step - 1 < teams))(lambda: down(step).start())

    def line_wait(step):
        pl.when(group >= step)(lambda: up(step).wait_recv())
        pl.when(group + step < teams)(lambda: down(step).wait_recv())

    def line_sent(step):
        pl.when((group < teams - 1) & (group >= step - 1))(lambda: up(step).wait_send())
        pl.when((group > 0) & (group + step - 1 < teams))(lambda: down(step).wait_send())

    for copy in swap_copies:
        copy.wait_recv()
    keep.wait()
    line_start(1)
    small_step(1)
    spread[1]()
    spread[2]()
    small_step(2)
    spread[3]()
    spread[4]()
    line_wait(1)
    line_start(2)
    for k in range(3, len(bits) + 1):
        small_step(k)
    for phase in spread[5:]:
        phase()
    for step in range(2, teams):
        line_wait(step)
        if step < steps:
            line_start(step + 1)
    for copy in swap_copies:
        copy.wait_send()
    for step in range(1, teams):
        line_sent(step)
    for k in range(len(bits)):
        small_copy(k).wait_send()


def front(tokens, mine, small, teams):
    block, width = tokens.shape
    team, rows, cols = mine.shape
    devices = team * teams
    bits = devices.bit_length() - 1
    dma = pltpu.SemaphoreType.DMA
    shape = jax.ShapeDtypeStruct
    return pl.pallas_call(
        functools.partial(front_kernel, team, teams),
        out_shape=(
            shape((team * block, width), bf16),
            shape((teams, team * rows, cols), bf16),
            shape((devices,) + small.shape, f32),
        ),
        in_specs=[vmem] * 3,
        out_specs=(anywhere,) * 3,
        scratch_shapes=spread_scratch(block, width)[1:]
        + [dma((team - 1,)), dma((team - 1,)), dma, dma((2 * teams,)), dma((2 * teams,)), dma((bits,)), dma((bits,)), dma],
        compiler_params=link_params(1),
        cost_estimate=cost(0, 200e6),
        name="front",
    )(tokens, mine, small)


def row_scale(values):
    return lax.rsqrt(jnp.mean(values * values, -1, keepdims=True) + epsilon)


def branch_kernel(
    carry, sum_bits, spread_bits, left_ref, right_ref, residual_ref, gain_ref, peak_ref, *refs,
):
    if carry:
        (both_own, both_y, gate_z, down_own, down_y), refs = refs[:5], refs[5:]
        (h2_ref, out_ref, peak_out, gate_full, up_full, down_full), refs = refs[:6], refs[6:]
        (total, to_core, from_core, chip_sum, arrived, sum_send, sum_recv, own, send_sems, recv_sems, local_sem,
         peak_in, peak_send, peak_recv, carry_send, carry_recv, carry_local) = refs
    else:
        (h2_ref, out_ref, peak_out), refs = refs[:3], refs[3:]
        (total, to_core, from_core, chip_sum, arrived, sum_send, sum_recv, own, send_sems, recv_sems, local_sem,
         peak_in, peak_send, peak_recv) = refs
    me = lax.axis_index(AXIS)
    block = total.shape[0]
    bits = [1 << k for k in range(peak_in.shape[0])]
    greet([flip_bit(me, bit) for bit in bits])
    peaks = Links(peak_send, peak_recv)

    def peak_copy(k):
        return peaks.copy(k, peak_out, peak_in.at[k], flip_bit(me, bits[k]))

    def peak_step(k):
        if k:
            peak_copy(k - 1).wait()
            peak_out[...] = jnp.maximum(peak_out[...], peak_in[k - 1])
        if k < len(bits):
            peak_copy(k).start()

    if carry:
        carried = Links(carry_send, carry_recv)
        high, middle = bit_of(me, 16), bit_of(me, 4)
        by_y, by_z = flip_bit(me, 4), flip_bit(me, 16)

        def rows_of(part, flip_z, flip_y):
            z, y = lax.rem(high + flip_z, 2), lax.rem(middle + flip_y, 2)
            return pl.ds(pl.multiple_of(z * 16 + part * 8 + y * 4, 4), 4)

        cols = gate_z.shape[2]

        def half(source, part, up=0):
            return source.at[pl.ds(part * 4, 4), :, pl.ds(up * cols, cols)]

        def unit(flip_z, flip_y):
            return lax.rem(high + flip_z, 2) * 2 + lax.rem(middle + flip_y, 2)

        kept = []
        for source, up, full, flips in (
            (both_own, 0, gate_full, (0, 0)), (both_y, 0, gate_full, (0, 1)), (gate_z, 0, gate_full, (1, 0)),
            (both_own, 1, up_full, (0, 0)), (both_y, 1, up_full, (0, 1)),
        ):
            for part in range(2):
                kept.append((half(source, part, up), full.at[rows_of(part, *flips)]))
        kept.append((down_own, down_full.at[unit(0, 0)]))
        kept.append((down_y, down_full.at[unit(0, 1)]))
        kept = [pltpu.make_async_copy(a, b, carry_local.at[i]) for i, (a, b) in enumerate(kept)]
        up_z = [
            carried.copy(part, half(both_own, part, 1), up_full.at[rows_of(part, 0, 0)], by_z)
            for part in range(2)
        ]
        gate_yz = [
            carried.copy(2 + part, half(gate_z, part), gate_full.at[rows_of(part, 1, 0)], by_y)
            for part in range(2)
        ]
        up_yz = [
            carried.copy(4 + part, up_full.at[rows_of(part, 1, 0)], up_full.at[rows_of(part, 1, 0)], by_y)
            for part in range(2)
        ]
        down_z = carried.copy(6, down_own, down_full.at[unit(0, 0)], by_z)
        for copy in up_z + gate_yz + kept:
            copy.start()

    def product(place, columns):
        rows = pl.ds(pl.multiple_of(place * block, block), block)
        return contract(left_ref[rows, :], right_ref[:, columns], 1, 0)

    peak_out[...] = peak_ref[...]
    peak_step(0)
    run(
        sum_block(
            sum_bits, product, total, to_core, from_core, chip_sum, arrived, Links(sum_send, sum_recv)
        )
    )
    h2 = residual_ref[...].astype(f32) + total[...]
    h2_ref[...] = h2
    own[...] = (h2 * row_scale(h2) * gain_ref[...]).astype(bf16)
    spread = spread_block(spread_bits, own, out_ref, Links(send_sems, recv_sems), local_sem)
    spread[0]()
    if carry:
        for part in range(2):
            up_z[part].wait_recv()
            up_yz[part].start()
        down_z.start()
    for k, phase in enumerate(spread[1:-1]):
        phase()
        if k < len(bits):
            peak_step(k + 1)
    for k in range(len(spread) - 2, len(bits)):
        peak_step(k + 1)
    spread[-1]()
    if carry:
        for copy in kept:
            copy.wait()
        for copy in gate_yz + up_yz + [down_z]:
            copy.wait_recv()
        for copy in up_z + gate_yz + up_yz + [down_z]:
            copy.wait_send()


def branch(left, right, residual, gain, peak, carry, sum_bits, spread_bits, bit_count):
    block, width = residual.shape
    dma = pltpu.SemaphoreType.DMA
    shape = jax.ShapeDtypeStruct
    out_shape = [shape((block, width), f32), shape((8 * block, width), bf16), shape((8, 128), f32)]
    scratch = sum_scratch(block, width) + spread_scratch(block, width)
    scratch += [pltpu.VMEM((bit_count, 8, 128), f32), dma((bit_count,)), dma((bit_count,))]
    if carry:
        out_shape += [
            shape((32,) + carry[2].shape[1:], bf16), shape((32,) + carry[2].shape[1:], bf16),
            shape((4,) + carry[3].shape, bf16),
        ]
        scratch += [dma((7,)), dma((7,)), dma((12,))]
    return pl.pallas_call(
        functools.partial(branch_kernel, bool(carry), sum_bits, spread_bits),
        out_shape=tuple(out_shape),
        in_specs=[vmem] * 5 + [anywhere] * len(carry),
        out_specs=tuple([vmem, anywhere, vmem] + [anywhere] * (len(out_shape) - 3)),
        scratch_shapes=scratch,
        compiler_params=link_params(2),
        cost_estimate=cost(16 * block * left.shape[1] * width, 300e6),
        name="attention_branch",
    )(left, right, residual, gain, peak, *carry)


def norm_back(values, gain, upstream):
    scaled = upstream * gain
    scale = row_scale(values)
    inner = jnp.mean(scaled * values, -1, keepdims=True)
    return scale * scaled - scale * scale * scale * values * inner


def ffn_back_kernel(
    sum_bits, spread_bits, gate_ref, up_ref, gate_w_ref, up_w_ref, h2_ref, cot_ref, gain_ref, residual_ref, out_ref,
    total, to_core, from_core, chip_sum, arrived, sum_send, sum_recv, own, send_sems, recv_sems, local_sem,
):
    me = lax.axis_index(AXIS)
    block = total.shape[0]
    greet([flip_bit(me, bit) for bit in sorted(set(sum_bits) | set(spread_bits))])

    def product(place, columns):
        rows = pl.ds(pl.multiple_of(place * block, block), block)
        return contract(gate_ref[rows, :], gate_w_ref[columns, :], 1, 1) + contract(
            up_ref[rows, :], up_w_ref[columns, :], 1, 1
        )

    run(
        sum_block(
            sum_bits, product, total, to_core, from_core, chip_sum, arrived, Links(sum_send, sum_recv)
        )
    )
    residual = cot_ref[...].astype(f32) + norm_back(h2_ref[...], gain_ref[...], total[...])
    residual_ref[...] = residual
    own[...] = residual.astype(bf16)
    run(spread_block(spread_bits, own, out_ref, Links(send_sems, recv_sems), local_sem))


def ffn_back(gate, up, gate_w, up_w, h2, cot, gain, sum_bits, spread_bits):
    block, width = h2.shape
    return pl.pallas_call(
        functools.partial(ffn_back_kernel, sum_bits, spread_bits),
        out_shape=(
            jax.ShapeDtypeStruct((block, width), f32),
            jax.ShapeDtypeStruct((8 * block, width), bf16),
        ),
        in_specs=[vmem] * 7,
        out_specs=(vmem, anywhere),
        scratch_shapes=sum_scratch(block, width) + spread_scratch(block, width),
        compiler_params=link_params(3),
        cost_estimate=cost(32 * block * gate.shape[1] * width, 250e6),
        name="ffn_back",
    )(gate, up, gate_w, up_w, h2, cot, gain)


def last_sums_kernel(
    sum_bits, ffn_bits, left_ref, other_ref, right_ref, tokens_ref, gain_ref, residual_ref, hidden_ref, down_ref, h2_ref,
    out_ref, mixed_ref, *scratch,
):
    count = len(scratch) // 2
    me = lax.axis_index(AXIS)
    total, ffn_total = scratch[0], scratch[count]
    block = total.shape[0]
    greet([flip_bit(me, bit) for bit in sorted(set(sum_bits) | set(ffn_bits))])

    def rows_of(place):
        return pl.ds(pl.multiple_of(place * block, block), block)

    def product(place, columns):
        rows = rows_of(place)
        middle = left_ref.shape[1]
        return contract(left_ref[rows, :], right_ref[columns, 0:middle], 1, 1) + contract(
            other_ref[rows, :], right_ref[columns, middle : 2 * middle], 1, 1
        )

    def ffn_product(place, columns):
        return contract(hidden_ref[rows_of(place), :], down_ref[:, columns], 1, 0)

    first = sum_block(sum_bits, product, *scratch[: count - 2], Links(*scratch[count - 2 : count]))
    second = sum_block(ffn_bits, ffn_product, *scratch[count:-2], Links(*scratch[-2:]))
    for one, other in zip(first, second):
        one()
        other()
    out_ref[...] = residual_ref[...] + norm_back(
        tokens_ref[...].astype(f32), gain_ref[...], total[...]
    )
    mixed_ref[...] = (h2_ref[...] + ffn_total[...]).astype(bf16)


def last_sums(left, other, right, tokens, gain, residual, hidden, down, h2, sum_bits, ffn_bits):
    block, width = tokens.shape
    return pl.pallas_call(
        functools.partial(last_sums_kernel, sum_bits, ffn_bits),
        out_shape=(
            jax.ShapeDtypeStruct((block, width), f32), jax.ShapeDtypeStruct((block, width), bf16),
        ),
        in_specs=[vmem] * 9,
        out_specs=(vmem, vmem),
        scratch_shapes=sum_scratch(block, width) * 2,
        compiler_params=link_params(4),
        cost_estimate=cost(16 * block * right.size // 8, 300e6),
        name="last_sums",
    )(left, other, right, tokens, gain, residual, hidden, down, h2)


def home_kernel(bits, places, sources, *refs):
    count = len(places)
    mine, refs = refs[:sources], refs[sources:]
    weights, gain_ref, outs, gain_out = refs[:count], refs[count], refs[count + 1 : 2 * count + 1], refs[2 * count + 1]
    arrived, (send_sems, recv_sems, local_sems) = refs[2 * count + 2 : -3], refs[-3:]
    me = lax.axis_index(AXIS)
    team = mine[0].shape[0]

    def mate(offset):
        device, place = me, 0
        for k, bit in enumerate(bits):
            moved = (offset >> k) % 2
            place = place + lax.rem(bit_of(me, bit) + moved, 2) * (1 << k)
            device = flip_bit(device, bit) if moved else device
        return device, place

    greet([mate(k)[0] for k in range(1, team)])
    links = Links(send_sems, recv_sems)
    own = mate(0)[1]
    copies, kept = [], []
    for i, (source, landed) in enumerate(zip(mine, arrived)):
        kept.append(pltpu.make_async_copy(source.at[own], landed.at[own], local_sems.at[i]))
        for k in range(1, team):
            device, place = mate(k)
            copies.append(links.copy(i * team + k, source.at[place], landed.at[own], device))
    for copy in copies + kept:
        copy.start()
    for copy in copies:
        copy.wait_recv()
    for copy in kept:
        copy.wait()
    for out, moves in zip(outs, places):
        for source, member, first, target, columns in moves:
            out[:, target : target + columns] = arrived[source][member, :, first : first + columns].astype(f32)
    total = jnp.zeros(gain_ref.shape, f32)
    for out, weight in zip(outs, weights):
        for first in range(0, out.shape[1], 1024):
            product = out[:, first : first + 1024] * weight[:, first : first + 1024].astype(f32)
            total += jnp.sum(product, 1, keepdims=True)
    gain_out[...] = total / gain_ref[...]
    for copy in copies:
        copy.wait_send()


def home(parts, weights, gain, bits, places, collective_id, name):
    shape = jax.ShapeDtypeStruct
    dma = pltpu.SemaphoreType.DMA
    count, slots = len(weights), len(parts) * parts[0].shape[0]
    return pl.pallas_call(
        functools.partial(home_kernel, bits, places, len(parts)),
        out_shape=tuple(shape(w.shape, f32) for w in weights) + (shape((gain.shape[0], 1), f32),),
        in_specs=[vmem] * (len(parts) + count + 1),
        out_specs=tuple([vmem] * (count + 1)),
        scratch_shapes=[pltpu.VMEM(part.shape, bf16) for part in parts]
        + [dma((slots,)), dma((slots,)), dma((len(parts),))],
        compiler_params=link_params(collective_id),
        cost_estimate=cost(1e6, 30e6),
        name=name,
    )(*parts, *weights, gain.astype(f32).reshape(-1, 1))


def body(
    tokens, block_of, clip_limit, norm_attn, w_query, w_key, w_value, w_out,
    norm_ffn, w_gate, w_up, w_down, cotangent,
):
    tok_rows, width = tokens.shape
    devices = lax.axis_size(AXIS)
    team = SEQ // tok_rows
    teams = devices // team
    head_total = width // HEAD_DIM
    heads = head_total // team
    head_cols = heads * HEAD_DIM
    ff_rows = w_down.shape[0]
    weight_rows = w_gate.shape[0]
    ff_cols = w_gate.shape[1] // team
    device = lax.axis_index(AXIS)
    mate = device % team
    bit_count = devices.bit_length() - 1
    attn_bits, ffn_bits = (1, 2, 4), (1, 2, 8)
    data_bits = [4] + [1 << k for k in range(4, bit_count)]
    in_team = [[g * team + b for b in range(team)] for g in range(teams)]
    across = [[g * team + b for g in range(teams)] for b in range(team)]
    ffn_team = [
        [g * 16 + z * 8 + y * 4 + c for z in range(2) for c in range(4)]
        for g in range(devices // 16)
        for y in range(2)
    ]

    def flip(x, bit):
        return lax.ppermute(x, AXIS, [(i, i ^ bit) for i in range(devices)])

    def gather_across(x):
        return lax.all_gather(x, AXIS, axis=0, tiled=True, axis_index_groups=across)

    def scatter_across(x):
        return lax.psum_scatter(
            x.astype(bf16), AXIS, scatter_dimension=0, tiled=True, axis_index_groups=across
        )

    def swap(x, groups):
        return lax.all_to_all(x, AXIS, 0, 0, tiled=True, axis_index_groups=groups)

    def dim_of(bit):
        return bit_count - bit.bit_length()

    def data_pieces(x):
        pieces = {0: x}
        for bit in reversed(data_bits):
            for key in list(pieces):
                pieces[key | bit] = flip(pieces[key], bit)
        return pieces

    def place_pieces(pieces, dims, shape):
        total = jnp.zeros(shape, bf16)
        for key, piece in pieces.items():
            start = [0] * len(shape)
            size = list(shape)
            for bit in data_bits:
                start[dims[bit]] = ((device // bit) + (1 if key & bit else 0)) % 2
                size[dims[bit]] = 1
            total = lax.dynamic_update_slice(total, piece.reshape(size), start)
        return total

    def after_bit(dims, bit):
        return {b: d - (d > dims[bit]) for b, d in dims.items() if b != bit}

    def data_sum(x, dims, bits):
        for bit in bits:
            mine = (device // bit) % 2
            keep = lax.dynamic_index_in_dim(x, mine, dims[bit], False)
            sent = flip(lax.dynamic_index_in_dim(x, 1 - mine, dims[bit], False), bit)
            x = (keep.astype(f32) + sent.astype(f32)).astype(bf16)
            dims = after_bit(dims, bit)
        return x

    def head_columns(weight):
        split = weight.reshape(weight_rows, heads, team, HEAD_DIM)
        return split.transpose(2, 0, 1, 3).reshape(team, weight_rows, head_cols)

    def ffn_out(weight):
        split = weight.reshape(weight_rows, devices // 16, 2, 2, 4, ff_rows)
        return split.transpose(2, 4, 0, 1, 3, 5).reshape(team, weight_rows, ff_cols)

    row_dims = {bit: dim_of(bit) for bit in data_bits}
    row_shape = (2,) * bit_count
    unit_dims = {bit: i for i, bit in enumerate(reversed(data_bits))}
    unit_shape = (2,) * len(data_bits)

    def tie(*values):
        return lax.optimization_barrier(values)

    by_head = [head_columns(w) for w in (w_query, w_key, w_value)]
    qkv_mine = jnp.concatenate(
        [w[:, :, p * PAIR : (p + 1) * PAIR] for p in range(heads // 2) for w in by_head], 2
    )
    gain_row = jnp.concatenate([norm_attn, norm_ffn]).astype(f32)
    gain_row = jnp.pad(gain_row, (0, 128 - 2 * weight_rows)).reshape(1, 128)
    block_rows = block_of.astype(f32).reshape(tok_rows // 128, 128)
    small = jnp.concatenate([gain_row, block_rows, jnp.zeros((7 - tok_rows // 128, 128), f32)])
    qkv_mine, gate_rows, up_rows = tie(qkv_mine, w_gate, w_up)
    both_mine = swap(jnp.concatenate([ffn_out(gate_rows), ffn_out(up_rows)], 2), ffn_team)
    team_tokens, qkv_w, gathered = front(tokens, qkv_mine, small, teams)
    qkv_w = qkv_w.reshape(width, 3 * head_cols)
    gain_attn = gathered[:, 0, :weight_rows].reshape(1, width)
    gain_ffn = gathered[:, 0, weight_rows : 2 * weight_rows].reshape(1, width)
    blocks = lax.dynamic_slice_in_dim(gathered, device - mate, team, 0)
    blocks = blocks[:, 1 : 1 + tok_rows // 128].astype(jnp.int32).reshape(SEQ)
    row_blocks, col_blocks = blocks.reshape(1, SEQ), blocks.reshape(SEQ, 1)
    both_mine, down_mine, qkv_w, out_mine = tie(both_mine, w_down, qkv_w, w_out)
    if weight_rows == HEAD_DIM:
        out_w = gather_across(out_mine)
    else:
        out_all = lax.all_gather(out_mine, AXIS, axis=0, tiled=True)
        out_w = lax.dynamic_index_in_dim(
            out_all.reshape(heads, team, HEAD_DIM, width), mate, 1, False
        ).reshape(head_cols, width)

    def whole_rows(mine):
        shape = row_shape + (weight_rows, ff_cols)
        return place_pieces(data_pieces(mine), row_dims, shape).reshape(width, ff_cols)

    team_tokens = team_tokens.astype(f32)
    normed_attn = (team_tokens * row_scale(team_tokens) * gain_attn).astype(bf16)
    qkv = contract(normed_attn, qkv_w, 1, 0)
    cosine, sine = rope_tables(SEQ, PAIR)
    qkv, cot_mine = tie(qkv, cotangent)
    if data_bits == [4, 16]:
        gate_z = flip(both_mine[:, :, :ff_cols], 16)
        carry = [both_mine, flip(both_mine, 4), gate_z, down_mine, flip(down_mine, 4)]
    else:
        carry = []
    query, key, value, attended, lse, peak = attend_forward(qkv, cosine, sine, row_blocks, col_blocks)
    peaks = jnp.where(
        (jnp.arange(head_total) % team) == mate, jnp.repeat(peak[0, :heads], team), -jnp.inf
    )
    peaks = jnp.broadcast_to(jnp.pad(peaks, (0, 128 - head_total))[None], (8, 128))
    after_attn, normed_ffn, peaks, *full = branch(
        attended, out_w, tokens, gain_ffn, peaks, carry, attn_bits, ffn_bits, bit_count
    )
    head_peak = peaks[0, :head_total]
    if carry:
        gate_w, up_w = (w.reshape(width, ff_cols) for w in full[:2])
        z_side, y_side = (device // 16) % 2, (device // 4) % 2
        passed = lax.dynamic_index_in_dim(full[2], (1 - z_side) * 2 + y_side, 0, True)
        down_w = lax.dynamic_update_slice(
            full[2], flip(passed, 4), ((1 - z_side) * 2 + 1 - y_side, 0, 0)
        ).reshape(ff_cols, width)
    else:
        gate_w, up_w = whole_rows(both_mine[:, :, :ff_cols]), whole_rows(both_mine[:, :, ff_cols:])
        down_w = place_pieces(
            data_pieces(down_mine), unit_dims, unit_shape + (ff_rows, width)
        ).reshape(ff_cols, width)
    gate_pre = contract(normed_ffn, gate_w, 1, 0)
    up_pre = contract(normed_ffn, up_w, 1, 0)
    sigmoid_gate = jax.nn.sigmoid(gate_pre)
    silu_gate = gate_pre * sigmoid_gate
    hidden = (silu_gate * up_pre).astype(bf16)

    team_cot = lax.all_gather(cot_mine, AXIS, axis=0, tiled=True, axis_index_groups=ffn_team)
    d_down = contract(hidden, team_cot, 0, 0).astype(bf16).reshape(unit_shape + (ff_rows, width))
    team_cot, d_down = tie(team_cot, d_down)
    d_hidden = contract(team_cot, down_w, 1, 1)
    grad_gate = (d_hidden * up_pre * sigmoid_gate * (1.0 + gate_pre * (1.0 - sigmoid_gate))).astype(bf16)
    grad_up = (d_hidden * silu_gate).astype(bf16)

    def row_part(grad):
        part = contract(normed_ffn, grad, 0, 0).astype(bf16)
        return part.reshape(row_shape + (weight_rows, ff_cols))

    d_gate = row_part(grad_gate)
    d_down = data_sum(d_down, unit_dims, data_bits[:1])
    grad_gate, d_down, d_gate = tie(grad_gate, d_down, d_gate)
    d_residual, branch_grad = ffn_back(
        grad_gate, grad_up, gate_w, up_w, after_attn, cotangent, gain_ffn, ffn_bits, attn_bits
    )
    unit_rest, row_rest = after_bit(unit_dims, data_bits[0]), after_bit(row_dims, data_bits[0])
    d_down = data_sum(d_down, unit_rest, data_bits[1:])
    d_gate = data_sum(d_gate, row_dims, data_bits[:1])
    branch_grad, grad_up = tie(branch_grad, grad_up)
    d_up = row_part(grad_up)
    grad_attended = contract(branch_grad, out_w, 1, 1).astype(bf16)
    grad_attended, d_up, d_down, d_gate = tie(grad_attended, d_up, d_down, d_gate)

    def heads_back(pair):
        grads = attend_backward(
            pair, query, key, value, grad_attended, lse, cosine, sine, row_blocks, col_blocks
        )
        return grads, scatter_across(contract(normed_attn, grads, 0, 0))

    grad_pairs, shares = [None] * (heads // 2), [None] * (heads // 2)
    grad_pairs[0], shares[0] = heads_back(0)
    d_gate = data_sum(d_gate, row_rest, data_bits[1:])
    d_up = data_sum(d_up, row_dims, data_bits[:1])
    grad_attended, _, d_gate, d_up = tie(grad_attended, grad_pairs[0], d_gate, d_up)
    for p in range(1, heads // 2):
        grad_pairs[p], shares[p] = heads_back(p)
    d_up = data_sum(d_up, row_rest, data_bits[1:])
    out_part = contract(attended, branch_grad, 0, 0)
    if weight_rows == HEAD_DIM:
        d_out = scatter_across(out_part).astype(f32)
    else:
        spread = jnp.where(
            (jnp.arange(team) == mate)[None, :, None, None],
            out_part.reshape(heads, 1, HEAD_DIM, width), 0.0,
        ).reshape(width, width)
        d_out = lax.psum_scatter(spread, AXIS, scatter_dimension=0, tiled=True)
    d_tokens, mixed = last_sums(
        *grad_pairs, qkv_w, tokens, gain_attn, d_residual, hidden, down_w, after_attn, attn_bits, ffn_bits
    )
    d_down = d_down.astype(f32)
    attn_places = tuple(
        tuple(
            (g // 2, b, i * PAIR + (g % 2) * HEAD_DIM, (g * team + b) * HEAD_DIM, HEAD_DIM)
            for g in range(heads) for b in range(team)
        )
        for i in range(3)
    )
    ffn_places = tuple(
        tuple(
            (i, z * 4 + c, (2 * h + y) * ff_rows, (h * 16 + z * 8 + y * 4 + c) * ff_rows, ff_rows)
            for h in range(devices // 16) for z in range(2) for y in range(2) for c in range(4)
        )
        for i in range(2)
    )
    shares = [share.reshape(team, weight_rows, 3 * PAIR) for share in shares]
    d_query, d_key, d_value, d_norm_attn = home(
        shares, (w_query, w_key, w_value), norm_attn, attn_bits, attn_places, 5, "home_attn"
    )
    d_gate, d_up = (d.reshape(team, weight_rows, ff_cols) for d in (d_gate, d_up))
    d_gate, d_up, d_norm_ffn = home(
        (d_gate, d_up), (w_gate, w_up), norm_ffn, ffn_bits, ffn_places, 6, "home_ffn"
    )
    d_norm_attn, d_norm_ffn = d_norm_attn[:, 0], d_norm_ffn[:, 0]
    clip_value = clip_limit.astype(f32)
    factor = jnp.sqrt(clip_value / jnp.maximum(head_peak, clip_value))
    factors = jnp.repeat(factor, HEAD_DIM)[None, :]
    clipped_query = (w_query.astype(f32) * factors).astype(bf16)
    clipped_key = (w_key.astype(f32) * factors).astype(bf16)
    return (
        mixed, d_tokens, d_norm_attn, d_query, d_key, d_value, d_out, d_norm_ffn,
        d_gate, d_up, d_down, head_peak, clipped_query, clipped_key,
    )


def solution(mesh):
    rows, whole = P(AXIS, None), P(AXIS)
    return jax.shard_map(
        body,
        mesh=mesh,
        in_specs=(rows, whole, P(), whole, rows, rows, rows, rows, whole, rows, rows, rows, rows),
        out_specs=(
            rows, rows, whole, rows, rows, rows, rows, whole, rows, rows, rows, P(), rows, rows,
        ),
        check_vma=False,
    )
```

time: 1030 us -> 1010 us (0.981)
  Pallas kernels: 444 us -> 687 us
  waiting for transfers between devices: 249 us -> 69 us
  starting transfers between devices: 51.1 us -> 12 us
  local copies, waits for them, and re-layouts: 74.3 us -> 45.3 us
  blocking collectives: 17.8 us -> 0 us
    pallas_call x5 -> x8, Pallas kernels: 345 us -> 568 us  [the longest x1 229 us: branch(): pl.pallas_call(functools.partial(branch_kernel, bool(carry), sum_bits, sp...]
    ppermute x28 -> x10, waiting for transfers between devices: 225 us -> 68.9 us  [flip(): return lax.ppermute(x, AXIS, [(i, i ^ bit) for i in range(devices)])]
    ppermute x28 -> x10, starting transfers between devices: 37.9 us -> 6.24 us  [flip(): return lax.ppermute(x, AXIS, [(i, i ^ bit) for i in range(devices)])]
    convert_element_type x15 -> x0, local copies, waits for them, and re-layouts: 28.5 us -> none  [the longest x3 11.5 us: body(): d_gate = ffn_home(d_gate_up[:, :, :ff_cols]).astype(f32)]
    all_gather x2 -> x1, waiting for transfers between devices: 23.1 us -> 0.01 us  [gather_across(): return lax.all_gather(x, AXIS, axis=0, tiled=True, axis_index_groups=across)]
    pallas_call x1, Pallas kernels: 98.9 us -> 119 us  [ffn_back(): pl.pallas_call(functools.partial(ffn_back_kernel, sum_bits, spread_bits),...]
    all_to_all x1 -> x0, blocking collectives: 17.8 us -> none  [swap(): return lax.all_to_all(x, AXIS, 0, 0, tiled=True, axis_index_groups=groups)]
  transfers between devices with their start and end apart: 37 -> 16, of which waited for: 16 -> 4; matrix products, arithmetic and copies ran while one was open for 19% -> 17% of each run, Pallas kernels for 34% -> 67%
where the time goes in v2:
time: 1010 us; the launch traced here: 996 us
  Pallas kernels  687 us (68%)
  matrix products  133 us (13%)
  waiting for transfers between devices  69 us (7%)
  local copies, waits for them, and re-layouts  45.3 us (4%)
  other arithmetic  34.7 us (3%)
  between operations  15.2 us (2%)
  starting transfers between devices  12 us (1%)
    pallas_call x1, Pallas kernels, branch(): pl.pallas_call(functools.partial(branch_kernel, bool(carry), sum_bits, sp...  229 us
    dot_general x11, matrix products, contract(): lax.dot_general(left, right, (((left_dim,), (right_dim,)), ((), ())), pre...  133 us
    pallas_call x1, Pallas kernels, ffn_back(): pl.pallas_call(functools.partial(ffn_back_kernel, sum_bits, spread_bits),...  119 us
    pallas_call x1, Pallas kernels, front(): pl.pallas_call(functools.partial(front_kernel, team, teams), out_shape=(s...  105 us
    pallas_call x1, Pallas kernels, last_sums(): pl.pallas_call(functools.partial(last_sums_kernel, sum_bits, ffn_bits), o...  97.7 us
    ppermute x10, waiting for transfers between devices, flip(): return lax.ppermute(x, AXIS, [(i, i ^ bit) for i in range(devices)])  68.9 us
    pallas_call x2, Pallas kernels, attend_backward(): pl.pallas_call(functools.partial(attend_backward_kernel, 2 * pair), grid=...  58 us
    pallas_call x2, Pallas kernels, home(): pl.pallas_call(functools.partial(home_kernel, bits, places, len(parts)),...  46.6 us
  transfers between devices with their start and end apart: 16, of which 4 were waited for; matrix products, arithmetic and copies ran while one was open for 17% of the time, Pallas kernels for 67%

profile of v2, /device:TPU:0, one launch (start us, length us, event | category | flops | bytes accessed | tf_op | source)
XLA Modules:
  0.0 996.1 jit_solution(13151375546079190724)
XLA Ops:
  7.2 1.5 reshape.174
  9.9 1.5 reshape.176
  13.8 1.6 slice_dynamic-update-slice_fusion.4
  16.7 1.6 slice_dynamic-update-slice_fusion.1
  20.5 1.5 reshape.182
  24.5 1.5 pad_maximum_fusion
  26.0 5.2 all-to-all-start
  32.1 104.7 %front.1 = (bf16[2048,2048]{1,0:T(8,128)(2,1)}, bf16[4,512,768]{2,1,0:T(8,128)(2,1)}, f32[32,8,128]{2,1,0:T(8,128)}) custom-call(bf16[256,2048]{1,0:T(8,128)(2,1)} %tokens_ref.3, bf16[8,64,768]{2,1,0:T(8,128)(2,1)} %slice_dynamic-update-slice_fusion.mine_ref, f32[8,128]{1,0:T(8,128)} %maximum_maximum_fusion.small_ref), custom_call_target="tpu_custom_call" | custom-call | bytes 200000000 | tf_op jit(solution)/shard_map/front/pallas_call | solution.py:529
  136.8 1.6 slice_reduce_fusion
  138.5 5.1 fusion
  143.7 12.5 %fusion.15.qkv_ref = f32[2048,768]{1,0:T(8,128)} fusion(bf16[2048,768]{1,0:T(8,128)(2,1)} %bitcast.107, bf16[2048,2048]{1,0:T(8,128)(2,1)} %get-tuple-element.64, f32[2048]{0:T(1024)S(1)} %mul.99, f32[2048]{0:T(1024)S(1)} %add_rsqrt_fusion), kind=kOutput, calls=%fused_computation.72 | convolution fusion | flops 6459228160 | bytes 17842176 | tf_op jit(solution)/shard_map/dot_general | solution.py:25
  158.7 1.5 collective-permute-start
  168.9 31.5 %attend_forward.1 = (bf16[2,2048,128]{2,1,0:T(8,128)(2,1)}, bf16[2,2048,128]{2,1,0:T(8,128)(2,1)}, bf16[2,2048,128]{2,1,0:T(8,128)(2,1)}, bf16[2048,256]{1,0:T(8...) custom-call(f32[2048,768]{1,0:T(8,128)} %fusion.15.qkv_ref, f32[2048,128]{1,0:T(8,128)} %copy.42.cos_ref, ...), custom_call_target="tpu_custom_call" | custom-call | flops 17179869184 | bytes 12582912 | tf_op jit(solution)/shard_map/attend_forward/pallas_call | solution.py:115
  201.2 14.2 %collective-permute-done.1.refs_2_ = bf16[8,64,1024]{2,1,0:T(8,128)(2,1)} collective-permute-done((bf16[8,64,1024]{2,1,0:T(8,128)(2,1)S(1)}, bf16[8,64,1024]{2,1,0:T(8,128)(2,1)}, u32[]{:S(2)}, u32[]{:S(2)}) %collective-permute-start.1) | collective-permute-done | bytes 1048608 | tf_op jit(solution)/shard_map/ppermute | solution.py:871
  215.4 13.2 %collective-permute-done.2.refs_4_ = bf16[256,2048]{1,0:T(8,128)(2,1)} collective-permute-done((bf16[256,2048]{1,0:T(8,128)(2,1)}, bf16[256,2048]{1,0:T(8,128)(2,1)}, u32[]{:S(2)}, u32[]{:S(2)}) %collective-permute-start.2) | collective-permute-done | bytes 1048608 | tf_op jit(solution)/shard_map/ppermute | solution.py:871
  229.3 229.2 %attention_branch.1 = (f32[256,2048]{1,0:T(8,128)}, bf16[2048,2048]{1,0:T(8,128)(2,1)}, f32[8,128]{1,0:T(8,128)}, bf16[32,64,1024]{2,1,0:T(8,128)(2,1)}, bf16[32...) custom-call(bf16[2048,256]{1,0:T(8,128)(2,1)} %get-tuple-element.75.left_ref, ...), custom_call_target="tpu_custom_call" | custom-call | flops 2147483648 | bytes 300000000 | tf_op jit(solution)/shard_map/attention_branch/pallas_call | solution.py:671
  458.4 1.4 constant_dynamic-slice_fusion
  460.6 14.6 %fusion.17 = f32[2048,1024]{1,0:T(8,128)} fusion(bf16[2048,2048]{1,0:T(8,128)(2,1)} %get-tuple-element.80, bf16[2048,1024]{1,0:T(8,128)(2,1)} %bitcast.121), kind=kOutput, calls=%fused_computation.73 | convolution fusion | flops 8589934592 | bytes 20971520 | tf_op jit(solution)/shard_map/dot_general | solution.py:25
  475.2 13.8 %multiply_convert_fusion.2 = (bf16[2048,1024]{1,0:T(8,128)(2,1)}, f32[2048,1024]{1,0:T(8,128)}) fusion(f32[2048,1024]{1,0:T(8,128)} %fusion.17, bf16[2048,2048]{1,0:T(8,128)(2,1)S(1)} %bitcast.120, bf16[2048,1024]{1,0:T(8,128)(2,1)S(1)} %bitcast.124), kind=kOutput, calls=%fused_computation.7 | convolution fusion | flops 8602517504 | bytes 33554432 | tf_op jit(solution)/shard_map/dot_general | solution.py:25
  490.0 12.7 %convolution_convert_fusion = bf16[1024,2048]{1,0:T(8,128)(2,1)S(1)} fusion(bf16[2048,1024]{1,0:T(8,128)(2,1)} %get-tuple-element.124.hidden_ref, bf16[2048,2048]{1,0:T(8,128)(2,1)} %all-gather.3.cloned.1.call-done), kind=kOutput, calls=%fused_computation.16 | convolution fusion | flops 8592031744 | bytes 16777216 | tf_op jit(solution)/shard_map/dot_general | solution.py:25
  502.9 1.5 collective-permute-start.4
  504.4 22.2 %multiply_convert_fusion = (bf16[2048,1024]{1,0:T(8,128)(2,1)}, bf16[2048,1024]{1,0:T(8,128)(2,1)}) fusion(f32[2048,1024]{1,0:T(8,128)} %fusion.17, f32[2048,1024]{1,0:T(8,128)} %get-tuple-element.125, bf16[2048,2048]{1,0:T(8,128)(2,1)} %all-gather.3.cloned.1.call-done, bf16[1024,2048]{1,0:T(8,128)(2,1)} %bitcast.17.down_ref), kind=kOutput, calls=%fused_computation.5 | convolution fusion | flops 8617197568 | bytes 37748736 | tf_op jit(solution)/shard_map/dot_general | solution.py:25
  526.6 12.7 %convolution_convert_fusion.2 = bf16[2048,1024]{1,0:T(8,128)(2,1)S(1)} fusion(bf16[2048,2048]{1,0:T(8,128)(2,1)} %get-tuple-element.80, bf16[2048,1024]{1,0:T(8,128)(2,1)} %get-tuple-element.86.gate_ref), kind=kOutput, calls=%fused_computation.18 | convolution fusion | flops 8592031744 | bytes 16777216 | tf_op jit(solution)/shard_map/dot_general | solution.py:25
  539.3 11.0 %collective-permute-done.4 = bf16[2,256,2048]{2,1,0:T(8,128)(2,1)} collective-permute-done((bf16[2,256,2048]{2,1,0:T(8,128)(2,1)S(1)}, bf16[2,256,2048]{2,1,0:T(8,128)(2,1)}, u32[]{:S(2)}, u32[]{:S(2)}) %collective-permute-start.4) | collective-permute-done | bytes 2097184 | tf_op jit(solution)/shard_map/ppermute | solution.py:871
  550.3 2.4 fusion.6
  552.6 1.5 dynamic-slice_bitcast_fusion.1
  555.7 119.4 %ffn_back.1 = (f32[256,2048]{1,0:T(8,128)}, bf16[2048,2048]{1,0:T(8,128)(2,1)}) custom-call(bf16[2048,1024]{1,0:T(8,128)(2,1)} %get-tuple-element.86.gate_ref, bf16[2048,1024]{1,0:T(8,128)(2,1)} %get-tuple-element.90.up_ref, bf16[2048,1024]{1,0:T(8,128)(2,1)} %bitcast.122, bf16[2048,1024]{1,0:T(8,128)(2,1)} %bitcast.123, ...), custom_call_target="tpu_custom_call" | custom-call | flops 17179869184 | bytes 250000000 | tf_op jit(solution)/shard_map/ffn_back/pallas_call | solution.py:717
  675.2 14.1 %convolution_convert_fusion.1 = bf16[2048,1024]{1,0:T(8,128)(2,1)} fusion(bf16[2048,2048]{1,0:T(8,128)(2,1)} %get-tuple-element.80, bf16[2048,1024]{1,0:T(8,128)(2,1)} %get-tuple-element.90.up_ref), kind=kOutput, calls=%fused_computation.17 | convolution fusion | flops 8592031744 | bytes 16777216 | tf_op jit(solution)/shard_map/dot_general | solution.py:25
  689.3 3.3 convolution_convert_fusion.5
  692.7 7.2 convolution_convert_fusion.6.grad_ref
  699.9 1.8 fusion.9
  701.7 2.6 fusion.5
  704.3 1.6 dynamic-slice_bitcast_fusion
  707.4 28.9 %attend_backward.2.left_ref = bf16[2048,384]{1,0:T(8,128)(2,1)} custom-call(bf16[2,2048,128]{2,1,0:T(8,128)(2,1)} %get-tuple-element.71.q_ref, bf16[2,2048,128]{2,1,0:T(8,128)(2,1)} %get-tuple-element.72.k_ref, bf16[2,2048,128]{2,1,0:T(8,128)(2,1)} %get-tuple-element.73.v_ref, bf16[2048,256]{1,0:T(8,128)(2,1)} %convolution_convert_fusion.6.grad_ref, ...), custom_call_target="tpu_custom_call" | custom-call | flops 21474836480 | bytes 6291456 | tf_op jit(solution)/shard_map/attend_backward/pallas_call | solution.py:179
  736.3 9.9 convolution_convert_fusion.4
  746.3 30.5 %collective-permute-done.7 = bf16[2,2,2,64,1024]{4,3,2,1,0:T(8,128)(2,1)} collective-permute-done((bf16[2,2,2,64,1024]{4,3,2,1,0:T(8,128)(2,1)}, bf16[2,2,2,64,1024]{4,3,2,1,0:T(8,128)(2,1)}, u32[]{:S(2)}, u32[]{:S(2)}) %collective-permute-start.7) | collective-permute-done | bytes 1048608 | tf_op jit(solution)/shard_map/ppermute | solution.py:871
  776.8 2.6 fusion.8
  779.4 3.4 fusion.4
  782.8 29.1 %attend_backward.3.other_ref = bf16[2048,384]{1,0:T(8,128)(2,1)} custom-call(bf16[2,2048,128]{2,1,0:T(8,128)(2,1)} %get-tuple-element.71.q_ref, bf16[2,2048,128]{2,1,0:T(8,128)(2,1)} %get-tuple-element.72.k_ref, bf16[2,2048,128]{2,1,0:T(8,128)(2,1)} %get-tuple-element.73.v_ref, bf16[2048,256]{1,0:T(8,128)(2,1)} %convolution_convert_fusion.6.grad_ref, ...), custom_call_target="tpu_custom_call" | custom-call | flops 21474836480 | bytes 6291456 | tf_op jit(solution)/shard_map/attend_backward/pallas_call | solution.py:179
  811.9 10.0 %convolution_convert_fusion.3 = bf16[2048,384]{1,0:T(8,128)(2,1)} fusion(bf16[2048,384]{1,0:T(8,128)(2,1)} %attend_backward.3.other_ref, bf16[2048,2048]{1,0:T(8,128)(2,1)} %get-tuple-element.64, f32[2048]{0:T(1024)S(1)} %copy-done.21, f32[2048]{0:T(1024)S(1)} %copy-done.23), kind=kOutput, calls=%fused_computation.19 | convolution fusion | flops 3238789120 | bytes 11550720 | tf_op jit(solution)/shard_map/dot_general | solution.py:25
  827.1 1.8 multiply_convert_fusion.3
  828.9 1.6 convert_element_type.189
  830.5 1.8 convert_element_type.184
  832.3 97.7 %last_sums.1 = (f32[256,2048]{1,0:T(8,128)}, bf16[256,2048]{1,0:T(8,128)(2,1)}) custom-call(bf16[2048,384]{1,0:T(8,128)(2,1)} %attend_backward.2.left_ref, bf16[2048,384]{1,0:T(8,128)(2,1)} %attend_backward.3.other_ref, bf16[2048,768]{1,0:T(8,128)(2,1)} %bitcast.108, bf16[256,2048]{1,0:T(8,128)(2,1)} %tokens_ref.3, f32[1,2048]{1,0:T(1,128)} %reshape_squeeze.7.gain_ref, ...), custom_call_target="tpu_custom_call" | custom-call | flops 805306368 | bytes 300000000 | tf_op jit(solution)/shard_map/last_sums/pallas_call | solution.py:768
  929.9 2.7 fusion.7
  932.6 31.3 %home_ffn.1 = (f32[64,8192]{1,0:T(8,128)}, f32[64,8192]{1,0:T(8,128)}, f32[64,1]{1,0:T(8,128)}) custom-call(bf16[8,64,1024]{2,1,0:T(8,128)(2,1)} %bitcast.105, bf16[8,64,1024]{2,1,0:T(8,128)(2,1)} %bitcast.106, bf16[64,8192]{1,0:T(8,128)(2,1)} %refs_2_.3, bf16[64,8192]{1,0:T(8,128)(2,1)} %refs_3_.4, f32[64,1]{1,0:T(8,128)} %copy.55.refs_4_), custom_call_target="tpu_custom_call" | custom-call | flops 1000000 | bytes 30000000 | tf_op jit(solution)/shard_map/home_ffn/pallas_call | solution.py:830
  963.9 1.4 reduce.4
  965.3 15.4 %home_attn.1 = (f32[64,2048]{1,0:T(8,128)}, f32[64,2048]{1,0:T(8,128)}, f32[64,2048]{1,0:T(8,128)}, f32[64,1]{1,0:T(8,128)}) custom-call(bf16[8,64,384]{2,1,0:T(8,128)(2,1)} %bitcast.112, bf16[8,64,384]{2,1,0:T(8,128)(2,1)} %bitcast.113, bf16[64,2048]{1,0:T(8,128)(2,1)} %refs_2_.2, bf16[64,2048]{1,0:T(8,128)(2,1)} %refs_3_.3, bf16[64,2048]{1,0:T(8,128)(2,1)} %refs_4_.1, ...), custom_call_target="tpu_custom_call" | custom-call | flops 1000000 | bytes 30000000 | tf_op jit(solution)/shard_map/home_attn/pallas_call | solution.py:830
  (156 shorter events, 41.6 us)
Async XLA Ops:
  7.2 5.5 copy-start.13
  8.7 10.2 %copy-start.7 = (bf16[64,8192]{1,0:T(8,128)(2,1)S(1)}, bf16[64,8192]{1,0:T(8,128)(2,1)}, u32[]{:S(2)}) copy-start(bf16[64,8192]{1,0:T(8,128)(2,1)} %refs_2_.3) | copy-start | bytes 3145732
  13.4 8.7 copy-start.6
  22.9 1.6 copy-start.8
  24.5 6.9 copy-start.26
  24.5 6.9 copy-start.28
  24.5 7.0 copy-start.24
  26.0 117.6 %all-to-all-start = ((bf16[8,64,2048]{2,1,0:T(8,128)(2,1)}), bf16[8,64,2048]{2,1,0:T(8,128)(2,1)S(1)}, u32[]{:S(2)}, u32[]{:S(2)}) async-start(bf16[8,64,2048]{2,1,0:T(8,128)(2,1)} %pad_maximum_fusion), calls=%async_computation | async-start | bytes 4194304 | tf_op jit(solution)/shard_map/all_to_all | solution.py:882
  31.3 197.4 %all-gather.5.cloned.1.call-start = ((), (), s32[]{:S(2)}) async-start(), calls=%async_computation.5 | async-start | bytes 1310720 | tf_op jit(solution)/shard_map/all_gather | solution.py:874
  138.5 5.2 copy-start.20
  143.6 12.6 %copy-start.22 = (f32[2048]{0:T(1024)}, f32[2048]{0:T(1024)S(1)}, u32[]{:S(2)}) copy-start(f32[2048]{0:T(1024)S(1)} %add_rsqrt_fusion) | copy-start | bytes 24580
  143.6 24.5 %copy-start.1 = (bf16[8,64,2048]{2,1,0:T(8,128)(2,1)}, bf16[8,64,2048]{2,1,0:T(8,128)(2,1)S(1)}, u32[]{:S(2)}) copy-start(bf16[8,64,2048]{2,1,0:T(8,128)(2,1)S(1)} %all-to-all-done.refs_0_) | copy-start | bytes 6291460
  143.7 346.3 %all-gather.3.cloned.1.call-start = ((), (), s32[]{:S(2)}) async-start(), calls=%async_computation.4 | async-start | bytes 9437184 | tf_op jit(solution)/shard_map/all_gather | solution.py:1000
  156.2 674.3 %reduce-scatter.8.cloned.1.call-start = ((), (), s32[]{:S(2)}) async-start(), calls=%async_computation.8 | async-start | bytes 1310720 | tf_op jit(solution)/shard_map/reduce_scatter | solution.py:877
  158.7 69.9 %collective-permute-start = (bf16[8,64,2048]{2,1,0:T(8,128)(2,1)S(1)}, bf16[8,64,2048]{2,1,0:T(8,128)(2,1)}, u32[]{:S(2)}, u32[]{:S(2)}) collective-permute-start(bf16[8,64,2048]{2,1,0:T(8,128)(2,1)S(1)} %all-to-all-done.refs_0_), channel_id=1, source_target_pairs={{0,4},{1,5},{2,6},{3,7},{4,0},{5,1},{6,2},{7,3},{8,12},{9,13},{10,... | collective-permute-start | bytes 6291464 | tf_op jit(solution)/shard_map/ppermute | solution.py:871
  161.0 6.4 copy-start.19
  168.2 47.2 %collective-permute-start.1 = (bf16[8,64,1024]{2,1,0:T(8,128)(2,1)S(1)}, bf16[8,64,1024]{2,1,0:T(8,128)(2,1)}, u32[]{:S(2)}, u32[]{:S(2)}) collective-permute-start(bf16[8,64,1024]{2,1,0:T(8,128)(2,1)S(1)} %slice.46), channel_id=1, source_target_pairs={{0,16},{1,17},{2,18},{3,19},{4,20},{5,21},{6,22},{7,23},{8,24},{9,... | collective-permute-start | bytes 3145736 | tf_op jit(solution)/shard_map/ppermute | solution.py:871
  168.3 60.4 %collective-permute-start.2 = (bf16[256,2048]{1,0:T(8,128)(2,1)}, bf16[256,2048]{1,0:T(8,128)(2,1)}, u32[]{:S(2)}, u32[]{:S(2)}) collective-permute-start(bf16[256,2048]{1,0:T(8,128)(2,1)} %refs_3_.2), channel_id=1, source_target_pairs={{0,4},{1,5},{2,6},{3,7},{4,0},{5,1},{6,2},{7,3},{8,12},{9,13},{10,... | collective-permute-start | bytes 3145736 | tf_op jit(solution)/shard_map/ppermute | solution.py:871
  458.4 16.7 %slice-start = ((s8[8388608]{0:T(1024)(128)(4,1)}), s8[4194304]{0:T(1024)(128)(4,1)S(1)}, s32[]{:S(2)}) async-start(s8[8388608]{0:T(1024)(128)(4,1)} %bitcast.119), calls=%async_computation.9 | async-start | bytes 8388608
  459.9 29.0 %collective-permute-start.3 = (bf16[1,256,2048]{2,1,0:T(8,128)(2,1)S(1)}, bf16[1,256,2048]{2,1,0:T(8,128)(2,1)S(1)}, u32[]{:S(2)}, u32[]{:S(2)}) collective-permute-start(bf16[1,256,2048]{2,1,0:T(8,128)(2,1)S(1)} %constant_dynamic-slice_fusion), channel_id=1, source_target_pairs={{0,4},{1,5},{2,6},{3,7},{4,0},{5,1},{6,2},{7,3},{8,12},{9,13},{10,... | collective-permute-start | bytes 3145736 | tf_op jit(solution)/shard_map/ppermute | solution.py:871
  460.6 14.6 %slice-start.1 = ((s8[8388608]{0:T(1024)(128)(4,1)}), s8[4194304]{0:T(1024)(128)(4,1)S(1)}, s32[]{:S(2)}) async-start(s8[8388608]{0:T(1024)(128)(4,1)} %bitcast.119), calls=%async_computation.10 | async-start | bytes 8388608
  460.6 14.6 %copy-start.25 = (bf16[32,64,1024]{2,1,0:T(8,128)(2,1)S(1)}, bf16[32,64,1024]{2,1,0:T(8,128)(2,1)}, u32[]{:S(2)}) copy-start(bf16[32,64,1024]{2,1,0:T(8,128)(2,1)} %get-tuple-element.82) | copy-start | bytes 12582916
  502.9 47.3 %collective-permute-start.4 = (bf16[2,256,2048]{2,1,0:T(8,128)(2,1)S(1)}, bf16[2,256,2048]{2,1,0:T(8,128)(2,1)}, u32[]{:S(2)}, u32[]{:S(2)}) collective-permute-start(bf16[2,256,2048]{2,1,0:T(8,128)(2,1)S(1)} %dynamic-slice_bitcast_fusion.2), channel_id=1, source_target_pairs={{0,4},{1,5},{2,6},{3,7},{4,0},{5,1},{6,2},{7,3},{8,12},{9,13},{10,... | collective-permute-start | bytes 6291464 | tf_op jit(solution)/shard_map/ppermute | solution.py:871
  539.3 14.9 %copy-start.4 = (bf16[2048,1024]{1,0:T(8,128)(2,1)}, bf16[2048,1024]{1,0:T(8,128)(2,1)S(1)}, u32[]{:S(2)}) copy-start(bf16[2048,1024]{1,0:T(8,128)(2,1)S(1)} %convolution_convert_fusion.2) | copy-start | bytes 12582916
  554.1 147.5 %collective-permute-start.6 = (bf16[2,2,2,2,64,1024]{5,4,3,2,1,0:T(8,128)(2,1)}, bf16[2,2,2,2,64,1024]{5,4,3,2,1,0:T(8,128)(2,1)}, u32[]{:S(2)}, u32[]{:S(2)}) collective-permute-start(bf16[2,2,2,2,64,1024]{5,4,3,2,1,0:T(8,128)(2,1)} %dynamic-slice_bitcast_fusion.1), channel_id=1, source_target_pairs={{0,4},{1,5},{2,6},{3,7},{4,0},{5,1},{6,2},{7,3},{8,12},{9,13},{10,... | collective-permute-start | bytes 6291464 | tf_op jit(solution)/shard_map/ppermute | solution.py:871
  554.7 145.2 %collective-permute-start.5 = (bf16[256,2048]{1,0:T(8,128)(2,1)S(1)}, bf16[256,2048]{1,0:T(8,128)(2,1)}, u32[]{:S(2)}, u32[]{:S(2)}) collective-permute-start(bf16[256,2048]{1,0:T(8,128)(2,1)S(1)} %dynamic-slice_bitcast_fusion.5), channel_id=1, source_target_pairs={{0,16},{1,17},{2,18},{3,19},{4,20},{5,21},{6,22},{7,23},{8,24},{9,... | collective-permute-start | bytes 3145736 | tf_op jit(solution)/shard_map/ppermute | solution.py:871
  675.1 14.1 %copy-start = (bf16[2048,2048]{1,0:T(8,128)(2,1)S(1)}, bf16[2048,2048]{1,0:T(8,128)(2,1)}, u32[]{:S(2)}) copy-start(bf16[2048,2048]{1,0:T(8,128)(2,1)} %get-tuple-element.89) | copy-start | bytes 25165828
  675.1 14.1 %copy-start.2 = (bf16[2048,256]{1,0:T(8,128)(2,1)S(1)}, bf16[2048,256]{1,0:T(8,128)(2,1)}, u32[]{:S(2)}) copy-start(bf16[2048,256]{1,0:T(8,128)(2,1)} %get-tuple-element.75.left_ref) | copy-start | bytes 3145732
  692.6 272.7 %reduce-scatter.4.cloned.1.call-start = ((), (), s32[]{:S(2)}) async-start(), calls=%async_computation.6 | async-start | bytes 1966080 | tf_op jit(solution)/shard_map/reduce_scatter | solution.py:877
  692.7 9.0 copy-start.5
  699.9 4.4 copy-start.3
  705.8 73.5 %collective-permute-start.8 = (bf16[2,2,2,2,64,1024]{5,4,3,2,1,0:T(8,128)(2,1)}, bf16[2,2,2,2,64,1024]{5,4,3,2,1,0:T(8,128)(2,1)}, u32[]{:S(2)}, u32[]{:S(2)}) collective-permute-start(bf16[2,2,2,2,64,1024]{5,4,3,2,1,0:T(8,128)(2,1)} %dynamic-slice_bitcast_fusion), channel_id=1, source_target_pairs={{0,4},{1,5},{2,6},{3,7},{4,0},{5,1},{6,2},{7,3},{8,12},{9,13},{10,... | collective-permute-start | bytes 6291464 | tf_op jit(solution)/shard_map/ppermute | solution.py:871
  707.4 69.4 %collective-permute-start.7 = (bf16[2,2,2,64,1024]{4,3,2,1,0:T(8,128)(2,1)}, bf16[2,2,2,64,1024]{4,3,2,1,0:T(8,128)(2,1)}, u32[]{:S(2)}, u32[]{:S(2)}) collective-permute-start(bf16[2,2,2,64,1024]{4,3,2,1,0:T(8,128)(2,1)} %dynamic-slice_bitcast_fusion.4), channel_id=1, source_target_pairs={{0,16},{1,17},{2,18},{3,19},{4,20},{5,21},{6,22},{7,23},{8,24},{9,... | collective-permute-start | bytes 3145736 | tf_op jit(solution)/shard_map/ppermute | solution.py:871
  707.4 28.9 %copy-start.21 = (f32[2048]{0:T(1024)S(1)}, f32[2048]{0:T(1024)}, u32[]{:S(2)}) copy-start(f32[2048]{0:T(1024)} %copy-done.20) | copy-start | bytes 24580
  707.4 28.9 %copy-start.23 = (f32[2048]{0:T(1024)S(1)}, f32[2048]{0:T(1024)}, u32[]{:S(2)}) copy-start(f32[2048]{0:T(1024)} %copy-done.22) | copy-start | bytes 24580
  746.2 219.0 %reduce-scatter.6.cloned.1.call-start = ((), (), s32[]{:S(2)}) async-start(), calls=%async_computation.7 | async-start | bytes 1966080 | tf_op jit(solution)/shard_map/reduce_scatter | solution.py:877
  811.9 11.1 %copy-start.27 = (bf16[64]{0:T(256)(128)(2,1)S(1)}, bf16[64]{0:T(256)(128)(2,1)}, u32[]{:S(2)}) copy-start(bf16[64]{0:T(256)(128)(2,1)} %param.21) | copy-start | bytes 388
  811.9 11.8 %copy-start.29 = (bf16[64]{0:T(256)(128)(2,1)S(1)}, bf16[64]{0:T(256)(128)(2,1)}, u32[]{:S(2)}) copy-start(bf16[64]{0:T(256)(128)(2,1)} %param.16) | copy-start | bytes 388
  811.9 12.5 %copy-start.18 = (f32[32,1,64]{2,1,0:T(1,128)S(1)}, f32[32,1,64]{2,1,0:T(1,128)}, u32[]{:S(2)}) copy-start(f32[32,1,64]{2,1,0:T(1,128)} %get-tuple-element.118) | copy-start | bytes 24580
  811.9 15.2 %copy-start.9 = (bf16[64,2048]{1,0:T(8,128)(2,1)S(1)}, bf16[64,2048]{1,0:T(8,128)(2,1)}, u32[]{:S(2)}) copy-start(bf16[64,2048]{1,0:T(8,128)(2,1)} %refs_2_.2) | copy-start | bytes 786436
  823.0 107.0 %collective-permute-start.9 = (bf16[2,2,2,64,1024]{4,3,2,1,0:T(8,128)(2,1)}, bf16[2,2,2,64,1024]{4,3,2,1,0:T(8,128)(2,1)}, u32[]{:S(2)}, u32[]{:S(2)}) collective-permute-start(bf16[2,2,2,64,1024]{4,3,2,1,0:T(8,128)(2,1)} %dynamic-slice_bitcast_fusion.3), channel_id=1, source_target_pairs={{0,16},{1,17},{2,18},{3,19},{4,20},{5,21},{6,22},{7,23},{8,24},{9,... | collective-permute-start | bytes 3145736 | tf_op jit(solution)/shard_map/ppermute | solution.py:871
  929.9 52.1 %copy-start.14 = (bf16[256,2048]{1,0:T(8,128)(2,1)S(1)}, bf16[256,2048]{1,0:T(8,128)(2,1)}, u32[]{:S(2)}) copy-start(bf16[256,2048]{1,0:T(8,128)(2,1)} %get-tuple-element.142) | copy-start | bytes 3145732
  932.6 50.4 %copy-start.10 = (f32[256,2048]{1,0:T(8,128)S(1)}, f32[256,2048]{1,0:T(8,128)}, u32[]{:S(2)}) copy-start(f32[256,2048]{1,0:T(8,128)} %get-tuple-element.143) | copy-start | bytes 6291460
  982.0 2.3 copy-start.17
  982.0 3.1 copy-start.16
  982.0 3.9 copy-start.15
  982.0 4.7 copy-start.12
  984.4 3.7 copy-start.11
Sparse Core Ops, SparseCore 0:
  143.8 25.2 all-gather.4
  170.7 87.1 all-gather.2
  692.7 31.0 reduce-scatter.7
  746.4 41.0 reduce-scatter.3
  822.0 75.0 reduce-scatter.5

commit v3 on v2

v3 whole, which is shorter than its diff:
```python
import functools

import jax
import jax.numpy as jnp
import numpy as np
from jax import lax
from jax.experimental import pallas as pl
from jax.experimental.pallas import tpu as pltpu
from jax.sharding import PartitionSpec as P

HEAD_DIM = 64
SEQ = 2048
BLOCK = 256
HALF = 128
LAST_CUT = 0
EARLY_UP = 512
BRANCH_CUT = 128
AXIS = "fsdp"
MESH = pl.DeviceIdType.MESH

epsilon = 1e-05
rope_base = 130000.0
bf16 = jnp.bfloat16
f32 = jnp.float32
vmem = pl.BlockSpec(memory_space=pltpu.VMEM)
anywhere = pl.BlockSpec(memory_space=pl.ANY)


def contract(left, right, left_dim, right_dim):
    return lax.dot_general(
        left, right, (((left_dim,), (right_dim,)), ((), ())), preferred_element_type=f32
    )


def rope_tables(length, width):
    half_dim = HEAD_DIM // 2
    inverse = rope_base ** (-np.arange(half_dim) * 2.0 / HEAD_DIM)
    angles = (np.arange(length, dtype=np.float32)[:, None] * inverse.astype(np.float32)).astype(np.float64)
    cosine, sine = np.cos(angles).astype(np.float32), np.sin(angles).astype(np.float32)
    repeats = width // HEAD_DIM
    return (
        jnp.asarray(np.tile(np.concatenate([cosine, cosine], 1), (1, repeats))),
        jnp.asarray(np.tile(np.concatenate([-sine, sine], 1), (1, repeats))),
    )


def swap_halves(rows):
    width = rows.shape[1]
    half = HEAD_DIM // 2
    lane = lax.broadcasted_iota(jnp.int32, rows.shape, 1)
    return jnp.where(
        lane % HEAD_DIM < half, pltpu.roll(rows, width - half, 1), pltpu.roll(rows, half, 1)
    )


PAIR = 2 * HEAD_DIM


def head_mask(shape, head):
    lane = lax.broadcasted_iota(jnp.int32, shape, 1)
    return (lane >= head * HEAD_DIM) & (lane < (head + 1) * HEAD_DIM)


def masked_scores(query, key_ref, row_ref, col_ref, q0, cols):
    tail = min(2 * BLOCK, cols)
    scores = contract(query, key_ref[0:cols, :], 1, 1)
    shown = row_ref[:, pl.ds(cols - tail, tail)] <= col_ref[pl.ds(q0, BLOCK), :]
    hidden = jnp.where(shown, scores[:, cols - tail :], -jnp.inf)
    return jnp.concatenate([scores[:, : cols - tail], hidden], 1) if tail < cols else hidden


def attend_forward_kernel(
    qkv_ref, cos_ref, sin_ref, row_ref, col_ref, q_ref, k_ref, v_ref, out_ref, lse_ref, peak_ref
):
    pairs, length, _ = q_ref.shape
    for t in range(length // BLOCK):
        rows = pl.ds(t * BLOCK, BLOCK)
        cosine, sine = cos_ref[rows, :], sin_ref[rows, :]
        for pair in range(pairs):
            first = 3 * pair * PAIR
            query = qkv_ref[rows, first : first + PAIR]
            query = (query * cosine + swap_halves(query) * sine).astype(bf16)
            q_ref[pair, rows, :] = (query.astype(f32) * HEAD_DIM ** (-0.5)).astype(bf16)
            key = qkv_ref[rows, first + PAIR : first + 2 * PAIR]
            k_ref[pair, rows, :] = (key * cosine + swap_halves(key) * sine).astype(bf16)
            v_ref[pair, rows, :] = qkv_ref[rows, first + 2 * PAIR : first + 3 * PAIR].astype(bf16)
    peak_ref[...] = jnp.full(peak_ref.shape, -jnp.inf, f32)
    lane = lax.broadcasted_iota(jnp.int32, (BLOCK, 128), 1)
    for t in range(length // BLOCK):
        q0 = t * BLOCK
        rows = pl.ds(q0, BLOCK)
        cols = min(q0 + 2 * BLOCK, length)

        @pl.loop(0, pairs)
        def _(pair):
            total = jnp.zeros((BLOCK, PAIR), f32)
            for sub in range(2):
                head = 2 * pair + sub
                mask = head_mask((BLOCK, PAIR), sub)
                query = jnp.where(mask, q_ref[pair, rows, :], 0).astype(bf16)
                scores = masked_scores(query, k_ref.at[pair], row_ref, col_ref, q0, cols)
                row_max = jnp.max(scores, 1, keepdims=True)
                numerators = jnp.exp(scores - row_max)
                totals = jnp.sum(numerators, 1, keepdims=True)
                mixed = contract(numerators.astype(bf16), v_ref[pair, 0:cols, :], 1, 0) / totals
                total = jnp.where(mask, mixed, total)
                lse_ref[rows, :] = jnp.where(lane == head, row_max + jnp.log(totals), lse_ref[rows, :])
                peak_ref[...] = jnp.where(
                    lax.broadcasted_iota(jnp.int32, peak_ref.shape, 1) == head,
                    jnp.maximum(peak_ref[...], jnp.max(row_max)),
                    peak_ref[...],
                )
            out_ref[rows, pl.ds(pl.multiple_of(pair * PAIR, PAIR), PAIR)] = total.astype(bf16)


def attend_forward(qkv, cosine, sine, row_blocks, col_blocks):
    length = qkv.shape[0]
    pairs = qkv.shape[1] // (3 * PAIR)
    shape = jax.ShapeDtypeStruct
    return pl.pallas_call(
        attend_forward_kernel,
        out_shape=(
            shape((pairs, length, PAIR), bf16),
            shape((pairs, length, PAIR), bf16),
            shape((pairs, length, PAIR), bf16),
            shape((length, pairs * PAIR), bf16),
            shape((length, 128), f32),
            shape((8, 128), f32),
        ),
        in_specs=[vmem] * 5,
        out_specs=tuple([vmem] * 6),
        compiler_params=pltpu.CompilerParams(vmem_limit_bytes=56 * 1024 * 1024),
        cost_estimate=pl.CostEstimate(
            flops=16 * pairs * length * length * PAIR, bytes_accessed=length * PAIR * pairs * 24,
            transcendentals=2 * pairs * length * length,
        ),
        name="attend_forward",
    )(qkv, cosine, sine, row_blocks, col_blocks)


def attend_backward_kernel(
    first_head, q_ref, k_ref, v_ref, grad_ref, lse_ref, cos_ref, sin_ref, row_ref, col_ref, out_ref, dk_ref, dv_ref
):
    length = q_ref.shape[0]
    dk_ref[...] = jnp.zeros_like(dk_ref)
    dv_ref[...] = jnp.zeros_like(dv_ref)
    lane = lax.broadcasted_iota(jnp.int32, (BLOCK, 128), 1)
    for t in range(length // BLOCK):
        q0 = t * BLOCK
        rows = pl.ds(q0, BLOCK)
        cols = min(q0 + 2 * BLOCK, length)

        def one_head(sub, dq):
            mask = head_mask((BLOCK, PAIR), sub)
            query = jnp.where(mask, q_ref[rows, :], 0).astype(bf16)
            grad = jnp.where(mask, grad_ref[rows, :], 0).astype(bf16)
            lse = jnp.sum(
                jnp.where(lane == first_head + sub, lse_ref[rows, :], 0.0), 1, keepdims=True
            )
            scores = masked_scores(query, k_ref, row_ref, col_ref, q0, cols)
            attention = jnp.exp(scores - lse)
            grad_attention = contract(grad, v_ref[0:cols, :], 1, 1)
            weighted = attention * grad_attention
            centre = jnp.sum(weighted, 1, keepdims=True)
            grad_scores = (weighted - attention * centre).astype(bf16)
            dv_ref[0:cols, :] += contract(attention.astype(bf16), grad, 0, 0)
            dk_ref[0:cols, :] += contract(grad_scores, query, 0, 0)
            return jnp.where(mask, contract(grad_scores, k_ref[0:cols, :], 1, 0), dq)

        dq = lax.fori_loop(0, 2, one_head, jnp.zeros((BLOCK, PAIR), f32)) * HEAD_DIM ** (-0.5)
        out_ref[rows, 0:PAIR] = (dq * cos_ref[rows, :] - swap_halves(dq) * sin_ref[rows, :]).astype(bf16)
    for t in range(length // BLOCK):
        rows = pl.ds(t * BLOCK, BLOCK)
        dk = dk_ref[rows, :]
        out_ref[rows, PAIR : 2 * PAIR] = (
            dk * cos_ref[rows, :] - swap_halves(dk) * sin_ref[rows, :]
        ).astype(bf16)
        out_ref[rows, 2 * PAIR : 3 * PAIR] = dv_ref[rows, :].astype(bf16)


def attend_backward(pair, query, key, value, grad, lse, cosine, sine, row_blocks, col_blocks):
    length = query.shape[1]
    heads = pl.BlockSpec((None, length, PAIR), lambda _: (pair, 0, 0))
    return pl.pallas_call(
        functools.partial(attend_backward_kernel, 2 * pair),
        grid=(1,),
        out_shape=jax.ShapeDtypeStruct((length, 3 * PAIR), bf16),
        in_specs=[heads] * 3 + [pl.BlockSpec((length, PAIR), lambda _: (0, pair))] + [vmem] * 5,
        out_specs=vmem,
        scratch_shapes=[pltpu.VMEM((length, PAIR), f32), pltpu.VMEM((length, PAIR), f32)],
        compiler_params=pltpu.CompilerParams(vmem_limit_bytes=56 * 1024 * 1024),
        cost_estimate=pl.CostEstimate(
            flops=40 * length * length * PAIR, bytes_accessed=length * PAIR * 24,
            transcendentals=2 * length * length,
        ),
        name="attend_backward",
    )(query, key, value, grad, lse, cosine, sine, row_blocks, col_blocks)


def bit_of(index, bit):
    return lax.rem(lax.div(index, bit), 2)


def flip_bit(index, bit):
    return index + bit - 2 * bit * bit_of(index, bit)


def team_mate(me, bits, offset):
    device, place = me, 0
    for k, bit in enumerate(bits):
        moved = (offset >> k) % 2
        place = place + lax.rem(bit_of(me, bit) + moved, 2) * (1 << k)
        device = flip_bit(device, bit) if moved else device
    return device, place


class Links:

    def __init__(self, send_sems, recv_sems):
        self.send_sems, self.recv_sems = send_sems, recv_sems

    def copy(self, slot, src, dst, device):
        return pltpu.make_async_remote_copy(
            src_ref=src, dst_ref=dst, send_sem=self.send_sems.at[slot],
            recv_sem=self.recv_sems.at[slot], device_id=(device,), device_id_type=MESH,
        )


def greet(partners):
    barrier = pltpu.get_barrier_semaphore()
    for partner in partners:
        pl.semaphore_signal(barrier, inc=1, device_id=(partner,), device_id_type=MESH)
    pl.semaphore_wait(barrier, len(partners))


def spread_block(bits, cut, own_ref, out_ref, links, local_sem):
    core, first, second = bits
    me = lax.axis_index(AXIS)
    sibling, next_a, next_b = (flip_bit(me, bit) for bit in bits)
    block = own_ref.shape[0]
    in_a, in_b = bit_of(me, first), bit_of(me, second)
    spans = {None: (0, block), 0: (0, cut), 1: (cut, block - cut)}

    def rows(flip_a, flip_b, part):
        place = bit_of(me, core)
        place = place + 2 * lax.rem(in_a + flip_a, 2) + 4 * lax.rem(in_b + flip_b, 2)
        start, size = spans[part]
        return pl.ds(pl.multiple_of(place * block + start, 16), size)

    def passed(slot, where, device):
        return links.copy(slot, out_ref.at[where], out_ref.at[where], device)

    def first_hand(slot, part, device):
        start, size = spans[part]
        return links.copy(slot, own_ref.at[pl.ds(start, size)], out_ref.at[rows(0, 0, part)], device)

    makers = {
        0: lambda: first_hand(0, 0, next_a),
        1: lambda: first_hand(1, 1, next_b),
        2: lambda: first_hand(2, 1, next_a),
        3: lambda: first_hand(3, 0, next_b),
        4: lambda: links.copy(4, own_ref, out_ref.at[rows(0, 0, None)], sibling),
        5: lambda: passed(5, rows(1, 0, 0), next_b),
        6: lambda: passed(6, rows(1, 0, 0), sibling),
        7: lambda: passed(7, rows(0, 1, 1), next_a),
        8: lambda: passed(8, rows(0, 1, 1), sibling),
        9: lambda: passed(9, rows(1, 0, 1), sibling),
        10: lambda: passed(10, rows(0, 1, 0), sibling),
        11: lambda: passed(11, rows(1, 1, 0), sibling),
        12: lambda: passed(12, rows(1, 1, 1), sibling),
    }
    needs = {0: 0, 1: 1, 2: 1, 3: 0, 4: None, 5: 0, 6: 0, 7: 1, 8: 1, 9: 1, 10: 0, 11: 0, 12: 1}
    copies = {slot: make() for slot, make in makers.items() if spans[needs[slot]][1]}
    keep = pltpu.make_async_copy(own_ref, out_ref.at[rows(0, 0, None)], local_sem)

    def begin():
        for slot in range(5):
            if slot in copies:
                copies[slot].start()
        keep.start()

    def hand_on(arrived, *sent):
        def phase():
            if arrived in copies:
                copies[arrived].wait_recv()
                for slot in sent:
                    copies[slot].start()

        return phase

    def finish():
        for slot in (4, 6, 8, 9, 10, 11, 12):
            if slot in copies:
                copies[slot].wait_recv()
        keep.wait()
        for slot in copies:
            copies[slot].wait_send()

    return [
        begin, hand_on(0, 5, 6), hand_on(1, 7, 8), hand_on(2, 9), hand_on(3, 10),
        hand_on(5, 11), hand_on(7, 12), finish,
    ]


def run(phases):
    for phase in phases:
        phase()


SPREAD_COPIES = 13
SUM_COPIES = 10


def sum_block(bits, cut, product, total, to_core, from_core, chip_sum, arrived, links):
    core, first, second = bits
    me = lax.axis_index(AXIS)
    sibling, next_a, next_b = (flip_bit(me, bit) for bit in bits)
    block, width = total.shape
    tile = 512

    def place(step, other_core):
        flip_a, flip_b = 1 - step // 2, 1 - step % 2
        return (
            lax.rem(bit_of(me, core) + other_core, 2)
            + 2 * lax.rem(bit_of(me, first) + flip_a, 2)
            + 4 * lax.rem(bit_of(me, second) + flip_b, 2)
        )

    low, high = (0, cut), (cut, block - cut)
    landing = range(6) if cut else {1: 0, 3: 1, 4: 2}

    def link(slot, step, span, device):
        return links.copy(slot, chip_sum.at[step, pl.ds(*span)], arrived.at[landing[slot - 4], pl.ds(0, span[1])], device)

    diag_a, diag_b = (link(4, 0, low, next_a) if cut else None), link(5, 0, high, next_b)
    plain_a, plain_b = (link(6, 1, low, next_a) if cut else None), link(7, 2, high, next_b)
    last_a, last_b = link(8, 1, high, next_a), (link(9, 2, low, next_b) if cut else None)

    def core_copy(step):
        return links.copy(step, to_core.at[step], from_core.at[step], sibling)

    def for_sibling():
        @pl.loop(0, 4)
        def _(step):
            @pl.loop(0, width // tile)
            def _(column):
                columns = pl.ds(pl.multiple_of(column * tile, tile), tile)
                to_core[step, :, columns] = product(place(step, 1), columns).astype(bf16)

            core_copy(step).start()

    def for_chip():
        @pl.loop(0, 4)
        def _(step):
            core_copy(step).wait_recv()

            @pl.loop(0, width // tile)
            def _(column):
                columns = pl.ds(pl.multiple_of(column * tile, tile), tile)
                summed = product(place(step, 0), columns) + from_core[step, :, columns].astype(f32)
                total[:, columns] = summed

                @pl.when(step < 3)
                def _():
                    chip_sum[step, :, columns] = summed.astype(bf16)

            @pl.when(step == 0)
            def _():
                if cut:
                    diag_a.start()
                diag_b.start()

            @pl.when(step == 1)
            def _():
                if cut:
                    plain_a.start()

            @pl.when(step == 2)
            def _():
                plain_b.start()

    def add(step, span, slot):
        rows = pl.ds(*span)
        chip_sum[step, rows, :] = (
            chip_sum[step, rows, :].astype(f32) + arrived[landing[slot], 0 : span[1], :].astype(f32)
        ).astype(bf16)

    def take(span, slot):
        total[pl.ds(*span), :] += arrived[landing[slot], 0 : span[1], :].astype(f32)

    def hand_on():
        if cut:
            diag_a.wait_recv()
            add(2, low, 0)
            last_b.start()
        diag_b.wait_recv()
        add(1, high, 1)
        last_a.start()

    def finish():
        if cut:
            plain_a.wait_recv()
            take(low, 2)
        plain_b.wait_recv()
        take(high, 3)
        if cut:
            last_b.wait_recv()
            take(low, 5)
        last_a.wait_recv()
        take(high, 4)

        @pl.loop(0, 4)
        def _(step):
            core_copy(step).wait_send()

        for copy in (diag_a, diag_b, plain_a, plain_b, last_a, last_b):
            if copy is not None:
                copy.wait_send()

    return for_sibling, for_chip, hand_on, finish


def sum_scratch(block, width, cut):
    return [
        pltpu.VMEM((block, width), f32),
        pltpu.VMEM((4, block, width), bf16),
        pltpu.VMEM((4, block, width), bf16),
        pltpu.VMEM((3, block, width), bf16),
        pltpu.VMEM((6 if cut else 3, block - cut, width), bf16),
        pltpu.SemaphoreType.DMA((SUM_COPIES,)),
        pltpu.SemaphoreType.DMA((SUM_COPIES,)),
    ]


def spread_scratch(block, width):
    return [
        pltpu.VMEM((block, width), bf16),
        pltpu.SemaphoreType.DMA((SPREAD_COPIES,)),
        pltpu.SemaphoreType.DMA((SPREAD_COPIES,)),
        pltpu.SemaphoreType.DMA,
    ]


def link_params(collective_id):
    return pltpu.CompilerParams(
        collective_id=collective_id, has_side_effects=True, vmem_limit_bytes=60 * 1024 * 1024
    )


def cost(flops, size):
    return pl.CostEstimate(flops=int(flops), bytes_accessed=int(size), transcendentals=0)


def row_scale(values):
    return lax.rsqrt(jnp.mean(values * values, -1, keepdims=True) + epsilon)


def front_kernel(
    team, teams, qkv_moves, ffn_moves, tokens_ref, query_ref, key_ref, value_ref, gate_ref, up_ref, small_ref,
    normed_out, weights_out, both_out, small_out,
    tokens_all, mine, both_mine, gain,
    send_sems, recv_sems, local_sem, swap_send, swap_recv, swap_local, line_send, line_recv, small_send, small_recv,
    both_send, both_recv, both_local, out_sems,
):
    me = lax.axis_index(AXIS)
    mate, group = lax.rem(me, team), lax.div(me, team)
    devices = team * teams
    mates = [group * team + lax.rem(mate + k, team) for k in range(1, team)]
    above, below = lax.rem(me + team, devices), lax.rem(me + devices - team, devices)
    ffn_mates = [team_mate(me, (1, 2, 8), k) for k in range(team)]
    rows = mine.shape[1]
    swaps, line, small = Links(swap_send, swap_recv), Links(line_send, line_recv), Links(small_send, small_recv)
    both = Links(both_send, both_recv)
    for i, member, source, target, columns in qkv_moves:
        weight = (query_ref, key_ref, value_ref)[i]
        mine[member, :, target : target + columns] = weight[:, source : source + columns]
    greet(
        mates + [lax.rem(me + k * team, devices) for k in range(1, teams)]
        + [device for device, _ in ffn_mates[4:]]
    )

    def share(place):
        return pl.ds(pl.multiple_of(place * rows, rows), rows)

    swap_copies = [
        swaps.copy(k, mine.at[lax.rem(mate + k + 1, team)], weights_out.at[group, share(mate)], mates[k])
        for k in range(team - 1)
    ]
    for copy in swap_copies:
        copy.start()
    keep = pltpu.make_async_copy(mine.at[mate], weights_out.at[group, share(mate)], swap_local)
    keep.start()
    small_out[me] = small_ref[...]

    others = [lax.rem(me + k * team, devices) for k in range(1, teams)]
    team_rows = pl.ds(pl.multiple_of(group * team, team), team)
    small_near = [
        small.copy(k, small_out.at[me], small_out.at[me], device) for k, device in enumerate(mates)
    ]
    small_far = [
        small.copy(team + k, small_out.at[team_rows], small_out.at[team_rows], device)
        for k, device in enumerate(others)
    ]
    for copy in small_near:
        copy.start()
    spread = spread_block(
        (1, 2, 4), HALF, tokens_ref, tokens_all, Links(send_sems, recv_sems), local_sem
    )
    for i, member, source, target, columns in ffn_moves:
        both_mine[member, :, target : target + columns] = (gate_ref, up_ref)[i][:, source : source + columns]

    def passed(slot, shard, device):
        return line.copy(slot, weights_out.at[shard], weights_out.at[shard], device)

    steps = teams - 1

    def up(step):
        return passed(step - 1, group - (step - 1), above)

    def down(step):
        return passed(steps + step - 1, group + (step - 1), below)

    def line_start(step):
        pl.when((group < teams - 1) & (group >= step - 1))(lambda: up(step).start())
        pl.when((group > 0) & (group + step - 1 < teams))(lambda: down(step).start())

    def line_wait(step):
        pl.when(group >= step)(lambda: up(step).wait_recv())
        pl.when(group + step < teams)(lambda: down(step).wait_recv())

    def line_sent(step):
        pl.when((group < teams - 1) & (group >= step - 1))(lambda: up(step).wait_send())
        pl.when((group > 0) & (group + step - 1 < teams))(lambda: down(step).wait_send())

    for copy in small_near:
        copy.wait_recv()
    for copy in small_far:
        copy.start()
    own_place = ffn_mates[0][1]
    both_copies = [
        both.copy(k, both_mine.at[ffn_mates[k][1]], both_out.at[own_place], ffn_mates[k][0])
        for k in range(1, team)
    ]
    for copy in both_copies:
        copy.start()
    both_keep = pltpu.make_async_copy(both_mine.at[own_place], both_out.at[own_place], both_local)
    both_keep.start()
    for copy in swap_copies:
        copy.wait_recv()
    keep.wait()
    line_start(1)
    spread[0]()
    for copy in small_far:
        copy.wait_recv()
    spread[1]()
    spread[2]()
    line_wait(1)
    line_start(2)
    spread[3]()
    spread[4]()
    width = tokens_all.shape[1]
    gains = width // devices
    for d in range(devices):
        gain[:, d * gains : (d + 1) * gains] = small_out[d, 0:1, 0:gains]
    for phase in spread[5:]:
        phase()
    block = tokens_ref.shape[0]

    def normed_copy(k):
        span = pl.ds(pl.multiple_of(k * block, block), block)
        return pltpu.make_async_copy(tokens_all.at[span], normed_out.at[span], out_sems.at[k])

    def norm_blocks(first, last):
        @pl.loop(first, last)
        def _(k):
            span = pl.ds(pl.multiple_of(k * block, block), block)
            values = tokens_all[span, :].astype(f32)
            tokens_all[span, :] = (values * row_scale(values) * gain[...]).astype(bf16)
            normed_copy(k).start()

    norm_blocks(0, 2)
    for step in range(2, teams):
        line_wait(step)
        if step < steps:
            line_start(step + 1)
        if step == 2:
            norm_blocks(2, team)
    for k in range(team):
        normed_copy(k).wait()
    for copy in both_copies:
        copy.wait_recv()
    both_keep.wait()
    for copy in swap_copies + both_copies:
        copy.wait_send()
    for step in range(1, teams):
        line_sent(step)
    for copy in small_near + small_far:
        copy.wait_send()


def front(tokens, weights, small, teams, qkv_moves, ffn_moves):
    block, width = tokens.shape
    team = 8
    rows, cols = weights[0].shape[0], 3 * width // team
    both_cols = 2 * weights[3].shape[1] // team
    devices = team * teams
    dma = pltpu.SemaphoreType.DMA
    shape = jax.ShapeDtypeStruct
    return pl.pallas_call(
        functools.partial(front_kernel, team, teams, qkv_moves, ffn_moves),
        out_shape=(
            shape((team * block, width), bf16),
            shape((teams, team * rows, cols), bf16),
            shape((team, rows, both_cols), bf16),
            shape((devices,) + small.shape, f32),
        ),
        in_specs=[vmem] * 7,
        out_specs=(anywhere, anywhere, anywhere, vmem),
        scratch_shapes=[
            pltpu.VMEM((team * block, width), bf16), pltpu.VMEM((team, rows, cols), bf16),
            pltpu.VMEM((team, rows, both_cols), bf16), pltpu.VMEM((1, width), f32),
        ]
        + spread_scratch(block, width)[1:]
        + [dma((team - 1,)), dma((team - 1,)), dma, dma((2 * teams,)), dma((2 * teams,)), dma((team + teams,)), dma((team + teams,))]
        + [dma((team,)), dma((team,)), dma, dma((team,))],
        compiler_params=link_params(1),
        cost_estimate=cost(0, 200e6),
        name="front",
    )(tokens, *weights, small)


def branch_kernel(
    carry, swap_bits, spread_bits, left_ref, right_ref, residual_ref, gain_ref, peak_ref, *refs,
):
    if carry:
        (both_own, both_y, both_z, down_own), refs = refs[:4], refs[4:]
        (h2_ref, out_ref, peak_out, gate_full, up_full, down_full), refs = refs[:6], refs[6:]
        (landed, together, swap_send, swap_recv, own, send_sems, recv_sems, local_sem,
         peak_in, peak_send, peak_recv, carry_send, carry_recv, carry_local) = refs
    else:
        (h2_ref, out_ref, peak_out), refs = refs[:3], refs[3:]
        (landed, together, swap_send, swap_recv, own, send_sems, recv_sems, local_sem,
         peak_in, peak_send, peak_recv) = refs
    me = lax.axis_index(AXIS)
    team, block, _ = landed.shape
    bits = [1 << k for k in range(peak_in.shape[0])]
    mates = [team_mate(me, swap_bits, k) for k in range(team)]
    greet([device for device, _ in mates[1:]] + [flip_bit(me, bit) for bit in bits if bit not in swap_bits])
    own_place = mates[0][1]

    def rows_at(place):
        return pl.ds(pl.multiple_of(place * block, block), block)

    swap_copies = [
        Links(swap_send, swap_recv).copy(k, left_ref.at[rows_at(mates[k][1])], landed.at[own_place], mates[k][0])
        for k in range(1, team)
    ]
    for copy in swap_copies:
        copy.start()
    peaks = Links(peak_send, peak_recv)

    def peak_copy(k):
        return peaks.copy(k, peak_out, peak_in.at[k], flip_bit(me, bits[k]))

    def peak_step(k):
        if k:
            peak_copy(k - 1).wait()
            peak_out[...] = jnp.maximum(peak_out[...], peak_in[k - 1])
        if k < len(bits):
            peak_copy(k).start()

    if carry:
        carried = Links(carry_send, carry_recv)
        high, middle = bit_of(me, 16), bit_of(me, 4)
        by_y, by_z = flip_bit(me, 4), flip_bit(me, 16)

        def rows_of(part, flip_z, flip_y):
            z, y = lax.rem(high + flip_z, 2), lax.rem(middle + flip_y, 2)
            return pl.ds(pl.multiple_of(z * 16 + part * 8 + y * 4, 4), 4)

        cols, early = both_own.shape[2] // 2, both_z.shape[2]

        def piece(source, part, first, last):
            return source.at[pl.ds(part * 4, 4), :, pl.ds(first, last - first)]

        def placed(part, flips, first, last):
            full, start = (gate_full, first) if last <= cols else (up_full, first - cols)
            return full.at[rows_of(part, *flips), :, pl.ds(start, last - first)]

        def unit(flip_z, flip_y):
            return lax.rem(high + flip_z, 2) * 2 + lax.rem(middle + flip_y, 2)

        spans = ((0, cols), (cols, 2 * cols))
        early_spans = ((0, cols), (cols, early))
        kept = []
        for source, flips, columns in ((both_own, (0, 0), spans), (both_y, (0, 1), spans), (both_z, (1, 0), early_spans)):
            for span in columns:
                for part in range(2):
                    kept.append((piece(source, part, *span), placed(part, flips, *span)))
        kept.append((down_own, down_full.at[unit(0, 0)]))
        kept = [pltpu.make_async_copy(a, b, carry_local.at[i]) for i, (a, b) in enumerate(kept)]
        late = (early, 2 * cols)
        up_z = [
            carried.copy(part, piece(both_own, part, *late), placed(part, (0, 0), *late), by_z) for part in range(2)
        ]
        early_yz = [
            carried.copy(2 + 2 * i + part, piece(both_z, part, *span), placed(part, (1, 0), *span), by_y)
            for i, span in enumerate(early_spans) for part in range(2)
        ]
        up_yz = [
            carried.copy(6 + part, placed(part, (1, 0), *late), placed(part, (1, 0), *late), by_y)
            for part in range(2)
        ]
        down_z = carried.copy(8, down_own, down_full.at[unit(0, 0)], by_z)
        down_y = carried.copy(9, down_own, down_full.at[unit(0, 0)], by_y)
        for copy in up_z + [down_y] + kept:
            copy.start()

    peak_out[...] = peak_ref[...]
    peak_step(0)
    landed[own_place] = left_ref[rows_at(own_place), :]
    for copy in swap_copies:
        copy.wait_recv()
    heads = landed.shape[2] // HEAD_DIM
    for b in range(team):
        for g in range(heads):
            first = (g * team + b) * HEAD_DIM
            together[:, first : first + HEAD_DIM] = landed[b, :, g * HEAD_DIM : (g + 1) * HEAD_DIM]
    tile = 512

    @pl.loop(0, own.shape[1] // tile)
    def _(column):
        columns = pl.ds(pl.multiple_of(column * tile, tile), tile)
        h2_ref[:, columns] = residual_ref[:, columns].astype(f32) + contract(
            together[...], right_ref[:, columns], 1, 0
        )

    h2 = h2_ref[...]
    own[...] = (h2 * row_scale(h2) * gain_ref[...]).astype(bf16)
    spread = spread_block(spread_bits, BRANCH_CUT, own, out_ref, Links(send_sems, recv_sems), local_sem)
    spread[0]()
    if carry:
        for copy in early_yz:
            copy.start()
        for part in range(2):
            up_z[part].wait_recv()
            up_yz[part].start()
        down_z.start()
    for k, phase in enumerate(spread[1:-1]):
        phase()
        if k < len(bits):
            peak_step(k + 1)
    for k in range(len(spread) - 2, len(bits)):
        peak_step(k + 1)
    spread[-1]()
    for copy in swap_copies:
        copy.wait_send()
    if carry:
        for copy in kept:
            copy.wait()
        for copy in early_yz + up_yz + [down_y, down_z]:
            copy.wait_recv()
        for copy in up_z + early_yz + up_yz + [down_y, down_z]:
            copy.wait_send()


def branch(left, right, residual, gain, peak, carry, swap_bits, spread_bits, bit_count):
    block, width = residual.shape
    dma = pltpu.SemaphoreType.DMA
    shape = jax.ShapeDtypeStruct
    out_shape = [shape((block, width), f32), shape((8 * block, width), bf16), shape((8, 128), f32)]
    scratch = [pltpu.VMEM((8, block, left.shape[1]), bf16), pltpu.VMEM((block, width), bf16), dma((8,)), dma((8,))]
    scratch += spread_scratch(block, width)
    scratch += [pltpu.VMEM((bit_count, 8, 128), f32), dma((bit_count,)), dma((bit_count,))]
    if carry:
        out_shape += [
            shape((32, carry[0].shape[1], carry[0].shape[2] // 2), bf16),
            shape((32, carry[0].shape[1], carry[0].shape[2] // 2), bf16),
            shape((4,) + carry[3].shape, bf16),
        ]
        scratch += [dma((10,)), dma((10,)), dma((13,))]
    return pl.pallas_call(
        functools.partial(branch_kernel, bool(carry), swap_bits, spread_bits),
        out_shape=tuple(out_shape),
        in_specs=[vmem] * (5 + len(carry)),
        out_specs=tuple([vmem, anywhere, vmem] + [anywhere] * (len(out_shape) - 3)),
        scratch_shapes=scratch,
        compiler_params=link_params(2),
        cost_estimate=cost(16 * block * left.shape[1] * width, 300e6),
        name="attention_branch",
    )(left, right, residual, gain, peak, *carry)


def norm_back(values, gain, upstream):
    scaled = upstream * gain
    scale = row_scale(values)
    inner = jnp.mean(scaled * values, -1, keepdims=True)
    return scale * scaled - scale * scale * scale * values * inner


def ffn_back_kernel(
    sum_bits, swap_bits, gate_ref, up_ref, gate_w_ref, up_w_ref, normed_ref, out_w_ref, h2_ref, cot_ref, gain_ref,
    residual_ref, branch_ref, heads_out, d_gate_out, d_up_out,
    total, to_core, from_core, chip_sum, arrived, sum_send, sum_recv,
    swap_send, swap_recv, local_sem, stage, stage_sems,
):
    me = lax.axis_index(AXIS)
    block, width = total.shape
    team = 1 << len(swap_bits)
    mates = [team_mate(me, swap_bits, k) for k in range(team)]
    greet(
        [device for device, _ in mates[1:]] + [flip_bit(me, bit) for bit in sum_bits if bit not in swap_bits]
    )

    def product(place, columns):
        rows = pl.ds(pl.multiple_of(place * block, block), block)
        return contract(gate_ref[rows, :], gate_w_ref[columns, :], 1, 1) + contract(
            up_ref[rows, :], up_w_ref[columns, :], 1, 1
        )

    side = stage.shape[2]
    count = width // side
    outs = (d_gate_out, d_up_out)

    def stage_copy(k, which):
        span = pl.ds(pl.multiple_of(k * side, side), side)
        slot = lax.rem(k, 2)
        return pltpu.make_async_copy(stage.at[slot, which], outs[which].at[span], stage_sems.at[slot, which])

    def gradients(first, last):
        @pl.loop(first, last)
        def _(k):
            @pl.when(k >= 2)
            def _():
                for which in range(2):
                    stage_copy(k - 2, which).wait()

            columns = normed_ref[:, pl.ds(pl.multiple_of(k * side, side), side)]
            slot = lax.rem(k, 2)
            stage[slot, 0] = contract(columns, gate_ref[...], 0, 0).astype(bf16)
            stage[slot, 1] = contract(columns, up_ref[...], 0, 0).astype(bf16)
            for which in range(2):
                stage_copy(k, which).start()

    for_sibling, for_chip, hand_on, finish = sum_block(
        sum_bits, HALF, product, total, to_core, from_core, chip_sum, arrived, Links(sum_send, sum_recv)
    )
    for_sibling()
    for_chip()
    gradients(0, 1)
    hand_on()
    gradients(1, count - 2)
    finish()
    residual = cot_ref[...].astype(f32) + norm_back(h2_ref[...], gain_ref[...], total[...])
    residual_ref[...] = residual
    branch_ref[...] = residual.astype(bf16)
    tile, share = team * HEAD_DIM, width // team
    for g in range(width // tile):
        heads = contract(branch_ref[...], out_w_ref[g * tile : (g + 1) * tile, :], 1, 1).astype(bf16)
        for b in range(team):
            first = b * share + g * HEAD_DIM
            to_core[0, :, first : first + HEAD_DIM] = heads[:, b * HEAD_DIM : (b + 1) * HEAD_DIM]
    own_place = mates[0][1]
    own_rows = pl.ds(pl.multiple_of(own_place * block, block), block)
    def heads_of(place):
        return to_core.at[0, :, pl.ds(pl.multiple_of(place * share, share), share)]

    swap_copies = [
        Links(swap_send, swap_recv).copy(k, heads_of(mates[k][1]), heads_out.at[own_rows], mates[k][0])
        for k in range(1, team)
    ]
    keep = pltpu.make_async_copy(heads_of(own_place), heads_out.at[own_rows], local_sem)
    for copy in swap_copies + [keep]:
        copy.start()
    gradients(count - 2, count)
    for copy in swap_copies:
        copy.wait_recv()
    for copy in swap_copies:
        copy.wait_send()
    keep.wait()
    for k in range(count - 2, count):
        for which in range(2):
            stage_copy(k, which).wait()


def ffn_back(gate, up, gate_w, up_w, normed, out_w, h2, cot, gain, sum_bits, swap_bits):
    block, width = h2.shape
    shape = jax.ShapeDtypeStruct
    dma = pltpu.SemaphoreType.DMA
    ff_cols = gate.shape[1]
    return pl.pallas_call(
        functools.partial(ffn_back_kernel, sum_bits, swap_bits),
        out_shape=(
            shape((block, width), f32), shape((block, width), bf16), shape((8 * block, width // 8), bf16),
            shape((width, ff_cols), bf16), shape((width, ff_cols), bf16),
        ),
        in_specs=[vmem] * 9,
        out_specs=(vmem, vmem, anywhere, anywhere, anywhere),
        scratch_shapes=sum_scratch(block, width, HALF)
        + [dma((8,)), dma((8,)), dma]
        + [pltpu.VMEM((2, 2, 256, ff_cols), bf16), dma((2, 2))],
        compiler_params=link_params(3),
        cost_estimate=cost(96 * block * ff_cols * width, 200e6),
        name="ffn_back",
    )(gate, up, gate_w, up_w, normed, out_w, h2, cot, gain)


def last_sums_kernel(
    sum_bits, ffn_bits, left_ref, other_ref, right_ref, tokens_ref, gain_ref, residual_ref, hidden_ref, down_ref, h2_ref,
    gate_ref, out_ref, mixed_ref, gate_out, *scratch,
):
    (swap_send, swap_recv, swap_local), scratch = scratch[-3:], scratch[:-3]
    count = len(scratch) // 2
    me = lax.axis_index(AXIS)
    total, ffn_total = scratch[0], scratch[count]
    block = total.shape[0]
    mates = [team_mate(me, ffn_bits, k) for k in range(8)]
    partners = [flip_bit(me, bit) for bit in sum_bits if bit not in ffn_bits]
    greet(partners + [device for device, _ in mates[1:]])
    swaps, own_place = Links(swap_send, swap_recv), mates[0][1]
    swap_copies = [
        swaps.copy(k, gate_ref.at[mates[k][1]], gate_out.at[own_place], mates[k][0]) for k in range(1, 8)
    ]
    keep = pltpu.make_async_copy(gate_ref.at[own_place], gate_out.at[own_place], swap_local)

    def rows_of(place):
        return pl.ds(pl.multiple_of(place * block, block), block)

    def product(place, columns):
        rows = rows_of(place)
        middle = left_ref.shape[1]
        return contract(left_ref[rows, :], right_ref[columns, 0:middle], 1, 1) + contract(
            other_ref[rows, :], right_ref[columns, middle : 2 * middle], 1, 1
        )

    def ffn_product(place, columns):
        return contract(hidden_ref[rows_of(place), :], down_ref[:, columns], 1, 0)

    first = sum_block(sum_bits, LAST_CUT, product, *scratch[: count - 2], Links(*scratch[count - 2 : count]))
    second = sum_block(ffn_bits, LAST_CUT, ffn_product, *scratch[count:-2], Links(*scratch[-2:]))
    run(first[:2])
    run(second[:2])
    for copy in swap_copies + [keep]:
        copy.start()
    for one, other in zip(first[2:], second[2:]):
        one()
        other()
    out_ref[...] = residual_ref[...] + norm_back(
        tokens_ref[...].astype(f32), gain_ref[...], total[...]
    )
    mixed_ref[...] = (h2_ref[...] + ffn_total[...]).astype(bf16)
    for copy in swap_copies:
        copy.wait_recv()
    for copy in swap_copies:
        copy.wait_send()
    keep.wait()


def last_sums(left, other, right, tokens, gain, residual, hidden, down, h2, d_gate, sum_bits, ffn_bits):
    block, width = tokens.shape
    return pl.pallas_call(
        functools.partial(last_sums_kernel, sum_bits, ffn_bits),
        out_shape=(
            jax.ShapeDtypeStruct((block, width), f32), jax.ShapeDtypeStruct((block, width), bf16),
            jax.ShapeDtypeStruct(d_gate.shape, bf16),
        ),
        in_specs=[vmem] * 9 + [anywhere],
        out_specs=(vmem, vmem, anywhere),
        scratch_shapes=sum_scratch(block, width, LAST_CUT) * 2
        + [pltpu.SemaphoreType.DMA((8,)), pltpu.SemaphoreType.DMA((8,)), pltpu.SemaphoreType.DMA],
        compiler_params=link_params(4),
        cost_estimate=cost(16 * block * right.size // 8, 300e6),
        name="last_sums",
    )(left, other, right, tokens, gain, residual, hidden, down, h2, d_gate)


def home_kernel(teams, places, gain_of, sources, *refs):
    count = len(places)
    kinds = max(gain_of) + 1
    mine, refs = refs[:sources], refs[sources:]
    weights, refs = refs[:count], refs[count:]
    gains, refs = refs[:kinds], refs[kinds:]
    outs, refs = refs[:count], refs[count:]
    gain_outs, refs = refs[:kinds], refs[kinds:]
    landed, (send_sems, recv_sems, local_sems) = list(refs[:-3]), refs[-3:]
    me = lax.axis_index(AXIS)
    members = mine[0].shape[0]
    links = Links(send_sems, recv_sems)
    greeted = {}
    for bits in teams:
        for k in range(1, members) if bits else ():
            device, _ = team_mate(me, bits, k)
            greeted[tuple(sorted(bit for j, bit in enumerate(bits) if (k >> j) % 2))] = device
    greet(list(greeted.values()))
    copies, kept, arrived = [], [], []
    for i, (source, bits) in enumerate(zip(mine, teams)):
        if not bits:
            arrived.append(source)
            continue
        target = landed.pop(0)
        arrived.append(target)
        own = team_mate(me, bits, 0)[1]
        kept.append(pltpu.make_async_copy(source.at[own], target.at[own], local_sems.at[i]))
        for k in range(1, members):
            device, place = team_mate(me, bits, k)
            copies.append(links.copy(i * members + k, source.at[place], target.at[own], device))
    for copy in copies + kept:
        copy.start()
    totals = [jnp.zeros(gain.shape, f32) for gain in gains]

    def settle(i):
        out, weight = outs[i], weights[i]
        for source, member, first, target, columns in places[i]:
            out[:, target : target + columns] = arrived[source][member, :, first : first + columns].astype(f32)
        for first in range(0, out.shape[1], 1024):
            product = out[:, first : first + 1024] * weight[:, first : first + 1024].astype(f32)
            totals[gain_of[i]] += jnp.sum(product, 1, keepdims=True)

    ready = [i for i in range(count) if all(not teams[move[0]] for move in places[i])]
    for i in ready:
        settle(i)
    for copy in copies:
        copy.wait_recv()
    for copy in kept:
        copy.wait()
    for i in range(count):
        if i not in ready:
            settle(i)
    for gain, total, out in zip(gains, totals, gain_outs):
        out[...] = total / gain[...]
    for copy in copies:
        copy.wait_send()


def home(parts, teams, weights, gains, gain_of, places):
    shape = jax.ShapeDtypeStruct
    dma = pltpu.SemaphoreType.DMA
    count, slots = len(weights), len(parts) * parts[0].shape[0]
    gains = [gain.astype(f32).reshape(-1, 1) for gain in gains]
    return pl.pallas_call(
        functools.partial(home_kernel, teams, places, gain_of, len(parts)),
        out_shape=tuple(shape(w.shape, f32) for w in weights) + tuple(shape(g.shape, f32) for g in gains),
        in_specs=[vmem] * (len(parts) + count + len(gains)),
        out_specs=tuple([vmem] * (count + len(gains))),
        scratch_shapes=[pltpu.VMEM(part.shape, bf16) for part, bits in zip(parts, teams) if bits]
        + [dma((slots,)), dma((slots,)), dma((len(parts),))],
        compiler_params=link_params(5),
        cost_estimate=cost(1e6, 60e6),
        name="home",
    )(*parts, *weights, *gains)


def body(
    tokens, block_of, clip_limit, norm_attn, w_query, w_key, w_value, w_out,
    norm_ffn, w_gate, w_up, w_down, cotangent,
):
    tok_rows, width = tokens.shape
    devices = lax.axis_size(AXIS)
    team = SEQ // tok_rows
    teams = devices // team
    head_total = width // HEAD_DIM
    heads = head_total // team
    head_cols = heads * HEAD_DIM
    ff_rows = w_down.shape[0]
    weight_rows = w_gate.shape[0]
    ff_cols = w_gate.shape[1] // team
    device = lax.axis_index(AXIS)
    mate = device % team
    bit_count = devices.bit_length() - 1
    attn_bits, ffn_bits = (1, 2, 4), (1, 2, 8)
    data_bits = [4] + [1 << k for k in range(4, bit_count)]
    in_team = [[g * team + b for b in range(team)] for g in range(teams)]
    across = [[g * team + b for g in range(teams)] for b in range(team)]
    ffn_team = [
        [g * 16 + z * 8 + y * 4 + c for z in range(2) for c in range(4)]
        for g in range(devices // 16)
        for y in range(2)
    ]

    def flip(x, bit):
        return lax.ppermute(x, AXIS, [(i, i ^ bit) for i in range(devices)])

    def gather_across(x):
        return lax.all_gather(x, AXIS, axis=0, tiled=True, axis_index_groups=across)

    def scatter_across(x):
        return lax.psum_scatter(
            x.astype(bf16), AXIS, scatter_dimension=0, tiled=True, axis_index_groups=across
        )

    def dim_of(bit):
        return bit_count - bit.bit_length()

    def data_pieces(x):
        pieces = {0: x}
        for bit in reversed(data_bits):
            for key in list(pieces):
                pieces[key | bit] = flip(pieces[key], bit)
        return pieces

    def place_pieces(pieces, dims, shape):
        total = jnp.zeros(shape, bf16)
        for key, piece in pieces.items():
            start = [0] * len(shape)
            size = list(shape)
            for bit in data_bits:
                start[dims[bit]] = ((device // bit) + (1 if key & bit else 0)) % 2
                size[dims[bit]] = 1
            total = lax.dynamic_update_slice(total, piece.reshape(size), start)
        return total

    def after_bit(dims, bit):
        return {b: d - (d > dims[bit]) for b, d in dims.items() if b != bit}

    def data_sum(x, dims, bits):
        for bit in bits:
            mine = (device // bit) % 2
            keep = lax.dynamic_index_in_dim(x, mine, dims[bit], False)
            sent = flip(lax.dynamic_index_in_dim(x, 1 - mine, dims[bit], False), bit)
            x = (keep.astype(f32) + sent.astype(f32)).astype(bf16)
            dims = after_bit(dims, bit)
        return x

    row_dims = {bit: dim_of(bit) for bit in data_bits}
    row_shape = (2,) * bit_count
    unit_dims = {bit: i for i, bit in enumerate(reversed(data_bits))}
    unit_shape = (2,) * len(data_bits)

    def tie(*values):
        return lax.optimization_barrier(values)

    qkv_moves = tuple(
        (i, b, (g * team + b) * HEAD_DIM, (3 * (g // 2) + i) * PAIR + (g % 2) * HEAD_DIM, HEAD_DIM)
        for i in range(3) for g in range(heads) for b in range(team)
    )
    ffn_units = tuple(
        (z * 4 + c, (2 * h + y) * ff_rows, (h * 16 + z * 8 + y * 4 + c) * ff_rows)
        for h in range(devices // 16) for z in range(2) for y in range(2) for c in range(4)
    )
    ffn_moves = tuple(
        (i, member, source, i * ff_cols + target, ff_rows)
        for i in range(2) for member, target, source in ffn_units
    )
    out_w = lax.all_gather(w_out, AXIS, axis=0, tiled=True)
    gain_row = jnp.concatenate([norm_attn, norm_ffn]).astype(f32)
    gain_row = jnp.pad(gain_row, (0, 128 - 2 * weight_rows)).reshape(1, 128)
    block_rows = block_of.astype(f32).reshape(tok_rows // 128, 128)
    small = jnp.concatenate([gain_row, block_rows, jnp.zeros((7 - tok_rows // 128, 128), f32)])
    normed_attn, qkv_w, both_mine, gathered = front(
        tokens, (w_query, w_key, w_value, w_gate, w_up), small, teams, qkv_moves, ffn_moves
    )
    qkv_w = qkv_w.reshape(width, 3 * head_cols)
    gain_attn = gathered[:, 0, :weight_rows].reshape(1, width)
    gain_ffn = gathered[:, 0, weight_rows : 2 * weight_rows].reshape(1, width)
    blocks = lax.dynamic_slice_in_dim(gathered, device - mate, team, 0)
    blocks = blocks[:, 1 : 1 + tok_rows // 128].astype(jnp.int32).reshape(SEQ)
    row_blocks, col_blocks = blocks.reshape(1, SEQ), blocks.reshape(SEQ, 1)
    both_mine, down_mine, qkv_w = tie(both_mine, w_down, qkv_w)

    def whole_rows(mine):
        shape = row_shape + (weight_rows, ff_cols)
        return place_pieces(data_pieces(mine), row_dims, shape).reshape(width, ff_cols)

    qkv = contract(normed_attn, qkv_w, 1, 0)
    cosine, sine = rope_tables(SEQ, PAIR)
    qkv, cot_mine = tie(qkv, cotangent)
    if data_bits == [4, 16]:
        early = ff_cols + EARLY_UP
        carry = [both_mine, flip(both_mine, 4), flip(both_mine[:, :, :early], 16), down_mine]
    else:
        carry = []
    query, key, value, attended, lse, peak = attend_forward(qkv, cosine, sine, row_blocks, col_blocks)
    peaks = jnp.where(
        (jnp.arange(head_total) % team) == mate, jnp.repeat(peak[0, :heads], team), -jnp.inf
    )
    peaks = jnp.broadcast_to(jnp.pad(peaks, (0, 128 - head_total))[None], (8, 128))
    after_attn, normed_ffn, peaks, *full = branch(
        attended, out_w, tokens, gain_ffn, peaks, carry, attn_bits, ffn_bits, bit_count
    )
    head_peak = peaks[0, :head_total]
    if carry:
        gate_w, up_w = (w.reshape(width, ff_cols) for w in full[:2])
        z_side, y_side = (device // 16) % 2, (device // 4) % 2
        passed = lax.dynamic_index_in_dim(full[2], (1 - z_side) * 2 + y_side, 0, True)
        down_w = lax.dynamic_update_slice(
            full[2], flip(passed, 4), ((1 - z_side) * 2 + 1 - y_side, 0, 0)
        ).reshape(ff_cols, width)
    else:
        gate_w, up_w = whole_rows(both_mine[:, :, :ff_cols]), whole_rows(both_mine[:, :, ff_cols:])
        down_w = place_pieces(
            data_pieces(down_mine), unit_dims, unit_shape + (ff_rows, width)
        ).reshape(ff_cols, width)
    gate_pre = contract(normed_ffn, gate_w, 1, 0)
    up_pre = contract(normed_ffn, up_w, 1, 0)
    sigmoid_gate = jax.nn.sigmoid(gate_pre)
    silu_gate = gate_pre * sigmoid_gate
    hidden = (silu_gate * up_pre).astype(bf16)

    team_cot = lax.all_gather(cot_mine, AXIS, axis=0, tiled=True, axis_index_groups=ffn_team)
    d_down = contract(hidden, team_cot, 0, 0).astype(bf16).reshape(unit_shape + (ff_rows, width))
    team_cot, d_down = tie(team_cot, d_down)
    d_hidden = contract(team_cot, down_w, 1, 1)
    grad_gate = (d_hidden * up_pre * sigmoid_gate * (1.0 + gate_pre * (1.0 - sigmoid_gate))).astype(bf16)
    grad_up = (d_hidden * silu_gate).astype(bf16)

    d_down = data_sum(d_down, unit_dims, data_bits[:1])
    unit_rest, row_rest = after_bit(unit_dims, data_bits[0]), after_bit(row_dims, data_bits[0])
    grad_gate, d_down = tie(grad_gate, d_down)
    d_residual, branch_mine, grad_attended, d_gate, d_up = ffn_back(
        grad_gate, grad_up, gate_w, up_w, normed_ffn, out_w, after_attn, cotangent, gain_ffn, ffn_bits, attn_bits
    )
    d_gate, d_up = (d.reshape(row_shape + (weight_rows, ff_cols)) for d in (d_gate, d_up))
    branch_grad = lax.all_gather(branch_mine, AXIS, axis=0, tiled=True, axis_index_groups=in_team)
    d_down = data_sum(d_down, unit_rest, data_bits[1:]).astype(f32)

    def heads_back(pair):
        return attend_backward(
            pair, query, key, value, grad_attended, lse, cosine, sine, row_blocks, col_blocks
        )

    grad_pairs, shares = [None] * (heads // 2), [None] * (heads // 2)
    grad_pairs[0] = heads_back(0)
    shares[0] = scatter_across(contract(normed_attn, grad_pairs[0], 0, 0))
    d_gate = data_sum(d_gate, row_dims, data_bits[:1])
    grad_attended, d_gate, d_up, d_down, _ = tie(grad_attended, d_gate, d_up, d_down, grad_pairs[0])
    d_gate = data_sum(d_gate, row_rest, data_bits[1:])
    d_up = data_sum(d_up, row_dims, data_bits[:1])
    for p in range(1, heads // 2):
        grad_pairs[p], d_up, d_gate = tie(heads_back(p), d_up, d_gate)
        shares[p] = scatter_across(contract(normed_attn, grad_pairs[p], 0, 0))
    d_up = data_sum(d_up, row_rest, data_bits[1:])
    d_gate = d_gate.reshape(team, weight_rows, ff_cols)
    out_part = contract(attended, branch_grad, 0, 0)
    if weight_rows == HEAD_DIM:
        d_out = scatter_across(out_part).astype(f32)
    else:
        spread = jnp.where(
            (jnp.arange(team) == mate)[None, :, None, None],
            out_part.reshape(heads, 1, HEAD_DIM, width), 0.0,
        ).reshape(width, width)
        d_out = lax.psum_scatter(spread, AXIS, scatter_dimension=0, tiled=True)
    d_tokens, mixed, d_gate = last_sums(
        *grad_pairs, qkv_w, tokens, gain_attn, d_residual, hidden, down_w, after_attn, d_gate, attn_bits, ffn_bits
    )
    places = [[], [], []]
    for i, b, source, target, columns in qkv_moves:
        places[i].append((target // (3 * PAIR), b, target % (3 * PAIR), source, columns))
    places += [
        [(heads // 2 + i, member, target, source, ff_rows) for member, target, source in ffn_units] for i in range(2)
    ]
    shares = [share.reshape(team, weight_rows, 3 * PAIR) for share in shares]
    d_query, d_key, d_value, d_gate, d_up, d_norm_attn, d_norm_ffn = home(
        shares + [d_gate, d_up.reshape(team, weight_rows, ff_cols)],
        (attn_bits,) * (heads // 2) + (None, ffn_bits),
        (w_query, w_key, w_value, w_gate, w_up), (norm_attn, norm_ffn), (0, 0, 0, 1, 1),
        tuple(tuple(p) for p in places),
    )
    d_norm_attn, d_norm_ffn = d_norm_attn[:, 0], d_norm_ffn[:, 0]
    clip_value = clip_limit.astype(f32)
    factor = jnp.sqrt(clip_value / jnp.maximum(head_peak, clip_value))
    factors = jnp.repeat(factor, HEAD_DIM)[None, :]
    clipped_query = (w_query.astype(f32) * factors).astype(bf16)
    clipped_key = (w_key.astype(f32) * factors).astype(bf16)
    return (
        mixed, d_tokens, d_norm_attn, d_query, d_key, d_value, d_out, d_norm_ffn,
        d_gate, d_up, d_down, head_peak, clipped_query, clipped_key,
    )


def solution(mesh):
    rows, whole = P(AXIS, None), P(AXIS)
    return jax.shard_map(
        body,
        mesh=mesh,
        in_specs=(rows, whole, P(), whole, rows, rows, rows, rows, whole, rows, rows, rows, rows),
        out_specs=(
            rows, rows, whole, rows, rows, rows, rows, whole, rows, rows, rows, P(), rows, rows,
        ),
        check_vma=False,
    )
```

time: 1010 us -> 894 us (0.89)
  Pallas kernels: 687 us -> 574 us
  waiting for transfers between devices: 69 us -> 135 us
  matrix products: 133 us -> 101 us
  local copies, waits for them, and re-layouts: 45.3 us -> 26.3 us
    pallas_call x5 -> x4, Pallas kernels: 500 us -> 347 us  [the longest x1 139 us: front(): pl.pallas_call(functools.partial(front_kernel, team, teams, qkv_moves, ff...]
    ppermute x10 -> x9, waiting for transfers between devices: 68.9 us -> 134 us  [flip(): return lax.ppermute(x, AXIS, [(i, i ^ bit) for i in range(devices)])]
    pallas_call x1, Pallas kernels: 97.7 us -> 136 us  [last_sums(): pl.pallas_call(functools.partial(last_sums_kernel, sum_bits, ffn_bits), o...]
    dot_general x11 -> x8, matrix products: 133 us -> 101 us  [contract(): lax.dot_general(left, right, (((left_dim,), (right_dim,)), ((), ())), pre...]
    reshape x17 -> x2, local copies, waits for them, and re-layouts: 12.7 us -> 1.42 us  [home(): gains = [gain.astype(f32).reshape(-1, 1) for gain in gains]]
  transfers between devices with their start and end apart: 16 -> 15, of which waited for: 4 -> 5; matrix products, arithmetic and copies ran while one was open for 17% -> 16% of each run, Pallas kernels for 67% -> 56%
where the time goes in v3:
time: 894 us; the launch traced here: 888 us
  Pallas kernels  574 us (64%)
  waiting for transfers between devices  135 us (15%)
  matrix products  101 us (11%)
  local copies, waits for them, and re-layouts  26.3 us (3%)
  other arithmetic  25.8 us (3%)
  between operations  15.4 us (2%)
  starting transfers between devices  9.75 us (1%)
    pallas_call x1, Pallas kernels, front(): pl.pallas_call(functools.partial(front_kernel, team, teams, qkv_moves, ff...  139 us
    pallas_call x1, Pallas kernels, last_sums(): pl.pallas_call(functools.partial(last_sums_kernel, sum_bits, ffn_bits), o...  136 us
    ppermute x9, waiting for transfers between devices, flip(): return lax.ppermute(x, AXIS, [(i, i ^ bit) for i in range(devices)])  134 us
    dot_general x8, matrix products, contract(): lax.dot_general(left, right, (((left_dim,), (right_dim,)), ((), ())), pre...  101 us
    pallas_call x1, Pallas kernels, branch(): pl.pallas_call(functools.partial(branch_kernel, bool(carry), swap_bits, s...  97.9 us
    pallas_call x1, Pallas kernels, ffn_back(): pl.pallas_call(functools.partial(ffn_back_kernel, sum_bits, swap_bits), o...  80.8 us
    pallas_call x2, Pallas kernels, attend_backward(): pl.pallas_call(functools.partial(attend_backward_kernel, 2 * pair), grid=...  58.2 us
    pallas_call x1, Pallas kernels, attend_forward(): pl.pallas_call(attend_forward_kernel, out_shape=(shape((pairs, length, PA...  33.3 us
  transfers between devices with their start and end apart: 15, of which 5 were waited for; matrix products, arithmetic and copies ran while one was open for 16% of the time, Pallas kernels for 56%

profile of v3, /device:TPU:0, one launch (start us, length us, event | category | flops | bytes accessed | tf_op | source)
XLA Modules:
  0.0 887.5 jit_solution(12533573037331323668)
XLA Ops:
  10.1 139.2 %front.1 = (bf16[2048,2048]{1,0:T(8,128)(2,1)}, bf16[4,512,768]{2,1,0:T(8,128)(2,1)}, bf16[8,64,2048]{2,1,0:T(8,128)(2,1)}, f32[32,8,128]{2,1,0:T(8,128)}) custom-call(bf16[256,2048]{1,0:T(8,128)(2,1)} %tokens_ref.3, bf16[64,2048]{1,0:T(8,128)(2,1)} %refs_4_.1, bf16[64,2048]{1,0:T(8,128)(2,1)} %refs_5_.1, bf16[64,2048]{1,0:T(8,128)(2,1)} %refs_6_.1, ...), custom_call_target="tpu_custom_call" | custom-call | bytes 200000000 | tf_op jit(solution)/shard_map/front/pallas_call | solution.py:609
  149.4 11.8 %fusion.8.qkv_ref = f32[2048,768]{1,0:T(8,128)} fusion(bf16[2048,2048]{1,0:T(8,128)(2,1)} %get-tuple-element.61, bf16[2048,768]{1,0:T(8,128)(2,1)} %bitcast.86), kind=kOutput, calls=%fused_computation.45 | convolution fusion | flops 6442450944 | bytes 17825792 | tf_op jit(solution)/shard_map/dot_general | solution.py:30
  161.3 1.5 collective-permute-start
  162.8 1.3 slice.21
  164.8 1.3 copy.34.col_ref
  166.2 33.3 %attend_forward.1 = (bf16[2,2048,128]{2,1,0:T(8,128)(2,1)}, bf16[2,2048,128]{2,1,0:T(8,128)(2,1)}, bf16[2,2048,128]{2,1,0:T(8,128)(2,1)}, bf16[2048,256]{1,0:T(8...) custom-call(f32[2048,768]{1,0:T(8,128)} %fusion.8.qkv_ref, f32[2048,128]{1,0:T(8,128)} %constant.141.clone.cos_ref, ...), custom_call_target="tpu_custom_call" | custom-call | flops 17179869184 | bytes 12582912 | tf_op jit(solution)/shard_map/attend_forward/pallas_call | solution.py:120
  200.3 1.7 slice_reduce_fusion
  202.7 30.8 %collective-permute-done.1.refs_2_ = bf16[8,64,1536]{2,1,0:T(8,128)(2,1)} collective-permute-done((bf16[8,64,1536]{2,1,0:T(8,128)(2,1)}, bf16[8,64,1536]{2,1,0:T(8,128)(2,1)}, u32[]{:S(2)}, u32[]{:S(2)}) %collective-permute-start.1) | collective-permute-done | bytes 1572896 | tf_op jit(solution)/shard_map/ppermute | solution.py:1081
  234.1 97.9 %attention_branch.1 = (f32[256,2048]{1,0:T(8,128)}, bf16[2048,2048]{1,0:T(8,128)(2,1)}, f32[8,128]{1,0:T(8,128)}, bf16[32,64,1024]{2,1,0:T(8,128)(2,1)}, bf16[32...) custom-call(bf16[2048,256]{1,0:T(8,128)(2,1)} %get-tuple-element.71.left_ref, ...), custom_call_target="tpu_custom_call" | custom-call | flops 2147483648 | bytes 300000000 | tf_op jit(solution)/shard_map/attention_branch/pallas_call | solution.py:782
  332.1 2.5 constant_dynamic-slice_fusion
  334.5 1.4 collective-permute-start.2
  336.0 14.6 %fusion.9 = f32[2048,1024]{1,0:T(8,128)} fusion(bf16[2048,2048]{1,0:T(8,128)(2,1)} %get-tuple-element.75.normed_ref, bf16[2048,1024]{1,0:T(8,128)(2,1)} %bitcast.96), kind=kOutput, calls=%fused_computation.46 | convolution fusion | flops 8589934592 | bytes 20971520 | tf_op jit(solution)/shard_map/dot_general | solution.py:30
  350.6 13.7 %multiply_convert_fusion.2 = (bf16[2048,1024]{1,0:T(8,128)(2,1)}, f32[2048,1024]{1,0:T(8,128)}) fusion(f32[2048,1024]{1,0:T(8,128)} %fusion.9, bf16[2048,2048]{1,0:T(8,128)(2,1)S(1)} %bitcast.95, bf16[2048,1024]{1,0:T(8,128)(2,1)S(1)} %bitcast.99), kind=kOutput, calls=%fused_computation.2 | convolution fusion | flops 8602517504 | bytes 33554432 | tf_op jit(solution)/shard_map/dot_general | solution.py:30
  364.3 12.7 %convolution_convert_fusion = bf16[1024,2048]{1,0:T(8,128)(2,1)S(1)} fusion(bf16[2048,1024]{1,0:T(8,128)(2,1)} %get-tuple-element.116.hidden_ref, bf16[2048,2048]{1,0:T(8,128)(2,1)} %all-gather.4.cloned.1.call-done), kind=kOutput, calls=%fused_computation.11 | convolution fusion | flops 8592031744 | bytes 16777216 | tf_op jit(solution)/shard_map/dot_general | solution.py:30
  377.9 2.8 copy-done.1
  380.8 21.8 %multiply_convert_fusion = (bf16[2048,1024]{1,0:T(8,128)(2,1)}, bf16[2048,1024]{1,0:T(8,128)(2,1)}) fusion(f32[2048,1024]{1,0:T(8,128)} %fusion.9, f32[2048,1024]{1,0:T(8,128)} %get-tuple-element.117, bf16[2048,2048]{1,0:T(8,128)(2,1)} %all-gather.4.cloned.1.call-done, bf16[1024,2048]{1,0:T(8,128)(2,1)S(1)} %bitcast.76), kind=kOutput, calls=%fused_computation | convolution fusion | flops 8617197568 | bytes 37748736 | tf_op jit(solution)/shard_map/dot_general | solution.py:30
  402.6 22.4 %collective-permute-done.3 = bf16[2,256,2048]{2,1,0:T(8,128)(2,1)} collective-permute-done((bf16[2,256,2048]{2,1,0:T(8,128)(2,1)S(1)}, bf16[2,256,2048]{2,1,0:T(8,128)(2,1)}, u32[]{:S(2)}, u32[]{:S(2)}) %collective-permute-start.3) | collective-permute-done | bytes 2097184 | tf_op jit(solution)/shard_map/ppermute | solution.py:1081
  425.0 3.0 fusion.3
  428.0 80.8 %ffn_back.1 = (f32[256,2048]{1,0:T(8,128)}, bf16[256,2048]{1,0:T(8,128)(2,1)}, bf16[2048,256]{1,0:T(8,128)(2,1)}, bf16[2048,1024]{1,0:T(8,128)(2,1)}, bf16[2048,1024]{1,0:T(8,128)(2,1)}) custom-call(bf16[2048,1024]{1,0:T(8,128)(2,1)} %get-tuple-element.81.gate_ref, bf16[2048,1024]{1,0:T(8,128)(2,1)} %get-tuple-element.112.up_ref, ...), custom_call_target="tpu_custom_call" | custom-call | flops 51539607552 | bytes 200000000 | tf_op jit(solution)/shard_map/ffn_back/pallas_call | solution.py:891
  508.9 1.0 dynamic-slice_bitcast_fusion.5
  510.0 1.6 collective-permute-start.5
  511.6 3.1 dynamic-slice_bitcast_fusion.1
  514.7 1.3 collective-permute-start.4
  516.0 29.1 %attend_backward.2.left_ref = bf16[2048,384]{1,0:T(8,128)(2,1)} custom-call(bf16[2,2048,128]{2,1,0:T(8,128)(2,1)} %get-tuple-element.67.q_ref, bf16[2,2048,128]{2,1,0:T(8,128)(2,1)} %get-tuple-element.68.k_ref, bf16[2,2048,128]{2,1,0:T(8,128)(2,1)} %get-tuple-element.69.v_ref, bf16[2048,256]{1,0:T(8,128)(2,1)} %get-tuple-element.88.grad_ref, ...), custom_call_target="tpu_custom_call" | custom-call | flops 21474836480 | bytes 6291456 | tf_op jit(solution)/shard_map/attend_backward/pallas_call | solution.py:184
  545.1 10.6 %convolution_convert_fusion.2 = bf16[2048,384]{1,0:T(8,128)(2,1)} fusion(bf16[2048,2048]{1,0:T(8,128)(2,1)} %get-tuple-element.61, bf16[2048,384]{1,0:T(8,128)(2,1)} %attend_backward.2.left_ref), kind=kOutput, calls=%fused_computation.13 | convolution fusion | flops 3222011904 | bytes 11534336 | tf_op jit(solution)/shard_map/dot_general | solution.py:30
  555.9 3.6 collective-permute-done.5
  559.5 1.7 fusion.7
  561.2 35.7 %collective-permute-done.4 = bf16[2,2,2,2,64,1024]{5,4,3,2,1,0:T(8,128)(2,1)} collective-permute-done((bf16[2,2,2,2,64,1024]{5,4,3,2,1,0:T(8,128)(2,1)}, bf16[2,2,2,2,64,1024]{5,4,3,2,1,0:T(8,128)(2,1)}, u32[]{:S(2)}, u32[]{:S(2)}) %collective-permute-start.4) | collective-permute-done | bytes 2097184 | tf_op jit(solution)/shard_map/ppermute | solution.py:1081
  596.9 2.6 fusion.2
  599.6 1.4 collective-permute-start.7
  601.2 1.5 collective-permute-start.6
  602.7 29.1 %attend_backward.3.other_ref = bf16[2048,384]{1,0:T(8,128)(2,1)} custom-call(bf16[2,2048,128]{2,1,0:T(8,128)(2,1)} %get-tuple-element.67.q_ref, bf16[2,2048,128]{2,1,0:T(8,128)(2,1)} %get-tuple-element.68.k_ref, bf16[2,2048,128]{2,1,0:T(8,128)(2,1)} %get-tuple-element.69.v_ref, bf16[2048,256]{1,0:T(8,128)(2,1)} %get-tuple-element.88.grad_ref, ...), custom_call_target="tpu_custom_call" | custom-call | flops 21474836480 | bytes 6291456 | tf_op jit(solution)/shard_map/attend_backward/pallas_call | solution.py:184
  631.8 41.5 %collective-permute-done.7 = bf16[2,2,2,64,1024]{4,3,2,1,0:T(8,128)(2,1)} collective-permute-done((bf16[2,2,2,64,1024]{4,3,2,1,0:T(8,128)(2,1)S(1)}, bf16[2,2,2,64,1024]{4,3,2,1,0:T(8,128)(2,1)}, u32[]{:S(2)}, u32[]{:S(2)}) %collective-permute-start.7) | collective-permute-done | bytes 1048608 | tf_op jit(solution)/shard_map/ppermute | solution.py:1081
  673.3 2.6 fusion.5
  675.9 2.7 fusion.1
  678.6 9.2 %convolution_convert_fusion.1 = bf16[2048,384]{1,0:T(8,128)(2,1)} fusion(bf16[2048,2048]{1,0:T(8,128)(2,1)} %get-tuple-element.61, bf16[2048,384]{1,0:T(8,128)(2,1)S(1)} %copy-done.11), kind=kOutput, calls=%fused_computation.12 | convolution fusion | flops 3222011904 | bytes 11534336 | tf_op jit(solution)/shard_map/dot_general | solution.py:30
  688.0 6.7 convolution_convert_fusion.3
  697.7 1.2 divide_sqrt_fusion
  699.1 1.8 multiply_convert_fusion.3
  700.9 135.6 %last_sums.1 = (f32[256,2048]{1,0:T(8,128)}, bf16[256,2048]{1,0:T(8,128)(2,1)}, bf16[8,64,1024]{2,1,0:T(8,128)(2,1)}) custom-call(bf16[2048,384]{1,0:T(8,128)(2,1)} %attend_backward.2.left_ref, bf16[2048,384]{1,0:T(8,128)(2,1)} %attend_backward.3.other_ref, bf16[2048,768]{1,0:T(8,128)(2,1)} %bitcast.87, bf16[256,2048]{1,0:T(8,128)(2,1)} %tokens_ref.3, ...), custom_call_target="tpu_custom_call" | custom-call | flops 805306368 | bytes 300000000 | tf_op jit(solution)/shard_map/last_sums/pallas_call | solution.py:961
  836.5 2.7 fusion.4
  839.2 29.2 %home.1 = (f32[64,2048]{1,0:T(8,128)}, f32[64,2048]{1,0:T(8,128)}, f32[64,2048]{1,0:T(8,128)}, f32[64,8192]{1,0:T(8,128)}, f32[64,8192]{1,0:T(8,128)}, /*index=5*/f32[64,1]{1,0:T(8,128)}, f32[64,1]{1,0:T(8,128)}) custom-call(bf16[8,64,384]{2,1,0:T(8,128)(2,1)} %bitcast.88, bf16[8,64,384]{2,1,0:T(8,128)(2,1)} %bitcast.89, ...), custom_call_target="tpu_custom_call" | custom-call | flops 1000000 | bytes 60000000 | tf_op jit(solution)/shard_map/home/pallas_call | solution.py:1040
  868.5 1.4 reduce.2
  869.9 1.4 reduce.3
  871.2 1.9 convert_element_type.169
  874.1 1.3 copy.57
  877.8 1.3 copy.61
  879.1 1.3 copy.62
  (100 shorter events, 13.3 us)
Async XLA Ops:
  7.2 226.3 %all-gather.6.cloned.1.call-start = ((), (), s32[]{:S(2)}) async-start(), calls=%async_computation.4 | async-start | bytes 8650752 | tf_op jit(solution)/shard_map/all_gather | solution.py:1144
  7.9 356.4 %all-gather.4.cloned.1.call-start = ((), (), s32[]{:S(2)}) async-start(), calls=%async_computation.3 | async-start | bytes 9437184 | tf_op jit(solution)/shard_map/all_gather | solution.py:1199
  149.4 11.9 %copy-start.3 = (bf16[8,64,2048]{2,1,0:T(8,128)(2,1)S(1)}, bf16[8,64,2048]{2,1,0:T(8,128)(2,1)}, u32[]{:S(2)}) copy-start(bf16[8,64,2048]{2,1,0:T(8,128)(2,1)} %get-tuple-element.73.refs_0_) | copy-start | bytes 6291460
  161.2 526.8 %all-gather.8.cloned.1.call-start = ((), (), s32[]{:S(2)}) async-start(), calls=%async_computation.7 | async-start | bytes 9437184 | tf_op jit(solution)/shard_map/all_gather | solution.py:1213
  161.3 72.2 %collective-permute-start = (bf16[8,64,2048]{2,1,0:T(8,128)(2,1)S(1)}, bf16[8,64,2048]{2,1,0:T(8,128)(2,1)}, u32[]{:S(2)}, u32[]{:S(2)}) collective-permute-start(bf16[8,64,2048]{2,1,0:T(8,128)(2,1)S(1)} %copy-done.3), channel_id=1, source_target_pairs={{0,4},{1,5},{2,6},{3,7},{4,0},{5,1},{6,2},{7,3},{8,12},{9,13},{10,... | collective-permute-start | bytes 6291464 | tf_op jit(solution)/shard_map/ppermute | solution.py:1081
  164.1 69.5 %collective-permute-start.1 = (bf16[8,64,1536]{2,1,0:T(8,128)(2,1)}, bf16[8,64,1536]{2,1,0:T(8,128)(2,1)}, u32[]{:S(2)}, u32[]{:S(2)}) collective-permute-start(bf16[8,64,1536]{2,1,0:T(8,128)(2,1)} %slice.21), channel_id=1, source_target_pairs={{0,16},{1,17},{2,18},{3,19},{4,20},{5,21},{6,22},{7,23},{8,24},{9,... | collective-permute-start | bytes 4718600 | tf_op jit(solution)/shard_map/ppermute | solution.py:1081
  164.8 1.4 copy-start.17
  332.0 18.5 %slice-start = ((s8[8388608]{0:T(1024)(128)(4,1)}), s8[4194304]{0:T(1024)(128)(4,1)S(1)}, s32[]{:S(2)}) async-start(s8[8388608]{0:T(1024)(128)(4,1)} %bitcast.94), calls=%async_computation.9 | async-start | bytes 8388608
  334.5 43.4 %collective-permute-start.2 = (bf16[1,256,2048]{2,1,0:T(8,128)(2,1)}, bf16[1,256,2048]{2,1,0:T(8,128)(2,1)S(1)}, u32[]{:S(2)}, u32[]{:S(2)}) collective-permute-start(bf16[1,256,2048]{2,1,0:T(8,128)(2,1)} %constant_dynamic-slice_fusion), channel_id=1, source_target_pairs={{0,4},{1,5},{2,6},{3,7},{4,0},{5,1},{6,2},{7,3},{8,12},{9,13},{10,... | collective-permute-start | bytes 3145736 | tf_op jit(solution)/shard_map/ppermute | solution.py:1081
  336.0 14.6 %slice-start.1 = ((s8[8388608]{0:T(1024)(128)(4,1)}), s8[4194304]{0:T(1024)(128)(4,1)S(1)}, s32[]{:S(2)}) async-start(s8[8388608]{0:T(1024)(128)(4,1)} %bitcast.94), calls=%async_computation.10 | async-start | bytes 8388608
  336.0 14.6 %copy-start.18 = (bf16[32,64,1024]{2,1,0:T(8,128)(2,1)S(1)}, bf16[32,64,1024]{2,1,0:T(8,128)(2,1)}, u32[]{:S(2)}) copy-start(bf16[32,64,1024]{2,1,0:T(8,128)(2,1)} %get-tuple-element.77) | copy-start | bytes 12582916
  377.0 3.8 copy-start.6
  377.0 3.7 copy-start.1
  377.2 47.8 %collective-permute-start.3 = (bf16[2,256,2048]{2,1,0:T(8,128)(2,1)S(1)}, bf16[2,256,2048]{2,1,0:T(8,128)(2,1)}, u32[]{:S(2)}, u32[]{:S(2)}) collective-permute-start(bf16[2,256,2048]{2,1,0:T(8,128)(2,1)S(1)} %dynamic-slice_bitcast_fusion.2), channel_id=1, source_target_pairs={{0,4},{1,5},{2,6},{3,7},{4,0},{5,1},{6,2},{7,3},{8,12},{9,13},{10,... | collective-permute-start | bytes 6291464 | tf_op jit(solution)/shard_map/ppermute | solution.py:1081
  380.8 21.8 %copy-start.2 = (bf16[4,256,2048]{2,1,0:T(8,128)(2,1)}, bf16[4,256,2048]{2,1,0:T(8,128)(2,1)S(1)}, u32[]{:S(2)}) copy-start(bf16[4,256,2048]{2,1,0:T(8,128)(2,1)S(1)} %constant_dynamic-update-slice_fusion) | copy-start | bytes 12582916
  508.9 330.4 %reduce-scatter.4.cloned.1.call-start = ((), (), s32[]{:S(2)}) async-start(), calls=%async_computation.5 | async-start | bytes 1966080 | tf_op jit(solution)/shard_map/reduce_scatter | solution.py:1087
  510.0 49.5 %collective-permute-start.5 = (bf16[256,2048]{1,0:T(8,128)(2,1)}, bf16[256,2048]{1,0:T(8,128)(2,1)S(1)}, u32[]{:S(2)}, u32[]{:S(2)}) collective-permute-start(bf16[256,2048]{1,0:T(8,128)(2,1)} %dynamic-slice_bitcast_fusion.5), channel_id=1, source_target_pairs={{0,16},{1,17},{2,18},{3,19},{4,20},{5,21},{6,22},{7,23},{8,24},{9,... | collective-permute-start | bytes 3145736 | tf_op jit(solution)/shard_map/ppermute | solution.py:1081
  514.7 82.2 %collective-permute-start.4 = (bf16[2,2,2,2,64,1024]{5,4,3,2,1,0:T(8,128)(2,1)}, bf16[2,2,2,2,64,1024]{5,4,3,2,1,0:T(8,128)(2,1)}, u32[]{:S(2)}, u32[]{:S(2)}) collective-permute-start(bf16[2,2,2,2,64,1024]{5,4,3,2,1,0:T(8,128)(2,1)} %dynamic-slice_bitcast_fusion.1), channel_id=1, source_target_pairs={{0,4},{1,5},{2,6},{3,7},{4,0},{5,1},{6,2},{7,3},{8,12},{9,13},{10,... | collective-permute-start | bytes 6291464 | tf_op jit(solution)/shard_map/ppermute | solution.py:1081
  555.8 283.4 %reduce-scatter.6.cloned.1.call-start = ((), (), s32[]{:S(2)}) async-start(), calls=%async_computation.6 | async-start | bytes 1966080 | tf_op jit(solution)/shard_map/reduce_scatter | solution.py:1087
  555.8 41.1 %copy-start.5 = (bf16[2048,1024]{1,0:T(8,128)(2,1)S(1)}, bf16[2048,1024]{1,0:T(8,128)(2,1)}, u32[]{:S(2)}) copy-start(bf16[2048,1024]{1,0:T(8,128)(2,1)} %get-tuple-element.85) | copy-start | bytes 12582916
  561.2 39.7 %copy-start.4 = (bf16[2048,1024]{1,0:T(8,128)(2,1)S(1)}, bf16[2048,1024]{1,0:T(8,128)(2,1)}, u32[]{:S(2)}) copy-start(bf16[2048,1024]{1,0:T(8,128)(2,1)} %get-tuple-element.86) | copy-start | bytes 12582916
  599.6 73.7 %collective-permute-start.7 = (bf16[2,2,2,64,1024]{4,3,2,1,0:T(8,128)(2,1)S(1)}, bf16[2,2,2,64,1024]{4,3,2,1,0:T(8,128)(2,1)}, u32[]{:S(2)}, u32[]{:S(2)}) collective-permute-start(bf16[2,2,2,64,1024]{4,3,2,1,0:T(8,128)(2,1)S(1)} %dynamic-slice_bitcast_fusion.4), channel_id=1, source_target_pairs={{0,16},{1,17},{2,18},{3,19},{4,20},{5,21},{6,22},{7,23},{8,24},{9,... | collective-permute-start | bytes 3145736 | tf_op jit(solution)/shard_map/ppermute | solution.py:1081
  601.2 74.7 %collective-permute-start.6 = (bf16[2,2,2,2,64,1024]{5,4,3,2,1,0:T(8,128)(2,1)S(1)}, bf16[2,2,2,2,64,1024]{5,4,3,2,1,0:T(8,128)(2,1)S(1)}, u32[]{:S(2)}, u32[]{:S(2)}) collective-permute-start(bf16[2,2,2,2,64,1024]{5,4,3,2,1,0:T(8,128)(2,1)S(1)} %dynamic-slice_bitcast_fusion), channel_id=1, source_target_pairs={{0,4},{1,5},{2,6},{3,7},{4,0},{5,1},{6,2},{7,3},{8,12},{9,13},{10,... | collective-permute-start | bytes 6291464 | tf_op jit(solution)/shard_map/ppermute | solution.py:1081
  631.8 46.8 %copy-start.11 = (bf16[2048,384]{1,0:T(8,128)(2,1)S(1)}, bf16[2048,384]{1,0:T(8,128)(2,1)}, u32[]{:S(2)}) copy-start(bf16[2048,384]{1,0:T(8,128)(2,1)} %attend_backward.3.other_ref) | copy-start | bytes 4718596
  678.6 9.4 %copy-start = (bf16[2048,256]{1,0:T(8,128)(2,1)S(1)}, bf16[2048,256]{1,0:T(8,128)(2,1)}, u32[]{:S(2)}) copy-start(bf16[2048,256]{1,0:T(8,128)(2,1)} %get-tuple-element.71.left_ref) | copy-start | bytes 3145732
  687.9 7.1 copy-start.19
  687.9 7.1 copy-start.16
  687.9 8.5 copy-start.20
  687.9 11.2 %copy-start.7 = (bf16[64,2048]{1,0:T(8,128)(2,1)S(1)}, bf16[64,2048]{1,0:T(8,128)(2,1)}, u32[]{:S(2)}) copy-start(bf16[64,2048]{1,0:T(8,128)(2,1)} %refs_4_.1) | copy-start | bytes 786436
  687.9 183.3 %reduce-scatter.8.cloned.1.call-start = ((), (), s32[]{:S(2)}) async-start(), calls=%async_computation.8 | async-start | bytes 1310720 | tf_op jit(solution)/shard_map/reduce_scatter | solution.py:1087
  694.9 141.7 %collective-permute-start.8 = (bf16[2,2,2,64,1024]{4,3,2,1,0:T(8,128)(2,1)S(1)}, bf16[2,2,2,64,1024]{4,3,2,1,0:T(8,128)(2,1)}, u32[]{:S(2)}, u32[]{:S(2)}) collective-permute-start(bf16[2,2,2,64,1024]{4,3,2,1,0:T(8,128)(2,1)S(1)} %dynamic-slice_bitcast_fusion.3), channel_id=1, source_target_pairs={{0,16},{1,17},{2,18},{3,19},{4,20},{5,21},{6,22},{7,23},{8,24},{9,... | collective-permute-start | bytes 3145736 | tf_op jit(solution)/shard_map/ppermute | solution.py:1081
  836.5 36.6 %copy-start.12 = (bf16[256,2048]{1,0:T(8,128)(2,1)S(1)}, bf16[256,2048]{1,0:T(8,128)(2,1)}, u32[]{:S(2)}) copy-start(bf16[256,2048]{1,0:T(8,128)(2,1)} %get-tuple-element.132) | copy-start | bytes 3145732
  839.2 34.9 %copy-start.8 = (f32[256,2048]{1,0:T(8,128)S(1)}, f32[256,2048]{1,0:T(8,128)}, u32[]{:S(2)}) copy-start(f32[256,2048]{1,0:T(8,128)} %get-tuple-element.133) | copy-start | bytes 6291460
  871.2 4.2 copy-start.15
  871.2 5.0 copy-start.14
  873.1 3.9 copy-start.13
  873.1 4.7 copy-start.10
  875.4 3.7 copy-start.9
Sparse Core Ops, SparseCore 0:
  10.9 117.5 all-gather.5
  161.3 79.0 all-gather.3
  509.0 87.7 all-gather.7
  599.5 60.6 reduce-scatter.3
  688.0 79.2 reduce-scatter.5
  769.5 42.5 reduce-scatter.7

commit v4 on v3

--- a/solution.py
+++ b/solution.py
@@ -13,7 +13,7 @@
 BLOCK = 256
 HALF = 128
 LAST_CUT = 0
-EARLY_UP = 512
+EARLY_HALVES = 3
 BRANCH_CUT = 128
 AXIS = "fsdp"
 MESH = pl.DeviceIdType.MESH
@@ -139,7 +139,8 @@
 
 
 def attend_backward_kernel(
-    first_head, q_ref, k_ref, v_ref, grad_ref, lse_ref, cos_ref, sin_ref, row_ref, col_ref, out_ref, dk_ref, dv_ref
+    first_head, q_ref, k_ref, v_ref, grad_ref, lse_ref, cos_ref, sin_ref, row_ref, col_ref, normed_ref,
+    out_ref, weight_ref, dk_ref, dv_ref,
 ):
     length = q_ref.shape[0]
     dk_ref[...] = jnp.zeros_like(dk_ref)
@@ -176,25 +177,33 @@
             dk * cos_ref[rows, :] - swap_halves(dk) * sin_ref[rows, :]
         ).astype(bf16)
         out_ref[rows, 2 * PAIR : 3 * PAIR] = dv_ref[rows, :].astype(bf16)
-
-
-def attend_backward(pair, query, key, value, grad, lse, cosine, sine, row_blocks, col_blocks):
-    length = query.shape[1]
+    side = 256
+
+    @pl.loop(0, normed_ref.shape[1] // side)
+    def _(k):
+        span = pl.ds(pl.multiple_of(k * side, side), side)
+        weight_ref[span, :] = contract(normed_ref[:, span], out_ref[...], 0, 0).astype(bf16)
+
+
+def attend_backward(pair, query, key, value, grad, lse, cosine, sine, row_blocks, col_blocks, normed):
+    length, width = normed.shape
     heads = pl.BlockSpec((None, length, PAIR), lambda _: (pair, 0, 0))
     return pl.pallas_call(
         functools.partial(attend_backward_kernel, 2 * pair),
         grid=(1,),
-        out_shape=jax.ShapeDtypeStruct((length, 3 * PAIR), bf16),
-        in_specs=[heads] * 3 + [pl.BlockSpec((length, PAIR), lambda _: (0, pair))] + [vmem] * 5,
-        out_specs=vmem,
+        out_shape=(
+            jax.ShapeDtypeStruct((length, 3 * PAIR), bf16), jax.ShapeDtypeStruct((width, 3 * PAIR), bf16),
+        ),
+        in_specs=[heads] * 3 + [pl.BlockSpec((length, PAIR), lambda _: (0, pair))] + [vmem] * 6,
+        out_specs=(vmem, vmem),
         scratch_shapes=[pltpu.VMEM((length, PAIR), f32), pltpu.VMEM((length, PAIR), f32)],
         compiler_params=pltpu.CompilerParams(vmem_limit_bytes=56 * 1024 * 1024),
         cost_estimate=pl.CostEstimate(
-            flops=40 * length * length * PAIR, bytes_accessed=length * PAIR * 24,
+            flops=40 * length * length * PAIR + 6 * length * width * PAIR, bytes_accessed=100_000_000,
             transcendentals=2 * length * length,
         ),
         name="attend_backward",
-    )(query, key, value, grad, lse, cosine, sine, row_blocks, col_blocks)
+    )(query, key, value, grad, lse, cosine, sine, row_blocks, col_blocks, normed)
 
 
 def bit_of(index, bit):
@@ -311,10 +320,11 @@
 SUM_COPIES = 10
 
 
-def sum_block(bits, cut, product, total, to_core, from_core, chip_sum, arrived, links):
-    core, first, second = bits
+def sum_block(bits, cut, swapped, product, total, to_core, from_core, chip_sum, arrived, links):
+    core = bits[0]
+    (first, weight_a), (second, weight_b) = ((bits[2], 4), (bits[1], 2)) if swapped else ((bits[1], 2), (bits[2], 4))
     me = lax.axis_index(AXIS)
-    sibling, next_a, next_b = (flip_bit(me, bit) for bit in bits)
+    sibling, next_a, next_b = flip_bit(me, core), flip_bit(me, first), flip_bit(me, second)
     block, width = total.shape
     tile = 512
 
@@ -322,8 +332,8 @@
         flip_a, flip_b = 1 - step // 2, 1 - step % 2
         return (
             lax.rem(bit_of(me, core) + other_core, 2)
-            + 2 * lax.rem(bit_of(me, first) + flip_a, 2)
-            + 4 * lax.rem(bit_of(me, second) + flip_b, 2)
+            + weight_a * lax.rem(bit_of(me, first) + flip_a, 2)
+            + weight_b * lax.rem(bit_of(me, second) + flip_b, 2)
         )
 
     low, high = (0, cut), (cut, block - cut)
@@ -456,12 +466,15 @@
 
 
 def front_kernel(
-    team, teams, qkv_moves, ffn_moves, tokens_ref, query_ref, key_ref, value_ref, gate_ref, up_ref, small_ref,
-    normed_out, weights_out, both_out, small_out,
-    tokens_all, mine, both_mine, gain,
+    team, teams, qkv_moves, ffn_moves, carry_bits, tokens_ref, query_ref, key_ref, value_ref, gate_ref, up_ref, small_ref, *refs,
+):
+    moved = len(carry_bits)
+    (carried, refs) = (refs[0], refs[1:]) if moved else (None, refs)
+    (normed_out, weights_out, both_out, small_out), refs = refs[:4], refs[4:]
+    carried_out, refs = refs[:moved], refs[moved:]
+    (tokens_all, mine, both_mine, gain,
     send_sems, recv_sems, local_sem, swap_send, swap_recv, swap_local, line_send, line_recv, small_send, small_recv,
-    both_send, both_recv, both_local, out_sems,
-):
+    both_send, both_recv, both_local, out_sems, *carry_sems) = refs
     me = lax.axis_index(AXIS)
     mate, group = lax.rem(me, team), lax.div(me, team)
     devices = team * teams
@@ -486,6 +499,9 @@
         swaps.copy(k, mine.at[lax.rem(mate + k + 1, team)], weights_out.at[group, share(mate)], mates[k])
         for k in range(team - 1)
     ]
+    crossing = [
+        Links(*carry_sems).copy(i, carried, carried_out[i], flip_bit(me, bit)) for i, bit in enumerate(carry_bits)
+    ]
     for copy in swap_copies:
         copy.start()
     keep = pltpu.make_async_copy(mine.at[mate], weights_out.at[group, share(mate)], swap_local)
@@ -507,7 +523,7 @@
         (1, 2, 4), HALF, tokens_ref, tokens_all, Links(send_sems, recv_sems), local_sem
     )
     for i, member, source, target, columns in ffn_moves:
-        both_mine[member, :, target : target + columns] = (gate_ref, up_ref)[i][:, source : source + columns]
+        both_mine[i * team + member, :, target : target + columns] = (gate_ref, up_ref)[i][:, source : source + columns]
 
     def passed(slot, shard, device):
         return line.copy(slot, weights_out.at[shard], weights_out.at[shard], device)
@@ -538,18 +554,26 @@
         copy.start()
     own_place = ffn_mates[0][1]
     both_copies = [
-        both.copy(k, both_mine.at[ffn_mates[k][1]], both_out.at[own_place], ffn_mates[k][0])
-        for k in range(1, team)
+        both.copy(
+            i * team + k, both_mine.at[i * team + ffn_mates[k][1]], both_out.at[i * team + own_place], ffn_mates[k][0]
+        )
+        for i in range(2) for k in range(1, team)
     ]
     for copy in both_copies:
         copy.start()
-    both_keep = pltpu.make_async_copy(both_mine.at[own_place], both_out.at[own_place], both_local)
-    both_keep.start()
+    both_keep = [
+        pltpu.make_async_copy(both_mine.at[i * team + own_place], both_out.at[i * team + own_place], both_local.at[i])
+        for i in range(2)
+    ]
+    for copy in both_keep:
+        copy.start()
     for copy in swap_copies:
         copy.wait_recv()
     keep.wait()
     line_start(1)
     spread[0]()
+    for copy in crossing:
+        copy.start()
     for copy in small_far:
         copy.wait_recv()
     spread[1]()
@@ -589,51 +613,55 @@
         normed_copy(k).wait()
     for copy in both_copies:
         copy.wait_recv()
-    both_keep.wait()
+    for copy in both_keep:
+        copy.wait()
     for copy in swap_copies + both_copies:
         copy.wait_send()
     for step in range(1, teams):
         line_sent(step)
     for copy in small_near + small_far:
         copy.wait_send()
-
-
-def front(tokens, weights, small, teams, qkv_moves, ffn_moves):
+    for copy in crossing:
+        copy.wait()
+
+
+def front(tokens, weights, small, teams, qkv_moves, ffn_moves, carried, carry_bits):
     block, width = tokens.shape
     team = 8
     rows, cols = weights[0].shape[0], 3 * width // team
-    both_cols = 2 * weights[3].shape[1] // team
+    both_cols = weights[3].shape[1] // team
     devices = team * teams
     dma = pltpu.SemaphoreType.DMA
     shape = jax.ShapeDtypeStruct
     return pl.pallas_call(
-        functools.partial(front_kernel, team, teams, qkv_moves, ffn_moves),
+        functools.partial(front_kernel, team, teams, qkv_moves, ffn_moves, carry_bits),
         out_shape=(
             shape((team * block, width), bf16),
             shape((teams, team * rows, cols), bf16),
-            shape((team, rows, both_cols), bf16),
+            shape((2 * team, rows, both_cols), bf16),
             shape((devices,) + small.shape, f32),
-        ),
-        in_specs=[vmem] * 7,
-        out_specs=(anywhere, anywhere, anywhere, vmem),
+        ) + tuple(shape(carried[0].shape, bf16) for _ in carry_bits),
+        in_specs=[vmem] * 7 + [anywhere] * len(carried),
+        out_specs=(anywhere, anywhere, anywhere, vmem) + (anywhere,) * len(carry_bits),
         scratch_shapes=[
             pltpu.VMEM((team * block, width), bf16), pltpu.VMEM((team, rows, cols), bf16),
-            pltpu.VMEM((team, rows, both_cols), bf16), pltpu.VMEM((1, width), f32),
+            pltpu.VMEM((2 * team, rows, both_cols), bf16), pltpu.VMEM((1, width), f32),
         ]
         + spread_scratch(block, width)[1:]
         + [dma((team - 1,)), dma((team - 1,)), dma, dma((2 * teams,)), dma((2 * teams,)), dma((team + teams,)), dma((team + teams,))]
-        + [dma((team,)), dma((team,)), dma, dma((team,))],
+        + [dma((2 * team,)), dma((2 * team,)), dma((2,)), dma((team,))]
+        + [dma((1,))] * (2 * len(carried)),
         compiler_params=link_params(1),
         cost_estimate=cost(0, 200e6),
         name="front",
-    )(tokens, *weights, small)
+    )(tokens, *weights, small, *carried)
 
 
 def branch_kernel(
     carry, swap_bits, spread_bits, left_ref, right_ref, residual_ref, gain_ref, peak_ref, *refs,
 ):
     if carry:
-        (both_own, both_y, both_z, down_own), refs = refs[:4], refs[4:]
+        (both_own, both_y, both_z, down_own, down_y), refs = refs[:5], refs[5:]
         (h2_ref, out_ref, peak_out, gate_full, up_full, down_full), refs = refs[:6], refs[6:]
         (landed, together, swap_send, swap_recv, own, send_sems, recv_sems, local_sem,
          peak_in, peak_send, peak_recv, carry_send, carry_recv, carry_local) = refs
@@ -678,42 +706,35 @@
             z, y = lax.rem(high + flip_z, 2), lax.rem(middle + flip_y, 2)
             return pl.ds(pl.multiple_of(z * 16 + part * 8 + y * 4, 4), 4)
 
-        cols, early = both_own.shape[2] // 2, both_z.shape[2]
-
-        def piece(source, part, first, last):
-            return source.at[pl.ds(part * 4, 4), :, pl.ds(first, last - first)]
-
-        def placed(part, flips, first, last):
-            full, start = (gate_full, first) if last <= cols else (up_full, first - cols)
-            return full.at[rows_of(part, *flips), :, pl.ds(start, last - first)]
+        early = both_z.shape[0] // 4
+
+        def piece(source, half):
+            return source.at[pl.ds(half * 4, 4)]
+
+        def placed(half, flips):
+            return (gate_full, up_full)[half // 2].at[rows_of(half % 2, *flips)]
 
         def unit(flip_z, flip_y):
             return lax.rem(high + flip_z, 2) * 2 + lax.rem(middle + flip_y, 2)
 
-        spans = ((0, cols), (cols, 2 * cols))
-        early_spans = ((0, cols), (cols, early))
         kept = []
-        for source, flips, columns in ((both_own, (0, 0), spans), (both_y, (0, 1), spans), (both_z, (1, 0), early_spans)):
-            for span in columns:
-                for part in range(2):
-                    kept.append((piece(source, part, *span), placed(part, flips, *span)))
+        for source, flips, halves in ((both_own, (0, 0), 4), (both_y, (0, 1), 4), (both_z, (1, 0), early)):
+            for half in range(halves):
+                kept.append((piece(source, half), placed(half, flips)))
         kept.append((down_own, down_full.at[unit(0, 0)]))
+        kept.append((down_y, down_full.at[unit(0, 1)]))
         kept = [pltpu.make_async_copy(a, b, carry_local.at[i]) for i, (a, b) in enumerate(kept)]
-        late = (early, 2 * cols)
         up_z = [
-            carried.copy(part, piece(both_own, part, *late), placed(part, (0, 0), *late), by_z) for part in range(2)
+            carried.copy(half, piece(both_own, half), placed(half, (0, 0)), by_z) for half in range(early, 4)
         ]
         early_yz = [
-            carried.copy(2 + 2 * i + part, piece(both_z, part, *span), placed(part, (1, 0), *span), by_y)
-            for i, span in enumerate(early_spans) for part in range(2)
+            carried.copy(4 + half, piece(both_z, half), placed(half, (1, 0)), by_y) for half in range(early)
         ]
         up_yz = [
-            carried.copy(6 + part, placed(part, (1, 0), *late), placed(part, (1, 0), *late), by_y)
-            for part in range(2)
+            carried.copy(4 + half, placed(half, (1, 0)), placed(half, (1, 0)), by_y) for half in range(early, 4)
         ]
         down_z = carried.copy(8, down_own, down_full.at[unit(0, 0)], by_z)
-        down_y = carried.copy(9, down_own, down_full.at[unit(0, 0)], by_y)
-        for copy in up_z + [down_y] + kept:
+        for copy in up_z + kept:
             copy.start()
 
     peak_out[...] = peak_ref[...]
@@ -721,6 +742,9 @@
     landed[own_place] = left_ref[rows_at(own_place), :]
     for copy in swap_copies:
         copy.wait_recv()
+    if carry:
+        for copy in early_yz:
+            copy.start()
     heads = landed.shape[2] // HEAD_DIM
     for b in range(team):
         for g in range(heads):
@@ -740,11 +764,9 @@
     spread = spread_block(spread_bits, BRANCH_CUT, own, out_ref, Links(send_sems, recv_sems), local_sem)
     spread[0]()
     if carry:
-        for copy in early_yz:
-            copy.start()
-        for part in range(2):
-            up_z[part].wait_recv()
-            up_yz[part].start()
+        for over, on in zip(up_z, up_yz):
+            over.wait_recv()
+            on.start()
         down_z.start()
     for k, phase in enumerate(spread[1:-1]):
         phase()
@@ -758,9 +780,9 @@
     if carry:
         for copy in kept:
             copy.wait()
-        for copy in early_yz + up_yz + [down_y, down_z]:
+        for copy in early_yz + up_yz + [down_z]:
             copy.wait_recv()
-        for copy in up_z + early_yz + up_yz + [down_y, down_z]:
+        for copy in up_z + early_yz + up_yz + [down_z]:
             copy.wait_send()
 
 
@@ -774,11 +796,10 @@
     scratch += [pltpu.VMEM((bit_count, 8, 128), f32), dma((bit_count,)), dma((bit_count,))]
     if carry:
         out_shape += [
-            shape((32, carry[0].shape[1], carry[0].shape[2] // 2), bf16),
-            shape((32, carry[0].shape[1], carry[0].shape[2] // 2), bf16),
+            shape((32,) + carry[0].shape[1:], bf16), shape((32,) + carry[0].shape[1:], bf16),
             shape((4,) + carry[3].shape, bf16),
         ]
-        scratch += [dma((10,)), dma((10,)), dma((13,))]
+        scratch += [dma((9,)), dma((9,)), dma((14,))]
     return pl.pallas_call(
         functools.partial(branch_kernel, bool(carry), swap_bits, spread_bits),
         out_shape=tuple(out_shape),
@@ -799,11 +820,18 @@
 
 
 def ffn_back_kernel(
-    sum_bits, swap_bits, gate_ref, up_ref, gate_w_ref, up_w_ref, normed_ref, out_w_ref, h2_ref, cot_ref, gain_ref,
-    residual_ref, branch_ref, heads_out, d_gate_out, d_up_out,
-    total, to_core, from_core, chip_sum, arrived, sum_send, sum_recv,
-    swap_send, swap_recv, local_sem, stage, stage_sems,
+    cross, sum_bits, swap_bits, gate_ref, up_ref, gate_w_ref, up_w_ref, normed_ref, out_w_ref, h2_ref, cot_ref, gain_ref, *refs,
 ):
+    (part_ref, refs) = (refs[0], refs[1:]) if cross else (None, refs)
+    (residual_ref, branch_ref, heads_out, d_up_out, d_gate_own), refs = refs[:5], refs[5:]
+    (d_gate_in, part_in, refs) = (refs[0], refs[1], refs[2:]) if cross else (None, None, refs)
+    (total, to_core, from_core, chip_sum, arrived, sum_send, sum_recv,
+     swap_send, swap_recv, local_sem, stage, stage_sems, own_sems, *more) = refs
+    if cross:
+        cross_send, cross_recv = more
+        crossing = Links(cross_send, cross_recv)
+    else:
+        (stage_gate,) = more
     me = lax.axis_index(AXIS)
     block, width = total.shape
     team = 1 << len(swap_bits)
@@ -818,32 +846,70 @@
             up_ref[rows, :], up_w_ref[columns, :], 1, 1
         )
 
-    side = stage.shape[2]
+    side, columns_ff = stage.shape[1:]
     count = width // side
-    outs = (d_gate_out, d_up_out)
-
-    def stage_copy(k, which):
-        span = pl.ds(pl.multiple_of(k * side, side), side)
-        slot = lax.rem(k, 2)
-        return pltpu.make_async_copy(stage.at[slot, which], outs[which].at[span], stage_sems.at[slot, which])
+    y_side, by_y = bit_of(me, 4), flip_bit(me, 4)
+    if cross:
+        part_copy = crossing.copy(count // 2, part_ref, part_in, by_y)
+        part_copy.start()
+
+    def parked(i, part):
+        row = i * side
+        rows = pl.ds(pl.multiple_of(lax.rem(row, block), 16), side)
+        return from_core.at[lax.div(row, block), rows, pl.ds(part * columns_ff, columns_ff)]
+
+    def cross_copy(i):
+        return crossing.copy(i, parked(i, 0), d_gate_in.at[i], by_y)
+
+    def own_copy(i):
+        return pltpu.make_async_copy(parked(i, 1), d_gate_own.at[i], own_sems.at[i])
+
+    def tile_of(step):
+        if not cross:
+            return step
+        theirs = step < count // 2
+        return jnp.where(theirs, 2 * step + 1 - y_side, 2 * step - count + y_side)
+
+    def up_copy(step):
+        span = pl.ds(pl.multiple_of(tile_of(step) * side, side), side)
+        slot = lax.rem(step, 2)
+        return pltpu.make_async_copy(stage.at[slot], d_up_out.at[span], stage_sems.at[slot])
+
+    def gate_copy(step):
+        span = pl.ds(pl.multiple_of(step * side, side), side)
+        slot = lax.rem(step, 2)
+        return pltpu.make_async_copy(stage_gate.at[slot], d_gate_own.at[span], own_sems.at[slot])
 
     def gradients(first, last):
         @pl.loop(first, last)
-        def _(k):
-            @pl.when(k >= 2)
+        def _(step):
+            @pl.when(step >= 2)
             def _():
-                for which in range(2):
-                    stage_copy(k - 2, which).wait()
-
-            columns = normed_ref[:, pl.ds(pl.multiple_of(k * side, side), side)]
-            slot = lax.rem(k, 2)
-            stage[slot, 0] = contract(columns, gate_ref[...], 0, 0).astype(bf16)
-            stage[slot, 1] = contract(columns, up_ref[...], 0, 0).astype(bf16)
-            for which in range(2):
-                stage_copy(k, which).start()
+                up_copy(step - 2).wait()
+                if not cross:
+                    gate_copy(step - 2).wait()
+
+            columns = normed_ref[:, pl.ds(pl.multiple_of(tile_of(step) * side, side), side)]
+            stage[lax.rem(step, 2)] = contract(columns, up_ref[...], 0, 0).astype(bf16)
+            up_copy(step).start()
+            tile = contract(columns, gate_ref[...], 0, 0).astype(bf16)
+            if not cross:
+                stage_gate[lax.rem(step, 2)] = tile
+                gate_copy(step).start()
+                return
+
+            @pl.when(step < count // 2)
+            def _():
+                parked(step, 0)[...] = tile
+                cross_copy(step).start()
+
+            @pl.when(step >= count // 2)
+            def _():
+                parked(step - count // 2, 1)[...] = tile
+                own_copy(step - count // 2).start()
 
     for_sibling, for_chip, hand_on, finish = sum_block(
-        sum_bits, HALF, product, total, to_core, from_core, chip_sum, arrived, Links(sum_send, sum_recv)
+        sum_bits, HALF, False, product, total, to_core, from_core, chip_sum, arrived, Links(sum_send, sum_recv)
     )
     for_sibling()
     for_chip()
@@ -878,31 +944,47 @@
     for copy in swap_copies:
         copy.wait_send()
     keep.wait()
-    for k in range(count - 2, count):
-        for which in range(2):
-            stage_copy(k, which).wait()
-
-
-def ffn_back(gate, up, gate_w, up_w, normed, out_w, h2, cot, gain, sum_bits, swap_bits):
+    for step in range(count - 2, count):
+        up_copy(step).wait()
+        if not cross:
+            gate_copy(step).wait()
+    if cross:
+        part_copy.wait()
+
+        @pl.loop(0, count // 2)
+        def _(i):
+            own_copy(i).wait()
+            cross_copy(i).wait()
+
+
+def ffn_back(gate, up, gate_w, up_w, normed, out_w, h2, cot, gain, part, side, sum_bits, swap_bits):
     block, width = h2.shape
     shape = jax.ShapeDtypeStruct
     dma = pltpu.SemaphoreType.DMA
-    ff_cols = gate.shape[1]
+    ff_cols, cross = gate.shape[1], side % 128 == 0
+    side = side if cross else 256
+    tiles = width // side // 2
+    if cross:
+        d_gate = (shape((tiles, side, ff_cols), bf16),) * 2 + (shape(part[0].shape, bf16),)
+        more = [dma((tiles + 1,)), dma((tiles + 1,))]
+    else:
+        d_gate, more = (shape((width, ff_cols), bf16),), [pltpu.VMEM((2, side, ff_cols), bf16)]
     return pl.pallas_call(
-        functools.partial(ffn_back_kernel, sum_bits, swap_bits),
+        functools.partial(ffn_back_kernel, cross, sum_bits, swap_bits),
         out_shape=(
             shape((block, width), f32), shape((block, width), bf16), shape((8 * block, width // 8), bf16),
-            shape((width, ff_cols), bf16), shape((width, ff_cols), bf16),
-        ),
-        in_specs=[vmem] * 9,
-        out_specs=(vmem, vmem, anywhere, anywhere, anywhere),
+            shape((width, ff_cols), bf16),
+        ) + d_gate,
+        in_specs=[vmem] * 9 + [anywhere] * len(part),
+        out_specs=(vmem, vmem) + (anywhere,) * (2 + len(d_gate)),
         scratch_shapes=sum_scratch(block, width, HALF)
         + [dma((8,)), dma((8,)), dma]
-        + [pltpu.VMEM((2, 2, 256, ff_cols), bf16), dma((2, 2))],
+        + [pltpu.VMEM((2, side, ff_cols), bf16), dma((2,)), dma((tiles,))]
+        + more,
         compiler_params=link_params(3),
         cost_estimate=cost(96 * block * ff_cols * width, 200e6),
         name="ffn_back",
-    )(gate, up, gate_w, up_w, normed, out_w, h2, cot, gain)
+    )(gate, up, gate_w, up_w, normed, out_w, h2, cot, gain, *part)
 
 
 def last_sums_kernel(
@@ -936,8 +1018,8 @@
     def ffn_product(place, columns):
         return contract(hidden_ref[rows_of(place), :], down_ref[:, columns], 1, 0)
 
-    first = sum_block(sum_bits, LAST_CUT, product, *scratch[: count - 2], Links(*scratch[count - 2 : count]))
-    second = sum_block(ffn_bits, LAST_CUT, ffn_product, *scratch[count:-2], Links(*scratch[-2:]))
+    first = sum_block(sum_bits, LAST_CUT, False, product, *scratch[: count - 2], Links(*scratch[count - 2 : count]))
+    second = sum_block(ffn_bits, LAST_CUT, False, ffn_product, *scratch[count:-2], Links(*scratch[-2:]))
     run(first[:2])
     run(second[:2])
     for copy in swap_copies + [keep]:
@@ -974,31 +1056,19 @@
     )(left, other, right, tokens, gain, residual, hidden, down, h2, d_gate)
 
 
-def home_kernel(teams, places, gain_of, sources, *refs):
-    count = len(places)
-    kinds = max(gain_of) + 1
-    mine, refs = refs[:sources], refs[sources:]
-    weights, refs = refs[:count], refs[count:]
-    gains, refs = refs[:kinds], refs[kinds:]
-    outs, refs = refs[:count], refs[count:]
-    gain_outs, refs = refs[:kinds], refs[kinds:]
-    landed, (send_sems, recv_sems, local_sems) = list(refs[:-3]), refs[-3:]
+def exchange_kernel(teams, sources, *refs):
+    mine, landed, (send_sems, recv_sems, local_sems) = refs[:sources], refs[sources : 2 * sources], refs[2 * sources :]
     me = lax.axis_index(AXIS)
     members = mine[0].shape[0]
     links = Links(send_sems, recv_sems)
     greeted = {}
     for bits in teams:
-        for k in range(1, members) if bits else ():
+        for k in range(1, members):
             device, _ = team_mate(me, bits, k)
             greeted[tuple(sorted(bit for j, bit in enumerate(bits) if (k >> j) % 2))] = device
     greet(list(greeted.values()))
-    copies, kept, arrived = [], [], []
-    for i, (source, bits) in enumerate(zip(mine, teams)):
-        if not bits:
-            arrived.append(source)
-            continue
-        target = landed.pop(0)
-        arrived.append(target)
+    copies, kept = [], []
+    for i, (source, target, bits) in enumerate(zip(mine, landed, teams)):
         own = team_mate(me, bits, 0)[1]
         kept.append(pltpu.make_async_copy(source.at[own], target.at[own], local_sems.at[i]))
         for k in range(1, members):
@@ -1006,46 +1076,54 @@
             copies.append(links.copy(i * members + k, source.at[place], target.at[own], device))
     for copy in copies + kept:
         copy.start()
+    for copy in copies:
+        copy.wait()
+    for copy in kept:
+        copy.wait()
+
+
+def exchange(parts, teams):
+    dma = pltpu.SemaphoreType.DMA
+    slots = len(parts) * parts[0].shape[0]
+    return pl.pallas_call(
+        functools.partial(exchange_kernel, teams, len(parts)),
+        out_shape=tuple(jax.ShapeDtypeStruct(part.shape, part.dtype) for part in parts),
+        in_specs=[vmem] * len(parts),
+        out_specs=tuple([vmem] * len(parts)),
+        scratch_shapes=[dma((slots,)), dma((slots,)), dma((len(parts),))],
+        compiler_params=link_params(5),
+        cost_estimate=cost(1e6, 40e6),
+        name="exchange",
+    )(*parts)
+
+
+def home_kernel(places, gain_of, sources, *refs):
+    count = len(places)
+    kinds = max(gain_of) + 1
+    parts, weights, gains = refs[:sources], refs[sources : sources + count], refs[sources + count : sources + count + kinds]
+    outs, gain_outs = refs[-count - kinds : -kinds], refs[-kinds:]
     totals = [jnp.zeros(gain.shape, f32) for gain in gains]
-
-    def settle(i):
-        out, weight = outs[i], weights[i]
+    for i, (out, weight) in enumerate(zip(outs, weights)):
         for source, member, first, target, columns in places[i]:
-            out[:, target : target + columns] = arrived[source][member, :, first : first + columns].astype(f32)
+            out[:, target : target + columns] = parts[source][member, :, first : first + columns].astype(f32)
         for first in range(0, out.shape[1], 1024):
             product = out[:, first : first + 1024] * weight[:, first : first + 1024].astype(f32)
             totals[gain_of[i]] += jnp.sum(product, 1, keepdims=True)
-
-    ready = [i for i in range(count) if all(not teams[move[0]] for move in places[i])]
-    for i in ready:
-        settle(i)
-    for copy in copies:
-        copy.wait_recv()
-    for copy in kept:
-        copy.wait()
-    for i in range(count):
-        if i not in ready:
-            settle(i)
     for gain, total, out in zip(gains, totals, gain_outs):
-        out[...] = total / gain[...]
-    for copy in copies:
-        copy.wait_send()
-
-
-def home(parts, teams, weights, gains, gain_of, places):
+        out[...] = jnp.broadcast_to(total / gain[...], (out.shape[1], 128)).T[0:1, :]
+
+
+def home(parts, weights, gains, gain_of, places):
     shape = jax.ShapeDtypeStruct
-    dma = pltpu.SemaphoreType.DMA
-    count, slots = len(weights), len(parts) * parts[0].shape[0]
+    count = len(weights)
     gains = [gain.astype(f32).reshape(-1, 1) for gain in gains]
     return pl.pallas_call(
-        functools.partial(home_kernel, teams, places, gain_of, len(parts)),
-        out_shape=tuple(shape(w.shape, f32) for w in weights) + tuple(shape(g.shape, f32) for g in gains),
+        functools.partial(home_kernel, places, gain_of, len(parts)),
+        out_shape=tuple(shape(w.shape, f32) for w in weights) + tuple(shape((1, g.shape[0]), f32) for g in gains),
         in_specs=[vmem] * (len(parts) + count + len(gains)),
         out_specs=tuple([vmem] * (count + len(gains))),
-        scratch_shapes=[pltpu.VMEM(part.shape, bf16) for part, bits in zip(parts, teams) if bits]
-        + [dma((slots,)), dma((slots,)), dma((len(parts),))],
-        compiler_params=link_params(5),
-        cost_estimate=cost(1e6, 60e6),
+        compiler_params=pltpu.CompilerParams(vmem_limit_bytes=40 * 1024 * 1024),
+        cost_estimate=cost(1e6, 30e6),
         name="home",
     )(*parts, *weights, *gains)
 
@@ -1138,7 +1216,7 @@
         for h in range(devices // 16) for z in range(2) for y in range(2) for c in range(4)
     )
     ffn_moves = tuple(
-        (i, member, source, i * ff_cols + target, ff_rows)
+        (i, member, source, target, ff_rows)
         for i in range(2) for member, target, source in ffn_units
     )
     out_w = lax.all_gather(w_out, AXIS, axis=0, tiled=True)
@@ -1146,8 +1224,10 @@
     gain_row = jnp.pad(gain_row, (0, 128 - 2 * weight_rows)).reshape(1, 128)
     block_rows = block_of.astype(f32).reshape(tok_rows // 128, 128)
     small = jnp.concatenate([gain_row, block_rows, jnp.zeros((7 - tok_rows // 128, 128), f32)])
-    normed_attn, qkv_w, both_mine, gathered = front(
-        tokens, (w_query, w_key, w_value, w_gate, w_up), small, teams, qkv_moves, ffn_moves
+    ahead = data_bits == [4, 16]
+    normed_attn, qkv_w, both_mine, gathered, *down_moved = front(
+        tokens, (w_query, w_key, w_value, w_gate, w_up), small, teams, qkv_moves, ffn_moves,
+        [w_down] if ahead else [], (4,) if ahead else (),
     )
     qkv_w = qkv_w.reshape(width, 3 * head_cols)
     gain_attn = gathered[:, 0, :weight_rows].reshape(1, width)
@@ -1155,7 +1235,7 @@
     blocks = lax.dynamic_slice_in_dim(gathered, device - mate, team, 0)
     blocks = blocks[:, 1 : 1 + tok_rows // 128].astype(jnp.int32).reshape(SEQ)
     row_blocks, col_blocks = blocks.reshape(1, SEQ), blocks.reshape(SEQ, 1)
-    both_mine, down_mine, qkv_w = tie(both_mine, w_down, qkv_w)
+    both_mine, qkv_w = tie(both_mine, qkv_w)
 
     def whole_rows(mine):
         shape = row_shape + (weight_rows, ff_cols)
@@ -1165,8 +1245,7 @@
     cosine, sine = rope_tables(SEQ, PAIR)
     qkv, cot_mine = tie(qkv, cotangent)
     if data_bits == [4, 16]:
-        early = ff_cols + EARLY_UP
-        carry = [both_mine, flip(both_mine, 4), flip(both_mine[:, :, :early], 16), down_mine]
+        carry = [both_mine, flip(both_mine, 4), flip(both_mine[: 4 * EARLY_HALVES], 16), w_down, *down_moved]
     else:
         carry = []
     query, key, value, attended, lse, peak = attend_forward(qkv, cosine, sine, row_blocks, col_blocks)
@@ -1186,9 +1265,9 @@
             full[2], flip(passed, 4), ((1 - z_side) * 2 + 1 - y_side, 0, 0)
         ).reshape(ff_cols, width)
     else:
-        gate_w, up_w = whole_rows(both_mine[:, :, :ff_cols]), whole_rows(both_mine[:, :, ff_cols:])
+        gate_w, up_w = whole_rows(both_mine[:team]), whole_rows(both_mine[team:])
         down_w = place_pieces(
-            data_pieces(down_mine), unit_dims, unit_shape + (ff_rows, width)
+            data_pieces(w_down), unit_dims, unit_shape + (ff_rows, width)
         ).reshape(ff_cols, width)
     gate_pre = contract(normed_ffn, gate_w, 1, 0)
     up_pre = contract(normed_ffn, up_w, 1, 0)
@@ -1203,31 +1282,48 @@
     grad_gate = (d_hidden * up_pre * sigmoid_gate * (1.0 + gate_pre * (1.0 - sigmoid_gate))).astype(bf16)
     grad_up = (d_hidden * silu_gate).astype(bf16)
 
-    d_down = data_sum(d_down, unit_dims, data_bits[:1])
     unit_rest, row_rest = after_bit(unit_dims, data_bits[0]), after_bit(row_dims, data_bits[0])
-    grad_gate, d_down = tie(grad_gate, d_down)
-    d_residual, branch_mine, grad_attended, d_gate, d_up = ffn_back(
-        grad_gate, grad_up, gate_w, up_w, normed_ffn, out_w, after_attn, cotangent, gain_ffn, ffn_bits, attn_bits
-    )
-    d_gate, d_up = (d.reshape(row_shape + (weight_rows, ff_cols)) for d in (d_gate, d_up))
+    row_values = (weight_rows, ff_cols)
+    crosses = data_bits == [4, 16]
+    if crosses:
+        y_side = (device // 4) % 2
+        kept = lax.dynamic_index_in_dim(d_down, y_side, unit_dims[4], False)
+        sent = lax.dynamic_index_in_dim(d_down, 1 - y_side, unit_dims[4], False)
+        ahead = flip(sent[0], 4)
+        grad_gate, ahead = tie(grad_gate, ahead)
+        beside = [sent[1]]
+    else:
+        beside = []
+    d_residual, branch_mine, grad_attended, d_up, *d_gate = ffn_back(
+        grad_gate, grad_up, gate_w, up_w, normed_ffn, out_w, after_attn, cotangent, gain_ffn, beside, 4 * weight_rows,
+        ffn_bits, attn_bits,
+    )
+    if crosses:
+        d_down = (kept.astype(f32) + jnp.stack([ahead, d_gate[2]]).astype(f32)).astype(bf16)
+        d_gate = (d_gate[0].astype(f32) + d_gate[1].astype(f32)).astype(bf16)
+        d_gate = d_gate.reshape((2,) * (bit_count - 1) + row_values)
+    else:
+        d_down = data_sum(d_down, unit_dims, data_bits[:1])
+        d_gate = data_sum(d_gate[0].reshape(row_shape + row_values), row_dims, data_bits[:1])
+    grad_attended, d_down, d_gate = tie(grad_attended, d_down, d_gate)
+    d_gate = data_sum(d_gate, row_rest, data_bits[1:])
     branch_grad = lax.all_gather(branch_mine, AXIS, axis=0, tiled=True, axis_index_groups=in_team)
-    d_down = data_sum(d_down, unit_rest, data_bits[1:]).astype(f32)
 
     def heads_back(pair):
         return attend_backward(
-            pair, query, key, value, grad_attended, lse, cosine, sine, row_blocks, col_blocks
+            pair, query, key, value, grad_attended, lse, cosine, sine, row_blocks, col_blocks, normed_attn
         )
 
     grad_pairs, shares = [None] * (heads // 2), [None] * (heads // 2)
-    grad_pairs[0] = heads_back(0)
-    shares[0] = scatter_across(contract(normed_attn, grad_pairs[0], 0, 0))
-    d_gate = data_sum(d_gate, row_dims, data_bits[:1])
-    grad_attended, d_gate, d_up, d_down, _ = tie(grad_attended, d_gate, d_up, d_down, grad_pairs[0])
-    d_gate = data_sum(d_gate, row_rest, data_bits[1:])
-    d_up = data_sum(d_up, row_dims, data_bits[:1])
+    grad_pairs[0], share = heads_back(0)
+    grad_attended, d_down, d_gate, d_up, share = tie(grad_attended, d_down, d_gate, d_up, share)
+    shares[0] = scatter_across(share)
+    d_down = data_sum(d_down, unit_rest, data_bits[1:]).astype(f32)
+    d_up = data_sum(d_up.reshape(row_shape + row_values), row_dims, data_bits[:1])
     for p in range(1, heads // 2):
-        grad_pairs[p], d_up, d_gate = tie(heads_back(p), d_up, d_gate)
-        shares[p] = scatter_across(contract(normed_attn, grad_pairs[p], 0, 0))
+        grad_pairs[p], share = heads_back(p)
+        grad_pairs[p], share, d_down, d_up, branch_grad = tie(grad_pairs[p], share, d_down, d_up, branch_grad)
+        shares[p] = scatter_across(share)
     d_up = data_sum(d_up, row_rest, data_bits[1:])
     d_gate = d_gate.reshape(team, weight_rows, ff_cols)
     out_part = contract(attended, branch_grad, 0, 0)
@@ -1249,13 +1345,14 @@
         [(heads // 2 + i, member, target, source, ff_rows) for member, target, source in ffn_units] for i in range(2)
     ]
     shares = [share.reshape(team, weight_rows, 3 * PAIR) for share in shares]
+    *shares, d_up = exchange(
+        shares + [d_up.reshape(team, weight_rows, ff_cols)], (attn_bits,) * (heads // 2) + (ffn_bits,)
+    )
     d_query, d_key, d_value, d_gate, d_up, d_norm_attn, d_norm_ffn = home(
-        shares + [d_gate, d_up.reshape(team, weight_rows, ff_cols)],
-        (attn_bits,) * (heads // 2) + (None, ffn_bits),
-        (w_query, w_key, w_value, w_gate, w_up), (norm_attn, norm_ffn), (0, 0, 0, 1, 1),
+        shares + [d_gate, d_up], (w_query, w_key, w_value, w_gate, w_up), (norm_attn, norm_ffn), (0, 0, 0, 1, 1),
         tuple(tuple(p) for p in places),
     )
-    d_norm_attn, d_norm_ffn = d_norm_attn[:, 0], d_norm_ffn[:, 0]
+    d_norm_attn, d_norm_ffn = d_norm_attn[0], d_norm_ffn[0]
     clip_value = clip_limit.astype(f32)
     factor = jnp.sqrt(clip_value / jnp.maximum(head_peak, clip_value))
     factors = jnp.repeat(factor, HEAD_DIM)[None, :]

time: 894 us -> 833 us (0.932)
  waiting for transfers between devices: 135 us -> 54.7 us
  Pallas kernels: 574 us -> 623 us
  matrix products: 101 us -> 82.2 us
    ppermute x9 -> x8, waiting for transfers between devices: 134 us -> 49.7 us  [flip(): return lax.ppermute(x, AXIS, [(i, i ^ bit) for i in range(devices)])]
    pallas_call x1, Pallas kernels: 136 us -> 156 us  [last_sums(): pl.pallas_call(functools.partial(last_sums_kernel, sum_bits, ffn_bits), o...]
    dot_general x8 -> x6, matrix products: 101 us -> 82.2 us  [contract(): lax.dot_general(left, right, (((left_dim,), (right_dim,)), ((), ())), pre...]
    pallas_call x2 -> x3, Pallas kernels: 110 us -> 129 us  [the longest x1 99.6 us: ffn_back(): pl.pallas_call(functools.partial(ffn_back_kernel, cross, sum_bits, swap_b...]
    pallas_call x2, Pallas kernels: 58.2 us -> 75.2 us  [attend_backward(): pl.pallas_call(functools.partial(attend_backward_kernel, 2 * pair), grid=...]
  transfers between devices with their start and end apart: 15 -> 14, of which waited for: 5 -> 5; matrix products, arithmetic and copies ran while one was open for 16% -> 13% of each run, Pallas kernels for 56% -> 60%
where the time goes in v4:
time: 833 us; the launch traced here: 826 us
  Pallas kernels  623 us (75%)
  matrix products  82.2 us (10%)
  waiting for transfers between devices  54.7 us (7%)
  local copies, waits for them, and re-layouts  24.3 us (3%)
  other arithmetic  18.1 us (2%)
  between operations  15.3 us (2%)
  starting transfers between devices  9.01 us (1%)
    pallas_call x1, Pallas kernels, last_sums(): pl.pallas_call(functools.partial(last_sums_kernel, sum_bits, ffn_bits), o...  156 us
    pallas_call x1, Pallas kernels, front(): pl.pallas_call(functools.partial(front_kernel, team, teams, qkv_moves, ff...  136 us
    pallas_call x1, Pallas kernels, ffn_back(): pl.pallas_call(functools.partial(ffn_back_kernel, cross, sum_bits, swap_b...  99.6 us
    pallas_call x1, Pallas kernels, branch(): pl.pallas_call(functools.partial(branch_kernel, bool(carry), swap_bits, s...  93.9 us
    dot_general x6, matrix products, contract(): lax.dot_general(left, right, (((left_dim,), (right_dim,)), ((), ())), pre...  82.2 us
    pallas_call x2, Pallas kernels, attend_backward(): pl.pallas_call(functools.partial(attend_backward_kernel, 2 * pair), grid=...  75.2 us
    ppermute x8, waiting for transfers between devices, flip(): return lax.ppermute(x, AXIS, [(i, i ^ bit) for i in range(devices)])  49.7 us
    pallas_call x1, Pallas kernels, attend_forward(): pl.pallas_call(attend_forward_kernel, out_shape=(shape((pairs, length, PA...  33.2 us
  transfers between devices with their start and end apart: 14, of which 5 were waited for; matrix products, arithmetic and copies ran while one was open for 13% of the time, Pallas kernels for 60%

profile of v4, /device:TPU:0, one launch (start us, length us, event | category | flops | bytes accessed | tf_op | source)
XLA Modules:
  0.0 826.2 jit_solution(7622508647049224528)
XLA Ops:
  10.1 135.6 %front.1 = (bf16[2048,2048]{1,0:T(8,128)(2,1)}, bf16[4,512,768]{2,1,0:T(8,128)(2,1)}, bf16[16,64,1024]{2,1,0:T(8,128)(2,1)}, f32[32,8,128]{2,1,0:T(8,128)}, bf16[256,2048]{1,0:T(8,128)(2,1)}) custom-call(bf16[256,2048]{1,0:T(8,128)(2,1)} %tokens_ref.3, bf16[64,2048]{1,0:T(8,128)(2,1)} %refs_4_.1, bf16[64,2048]{1,0:T(8,128)(2,1)} %refs_5_.1, ...), custom_call_target="tpu_custom_call" | custom-call | bytes 200000000 | tf_op jit(solution)/shard_map/front/pallas_call | solution.py:636
  145.8 11.8 %fusion.7.qkv_ref = f32[2048,768]{1,0:T(8,128)} fusion(bf16[2048,2048]{1,0:T(8,128)(2,1)} %get-tuple-element.76.normed_ref, bf16[2048,768]{1,0:T(8,128)(2,1)} %bitcast.83), kind=kOutput, calls=%fused_computation.42 | convolution fusion | flops 6442450944 | bytes 17825792 | tf_op jit(solution)/shard_map/dot_general | solution.py:30
  157.7 2.4 collective-permute-start
  160.0 1.4 slice.29
  162.1 1.3 copy.33.col_ref
  163.5 33.2 %attend_forward.1 = (bf16[2,2048,128]{2,1,0:T(8,128)(2,1)}, bf16[2,2048,128]{2,1,0:T(8,128)(2,1)}, bf16[2,2048,128]{2,1,0:T(8,128)(2,1)}, bf16[2048,256]{1,0:T(8...) custom-call(f32[2048,768]{1,0:T(8,128)} %fusion.7.qkv_ref, f32[2048,128]{1,0:T(8,128)} %constant.133.clone.cos_ref, ...), custom_call_target="tpu_custom_call" | custom-call | flops 17179869184 | bytes 12582912 | tf_op jit(solution)/shard_map/attend_forward/pallas_call | solution.py:120
  197.6 1.7 slice_reduce_fusion
  200.0 30.9 %collective-permute-done.1.refs_2_ = bf16[12,64,1024]{2,1,0:T(8,128)(2,1)} collective-permute-done((bf16[12,64,1024]{2,1,0:T(8,128)(2,1)}, bf16[12,64,1024]{2,1,0:T(8,128)(2,1)}, u32[]{:S(2)}, u32[]{:S(2)}) %collective-permute-start.1) | collective-permute-done | bytes 1572896 | tf_op jit(solution)/shard_map/ppermute | solution.py:1159
  231.4 93.9 %attention_branch.1 = (f32[256,2048]{1,0:T(8,128)}, bf16[2048,2048]{1,0:T(8,128)(2,1)}, f32[8,128]{1,0:T(8,128)}, bf16[32,64,1024]{2,1,0:T(8,128)(2,1)}, bf16[32...) custom-call(bf16[2048,256]{1,0:T(8,128)(2,1)} %get-tuple-element.86.left_ref, ...), custom_call_target="tpu_custom_call" | custom-call | flops 2147483648 | bytes 300000000 | tf_op jit(solution)/shard_map/attention_branch/pallas_call | solution.py:803
  325.4 2.5 constant_dynamic-slice_fusion
  327.8 0.9 collective-permute-start.2
  328.8 14.6 %fusion.8 = f32[2048,1024]{1,0:T(8,128)} fusion(bf16[2048,2048]{1,0:T(8,128)(2,1)} %get-tuple-element.90.normed_ref, bf16[2048,1024]{1,0:T(8,128)(2,1)} %bitcast.95), kind=kOutput, calls=%fused_computation.43 | convolution fusion | flops 8589934592 | bytes 20971520 | tf_op jit(solution)/shard_map/dot_general | solution.py:30
  343.4 13.7 %multiply_convert_fusion.2 = (bf16[2048,1024]{1,0:T(8,128)(2,1)}, f32[2048,1024]{1,0:T(8,128)}) fusion(f32[2048,1024]{1,0:T(8,128)} %fusion.8, bf16[2048,2048]{1,0:T(8,128)(2,1)S(1)} %bitcast.94, bf16[2048,1024]{1,0:T(8,128)(2,1)S(1)} %bitcast.98), kind=kOutput, calls=%fused_computation.2 | convolution fusion | flops 8602517504 | bytes 33554432 | tf_op jit(solution)/shard_map/dot_general | solution.py:30
  357.1 12.7 %convolution_convert_fusion = bf16[1024,2048]{1,0:T(8,128)(2,1)S(1)} fusion(bf16[2048,1024]{1,0:T(8,128)(2,1)} %get-tuple-element.148.hidden_ref, bf16[2048,2048]{1,0:T(8,128)(2,1)} %all-gather.4.cloned.1.call-done), kind=kOutput, calls=%fused_computation.10 | convolution fusion | flops 8592031744 | bytes 16777216 | tf_op jit(solution)/shard_map/dot_general | solution.py:30
  369.8 1.2 dynamic-slice_bitcast_fusion.1
  370.9 1.1 collective-permute-start.3
  372.1 1.7 copy-done.10
  374.0 21.7 %multiply_convert_fusion = (bf16[2048,1024]{1,0:T(8,128)(2,1)}, bf16[2048,1024]{1,0:T(8,128)(2,1)}) fusion(f32[2048,1024]{1,0:T(8,128)} %fusion.8, f32[2048,1024]{1,0:T(8,128)} %get-tuple-element.149, bf16[2048,2048]{1,0:T(8,128)(2,1)} %all-gather.4.cloned.1.call-done, bf16[1024,2048]{1,0:T(8,128)(2,1)S(1)} %bitcast.75), kind=kOutput, calls=%fused_computation | convolution fusion | flops 8617197568 | bytes 37748736 | tf_op jit(solution)/shard_map/dot_general | solution.py:30
  396.1 99.6 %ffn_back.1 = (f32[256,2048]{1,0:T(8,128)}, bf16[256,2048]{1,0:T(8,128)(2,1)}, bf16[2048,256]{1,0:T(8,128)(2,1)}, bf16[2048,1024]{1,0:T(8,128)(2,1)}, bf16[4,256...) custom-call(bf16[2048,1024]{1,0:T(8,128)(2,1)} %get-tuple-element.96.gate_ref, ...), custom_call_target="tpu_custom_call" | custom-call | flops 51539607552 | bytes 200000000 | tf_op jit(solution)/shard_map/ffn_back/pallas_call | solution.py:972
  495.8 3.4 add_convert_fusion
  499.5 0.8 fusion.2
  500.5 3.1 collective-permute-start.4
  503.5 37.8 %attend_backward.2 = (bf16[2048,384]{1,0:T(8,128)(2,1)}, bf16[2048,384]{1,0:T(8,128)(2,1)}) custom-call(bf16[2,2048,128]{2,1,0:T(8,128)(2,1)} %get-tuple-element.82.q_ref, bf16[2,2048,128]{2,1,0:T(8,128)(2,1)} %get-tuple-element.83.k_ref, bf16[2,2048,128]{2,1,0:T(8,128)(2,1)} %get-tuple-element.84.v_ref, bf16[2048,256]{1,0:T(8,128)(2,1)} %get-tuple-element.110.grad_ref, ...), custom_call_target="tpu_custom_call" | custom-call | flops 24696061952 | bytes 100000000 | tf_op jit(solution)/shard_map/attend_backward/pallas_call | solution.py:191
  541.3 8.3 %collective-permute-done.4 = bf16[2,2,2,64,1024]{4,3,2,1,0:T(8,128)(2,1)S(1)} collective-permute-done((bf16[2,2,2,64,1024]{4,3,2,1,0:T(8,128)(2,1)S(1)}, bf16[2,2,2,64,1024]{4,3,2,1,0:T(8,128)(2,1)S(1)}, u32[]{:S(2)}, u32[]{:S(2)}) %collective-permute-start.4) | collective-permute-done | bytes 1048608 | tf_op jit(solution)/shard_map/ppermute | solution.py:1159
  549.7 1.4 fusion.5
  551.1 1.8 dynamic-slice_bitcast_fusion
  552.9 1.3 collective-permute-start.6
  554.2 1.0 dynamic-slice_bitcast_fusion.4
  555.2 37.5 %attend_backward.3 = (bf16[2048,384]{1,0:T(8,128)(2,1)}, bf16[2048,384]{1,0:T(8,128)(2,1)}) custom-call(bf16[2,2048,128]{2,1,0:T(8,128)(2,1)} %get-tuple-element.82.q_ref, bf16[2,2048,128]{2,1,0:T(8,128)(2,1)} %get-tuple-element.83.k_ref, bf16[2,2048,128]{2,1,0:T(8,128)(2,1)} %get-tuple-element.84.v_ref, bf16[2048,256]{1,0:T(8,128)(2,1)} %get-tuple-element.110.grad_ref, ...), custom_call_target="tpu_custom_call" | custom-call | flops 24696061952 | bytes 100000000 | tf_op jit(solution)/shard_map/attend_backward/pallas_call | solution.py:191
  592.7 10.1 %collective-permute-done.5 = bf16[256,2048]{1,0:T(8,128)(2,1)S(1)} collective-permute-done((bf16[256,2048]{1,0:T(8,128)(2,1)}, bf16[256,2048]{1,0:T(8,128)(2,1)S(1)}, u32[]{:S(2)}, u32[]{:S(2)}) %collective-permute-start.5) | collective-permute-done | bytes 1048608 | tf_op jit(solution)/shard_map/ppermute | solution.py:1159
  602.8 1.7 fusion.6
  604.5 1.0 fusion.1
  605.5 7.8 convolution_convert_fusion.1
  614.5 1.1 dynamic-slice_bitcast_fusion.3
  617.1 1.2 divide_sqrt_fusion
  618.4 0.9 multiply_convert_fusion.3
  619.3 155.8 %last_sums.1 = (f32[256,2048]{1,0:T(8,128)}, bf16[256,2048]{1,0:T(8,128)(2,1)}, bf16[8,64,1024]{2,1,0:T(8,128)(2,1)}) custom-call(bf16[2048,384]{1,0:T(8,128)(2,1)} %get-tuple-element.105.left_ref, bf16[2048,384]{1,0:T(8,128)(2,1)} %get-tuple-element.116.other_ref, bf16[2048,768]{1,0:T(8,128)(2,1)} %bitcast.84, bf16[256,2048]{1,0:T(8,128)(2,1)} %tokens_ref.3, ...), custom_call_target="tpu_custom_call" | custom-call | flops 805306368 | bytes 300000000 | tf_op jit(solution)/shard_map/last_sums/pallas_call | solution.py:1043
  775.2 3.1 fusion.3
  778.3 1.8 convert_element_type.157
  780.1 3.2 reduce-scatter.6.cloned.1.call-done
  783.3 25.9 %exchange.1 = (bf16[8,64,384]{2,1,0:T(8,128)(2,1)}, bf16[8,64,384]{2,1,0:T(8,128)(2,1)}, bf16[8,64,1024]{2,1,0:T(8,128)(2,1)}) custom-call(bf16[8,64,384]{2,1,0:T(8,128)(2,1)} %bitcast.87, bf16[8,64,384]{2,1,0:T(8,128)(2,1)} %bitcast.88, bf16[8,64,1024]{2,1,0:T(8,128)(2,1)} %bitcast.82), custom_call_target="tpu_custom_call" | custom-call | flops 1000000 | bytes 40000000 | tf_op jit(solution)/shard_map/exchange/pallas_call | solution.py:1088
  809.2 1.2 copy-done.5
  810.4 1.2 copy-done.6
  811.7 1.0 copy-done.7
  812.7 1.0 copy-done.8
  813.7 3.2 home.1
  816.9 1.0 copy.47
  817.9 1.3 copy.48
  (95 shorter events, 9.2 us)
Async XLA Ops:
  7.2 223.7 %all-gather.6.cloned.1.call-start = ((), (), s32[]{:S(2)}) async-start(), calls=%async_computation.4 | async-start | bytes 8650752 | tf_op jit(solution)/shard_map/all_gather | solution.py:1222
  7.9 349.1 %all-gather.4.cloned.1.call-start = ((), (), s32[]{:S(2)}) async-start(), calls=%async_computation.3 | async-start | bytes 9437184 | tf_op jit(solution)/shard_map/all_gather | solution.py:1278
  145.8 11.9 %copy-start.12 = (bf16[16,64,1024]{2,1,0:T(8,128)(2,1)S(1)}, bf16[16,64,1024]{2,1,0:T(8,128)(2,1)}, u32[]{:S(2)}) copy-start(bf16[16,64,1024]{2,1,0:T(8,128)(2,1)} %get-tuple-element.88.refs_0_) | copy-start | bytes 6291460
  157.6 447.9 %all-gather.8.cloned.1.call-start = ((), (), s32[]{:S(2)}) async-start(), calls=%async_computation.5 | async-start | bytes 9437184 | tf_op jit(solution)/shard_map/all_gather | solution.py:1310
  157.7 73.2 %collective-permute-start = (bf16[16,64,1024]{2,1,0:T(8,128)(2,1)S(1)}, bf16[16,64,1024]{2,1,0:T(8,128)(2,1)}, u32[]{:S(2)}, u32[]{:S(2)}) collective-permute-start(bf16[16,64,1024]{2,1,0:T(8,128)(2,1)S(1)} %copy-done.12), channel_id=1, source_target_pairs={{0,4},{1,5},{2,6},{3,7},{4,0},{5,1},{6,2},{7,3},{8,12},{9,13},{10,... | collective-permute-start | bytes 6291464 | tf_op jit(solution)/shard_map/ppermute | solution.py:1159
  161.4 69.5 %collective-permute-start.1 = (bf16[12,64,1024]{2,1,0:T(8,128)(2,1)}, bf16[12,64,1024]{2,1,0:T(8,128)(2,1)}, u32[]{:S(2)}, u32[]{:S(2)}) collective-permute-start(bf16[12,64,1024]{2,1,0:T(8,128)(2,1)} %slice.29), channel_id=1, source_target_pairs={{0,16},{1,17},{2,18},{3,19},{4,20},{5,21},{6,22},{7,23},{8,24},{9,... | collective-permute-start | bytes 4718600 | tf_op jit(solution)/shard_map/ppermute | solution.py:1159
  162.1 1.4 copy-start.20
  325.4 18.0 %slice-start = ((s8[8388608]{0:T(1024)(128)(4,1)}), s8[4194304]{0:T(1024)(128)(4,1)S(1)}, s32[]{:S(2)}) async-start(s8[8388608]{0:T(1024)(128)(4,1)} %bitcast.93), calls=%async_computation.9 | async-start | bytes 8388608
  327.8 44.2 %collective-permute-start.2 = (bf16[1,256,2048]{2,1,0:T(8,128)(2,1)}, bf16[1,256,2048]{2,1,0:T(8,128)(2,1)S(1)}, u32[]{:S(2)}, u32[]{:S(2)}) collective-permute-start(bf16[1,256,2048]{2,1,0:T(8,128)(2,1)} %constant_dynamic-slice_fusion), channel_id=1, source_target_pairs={{0,4},{1,5},{2,6},{3,7},{4,0},{5,1},{6,2},{7,3},{8,12},{9,13},{10,... | collective-permute-start | bytes 3145736 | tf_op jit(solution)/shard_map/ppermute | solution.py:1159
  328.8 14.6 %slice-start.1 = ((s8[8388608]{0:T(1024)(128)(4,1)}), s8[4194304]{0:T(1024)(128)(4,1)S(1)}, s32[]{:S(2)}) async-start(s8[8388608]{0:T(1024)(128)(4,1)} %bitcast.93), calls=%async_computation.10 | async-start | bytes 8388608
  328.8 14.6 %copy-start.21 = (bf16[32,64,1024]{2,1,0:T(8,128)(2,1)S(1)}, bf16[32,64,1024]{2,1,0:T(8,128)(2,1)}, u32[]{:S(2)}) copy-start(bf16[32,64,1024]{2,1,0:T(8,128)(2,1)} %get-tuple-element.92) | copy-start | bytes 12582916
  369.7 4.2 copy-start.13
  369.8 4.1 copy-start.10
  370.9 25.1 %collective-permute-start.3 = (bf16[256,2048]{1,0:T(8,128)(2,1)S(1)}, bf16[256,2048]{1,0:T(8,128)(2,1)S(1)}, u32[]{:S(2)}, u32[]{:S(2)}) collective-permute-start(bf16[256,2048]{1,0:T(8,128)(2,1)S(1)} %get-tuple-element.145), channel_id=1, source_target_pairs={{0,4},{1,5},{2,6},{3,7},{4,0},{5,1},{6,2},{7,3},{8,12},{9,13},{10,... | collective-permute-start | bytes 3145736 | tf_op jit(solution)/shard_map/ppermute | solution.py:1159
  373.9 21.7 %copy-start.11 = (bf16[4,256,2048]{2,1,0:T(8,128)(2,1)}, bf16[4,256,2048]{2,1,0:T(8,128)(2,1)S(1)}, u32[]{:S(2)}) copy-start(bf16[4,256,2048]{2,1,0:T(8,128)(2,1)S(1)} %constant_dynamic-update-slice_fusion) | copy-start | bytes 12582916
  495.7 282.6 %reduce-scatter.8.cloned.1.call-start = ((), (), s32[]{:S(2)}) async-start(), calls=%async_computation.8 | async-start | bytes 1310720 | tf_op jit(solution)/shard_map/reduce_scatter | solution.py:1165
  495.8 3.5 copy-start.14
  495.8 3.7 copy-start.17
  500.5 49.2 %collective-permute-start.4 = (bf16[2,2,2,64,1024]{4,3,2,1,0:T(8,128)(2,1)S(1)}, bf16[2,2,2,64,1024]{4,3,2,1,0:T(8,128)(2,1)S(1)}, u32[]{:S(2)}, u32[]{:S(2)}) collective-permute-start(bf16[2,2,2,64,1024]{4,3,2,1,0:T(8,128)(2,1)S(1)} %dynamic-slice_bitcast_fusion.5), channel_id=1, source_target_pairs={{0,16},{1,17},{2,18},{3,19},{4,20},{5,21},{6,22},{7,23},{8,24},{9,... | collective-permute-start | bytes 3145736 | tf_op jit(solution)/shard_map/ppermute | solution.py:1159
  552.9 51.6 %collective-permute-start.6 = (bf16[2,2,2,2,64,1024]{5,4,3,2,1,0:T(8,128)(2,1)S(1)}, bf16[2,2,2,2,64,1024]{5,4,3,2,1,0:T(8,128)(2,1)S(1)}, u32[]{:S(2)}, u32[]{:S(2)}) collective-permute-start(bf16[2,2,2,2,64,1024]{5,4,3,2,1,0:T(8,128)(2,1)S(1)} %dynamic-slice_bitcast_fusion), channel_id=1, source_target_pairs={{0,4},{1,5},{2,6},{3,7},{4,0},{5,1},{6,2},{7,3},{8,12},{9,13},{10,... | collective-permute-start | bytes 6291464 | tf_op jit(solution)/shard_map/ppermute | solution.py:1159
  555.2 47.6 %collective-permute-start.5 = (bf16[256,2048]{1,0:T(8,128)(2,1)}, bf16[256,2048]{1,0:T(8,128)(2,1)S(1)}, u32[]{:S(2)}, u32[]{:S(2)}) collective-permute-start(bf16[256,2048]{1,0:T(8,128)(2,1)} %dynamic-slice_bitcast_fusion.4), channel_id=1, source_target_pairs={{0,16},{1,17},{2,18},{3,19},{4,20},{5,21},{6,22},{7,23},{8,24},{9,... | collective-permute-start | bytes 3145736 | tf_op jit(solution)/shard_map/ppermute | solution.py:1159
  592.7 11.8 %copy-start.15 = (bf16[2048,1024]{1,0:T(8,128)(2,1)S(1)}, bf16[2048,1024]{1,0:T(8,128)(2,1)}, u32[]{:S(2)}) copy-start(bf16[2048,1024]{1,0:T(8,128)(2,1)} %get-tuple-element.114) | copy-start | bytes 12582916
  605.4 9.0 %copy-start.9 = (bf16[2,2,2,2,64,1024]{5,4,3,2,1,0:T(8,128)(2,1)}, bf16[2,2,2,2,64,1024]{5,4,3,2,1,0:T(8,128)(2,1)S(1)}, u32[]{:S(2)}) copy-start(bf16[2,2,2,2,64,1024]{5,4,3,2,1,0:T(8,128)(2,1)S(1)} %fusion.1) | copy-start | bytes 6291460
  613.2 2.3 copy-start.22
  613.2 2.3 copy-start.19
  613.2 3.1 copy-start.23
  613.2 5.2 copy-start.2
  613.2 5.2 copy-start.3
  613.3 166.8 %reduce-scatter.4.cloned.1.call-start = ((), (), s32[]{:S(2)}) async-start(), calls=%async_computation.6 | async-start | bytes 1966080 | tf_op jit(solution)/shard_map/reduce_scatter | solution.py:1165
  613.9 169.4 %reduce-scatter.6.cloned.1.call-start = ((), (), s32[]{:S(2)}) async-start(), calls=%async_computation.7 | async-start | bytes 1966080 | tf_op jit(solution)/shard_map/reduce_scatter | solution.py:1165
  615.5 159.6 %collective-permute-start.7 = (bf16[2,2,2,64,1024]{4,3,2,1,0:T(8,128)(2,1)}, bf16[2,2,2,64,1024]{4,3,2,1,0:T(8,128)(2,1)}, u32[]{:S(2)}, u32[]{:S(2)}) collective-permute-start(bf16[2,2,2,64,1024]{4,3,2,1,0:T(8,128)(2,1)} %dynamic-slice_bitcast_fusion.3), channel_id=1, source_target_pairs={{0,16},{1,17},{2,18},{3,19},{4,20},{5,21},{6,22},{7,23},{8,24},{9,... | collective-permute-start | bytes 3145736 | tf_op jit(solution)/shard_map/ppermute | solution.py:1159
  775.1 34.1 %copy-start = (bf16[64,8192]{1,0:T(8,128)(2,1)S(1)}, bf16[64,8192]{1,0:T(8,128)(2,1)}, u32[]{:S(2)}) copy-start(bf16[64,8192]{1,0:T(8,128)(2,1)} %refs_7_.1) | copy-start | bytes 3145732
  775.1 34.1 %copy-start.1 = (bf16[64,8192]{1,0:T(8,128)(2,1)S(1)}, bf16[64,8192]{1,0:T(8,128)(2,1)}, u32[]{:S(2)}) copy-start(bf16[64,8192]{1,0:T(8,128)(2,1)} %refs_8_.1) | copy-start | bytes 3145732
  775.1 34.1 %copy-start.4 = (bf16[64,2048]{1,0:T(8,128)(2,1)S(1)}, bf16[64,2048]{1,0:T(8,128)(2,1)}, u32[]{:S(2)}) copy-start(bf16[64,2048]{1,0:T(8,128)(2,1)} %refs_6_.1) | copy-start | bytes 786436
  809.2 1.2 copy-start.5
  810.4 1.2 copy-start.6
  811.7 1.0 copy-start.7
  812.7 1.0 copy-start.8
  813.7 3.2 copy-start.18
  813.7 4.2 copy-start.16
Sparse Core Ops, SparseCore 0:
  10.9 117.1 all-gather.5
  157.7 79.6 all-gather.3
  495.8 54.1 all-gather.7
  613.4 68.3 reduce-scatter.7
  684.6 54.6 reduce-scatter.3
  741.6 41.6 reduce-scatter.5

commit v5 on v4

--- a/solution.py
+++ b/solution.py
@@ -733,7 +733,6 @@
         up_yz = [
             carried.copy(4 + half, placed(half, (1, 0)), placed(half, (1, 0)), by_y) for half in range(early, 4)
         ]
-        down_z = carried.copy(8, down_own, down_full.at[unit(0, 0)], by_z)
         for copy in up_z + kept:
             copy.start()
 
@@ -767,7 +766,6 @@
         for over, on in zip(up_z, up_yz):
             over.wait_recv()
             on.start()
-        down_z.start()
     for k, phase in enumerate(spread[1:-1]):
         phase()
         if k < len(bits):
@@ -780,9 +778,9 @@
     if carry:
         for copy in kept:
             copy.wait()
-        for copy in early_yz + up_yz + [down_z]:
+        for copy in early_yz + up_yz:
             copy.wait_recv()
-        for copy in up_z + early_yz + up_yz + [down_z]:
+        for copy in up_z + early_yz + up_yz:
             copy.wait_send()
 
 
@@ -799,7 +797,7 @@
             shape((32,) + carry[0].shape[1:], bf16), shape((32,) + carry[0].shape[1:], bf16),
             shape((4,) + carry[3].shape, bf16),
         ]
-        scratch += [dma((9,)), dma((9,)), dma((14,))]
+        scratch += [dma((8,)), dma((8,)), dma((14,))]
     return pl.pallas_call(
         functools.partial(branch_kernel, bool(carry), swap_bits, spread_bits),
         out_shape=tuple(out_shape),
@@ -1019,7 +1017,7 @@
         return contract(hidden_ref[rows_of(place), :], down_ref[:, columns], 1, 0)
 
     first = sum_block(sum_bits, LAST_CUT, False, product, *scratch[: count - 2], Links(*scratch[count - 2 : count]))
-    second = sum_block(ffn_bits, LAST_CUT, False, ffn_product, *scratch[count:-2], Links(*scratch[-2:]))
+    second = sum_block(ffn_bits, LAST_CUT, True, ffn_product, *scratch[count:-2], Links(*scratch[-2:]))
     run(first[:2])
     run(second[:2])
     for copy in swap_copies + [keep]:
@@ -1253,16 +1251,21 @@
         (jnp.arange(head_total) % team) == mate, jnp.repeat(peak[0, :heads], team), -jnp.inf
     )
     peaks = jnp.broadcast_to(jnp.pad(peaks, (0, 128 - head_total))[None], (8, 128))
+    if carry:
+        carry[2], down_sent = tie(carry[2], w_down)
+        over = flip(down_sent, 16)
     after_attn, normed_ffn, peaks, *full = branch(
         attended, out_w, tokens, gain_ffn, peaks, carry, attn_bits, ffn_bits, bit_count
     )
     head_peak = peaks[0, :head_total]
+    if carry:
+        normed_ffn, over = tie(normed_ffn, over)
     if carry:
         gate_w, up_w = (w.reshape(width, ff_cols) for w in full[:2])
         z_side, y_side = (device // 16) % 2, (device // 4) % 2
-        passed = lax.dynamic_index_in_dim(full[2], (1 - z_side) * 2 + y_side, 0, True)
+        full_down = lax.dynamic_update_slice(full[2], over[None], ((1 - z_side) * 2 + y_side, 0, 0))
         down_w = lax.dynamic_update_slice(
-            full[2], flip(passed, 4), ((1 - z_side) * 2 + 1 - y_side, 0, 0)
+            full_down, flip(over, 4)[None], ((1 - z_side) * 2 + 1 - y_side, 0, 0)
         ).reshape(ff_cols, width)
     else:
         gate_w, up_w = whole_rows(both_mine[:team]), whole_rows(both_mine[team:])
@@ -1316,7 +1319,9 @@
 
     grad_pairs, shares = [None] * (heads // 2), [None] * (heads // 2)
     grad_pairs[0], share = heads_back(0)
-    grad_attended, d_down, d_gate, d_up, share = tie(grad_attended, d_down, d_gate, d_up, share)
+    grad_attended, d_down, d_gate, d_up, share, branch_grad = tie(
+        grad_attended, d_down, d_gate, d_up, share, branch_grad
+    )
     shares[0] = scatter_across(share)
     d_down = data_sum(d_down, unit_rest, data_bits[1:]).astype(f32)
     d_up = data_sum(d_up.reshape(row_shape + row_values), row_dims, data_bits[:1])
@@ -1325,6 +1330,7 @@
         grad_pairs[p], share, d_down, d_up, branch_grad = tie(grad_pairs[p], share, d_down, d_up, branch_grad)
         shares[p] = scatter_across(share)
     d_up = data_sum(d_up, row_rest, data_bits[1:])
+    grad_pairs[0], shares[0] = tie(grad_pairs[0], shares[0])
     d_gate = d_gate.reshape(team, weight_rows, ff_cols)
     out_part = contract(attended, branch_grad, 0, 0)
     if weight_rows == HEAD_DIM:

time: 833 us -> 842 us (1.011)
  waiting for transfers between devices: 54.7 us -> 110 us
  Pallas kernels: 623 us -> 574 us
    ppermute x8 -> x9, waiting for transfers between devices: 49.7 us -> 109 us  [flip(): return lax.ppermute(x, AXIS, [(i, i ^ bit) for i in range(devices)])]
    pallas_call x1, Pallas kernels: 156 us -> 123 us  [last_sums(): pl.pallas_call(functools.partial(last_sums_kernel, sum_bits, ffn_bits), o...]
    pallas_call x1, Pallas kernels: 93.9 us -> 79 us  [branch(): pl.pallas_call(functools.partial(branch_kernel, bool(carry), swap_bits, s...]
  transfers between devices with their start and end apart: 14 -> 15, of which waited for: 5 -> 3; matrix products, arithmetic and copies ran while one was open for 13% -> 14% of each run, Pallas kernels for 60% -> 53%
where the time goes in v5:
time: 842 us; the launch traced here: 836 us
  Pallas kernels  574 us (68%)
  waiting for transfers between devices  110 us (13%)
  matrix products  82.3 us (10%)
  local copies, waits for them, and re-layouts  24.1 us (3%)
  other arithmetic  19.7 us (2%)
  between operations  15.3 us (2%)
  starting transfers between devices  9.66 us (1%)
    pallas_call x1, Pallas kernels, front(): pl.pallas_call(functools.partial(front_kernel, team, teams, qkv_moves, ff...  136 us
    pallas_call x1, Pallas kernels, last_sums(): pl.pallas_call(functools.partial(last_sums_kernel, sum_bits, ffn_bits), o...  123 us
    ppermute x9, waiting for transfers between devices, flip(): return lax.ppermute(x, AXIS, [(i, i ^ bit) for i in range(devices)])  109 us
    pallas_call x1, Pallas kernels, ffn_back(): pl.pallas_call(functools.partial(ffn_back_kernel, cross, sum_bits, swap_b...  100 us
    dot_general x6, matrix products, contract(): lax.dot_general(left, right, (((left_dim,), (right_dim,)), ((), ())), pre...  82.3 us
    pallas_call x1, Pallas kernels, branch(): pl.pallas_call(functools.partial(branch_kernel, bool(carry), swap_bits, s...  79 us
    pallas_call x2, Pallas kernels, attend_backward(): pl.pallas_call(functools.partial(attend_backward_kernel, 2 * pair), grid=...  75.4 us
    pallas_call x1, Pallas kernels, attend_forward(): pl.pallas_call(attend_forward_kernel, out_shape=(shape((pairs, length, PA...  32.1 us
  transfers between devices with their start and end apart: 15, of which 3 were waited for; matrix products, arithmetic and copies ran while one was open for 14% of the time, Pallas kernels for 53%

profile of v5, /device:TPU:0, one launch (start us, length us, event | category | flops | bytes accessed | tf_op | source)
XLA Modules:
  0.0 835.5 jit_solution(4520563499104016040)
XLA Ops:
  10.1 135.6 %front.1 = (bf16[2048,2048]{1,0:T(8,128)(2,1)}, bf16[4,512,768]{2,1,0:T(8,128)(2,1)}, bf16[16,64,1024]{2,1,0:T(8,128)(2,1)}, f32[32,8,128]{2,1,0:T(8,128)}, bf16[256,2048]{1,0:T(8,128)(2,1)}) custom-call(bf16[256,2048]{1,0:T(8,128)(2,1)} %tokens_ref.3, bf16[64,2048]{1,0:T(8,128)(2,1)} %refs_4_.1, bf16[64,2048]{1,0:T(8,128)(2,1)} %refs_5_.1, ...), custom_call_target="tpu_custom_call" | custom-call | bytes 200000000 | tf_op jit(solution)/shard_map/front/pallas_call | solution.py:636
  145.8 11.8 %fusion.7.qkv_ref = f32[2048,768]{1,0:T(8,128)} fusion(bf16[2048,2048]{1,0:T(8,128)(2,1)} %get-tuple-element.83.normed_ref, bf16[2048,768]{1,0:T(8,128)(2,1)} %bitcast.87), kind=kOutput, calls=%fused_computation.42 | convolution fusion | flops 6442450944 | bytes 17825792 | tf_op jit(solution)/shard_map/dot_general | solution.py:30
  157.7 1.4 slice.29
  159.3 2.0 collective-permute-start
  161.3 0.8 dynamic-slice_convert_fusion
  162.1 1.3 copy.33.col_ref
  163.4 65.8 %collective-permute-done.1.refs_2_ = bf16[12,64,1024]{2,1,0:T(8,128)(2,1)} collective-permute-done((bf16[12,64,1024]{2,1,0:T(8,128)(2,1)}, bf16[12,64,1024]{2,1,0:T(8,128)(2,1)}, u32[]{:S(2)}, u32[]{:S(2)}) %collective-permute-start.1) | collective-permute-done | bytes 1572896 | tf_op jit(solution)/shard_map/ppermute | solution.py:1157
  229.2 32.1 %attend_forward.1 = (bf16[2,2048,128]{2,1,0:T(8,128)(2,1)}, bf16[2,2048,128]{2,1,0:T(8,128)(2,1)}, bf16[2,2048,128]{2,1,0:T(8,128)(2,1)}, bf16[2048,256]{1,0:T(8...) custom-call(f32[2048,768]{1,0:T(8,128)} %fusion.7.qkv_ref, f32[2048,128]{1,0:T(8,128)} %constant.129.clone.cos_ref, ...), custom_call_target="tpu_custom_call" | custom-call | flops 17179869184 | bytes 12582912 | tf_op jit(solution)/shard_map/attend_forward/pallas_call | solution.py:120
  262.1 1.7 slice_reduce_fusion
  265.1 79.0 %attention_branch.1 = (f32[256,2048]{1,0:T(8,128)}, bf16[2048,2048]{1,0:T(8,128)(2,1)}, f32[8,128]{1,0:T(8,128)}, bf16[32,64,1024]{2,1,0:T(8,128)(2,1)}, bf16[32...) custom-call(bf16[2048,256]{1,0:T(8,128)(2,1)} %get-tuple-element.93.left_ref, ...), custom_call_target="tpu_custom_call" | custom-call | flops 2147483648 | bytes 300000000 | tf_op jit(solution)/shard_map/attention_branch/pallas_call | solution.py:801
  344.8 14.6 %fusion.8 = f32[2048,1024]{1,0:T(8,128)} fusion(bf16[2048,2048]{1,0:T(8,128)(2,1)} %get-tuple-element.100.normed_ref, bf16[2048,1024]{1,0:T(8,128)(2,1)} %bitcast.97), kind=kOutput, calls=%fused_computation.43 | convolution fusion | flops 8589934592 | bytes 20971520 | tf_op jit(solution)/shard_map/dot_general | solution.py:30
  359.4 13.7 %multiply_convert_fusion.2 = (bf16[2048,1024]{1,0:T(8,128)(2,1)}, f32[2048,1024]{1,0:T(8,128)}) fusion(f32[2048,1024]{1,0:T(8,128)} %fusion.8, bf16[2048,2048]{1,0:T(8,128)(2,1)S(1)} %copy-done.22, bf16[2048,1024]{1,0:T(8,128)(2,1)S(1)} %bitcast.100), kind=kOutput, calls=%fused_computation.2 | convolution fusion | flops 8602517504 | bytes 33554432 | tf_op jit(solution)/shard_map/dot_general | solution.py:30
  373.1 12.7 %convolution_convert_fusion = bf16[1024,2048]{1,0:T(8,128)(2,1)S(1)} fusion(bf16[2048,1024]{1,0:T(8,128)(2,1)} %get-tuple-element.162.hidden_ref, bf16[2048,2048]{1,0:T(8,128)(2,1)} %all-gather.4.cloned.1.call-done), kind=kOutput, calls=%fused_computation.10 | convolution fusion | flops 8592031744 | bytes 16777216 | tf_op jit(solution)/shard_map/dot_general | solution.py:30
  385.8 1.2 dynamic-slice_bitcast_fusion.1
  386.9 1.5 collective-permute-start.4
  388.4 1.4 copy-done.11
  389.8 1.3 bitcast_dynamic-update-slice_fusion.1
  391.3 21.7 %multiply_convert_fusion = (bf16[2048,1024]{1,0:T(8,128)(2,1)}, bf16[2048,1024]{1,0:T(8,128)(2,1)}) fusion(f32[2048,1024]{1,0:T(8,128)} %fusion.8, f32[2048,1024]{1,0:T(8,128)} %get-tuple-element.163, bf16[2048,2048]{1,0:T(8,128)(2,1)} %all-gather.4.cloned.1.call-done, bf16[1024,2048]{1,0:T(8,128)(2,1)S(1)} %bitcast.79), kind=kOutput, calls=%fused_computation | convolution fusion | flops 8617197568 | bytes 37748736 | tf_op jit(solution)/shard_map/dot_general | solution.py:30
  413.0 100.0 %ffn_back.1 = (f32[256,2048]{1,0:T(8,128)}, bf16[256,2048]{1,0:T(8,128)(2,1)}, bf16[2048,256]{1,0:T(8,128)(2,1)}, bf16[2048,1024]{1,0:T(8,128)(2,1)}, bf16[4,256...) custom-call(bf16[2048,1024]{1,0:T(8,128)(2,1)} %get-tuple-element.107.gate_ref, ...), custom_call_target="tpu_custom_call" | custom-call | flops 51539607552 | bytes 200000000 | tf_op jit(solution)/shard_map/ffn_back/pallas_call | solution.py:970
  513.1 3.4 add_convert_fusion
  516.9 0.8 fusion.2
  517.8 2.9 collective-permute-start.5
  520.7 37.9 %attend_backward.2 = (bf16[2048,384]{1,0:T(8,128)(2,1)}, bf16[2048,384]{1,0:T(8,128)(2,1)}) custom-call(bf16[2,2048,128]{2,1,0:T(8,128)(2,1)} %get-tuple-element.89.q_ref, bf16[2,2048,128]{2,1,0:T(8,128)(2,1)} %get-tuple-element.90.k_ref, bf16[2,2048,128]{2,1,0:T(8,128)(2,1)} %get-tuple-element.91.v_ref, bf16[2048,256]{1,0:T(8,128)(2,1)} %get-tuple-element.124.grad_ref, ...), custom_call_target="tpu_custom_call" | custom-call | flops 24696061952 | bytes 100000000 | tf_op jit(solution)/shard_map/attend_backward/pallas_call | solution.py:191
  558.7 8.3 collective-permute-done.5
  567.0 1.4 fusion.5
  568.4 3.1 dynamic-slice_bitcast_fusion
  571.5 1.1 collective-permute-start.7
  572.6 1.0 dynamic-slice_bitcast_fusion.4
  573.6 1.0 collective-permute-start.6
  574.7 37.5 %attend_backward.3 = (bf16[2048,384]{1,0:T(8,128)(2,1)}, bf16[2048,384]{1,0:T(8,128)(2,1)}) custom-call(bf16[2,2048,128]{2,1,0:T(8,128)(2,1)} %get-tuple-element.89.q_ref, bf16[2,2048,128]{2,1,0:T(8,128)(2,1)} %get-tuple-element.90.k_ref, bf16[2,2048,128]{2,1,0:T(8,128)(2,1)} %get-tuple-element.91.v_ref, bf16[2048,256]{1,0:T(8,128)(2,1)} %get-tuple-element.124.grad_ref, ...), custom_call_target="tpu_custom_call" | custom-call | flops 24696061952 | bytes 100000000 | tf_op jit(solution)/shard_map/attend_backward/pallas_call | solution.py:191
  612.1 34.7 %collective-permute-done.6 = bf16[256,2048]{1,0:T(8,128)(2,1)S(1)} collective-permute-done((bf16[256,2048]{1,0:T(8,128)(2,1)}, bf16[256,2048]{1,0:T(8,128)(2,1)S(1)}, u32[]{:S(2)}, u32[]{:S(2)}) %collective-permute-start.6) | collective-permute-done | bytes 1048608 | tf_op jit(solution)/shard_map/ppermute | solution.py:1157
  646.8 1.7 fusion.6
  648.5 2.5 fusion.1
  651.1 7.8 convolution_convert_fusion.1
  659.5 1.1 dynamic-slice_bitcast_fusion.3
  662.2 1.2 divide_sqrt_fusion
  663.5 0.9 multiply_convert_fusion.3
  664.4 123.3 %last_sums.1 = (f32[256,2048]{1,0:T(8,128)}, bf16[256,2048]{1,0:T(8,128)(2,1)}, bf16[8,64,1024]{2,1,0:T(8,128)(2,1)}) custom-call(bf16[2048,384]{1,0:T(8,128)(2,1)} %get-tuple-element.123.left_ref, bf16[2048,384]{1,0:T(8,128)(2,1)} %get-tuple-element.130.other_ref, bf16[2048,768]{1,0:T(8,128)(2,1)} %bitcast.88, bf16[256,2048]{1,0:T(8,128)(2,1)} %tokens_ref.3, ...), custom_call_target="tpu_custom_call" | custom-call | flops 805306368 | bytes 300000000 | tf_op jit(solution)/shard_map/last_sums/pallas_call | solution.py:1041
  787.7 3.1 fusion.3
  790.8 1.8 convert_element_type.157
  792.6 25.8 %exchange.1 = (bf16[8,64,384]{2,1,0:T(8,128)(2,1)}, bf16[8,64,384]{2,1,0:T(8,128)(2,1)}, bf16[8,64,1024]{2,1,0:T(8,128)(2,1)}) custom-call(bf16[8,64,384]{2,1,0:T(8,128)(2,1)} %bitcast.91, bf16[8,64,384]{2,1,0:T(8,128)(2,1)} %bitcast.92, bf16[8,64,1024]{2,1,0:T(8,128)(2,1)} %bitcast.86), custom_call_target="tpu_custom_call" | custom-call | flops 1000000 | bytes 40000000 | tf_op jit(solution)/shard_map/exchange/pallas_call | solution.py:1086
  818.5 1.2 copy-done.5
  819.7 1.2 copy-done.6
  821.0 1.0 copy-done.7
  822.0 1.0 copy-done.8
  822.9 3.2 home.1
  826.2 1.0 copy.48
  827.1 1.3 copy.49
  (96 shorter events, 8.5 us)
Async XLA Ops:
  7.2 257.4 %all-gather.6.cloned.1.call-start = ((), (), s32[]{:S(2)}) async-start(), calls=%async_computation.4 | async-start | bytes 8650752 | tf_op jit(solution)/shard_map/all_gather | solution.py:1220
  7.9 365.2 %all-gather.4.cloned.1.call-start = ((), (), s32[]{:S(2)}) async-start(), calls=%async_computation.3 | async-start | bytes 9437184 | tf_op jit(solution)/shard_map/all_gather | solution.py:1281
  145.7 11.9 %copy-start.10 = (bf16[16,64,1024]{2,1,0:T(8,128)(2,1)S(1)}, bf16[16,64,1024]{2,1,0:T(8,128)(2,1)}, u32[]{:S(2)}) copy-start(bf16[16,64,1024]{2,1,0:T(8,128)(2,1)} %get-tuple-element.95.refs_0_) | copy-start | bytes 6291460
  157.6 71.6 %copy-start.16 = (bf16[256,2048]{1,0:T(8,128)(2,1)S(1)}, bf16[256,2048]{1,0:T(8,128)(2,1)}, u32[]{:S(2)}) copy-start(bf16[256,2048]{1,0:T(8,128)(2,1)} %refs_3_.1) | copy-start | bytes 3145732
  157.6 410.8 %all-gather.8.cloned.1.call-start = ((), (), s32[]{:S(2)}) async-start(), calls=%async_computation.5 | async-start | bytes 9437184 | tf_op jit(solution)/shard_map/all_gather | solution.py:1313
  159.0 70.2 %collective-permute-start.1 = (bf16[12,64,1024]{2,1,0:T(8,128)(2,1)}, bf16[12,64,1024]{2,1,0:T(8,128)(2,1)}, u32[]{:S(2)}, u32[]{:S(2)}) collective-permute-start(bf16[12,64,1024]{2,1,0:T(8,128)(2,1)} %slice.29), channel_id=1, source_target_pairs={{0,16},{1,17},{2,18},{3,19},{4,20},{5,21},{6,22},{7,23},{8,24},{9,... | collective-permute-start | bytes 4718600 | tf_op jit(solution)/shard_map/ppermute | solution.py:1157
  159.3 105.2 %collective-permute-start = (bf16[16,64,1024]{2,1,0:T(8,128)(2,1)S(1)}, bf16[16,64,1024]{2,1,0:T(8,128)(2,1)}, u32[]{:S(2)}, u32[]{:S(2)}) collective-permute-start(bf16[16,64,1024]{2,1,0:T(8,128)(2,1)S(1)} %copy-done.10), channel_id=1, source_target_pairs={{0,4},{1,5},{2,6},{3,7},{4,0},{5,1},{6,2},{7,3},{8,12},{9,13},{10,... | collective-permute-start | bytes 6291464 | tf_op jit(solution)/shard_map/ppermute | solution.py:1157
  162.1 67.1 %copy-start.21 = (s32[8,2,128]{2,1,0:T(2,128)}, s32[8,2,128]{2,1,0:T(2,128)S(1)}, u32[]{:S(2)}) copy-start(s32[8,2,128]{2,1,0:T(2,128)S(1)} %dynamic-slice_convert_fusion) | copy-start | bytes 24580
  229.2 114.9 %collective-permute-start.2 = (bf16[256,2048]{1,0:T(8,128)(2,1)S(1)}, bf16[256,2048]{1,0:T(8,128)(2,1)}, u32[]{:S(2)}, u32[]{:S(2)}) collective-permute-start(bf16[256,2048]{1,0:T(8,128)(2,1)S(1)} %copy-done.16), channel_id=1, source_target_pairs={{0,16},{1,17},{2,18},{3,19},{4,20},{5,21},{6,22},{7,23},{8,24},{9,... | collective-permute-start | bytes 3145736 | tf_op jit(solution)/shard_map/ppermute | solution.py:1157
  344.2 47.0 %collective-permute-start.3 = (bf16[256,2048]{1,0:T(8,128)(2,1)}, bf16[256,2048]{1,0:T(8,128)(2,1)S(1)}, u32[]{:S(2)}, u32[]{:S(2)}) collective-permute-start(bf16[256,2048]{1,0:T(8,128)(2,1)} %collective-permute-done.2), channel_id=1, source_target_pairs={{0,4},{1,5},{2,6},{3,7},{4,0},{5,1},{6,2},{7,3},{8,12},{9,13},{10,... | collective-permute-start | bytes 3145736 | tf_op jit(solution)/shard_map/ppermute | solution.py:1157
  344.8 14.6 %copy-start.22 = (bf16[2048,2048]{1,0:T(8,128)(2,1)S(1)}, bf16[2048,2048]{1,0:T(8,128)(2,1)}, u32[]{:S(2)}) copy-start(bf16[2048,2048]{1,0:T(8,128)(2,1)} %get-tuple-element.100.normed_ref) | copy-start | bytes 25165828
  344.8 14.6 %copy-start.23 = (bf16[32,64,1024]{2,1,0:T(8,128)(2,1)S(1)}, bf16[32,64,1024]{2,1,0:T(8,128)(2,1)}, u32[]{:S(2)}) copy-start(bf16[32,64,1024]{2,1,0:T(8,128)(2,1)} %get-tuple-element.102) | copy-start | bytes 12582916
  385.8 5.5 copy-start.13
  385.8 4.1 copy-start.11
  386.9 26.1 %collective-permute-start.4 = (bf16[256,2048]{1,0:T(8,128)(2,1)S(1)}, bf16[256,2048]{1,0:T(8,128)(2,1)S(1)}, u32[]{:S(2)}, u32[]{:S(2)}) collective-permute-start(bf16[256,2048]{1,0:T(8,128)(2,1)S(1)} %get-tuple-element.159), channel_id=1, source_target_pairs={{0,4},{1,5},{2,6},{3,7},{4,0},{5,1},{6,2},{7,3},{8,12},{9,13},{10,... | collective-permute-start | bytes 3145736 | tf_op jit(solution)/shard_map/ppermute | solution.py:1157
  391.3 21.7 %copy-start.12 = (bf16[4,256,2048]{2,1,0:T(8,128)(2,1)}, bf16[4,256,2048]{2,1,0:T(8,128)(2,1)S(1)}, u32[]{:S(2)}) copy-start(bf16[4,256,2048]{2,1,0:T(8,128)(2,1)S(1)} %bitcast_dynamic-update-slice_fusion) | copy-start | bytes 12582916
  513.0 151.4 %reduce-scatter.4.cloned.1.call-start = ((), (), s32[]{:S(2)}) async-start(), calls=%async_computation.6 | async-start | bytes 1966080 | tf_op jit(solution)/shard_map/reduce_scatter | solution.py:1163
  513.1 3.5 copy-start.14
  513.1 3.7 copy-start.18
  517.8 49.2 %collective-permute-start.5 = (bf16[2,2,2,64,1024]{4,3,2,1,0:T(8,128)(2,1)S(1)}, bf16[2,2,2,64,1024]{4,3,2,1,0:T(8,128)(2,1)S(1)}, u32[]{:S(2)}, u32[]{:S(2)}) collective-permute-start(bf16[2,2,2,64,1024]{4,3,2,1,0:T(8,128)(2,1)S(1)} %dynamic-slice_bitcast_fusion.5), channel_id=1, source_target_pairs={{0,16},{1,17},{2,18},{3,19},{4,20},{5,21},{6,22},{7,23},{8,24},{9,... | collective-permute-start | bytes 3145736 | tf_op jit(solution)/shard_map/ppermute | solution.py:1157
  571.5 77.0 %collective-permute-start.7 = (bf16[2,2,2,2,64,1024]{5,4,3,2,1,0:T(8,128)(2,1)}, bf16[2,2,2,2,64,1024]{5,4,3,2,1,0:T(8,128)(2,1)}, u32[]{:S(2)}, u32[]{:S(2)}) collective-permute-start(bf16[2,2,2,2,64,1024]{5,4,3,2,1,0:T(8,128)(2,1)} %dynamic-slice_bitcast_fusion), channel_id=1, source_target_pairs={{0,4},{1,5},{2,6},{3,7},{4,0},{5,1},{6,2},{7,3},{8,12},{9,13},{10,... | collective-permute-start | bytes 6291464 | tf_op jit(solution)/shard_map/ppermute | solution.py:1157
  573.6 73.2 %collective-permute-start.6 = (bf16[256,2048]{1,0:T(8,128)(2,1)}, bf16[256,2048]{1,0:T(8,128)(2,1)S(1)}, u32[]{:S(2)}, u32[]{:S(2)}) collective-permute-start(bf16[256,2048]{1,0:T(8,128)(2,1)} %dynamic-slice_bitcast_fusion.4), channel_id=1, source_target_pairs={{0,16},{1,17},{2,18},{3,19},{4,20},{5,21},{6,22},{7,23},{8,24},{9,... | collective-permute-start | bytes 3145736 | tf_op jit(solution)/shard_map/ppermute | solution.py:1157
  574.6 216.2 %reduce-scatter.8.cloned.1.call-start = ((), (), s32[]{:S(2)}) async-start(), calls=%async_computation.8 | async-start | bytes 1310720 | tf_op jit(solution)/shard_map/reduce_scatter | solution.py:1163
  612.1 36.4 %copy-start.15 = (bf16[2048,1024]{1,0:T(8,128)(2,1)S(1)}, bf16[2048,1024]{1,0:T(8,128)(2,1)}, u32[]{:S(2)}) copy-start(bf16[2048,1024]{1,0:T(8,128)(2,1)} %get-tuple-element.128) | copy-start | bytes 12582916
  651.1 8.4 %copy-start.9 = (bf16[2,2,2,2,64,1024]{5,4,3,2,1,0:T(8,128)(2,1)}, bf16[2,2,2,2,64,1024]{5,4,3,2,1,0:T(8,128)(2,1)S(1)}, u32[]{:S(2)}) copy-start(bf16[2,2,2,2,64,1024]{5,4,3,2,1,0:T(8,128)(2,1)S(1)} %fusion.1) | copy-start | bytes 6291460
  658.9 1.7 copy-start.24
  658.9 1.7 copy-start.20
  658.9 2.5 copy-start.25
  658.9 4.6 copy-start.2
  658.9 4.6 copy-start.3
  658.9 133.7 %reduce-scatter.6.cloned.1.call-start = ((), (), s32[]{:S(2)}) async-start(), calls=%async_computation.7 | async-start | bytes 1966080 | tf_op jit(solution)/shard_map/reduce_scatter | solution.py:1163
  660.6 127.1 %collective-permute-start.8 = (bf16[2,2,2,64,1024]{4,3,2,1,0:T(8,128)(2,1)}, bf16[2,2,2,64,1024]{4,3,2,1,0:T(8,128)(2,1)}, u32[]{:S(2)}, u32[]{:S(2)}) collective-permute-start(bf16[2,2,2,64,1024]{4,3,2,1,0:T(8,128)(2,1)} %dynamic-slice_bitcast_fusion.3), channel_id=1, source_target_pairs={{0,16},{1,17},{2,18},{3,19},{4,20},{5,21},{6,22},{7,23},{8,24},{9,... | collective-permute-start | bytes 3145736 | tf_op jit(solution)/shard_map/ppermute | solution.py:1157
  787.7 30.8 %copy-start = (bf16[64,8192]{1,0:T(8,128)(2,1)S(1)}, bf16[64,8192]{1,0:T(8,128)(2,1)}, u32[]{:S(2)}) copy-start(bf16[64,8192]{1,0:T(8,128)(2,1)} %refs_7_.1) | copy-start | bytes 3145732
  787.7 30.8 %copy-start.1 = (bf16[64,8192]{1,0:T(8,128)(2,1)S(1)}, bf16[64,8192]{1,0:T(8,128)(2,1)}, u32[]{:S(2)}) copy-start(bf16[64,8192]{1,0:T(8,128)(2,1)} %refs_8_.1) | copy-start | bytes 3145732
  787.7 30.8 %copy-start.4 = (bf16[64,2048]{1,0:T(8,128)(2,1)S(1)}, bf16[64,2048]{1,0:T(8,128)(2,1)}, u32[]{:S(2)}) copy-start(bf16[64,2048]{1,0:T(8,128)(2,1)} %refs_6_.1) | copy-start | bytes 786436
  818.5 1.2 copy-start.5
  819.7 1.2 copy-start.6
  821.0 1.0 copy-start.7
  821.9 1.0 copy-start.8
  822.9 3.2 copy-start.19
  822.9 4.2 copy-start.17
Sparse Core Ops, SparseCore 0:
  10.9 117.1 all-gather.5
  157.7 79.3 all-gather.3
  513.2 53.6 all-gather.7
  574.7 58.9 reduce-scatter.3
  659.1 68.5 reduce-scatter.7
  729.9 45.3 reduce-scatter.5

commit v6 on v5

--- a/solution.py
+++ b/solution.py
@@ -820,9 +820,9 @@
 def ffn_back_kernel(
     cross, sum_bits, swap_bits, gate_ref, up_ref, gate_w_ref, up_w_ref, normed_ref, out_w_ref, h2_ref, cot_ref, gain_ref, *refs,
 ):
-    (part_ref, refs) = (refs[0], refs[1:]) if cross else (None, refs)
+    (part_ref, over_ref, refs) = (refs[0], refs[1], refs[2:]) if cross else (None, None, refs)
     (residual_ref, branch_ref, heads_out, d_up_out, d_gate_own), refs = refs[:5], refs[5:]
-    (d_gate_in, part_in, refs) = (refs[0], refs[1], refs[2:]) if cross else (None, None, refs)
+    (d_gate_in, part_in, over_in), refs = (refs[:3], refs[3:]) if cross else ((None,) * 3, refs)
     (total, to_core, from_core, chip_sum, arrived, sum_send, sum_recv,
      swap_send, swap_recv, local_sem, stage, stage_sems, own_sems, *more) = refs
     if cross:
@@ -836,6 +836,7 @@
     mates = [team_mate(me, swap_bits, k) for k in range(team)]
     greet(
         [device for device, _ in mates[1:]] + [flip_bit(me, bit) for bit in sum_bits if bit not in swap_bits]
+        + ([flip_bit(me, 16)] if cross else [])
     )
 
     def product(place, columns):
@@ -849,6 +850,7 @@
     y_side, by_y = bit_of(me, 4), flip_bit(me, 4)
     if cross:
         part_copy = crossing.copy(count // 2, part_ref, part_in, by_y)
+        over_copy = crossing.copy(count // 2 + 1, over_ref, over_in, flip_bit(me, 16))
         part_copy.start()
 
     def parked(i, part):
@@ -915,6 +917,8 @@
     hand_on()
     gradients(1, count - 2)
     finish()
+    if cross:
+        over_copy.start()
     residual = cot_ref[...].astype(f32) + norm_back(h2_ref[...], gain_ref[...], total[...])
     residual_ref[...] = residual
     branch_ref[...] = residual.astype(bf16)
@@ -948,6 +952,7 @@
             gate_copy(step).wait()
     if cross:
         part_copy.wait()
+        over_copy.wait()
 
         @pl.loop(0, count // 2)
         def _(i):
@@ -963,8 +968,8 @@
     side = side if cross else 256
     tiles = width // side // 2
     if cross:
-        d_gate = (shape((tiles, side, ff_cols), bf16),) * 2 + (shape(part[0].shape, bf16),)
-        more = [dma((tiles + 1,)), dma((tiles + 1,))]
+        d_gate = (shape((tiles, side, ff_cols), bf16),) * 2 + (shape(part[0].shape, bf16),) * 2
+        more = [dma((tiles + 2,)), dma((tiles + 2,))]
     else:
         d_gate, more = (shape((width, ff_cols), bf16),), [pltpu.VMEM((2, side, ff_cols), bf16)]
     return pl.pallas_call(
@@ -986,9 +991,14 @@
 
 
 def last_sums_kernel(
-    sum_bits, ffn_bits, left_ref, other_ref, right_ref, tokens_ref, gain_ref, residual_ref, hidden_ref, down_ref, h2_ref,
-    gate_ref, out_ref, mixed_ref, gate_out, *scratch,
+    carry_bits, sum_bits, ffn_bits, left_ref, other_ref, right_ref, tokens_ref, gain_ref, residual_ref, hidden_ref,
+    down_ref, h2_ref, gate_ref, *refs,
 ):
+    moved = len(carry_bits)
+    carried, (out_ref, mixed_ref, gate_out), refs = refs[:moved], refs[moved : moved + 3], refs[moved + 3 :]
+    carried_out, scratch = refs[:moved], refs[moved:]
+    if moved:
+        carry_sems, scratch = scratch[-2:], scratch[:-2]
     (swap_send, swap_recv, swap_local), scratch = scratch[-3:], scratch[:-3]
     count = len(scratch) // 2
     me = lax.axis_index(AXIS)
@@ -996,7 +1006,12 @@
     block = total.shape[0]
     mates = [team_mate(me, ffn_bits, k) for k in range(8)]
     partners = [flip_bit(me, bit) for bit in sum_bits if bit not in ffn_bits]
-    greet(partners + [device for device, _ in mates[1:]])
+    greet(partners + [device for device, _ in mates[1:]] + [flip_bit(me, bit) for bit in carry_bits])
+    crossing = [
+        Links(*carry_sems).copy(i, carried[i], carried_out[i], flip_bit(me, bit)) for i, bit in enumerate(carry_bits)
+    ]
+    for copy in crossing:
+        copy.start()
     swaps, own_place = Links(swap_send, swap_recv), mates[0][1]
     swap_copies = [
         swaps.copy(k, gate_ref.at[mates[k][1]], gate_out.at[own_place], mates[k][0]) for k in range(1, 8)
@@ -1034,24 +1049,27 @@
     for copy in swap_copies:
         copy.wait_send()
     keep.wait()
-
-
-def last_sums(left, other, right, tokens, gain, residual, hidden, down, h2, d_gate, sum_bits, ffn_bits):
+    for copy in crossing:
+        copy.wait()
+
+
+def last_sums(left, other, right, tokens, gain, residual, hidden, down, h2, d_gate, carry, carry_bits, sum_bits, ffn_bits):
     block, width = tokens.shape
     return pl.pallas_call(
-        functools.partial(last_sums_kernel, sum_bits, ffn_bits),
+        functools.partial(last_sums_kernel, carry_bits, sum_bits, ffn_bits),
         out_shape=(
             jax.ShapeDtypeStruct((block, width), f32), jax.ShapeDtypeStruct((block, width), bf16),
             jax.ShapeDtypeStruct(d_gate.shape, bf16),
-        ),
-        in_specs=[vmem] * 9 + [anywhere],
-        out_specs=(vmem, vmem, anywhere),
+        ) + tuple(jax.ShapeDtypeStruct(x.shape, x.dtype) for x in carry),
+        in_specs=[vmem] * 9 + [anywhere] * (1 + len(carry)),
+        out_specs=(vmem, vmem, anywhere) + (anywhere,) * len(carry),
         scratch_shapes=sum_scratch(block, width, LAST_CUT) * 2
-        + [pltpu.SemaphoreType.DMA((8,)), pltpu.SemaphoreType.DMA((8,)), pltpu.SemaphoreType.DMA],
+        + [pltpu.SemaphoreType.DMA((8,)), pltpu.SemaphoreType.DMA((8,)), pltpu.SemaphoreType.DMA]
+        + [pltpu.SemaphoreType.DMA((1,))] * (2 * len(carry)),
         compiler_params=link_params(4),
         cost_estimate=cost(16 * block * right.size // 8, 300e6),
         name="last_sums",
-    )(left, other, right, tokens, gain, residual, hidden, down, h2, d_gate)
+    )(left, other, right, tokens, gain, residual, hidden, down, h2, d_gate, *carry)
 
 
 def exchange_kernel(teams, sources, *refs):
@@ -1252,7 +1270,7 @@
     )
     peaks = jnp.broadcast_to(jnp.pad(peaks, (0, 128 - head_total))[None], (8, 128))
     if carry:
-        carry[2], down_sent = tie(carry[2], w_down)
+        carry[2], attended, down_sent = tie(carry[2], attended, w_down)
         over = flip(down_sent, 16)
     after_attn, normed_ffn, peaks, *full = branch(
         attended, out_w, tokens, gain_ffn, peaks, carry, attn_bits, ffn_bits, bit_count
@@ -1289,12 +1307,14 @@
     row_values = (weight_rows, ff_cols)
     crosses = data_bits == [4, 16]
     if crosses:
-        y_side = (device // 4) % 2
+        y_side, z_side = (device // 4) % 2, (device // 16) % 2
         kept = lax.dynamic_index_in_dim(d_down, y_side, unit_dims[4], False)
         sent = lax.dynamic_index_in_dim(d_down, 1 - y_side, unit_dims[4], False)
-        ahead = flip(sent[0], 4)
-        grad_gate, ahead = tie(grad_gate, ahead)
-        beside = [sent[1]]
+        mine, theirs = (lax.dynamic_index_in_dim(kept, z, 0, False) for z in (z_side, 1 - z_side))
+        to_mine, to_theirs = (lax.dynamic_index_in_dim(sent, z, 0, False) for z in (z_side, 1 - z_side))
+        theirs = (theirs.astype(f32) + flip(to_theirs, 4).astype(f32)).astype(bf16)
+        grad_gate, theirs = tie(grad_gate, theirs)
+        beside = [to_mine, theirs]
     else:
         beside = []
     d_residual, branch_mine, grad_attended, d_up, *d_gate = ffn_back(
@@ -1302,13 +1322,15 @@
         ffn_bits, attn_bits,
     )
     if crosses:
-        d_down = (kept.astype(f32) + jnp.stack([ahead, d_gate[2]]).astype(f32)).astype(bf16)
+        d_down = mine.astype(f32) + d_gate[2].astype(f32) + d_gate[3].astype(f32)
         d_gate = (d_gate[0].astype(f32) + d_gate[1].astype(f32)).astype(bf16)
         d_gate = d_gate.reshape((2,) * (bit_count - 1) + row_values)
     else:
         d_down = data_sum(d_down, unit_dims, data_bits[:1])
         d_gate = data_sum(d_gate[0].reshape(row_shape + row_values), row_dims, data_bits[:1])
-    grad_attended, d_down, d_gate = tie(grad_attended, d_down, d_gate)
+    if not crosses:
+        d_down = data_sum(d_down, unit_rest, data_bits[1:]).astype(f32)
+    grad_attended, d_gate = tie(grad_attended, d_gate)
     d_gate = data_sum(d_gate, row_rest, data_bits[1:])
     branch_grad = lax.all_gather(branch_mine, AXIS, axis=0, tiled=True, axis_index_groups=in_team)
 
@@ -1319,19 +1341,29 @@
 
     grad_pairs, shares = [None] * (heads // 2), [None] * (heads // 2)
     grad_pairs[0], share = heads_back(0)
-    grad_attended, d_down, d_gate, d_up, share, branch_grad = tie(
-        grad_attended, d_down, d_gate, d_up, share, branch_grad
-    )
+    grad_attended, d_gate, d_up, share, branch_grad = tie(grad_attended, d_gate, d_up, share, branch_grad)
     shares[0] = scatter_across(share)
-    d_down = data_sum(d_down, unit_rest, data_bits[1:]).astype(f32)
     d_up = data_sum(d_up.reshape(row_shape + row_values), row_dims, data_bits[:1])
     for p in range(1, heads // 2):
         grad_pairs[p], share = heads_back(p)
-        grad_pairs[p], share, d_down, d_up, branch_grad = tie(grad_pairs[p], share, d_down, d_up, branch_grad)
+        grad_pairs[p], share, d_up = tie(grad_pairs[p], share, d_up)
         shares[p] = scatter_across(share)
-    d_up = data_sum(d_up, row_rest, data_bits[1:])
+    sent, sent_bits = [], ()
+    if crosses:
+        kept_up = lax.dynamic_index_in_dim(d_up, z_side, row_rest[16], False)
+        sent, sent_bits = [lax.dynamic_index_in_dim(d_up, 1 - z_side, row_rest[16], False)], (16,)
+        kept_up, sent[0] = (d.reshape(team, weight_rows, ff_cols) for d in (kept_up, sent[0]))
+    else:
+        d_up = data_sum(d_up, row_rest, data_bits[1:])
     grad_pairs[0], shares[0] = tie(grad_pairs[0], shares[0])
     d_gate = d_gate.reshape(team, weight_rows, ff_cols)
+    d_tokens, mixed, d_gate, *landed = last_sums(
+        *grad_pairs, qkv_w, tokens, gain_attn, d_residual, hidden, down_w, after_attn, d_gate, sent, sent_bits,
+        attn_bits, ffn_bits,
+    )
+    if crosses:
+        d_up = (kept_up.astype(f32) + landed[0].astype(f32)).astype(bf16)
+    d_tokens, attended = tie(d_tokens, attended)
     out_part = contract(attended, branch_grad, 0, 0)
     if weight_rows == HEAD_DIM:
         d_out = scatter_across(out_part).astype(f32)
@@ -1341,9 +1373,6 @@
             out_part.reshape(heads, 1, HEAD_DIM, width), 0.0,
         ).reshape(width, width)
         d_out = lax.psum_scatter(spread, AXIS, scatter_dimension=0, tiled=True)
-    d_tokens, mixed, d_gate = last_sums(
-        *grad_pairs, qkv_w, tokens, gain_attn, d_residual, hidden, down_w, after_attn, d_gate, attn_bits, ffn_bits
-    )
     places = [[], [], []]
     for i, b, source, target, columns in qkv_moves:
         places[i].append((target // (3 * PAIR), b, target % (3 * PAIR), source, columns))

time: 842 us -> 822 us (0.976)
  waiting for transfers between devices: 110 us -> 54.2 us
  Pallas kernels: 574 us -> 611 us
    ppermute x9 -> x7, waiting for transfers between devices: 109 us -> 52.2 us  [flip(): return lax.ppermute(x, AXIS, [(i, i ^ bit) for i in range(devices)])]
    pallas_call x1, Pallas kernels: 79 us -> 102 us  [branch(): pl.pallas_call(functools.partial(branch_kernel, bool(carry), swap_bits, s...]
    pallas_call x1, Pallas kernels: 100 us -> 115 us  [ffn_back(): pl.pallas_call(functools.partial(ffn_back_kernel, cross, sum_bits, swap_b...]
  transfers between devices with their start and end apart: 15 -> 13, of which waited for: 3 -> 4; matrix products, arithmetic and copies ran while one was open for 14% -> 14% of each run, Pallas kernels for 53% -> 61%
where the time goes in v6:
time: 822 us; the launch traced here: 815 us
  Pallas kernels  611 us (74%)
  matrix products  81.3 us (10%)
  waiting for transfers between devices  54.2 us (7%)
  other arithmetic  23.7 us (3%)
  local copies, waits for them, and re-layouts  23.3 us (3%)
  between operations  15.4 us (2%)
    pallas_call x1, Pallas kernels, front(): pl.pallas_call(functools.partial(front_kernel, team, teams, qkv_moves, ff...  136 us
    pallas_call x1, Pallas kernels, last_sums(): pl.pallas_call(functools.partial(last_sums_kernel, carry_bits, sum_bits,...  118 us
    pallas_call x1, Pallas kernels, ffn_back(): pl.pallas_call(functools.partial(ffn_back_kernel, cross, sum_bits, swap_b...  115 us
    pallas_call x1, Pallas kernels, branch(): pl.pallas_call(functools.partial(branch_kernel, bool(carry), swap_bits, s...  102 us
    dot_general x6, matrix products, contract(): lax.dot_general(left, right, (((left_dim,), (right_dim,)), ((), ())), pre...  81.3 us
    pallas_call x2, Pallas kernels, attend_backward(): pl.pallas_call(functools.partial(attend_backward_kernel, 2 * pair), grid=...  76 us
    ppermute x7, waiting for transfers between devices, flip(): return lax.ppermute(x, AXIS, [(i, i ^ bit) for i in range(devices)])  52.2 us
    pallas_call x1, Pallas kernels, attend_forward(): pl.pallas_call(attend_forward_kernel, out_shape=(shape((pairs, length, PA...  33 us
  transfers between devices with their start and end apart: 13, of which 4 were waited for; matrix products, arithmetic and copies ran while one was open for 14% of the time, Pallas kernels for 61%

profile of v6, /device:TPU:0, one launch (start us, length us, event | category | flops | bytes accessed | tf_op | source)
XLA Modules:
  0.0 815.1 jit_solution(17894217532345333472)
XLA Ops:
  8.0 0.7 maximum_convert_fusion
  10.1 135.6 %front.1 = (bf16[2048,2048]{1,0:T(8,128)(2,1)}, bf16[4,512,768]{2,1,0:T(8,128)(2,1)}, bf16[16,64,1024]{2,1,0:T(8,128)(2,1)}, f32[32,8,128]{2,1,0:T(8,128)}, bf16[256,2048]{1,0:T(8,128)(2,1)}) custom-call(bf16[256,2048]{1,0:T(8,128)(2,1)} %tokens_ref.3, bf16[64,2048]{1,0:T(8,128)(2,1)} %refs_4_.1, bf16[64,2048]{1,0:T(8,128)(2,1)} %refs_5_.1, ...), custom_call_target="tpu_custom_call" | custom-call | bytes 200000000 | tf_op jit(solution)/shard_map/front/pallas_call | solution.py:636
  145.8 11.8 %fusion.6.qkv_ref = f32[2048,768]{1,0:T(8,128)} fusion(bf16[2048,2048]{1,0:T(8,128)(2,1)} %get-tuple-element.84.normed_ref, bf16[2048,768]{1,0:T(8,128)(2,1)} %bitcast.82), kind=kOutput, calls=%fused_computation.41 | convolution fusion | flops 6442450944 | bytes 17825792 | tf_op jit(solution)/shard_map/dot_general | solution.py:30
  157.7 2.4 collective-permute-start.1
  160.0 1.4 slice.19
  161.4 0.8 dynamic-slice_convert_fusion
  162.1 1.3 copy.32.col_ref
  163.5 33.0 %attend_forward.1 = (bf16[2,2048,128]{2,1,0:T(8,128)(2,1)}, bf16[2,2048,128]{2,1,0:T(8,128)(2,1)}, bf16[2,2048,128]{2,1,0:T(8,128)(2,1)}, bf16[2048,256]{1,0:T(8...) custom-call(f32[2048,768]{1,0:T(8,128)} %fusion.6.qkv_ref, f32[2048,128]{1,0:T(8,128)} %constant.209.clone.cos_ref, ...), custom_call_target="tpu_custom_call" | custom-call | flops 17179869184 | bytes 12582912 | tf_op jit(solution)/shard_map/attend_forward/pallas_call | solution.py:120
  196.5 34.4 %collective-permute-done.refs_2_ = bf16[12,64,1024]{2,1,0:T(8,128)(2,1)} collective-permute-done((bf16[12,64,1024]{2,1,0:T(8,128)(2,1)}, bf16[12,64,1024]{2,1,0:T(8,128)(2,1)}, u32[]{:S(2)}, u32[]{:S(2)}) %collective-permute-start) | collective-permute-done | bytes 1572896 | tf_op jit(solution)/shard_map/ppermute | solution.py:1175
  230.8 1.7 slice_reduce_fusion
  233.2 0.7 slice_bitcast_fusion.1
  234.8 102.2 %attention_branch.1 = (f32[256,2048]{1,0:T(8,128)}, bf16[2048,2048]{1,0:T(8,128)(2,1)}, f32[8,128]{1,0:T(8,128)}, bf16[32,64,1024]{2,1,0:T(8,128)(2,1)}, bf16[32...) custom-call(bf16[2048,256]{1,0:T(8,128)(2,1)} %get-tuple-element.146.left_ref, ...), custom_call_target="tpu_custom_call" | custom-call | flops 2147483648 | bytes 300000000 | tf_op jit(solution)/shard_map/attention_branch/pallas_call | solution.py:801
  337.6 14.6 %fusion.7 = f32[2048,1024]{1,0:T(8,128)} fusion(bf16[2048,2048]{1,0:T(8,128)(2,1)} %get-tuple-element.102.normed_ref, bf16[2048,1024]{1,0:T(8,128)(2,1)} %bitcast.90), kind=kOutput, calls=%fused_computation.42 | convolution fusion | flops 8589934592 | bytes 20971520 | tf_op jit(solution)/shard_map/dot_general | solution.py:30
  352.2 13.7 %multiply_convert_fusion.2 = (bf16[2048,1024]{1,0:T(8,128)(2,1)}, f32[2048,1024]{1,0:T(8,128)}) fusion(f32[2048,1024]{1,0:T(8,128)} %fusion.7, bf16[2048,2048]{1,0:T(8,128)(2,1)S(1)} %copy-done.19, bf16[2048,1024]{1,0:T(8,128)(2,1)S(1)} %bitcast.93), kind=kOutput, calls=%fused_computation.2 | convolution fusion | flops 8602517504 | bytes 33554432 | tf_op jit(solution)/shard_map/dot_general | solution.py:30
  365.9 12.7 %convolution_convert_fusion = bf16[1024,2048]{1,0:T(8,128)(2,1)S(1)} fusion(bf16[2048,1024]{1,0:T(8,128)(2,1)} %get-tuple-element.166.hidden_ref, bf16[2048,2048]{1,0:T(8,128)(2,1)} %all-gather.4.cloned.1.call-done), kind=kOutput, calls=%fused_computation.8 | convolution fusion | flops 8592031744 | bytes 16777216 | tf_op jit(solution)/shard_map/dot_general | solution.py:30
  378.6 1.2 dynamic-slice_bitcast_fusion.2
  379.8 1.5 collective-permute-start.4
  381.3 1.4 copy-done.11
  382.7 1.3 bitcast_dynamic-update-slice_fusion.1
  384.2 21.7 %multiply_convert_fusion = (bf16[2048,1024]{1,0:T(8,128)(2,1)}, bf16[2048,1024]{1,0:T(8,128)(2,1)}) fusion(f32[2048,1024]{1,0:T(8,128)} %fusion.7, f32[2048,1024]{1,0:T(8,128)} %get-tuple-element.167, bf16[2048,2048]{1,0:T(8,128)(2,1)} %all-gather.4.cloned.1.call-done, bf16[1024,2048]{1,0:T(8,128)(2,1)S(1)} %bitcast.73), kind=kOutput, calls=%fused_computation | convolution fusion | flops 8617197568 | bytes 37748736 | tf_op jit(solution)/shard_map/dot_general | solution.py:30
  405.9 2.6 fusion.5.refs_1_
  408.5 115.1 %ffn_back.1 = (f32[256,2048]{1,0:T(8,128)}, bf16[256,2048]{1,0:T(8,128)(2,1)}, bf16[2048,256]{1,0:T(8,128)(2,1)}, bf16[2048,1024]{1,0:T(8,128)(2,1)}, bf16[4,256...) custom-call(bf16[2048,1024]{1,0:T(8,128)(2,1)} %get-tuple-element.10, ...), custom_call_target="tpu_custom_call" | custom-call | flops 51539607552 | bytes 200000000 | tf_op jit(solution)/shard_map/ffn_back/pallas_call | solution.py:975
  523.7 3.2 add_convert_fusion
  527.1 38.7 %attend_backward.2 = (bf16[2048,384]{1,0:T(8,128)(2,1)}, bf16[2048,384]{1,0:T(8,128)(2,1)}) custom-call(bf16[2,2048,128]{2,1,0:T(8,128)(2,1)} %get-tuple-element.90.q_ref, bf16[2,2048,128]{2,1,0:T(8,128)(2,1)} %get-tuple-element.91.k_ref, bf16[2,2048,128]{2,1,0:T(8,128)(2,1)} %get-tuple-element.92.v_ref, bf16[2048,256]{1,0:T(8,128)(2,1)} %get-tuple-element.124.grad_ref, ...), custom_call_target="tpu_custom_call" | custom-call | flops 24696061952 | bytes 100000000 | tf_op jit(solution)/shard_map/attend_backward/pallas_call | solution.py:191
  565.8 8.3 %collective-permute-done.5 = bf16[2,2,2,64,1024]{4,3,2,1,0:T(8,128)(2,1)S(1)} collective-permute-done((bf16[2,2,2,64,1024]{4,3,2,1,0:T(8,128)(2,1)S(1)}, bf16[2,2,2,64,1024]{4,3,2,1,0:T(8,128)(2,1)S(1)}, u32[]{:S(2)}, u32[]{:S(2)}) %collective-permute-start.5) | collective-permute-done | bytes 1048608 | tf_op jit(solution)/shard_map/ppermute | solution.py:1175
  574.1 1.4 fusion.4
  575.6 1.2 all-gather.8.cloned.1.call-done
  576.9 1.8 dynamic-slice_bitcast_fusion
  578.7 1.2 collective-permute-start.6
  579.9 37.3 %attend_backward.3 = (bf16[2048,384]{1,0:T(8,128)(2,1)}, bf16[2048,384]{1,0:T(8,128)(2,1)}) custom-call(bf16[2,2048,128]{2,1,0:T(8,128)(2,1)} %get-tuple-element.90.q_ref, bf16[2,2048,128]{2,1,0:T(8,128)(2,1)} %get-tuple-element.91.k_ref, bf16[2,2048,128]{2,1,0:T(8,128)(2,1)} %get-tuple-element.92.v_ref, bf16[2048,256]{1,0:T(8,128)(2,1)} %get-tuple-element.124.grad_ref, ...), custom_call_target="tpu_custom_call" | custom-call | flops 24696061952 | bytes 100000000 | tf_op jit(solution)/shard_map/attend_backward/pallas_call | solution.py:191
  617.2 9.5 %collective-permute-done.6 = bf16[2,2,2,2,64,1024]{5,4,3,2,1,0:T(8,128)(2,1)} collective-permute-done((bf16[2,2,2,2,64,1024]{5,4,3,2,1,0:T(8,128)(2,1)S(1)}, bf16[2,2,2,2,64,1024]{5,4,3,2,1,0:T(8,128)(2,1)}, u32[]{:S(2)}, u32[]{:S(2)}) %collective-permute-start.6) | collective-permute-done | bytes 2097184 | tf_op jit(solution)/shard_map/ppermute | solution.py:1175
  626.7 2.7 fusion.1
  630.2 1.6 constant_dynamic-slice_fusion
  631.8 118.2 %last_sums.1 = (f32[256,2048]{1,0:T(8,128)}, bf16[256,2048]{1,0:T(8,128)(2,1)}, bf16[8,64,1024]{2,1,0:T(8,128)(2,1)}, bf16[8,64,1024]{2,1,0:T(8,128)(2,1)}) custom-call(bf16[2048,384]{1,0:T(8,128)(2,1)} %get-tuple-element.123.left_ref, bf16[2048,384]{1,0:T(8,128)(2,1)} %get-tuple-element.128.other_ref, bf16[2048,768]{1,0:T(8,128)(2,1)} %bitcast.83, ...), custom_call_target="tpu_custom_call" | custom-call | flops 805306368 | bytes 300000000 | tf_op jit(solution)/shard_map/last_sums/pallas_call | solution.py:1058
  750.0 6.8 convolution_convert_fusion.1
  757.7 1.2 divide_sqrt_fusion
  759.1 0.9 multiply_convert_fusion.3
  760.0 3.9 fusion.2
  763.9 2.9 fusion.3.refs_2_
  766.8 27.9 %exchange.1 = (bf16[8,64,384]{2,1,0:T(8,128)(2,1)}, bf16[8,64,384]{2,1,0:T(8,128)(2,1)}, bf16[8,64,1024]{2,1,0:T(8,128)(2,1)}) custom-call(bf16[8,64,384]{2,1,0:T(8,128)(2,1)} %bitcast.84, bf16[8,64,384]{2,1,0:T(8,128)(2,1)} %bitcast.85, bf16[8,64,1024]{2,1,0:T(8,128)(2,1)} %fusion.3.refs_2_), custom_call_target="tpu_custom_call" | custom-call | flops 1000000 | bytes 40000000 | tf_op jit(solution)/shard_map/exchange/pallas_call | solution.py:1104
  794.8 1.2 copy-done.5
  796.0 1.2 copy-done.6
  797.2 1.0 copy-done.7
  798.2 1.0 copy-done.8
  799.2 3.2 home.1
  802.4 1.9 convert_element_type.149
  804.4 2.3 copy.44
  806.7 1.3 copy.45
  (85 shorter events, 5.9 us)
Async XLA Ops:
  7.2 227.0 %all-gather.6.cloned.1.call-start = ((), (), s32[]{:S(2)}) async-start(), calls=%async_computation.4 | async-start | bytes 8650752 | tf_op jit(solution)/shard_map/all_gather | solution.py:1238
  7.9 358.0 %all-gather.4.cloned.1.call-start = ((), (), s32[]{:S(2)}) async-start(), calls=%async_computation.3 | async-start | bytes 9437184 | tf_op jit(solution)/shard_map/all_gather | solution.py:1299
  145.7 11.9 %copy-start.10 = (bf16[16,64,1024]{2,1,0:T(8,128)(2,1)S(1)}, bf16[16,64,1024]{2,1,0:T(8,128)(2,1)}, u32[]{:S(2)}) copy-start(bf16[16,64,1024]{2,1,0:T(8,128)(2,1)} %get-tuple-element.94.refs_0_) | copy-start | bytes 6291460
  157.6 419.2 %all-gather.8.cloned.1.call-start = ((), (), s32[]{:S(2)}) async-start(), calls=%async_computation.5 | async-start | bytes 9437184 | tf_op jit(solution)/shard_map/all_gather | solution.py:1335
  157.7 76.5 %collective-permute-start.1 = (bf16[16,64,1024]{2,1,0:T(8,128)(2,1)S(1)}, bf16[16,64,1024]{2,1,0:T(8,128)(2,1)}, u32[]{:S(2)}, u32[]{:S(2)}) collective-permute-start(bf16[16,64,1024]{2,1,0:T(8,128)(2,1)S(1)} %copy-done.10), channel_id=1, source_target_pairs={{0,4},{1,5},{2,6},{3,7},{4,0},{5,1},{6,2},{7,3},{8,12},{9,13},{10,... | collective-permute-start | bytes 6291464 | tf_op jit(solution)/shard_map/ppermute | solution.py:1175
  161.4 69.5 %collective-permute-start = (bf16[12,64,1024]{2,1,0:T(8,128)(2,1)}, bf16[12,64,1024]{2,1,0:T(8,128)(2,1)}, u32[]{:S(2)}, u32[]{:S(2)}) collective-permute-start(bf16[12,64,1024]{2,1,0:T(8,128)(2,1)} %slice.19), channel_id=1, source_target_pairs={{0,16},{1,17},{2,18},{3,19},{4,20},{5,21},{6,22},{7,23},{8,24},{9,... | collective-permute-start | bytes 4718600 | tf_op jit(solution)/shard_map/ppermute | solution.py:1175
  162.1 1.4 copy-start.18
  163.5 67.3 %copy-start.15 = (bf16[256,2048]{1,0:T(8,128)(2,1)S(1)}, bf16[256,2048]{1,0:T(8,128)(2,1)}, u32[]{:S(2)}) copy-start(bf16[256,2048]{1,0:T(8,128)(2,1)} %refs_3_.1) | copy-start | bytes 3145732
  230.8 106.1 %collective-permute-start.2 = (bf16[256,2048]{1,0:T(8,128)(2,1)S(1)}, bf16[256,2048]{1,0:T(8,128)(2,1)}, u32[]{:S(2)}, u32[]{:S(2)}) collective-permute-start(bf16[256,2048]{1,0:T(8,128)(2,1)S(1)} %copy-done.15), channel_id=1, source_target_pairs={{0,16},{1,17},{2,18},{3,19},{4,20},{5,21},{6,22},{7,23},{8,24},{9,... | collective-permute-start | bytes 3145736 | tf_op jit(solution)/shard_map/ppermute | solution.py:1175
  337.0 47.0 %collective-permute-start.3 = (bf16[256,2048]{1,0:T(8,128)(2,1)}, bf16[256,2048]{1,0:T(8,128)(2,1)S(1)}, u32[]{:S(2)}, u32[]{:S(2)}) collective-permute-start(bf16[256,2048]{1,0:T(8,128)(2,1)} %collective-permute-done.2), channel_id=1, source_target_pairs={{0,4},{1,5},{2,6},{3,7},{4,0},{5,1},{6,2},{7,3},{8,12},{9,13},{10,... | collective-permute-start | bytes 3145736 | tf_op jit(solution)/shard_map/ppermute | solution.py:1175
  337.6 14.6 %copy-start.19 = (bf16[2048,2048]{1,0:T(8,128)(2,1)S(1)}, bf16[2048,2048]{1,0:T(8,128)(2,1)}, u32[]{:S(2)}) copy-start(bf16[2048,2048]{1,0:T(8,128)(2,1)} %get-tuple-element.102.normed_ref) | copy-start | bytes 25165828
  337.6 14.6 %copy-start.20 = (bf16[32,64,1024]{2,1,0:T(8,128)(2,1)S(1)}, bf16[32,64,1024]{2,1,0:T(8,128)(2,1)}, u32[]{:S(2)}) copy-start(bf16[32,64,1024]{2,1,0:T(8,128)(2,1)} %get-tuple-element.104) | copy-start | bytes 12582916
  378.6 5.5 copy-start.14
  378.6 4.1 copy-start.11
  379.8 26.1 %collective-permute-start.4 = (bf16[256,2048]{1,0:T(8,128)(2,1)S(1)}, bf16[256,2048]{1,0:T(8,128)(2,1)S(1)}, u32[]{:S(2)}, u32[]{:S(2)}) collective-permute-start(bf16[256,2048]{1,0:T(8,128)(2,1)S(1)} %get-tuple-element.161), channel_id=1, source_target_pairs={{0,4},{1,5},{2,6},{3,7},{4,0},{5,1},{6,2},{7,3},{8,12},{9,13},{10,... | collective-permute-start | bytes 3145736 | tf_op jit(solution)/shard_map/ppermute | solution.py:1175
  384.2 21.7 %copy-start.12 = (bf16[4,256,2048]{2,1,0:T(8,128)(2,1)}, bf16[4,256,2048]{2,1,0:T(8,128)(2,1)S(1)}, u32[]{:S(2)}) copy-start(bf16[4,256,2048]{2,1,0:T(8,128)(2,1)S(1)} %bitcast_dynamic-update-slice_fusion) | copy-start | bytes 12582916
  523.7 108.1 %reduce-scatter.4.cloned.1.call-start = ((), (), s32[]{:S(2)}) async-start(), calls=%async_computation.6 | async-start | bytes 1966080 | tf_op jit(solution)/shard_map/reduce_scatter | solution.py:1181
  527.0 47.1 %collective-permute-start.5 = (bf16[2,2,2,64,1024]{4,3,2,1,0:T(8,128)(2,1)S(1)}, bf16[2,2,2,64,1024]{4,3,2,1,0:T(8,128)(2,1)S(1)}, u32[]{:S(2)}, u32[]{:S(2)}) collective-permute-start(bf16[2,2,2,64,1024]{4,3,2,1,0:T(8,128)(2,1)S(1)} %dynamic-slice_bitcast_fusion.1), channel_id=1, source_target_pairs={{0,16},{1,17},{2,18},{3,19},{4,20},{5,21},{6,22},{7,23},{8,24},{9,... | collective-permute-start | bytes 3145736 | tf_op jit(solution)/shard_map/ppermute | solution.py:1175
  576.8 190.0 %reduce-scatter.6.cloned.1.call-start = ((), (), s32[]{:S(2)}) async-start(), calls=%async_computation.7 | async-start | bytes 1966080 | tf_op jit(solution)/shard_map/reduce_scatter | solution.py:1181
  578.7 48.0 %copy-start.13 = (bf16[2048,1024]{1,0:T(8,128)(2,1)S(1)}, bf16[2048,1024]{1,0:T(8,128)(2,1)}, u32[]{:S(2)}) copy-start(bf16[2048,1024]{1,0:T(8,128)(2,1)} %get-tuple-element.127) | copy-start | bytes 12582916
  578.7 48.0 %collective-permute-start.6 = (bf16[2,2,2,2,64,1024]{5,4,3,2,1,0:T(8,128)(2,1)S(1)}, bf16[2,2,2,2,64,1024]{5,4,3,2,1,0:T(8,128)(2,1)}, u32[]{:S(2)}, u32[]{:S(2)}) collective-permute-start(bf16[2,2,2,2,64,1024]{5,4,3,2,1,0:T(8,128)(2,1)S(1)} %dynamic-slice_bitcast_fusion), channel_id=1, source_target_pairs={{0,4},{1,5},{2,6},{3,7},{4,0},{5,1},{6,2},{7,3},{8,12},{9,13},{10,... | collective-permute-start | bytes 6291464 | tf_op jit(solution)/shard_map/ppermute | solution.py:1175
  617.2 12.3 %copy-start.17 = (f32[32,64]{1,0:T(8,128)S(1)}, f32[32,64]{1,0:T(8,128)}, u32[]{:S(2)}) copy-start(f32[32,64]{1,0:T(8,128)} %get-tuple-element.154) | copy-start | bytes 24580
  629.4 173.0 %reduce-scatter.8.cloned.1.call-start = ((), (), s32[]{:S(2)}) async-start(), calls=%async_computation.8 | async-start | bytes 1310720 | tf_op jit(solution)/shard_map/reduce_scatter | solution.py:1181
  631.8 118.2 %copy-start.9 = (bf16[2048,256]{1,0:T(8,128)(2,1)S(1)}, bf16[2048,256]{1,0:T(8,128)(2,1)}, u32[]{:S(2)}) copy-start(bf16[2048,256]{1,0:T(8,128)(2,1)} %get-tuple-element.146.left_ref) | copy-start | bytes 3145732
  750.0 6.9 copy-start.21
  750.0 7.0 copy-start.22
  750.0 9.0 %copy-start.2 = (bf16[64,2048]{1,0:T(8,128)(2,1)S(1)}, bf16[64,2048]{1,0:T(8,128)(2,1)}, u32[]{:S(2)}) copy-start(bf16[64,2048]{1,0:T(8,128)(2,1)} %refs_4_.1) | copy-start | bytes 786436
  750.0 9.0 %copy-start.3 = (bf16[64,2048]{1,0:T(8,128)(2,1)S(1)}, bf16[64,2048]{1,0:T(8,128)(2,1)}, u32[]{:S(2)}) copy-start(bf16[64,2048]{1,0:T(8,128)(2,1)} %refs_5_.1) | copy-start | bytes 786436
  760.0 34.8 %copy-start = (bf16[64,8192]{1,0:T(8,128)(2,1)S(1)}, bf16[64,8192]{1,0:T(8,128)(2,1)}, u32[]{:S(2)}) copy-start(bf16[64,8192]{1,0:T(8,128)(2,1)} %refs_7_.1) | copy-start | bytes 3145732
  760.0 34.8 %copy-start.1 = (bf16[64,8192]{1,0:T(8,128)(2,1)S(1)}, bf16[64,8192]{1,0:T(8,128)(2,1)}, u32[]{:S(2)}) copy-start(bf16[64,8192]{1,0:T(8,128)(2,1)} %refs_8_.1) | copy-start | bytes 3145732
  760.0 34.8 %copy-start.4 = (bf16[64,2048]{1,0:T(8,128)(2,1)S(1)}, bf16[64,2048]{1,0:T(8,128)(2,1)}, u32[]{:S(2)}) copy-start(bf16[64,2048]{1,0:T(8,128)(2,1)} %refs_6_.1) | copy-start | bytes 786436
  794.8 1.2 copy-start.5
  796.0 1.2 copy-start.6
  797.2 1.0 copy-start.7
  798.2 1.0 copy-start.8
  802.4 4.2 copy-start.16
Sparse Core Ops, SparseCore 0:
  10.9 117.1 all-gather.5
  157.7 79.7 all-gather.3
  523.8 52.9 all-gather.7
  579.5 35.2 reduce-scatter.3
  629.5 64.6 reduce-scatter.5
  757.0 34.1 reduce-scatter.7

commit v7 on v6

--- a/solution.py
+++ b/solution.py
@@ -70,20 +70,24 @@
 
 
 def attend_forward_kernel(
-    qkv_ref, cos_ref, sin_ref, row_ref, col_ref, q_ref, k_ref, v_ref, out_ref, lse_ref, peak_ref
+    normed_ref, qkv_w_ref, cos_ref, sin_ref, row_ref, col_ref, q_ref, k_ref, v_ref, out_ref, lse_ref, peak_ref
 ):
     pairs, length, _ = q_ref.shape
-    for t in range(length // BLOCK):
-        rows = pl.ds(t * BLOCK, BLOCK)
+
+    @pl.loop(0, length // BLOCK)
+    def _(t):
+        rows = pl.ds(pl.multiple_of(t * BLOCK, BLOCK), BLOCK)
         cosine, sine = cos_ref[rows, :], sin_ref[rows, :]
         for pair in range(pairs):
             first = 3 * pair * PAIR
-            query = qkv_ref[rows, first : first + PAIR]
+            qkv = contract(normed_ref[rows, :], qkv_w_ref[:, first : first + 3 * PAIR], 1, 0)
+            query = qkv[:, 0:PAIR]
             query = (query * cosine + swap_halves(query) * sine).astype(bf16)
             q_ref[pair, rows, :] = (query.astype(f32) * HEAD_DIM ** (-0.5)).astype(bf16)
-            key = qkv_ref[rows, first + PAIR : first + 2 * PAIR]
+            key = qkv[:, PAIR : 2 * PAIR]
             k_ref[pair, rows, :] = (key * cosine + swap_halves(key) * sine).astype(bf16)
-            v_ref[pair, rows, :] = qkv_ref[rows, first + 2 * PAIR : first + 3 * PAIR].astype(bf16)
+            v_ref[pair, rows, :] = qkv[:, 2 * PAIR : 3 * PAIR].astype(bf16)
+
     peak_ref[...] = jnp.full(peak_ref.shape, -jnp.inf, f32)
     lane = lax.broadcasted_iota(jnp.int32, (BLOCK, 128), 1)
     for t in range(length // BLOCK):
@@ -113,9 +117,9 @@
             out_ref[rows, pl.ds(pl.multiple_of(pair * PAIR, PAIR), PAIR)] = total.astype(bf16)
 
 
-def attend_forward(qkv, cosine, sine, row_blocks, col_blocks):
-    length = qkv.shape[0]
-    pairs = qkv.shape[1] // (3 * PAIR)
+def attend_forward(normed, qkv_w, cosine, sine, row_blocks, col_blocks):
+    length = normed.shape[0]
+    pairs = qkv_w.shape[1] // (3 * PAIR)
     shape = jax.ShapeDtypeStruct
     return pl.pallas_call(
         attend_forward_kernel,
@@ -127,15 +131,15 @@
             shape((length, 128), f32),
             shape((8, 128), f32),
         ),
-        in_specs=[vmem] * 5,
+        in_specs=[vmem] * 6,
         out_specs=tuple([vmem] * 6),
         compiler_params=pltpu.CompilerParams(vmem_limit_bytes=56 * 1024 * 1024),
         cost_estimate=pl.CostEstimate(
-            flops=16 * pairs * length * length * PAIR, bytes_accessed=length * PAIR * pairs * 24,
+            flops=16 * pairs * length * length * PAIR + 2 * normed.size * qkv_w.shape[1], bytes_accessed=100_000_000,
             transcendentals=2 * pairs * length * length,
         ),
         name="attend_forward",
-    )(qkv, cosine, sine, row_blocks, col_blocks)
+    )(normed, qkv_w, cosine, sine, row_blocks, col_blocks)
 
 
 def attend_backward_kernel(
@@ -913,12 +917,12 @@
     )
     for_sibling()
     for_chip()
+    if cross:
+        over_copy.start()
     gradients(0, 1)
     hand_on()
     gradients(1, count - 2)
     finish()
-    if cross:
-        over_copy.start()
     residual = cot_ref[...].astype(f32) + norm_back(h2_ref[...], gain_ref[...], total[...])
     residual_ref[...] = residual
     branch_ref[...] = residual.astype(bf16)
@@ -1032,7 +1036,7 @@
         return contract(hidden_ref[rows_of(place), :], down_ref[:, columns], 1, 0)
 
     first = sum_block(sum_bits, LAST_CUT, False, product, *scratch[: count - 2], Links(*scratch[count - 2 : count]))
-    second = sum_block(ffn_bits, LAST_CUT, True, ffn_product, *scratch[count:-2], Links(*scratch[-2:]))
+    second = sum_block(ffn_bits, HALF, True, ffn_product, *scratch[count:-2], Links(*scratch[-2:]))
     run(first[:2])
     run(second[:2])
     for copy in swap_copies + [keep]:
@@ -1063,7 +1067,7 @@
         ) + tuple(jax.ShapeDtypeStruct(x.shape, x.dtype) for x in carry),
         in_specs=[vmem] * 9 + [anywhere] * (1 + len(carry)),
         out_specs=(vmem, vmem, anywhere) + (anywhere,) * len(carry),
-        scratch_shapes=sum_scratch(block, width, LAST_CUT) * 2
+        scratch_shapes=sum_scratch(block, width, LAST_CUT) + sum_scratch(block, width, HALF)
         + [pltpu.SemaphoreType.DMA((8,)), pltpu.SemaphoreType.DMA((8,)), pltpu.SemaphoreType.DMA]
         + [pltpu.SemaphoreType.DMA((1,))] * (2 * len(carry)),
         compiler_params=link_params(4),
@@ -1235,7 +1239,6 @@
         (i, member, source, target, ff_rows)
         for i in range(2) for member, target, source in ffn_units
     )
-    out_w = lax.all_gather(w_out, AXIS, axis=0, tiled=True)
     gain_row = jnp.concatenate([norm_attn, norm_ffn]).astype(f32)
     gain_row = jnp.pad(gain_row, (0, 128 - 2 * weight_rows)).reshape(1, 128)
     block_rows = block_of.astype(f32).reshape(tok_rows // 128, 128)
@@ -1251,26 +1254,28 @@
     blocks = lax.dynamic_slice_in_dim(gathered, device - mate, team, 0)
     blocks = blocks[:, 1 : 1 + tok_rows // 128].astype(jnp.int32).reshape(SEQ)
     row_blocks, col_blocks = blocks.reshape(1, SEQ), blocks.reshape(SEQ, 1)
-    both_mine, qkv_w = tie(both_mine, qkv_w)
+    both_mine, qkv_w, out_mine = tie(both_mine, qkv_w, w_out)
+    out_w = lax.all_gather(out_mine, AXIS, axis=0, tiled=True)
 
     def whole_rows(mine):
         shape = row_shape + (weight_rows, ff_cols)
         return place_pieces(data_pieces(mine), row_dims, shape).reshape(width, ff_cols)
 
-    qkv = contract(normed_attn, qkv_w, 1, 0)
     cosine, sine = rope_tables(SEQ, PAIR)
-    qkv, cot_mine = tie(qkv, cotangent)
     if data_bits == [4, 16]:
         carry = [both_mine, flip(both_mine, 4), flip(both_mine[: 4 * EARLY_HALVES], 16), w_down, *down_moved]
     else:
         carry = []
-    query, key, value, attended, lse, peak = attend_forward(qkv, cosine, sine, row_blocks, col_blocks)
+    query, key, value, attended, lse, peak = attend_forward(
+        normed_attn, qkv_w, cosine, sine, row_blocks, col_blocks
+    )
+    cot_mine = cotangent
     peaks = jnp.where(
         (jnp.arange(head_total) % team) == mate, jnp.repeat(peak[0, :heads], team), -jnp.inf
     )
     peaks = jnp.broadcast_to(jnp.pad(peaks, (0, 128 - head_total))[None], (8, 128))
     if carry:
-        carry[2], attended, down_sent = tie(carry[2], attended, w_down)
+        carry[1], carry[2], attended, down_sent, cot_mine = tie(carry[1], carry[2], attended, w_down, cotangent)
         over = flip(down_sent, 16)
     after_attn, normed_ffn, peaks, *full = branch(
         attended, out_w, tokens, gain_ffn, peaks, carry, attn_bits, ffn_bits, bit_count

time: 822 us -> 845 us (1.028)
  waiting for transfers between devices: 54.2 us -> 137 us
  Pallas kernels: 611 us -> 563 us
  matrix products: 81.3 us -> 69.5 us
    all_gather x1, waiting for transfers between devices: 0.02 us -> 87.5 us  [body(): out_w = lax.all_gather(out_mine, AXIS, axis=0, tiled=True)]
    pallas_call x1, Pallas kernels: 136 us -> 101 us  [front(): pl.pallas_call(functools.partial(front_kernel, team, teams, qkv_moves, ff...]
    dot_general x6 -> x5, matrix products: 81.3 us -> 69.5 us  [contract(): lax.dot_general(left, right, (((left_dim,), (right_dim,)), ((), ())), pre...]
    pallas_call x1, Pallas kernels: 115 us -> 105 us  [ffn_back(): pl.pallas_call(functools.partial(ffn_back_kernel, cross, sum_bits, swap_b...]
    pallas_call x1, Pallas kernels: 33 us -> 42.6 us  [attend_forward(): pl.pallas_call(attend_forward_kernel, out_shape=(shape((pairs, length, PA...]
  transfers between devices with their start and end apart: 13 -> 13, of which waited for: 4 -> 6; matrix products, arithmetic and copies ran while one was open for 14% -> 12% of each run, Pallas kernels for 61% -> 42%
where the time goes in v7:
time: 845 us; the launch traced here: 841 us
  Pallas kernels  563 us (67%)
  waiting for transfers between devices  137 us (16%)
  matrix products  69.5 us (8%)
  local copies, waits for them, and re-layouts  27 us (3%)
  other arithmetic  23.6 us (3%)
  between operations  15.4 us (2%)
    pallas_call x1, Pallas kernels, last_sums(): pl.pallas_call(functools.partial(last_sums_kernel, carry_bits, sum_bits,...  111 us
    pallas_call x1, Pallas kernels, ffn_back(): pl.pallas_call(functools.partial(ffn_back_kernel, cross, sum_bits, swap_b...  105 us
    pallas_call x1, Pallas kernels, front(): pl.pallas_call(functools.partial(front_kernel, team, teams, qkv_moves, ff...  101 us
    pallas_call x1, Pallas kernels, branch(): pl.pallas_call(functools.partial(branch_kernel, bool(carry), swap_bits, s...  95.5 us
    all_gather x1, waiting for transfers between devices, body(): out_w = lax.all_gather(out_mine, AXIS, axis=0, tiled=True)  87.5 us
    pallas_call x2, Pallas kernels, attend_backward(): pl.pallas_call(functools.partial(attend_backward_kernel, 2 * pair), grid=...  76 us
    dot_general x5, matrix products, contract(): lax.dot_general(left, right, (((left_dim,), (right_dim,)), ((), ())), pre...  69.5 us
    ppermute x7, waiting for transfers between devices, flip(): return lax.ppermute(x, AXIS, [(i, i ^ bit) for i in range(devices)])  49.3 us
  transfers between devices with their start and end apart: 13, of which 6 were waited for; matrix products, arithmetic and copies ran while one was open for 12% of the time, Pallas kernels for 42%

profile of v7, /device:TPU:0, one launch (start us, length us, event | category | flops | bytes accessed | tf_op | source)
XLA Modules:
  0.0 841.0 jit_solution(13520507788555771115)
XLA Ops:
  7.2 0.7 convert_bitcast_fusion
  7.9 0.7 maximum_convert_fusion
  9.4 101.0 %front.1 = (bf16[2048,2048]{1,0:T(8,128)(2,1)}, bf16[4,512,768]{2,1,0:T(8,128)(2,1)}, bf16[16,64,1024]{2,1,0:T(8,128)(2,1)}, f32[32,8,128]{2,1,0:T(8,128)}, bf16[256,2048]{1,0:T(8,128)(2,1)}) custom-call(bf16[256,2048]{1,0:T(8,128)(2,1)} %tokens_ref.3, bf16[64,2048]{1,0:T(8,128)(2,1)} %refs_4_.1, bf16[64,2048]{1,0:T(8,128)(2,1)} %refs_5_.1, ...), custom_call_target="tpu_custom_call" | custom-call | bytes 200000000 | tf_op jit(solution)/shard_map/front/pallas_call | solution.py:640
  110.5 1.5 collective-permute-start
  111.9 2.7 slice.19
  114.7 0.8 dynamic-slice_convert_fusion
  115.5 1.3 copy.32.col_ref
  116.8 42.6 %attend_forward.1 = (bf16[2,2048,128]{2,1,0:T(8,128)(2,1)}, bf16[2,2048,128]{2,1,0:T(8,128)(2,1)}, bf16[2,2048,128]{2,1,0:T(8,128)(2,1)}, bf16[2048,256]{1,0:T(8...) custom-call(bf16[2048,2048]{1,0:T(8,128)(2,1)} %get-tuple-element.85.normed_ref, bf16[2048,768]{1,0:T(8,128)(2,1)} %bitcast.80, ...), custom_call_target="tpu_custom_call" | custom-call | flops 23622320128 | bytes 100000000 | tf_op jit(solution)/shard_map/attend_forward/pallas_call | solution.py:124
  159.4 30.2 %collective-permute-done.1.refs_2_ = bf16[12,64,1024]{2,1,0:T(8,128)(2,1)} collective-permute-done((bf16[12,64,1024]{2,1,0:T(8,128)(2,1)}, bf16[12,64,1024]{2,1,0:T(8,128)(2,1)}, u32[]{:S(2)}, u32[]{:S(2)}) %collective-permute-start.1) | collective-permute-done | bytes 1572896 | tf_op jit(solution)/shard_map/ppermute | solution.py:1179
  189.9 2.0 slice_reduce_fusion
  192.6 0.7 slice_bitcast_fusion.1
  193.5 87.5 %all-gather.6.cloned.1.call-done.right_ref.out_w_ref = bf16[2048,2048]{1,0:T(8,128)(2,1)} async-done(((bf16[64,2048]{1,0:T(8,128)(2,1)}), bf16[2048,2048]{1,0:T(8,128)(2,1)}) %all-gather.6.cloned.1.call-update) | async-done | bytes 8388624 | tf_op jit(solution)/shard_map/all_gather | solution.py:1258
  281.6 95.5 %attention_branch.1 = (f32[256,2048]{1,0:T(8,128)}, bf16[2048,2048]{1,0:T(8,128)(2,1)}, f32[8,128]{1,0:T(8,128)}, bf16[32,64,1024]{2,1,0:T(8,128)(2,1)}, bf16[32...) custom-call(bf16[2048,256]{1,0:T(8,128)(2,1)} %get-tuple-element.148.left_ref, ...), custom_call_target="tpu_custom_call" | custom-call | flops 2147483648 | bytes 300000000 | tf_op jit(solution)/shard_map/attention_branch/pallas_call | solution.py:805
  377.1 1.6 collective-permute-start.3
  378.6 2.5 bitcast_dynamic-update-slice_fusion.1
  381.1 14.6 %fusion.6 = f32[2048,1024]{1,0:T(8,128)} fusion(bf16[2048,2048]{1,0:T(8,128)(2,1)} %get-tuple-element.104.normed_ref, bf16[2048,1024]{1,0:T(8,128)(2,1)} %bitcast.90), kind=kOutput, calls=%fused_computation.41 | convolution fusion | flops 8589934592 | bytes 20971520 | tf_op jit(solution)/shard_map/dot_general | solution.py:30
  395.7 13.7 %multiply_convert_fusion.2 = (bf16[2048,1024]{1,0:T(8,128)(2,1)}, f32[2048,1024]{1,0:T(8,128)}) fusion(f32[2048,1024]{1,0:T(8,128)} %fusion.6, bf16[2048,2048]{1,0:T(8,128)(2,1)S(1)} %bitcast.89, bf16[2048,1024]{1,0:T(8,128)(2,1)S(1)} %bitcast.93), kind=kOutput, calls=%fused_computation.2 | convolution fusion | flops 8602517504 | bytes 33554432 | tf_op jit(solution)/shard_map/dot_general | solution.py:30
  409.4 12.7 %convolution_convert_fusion = bf16[1024,2048]{1,0:T(8,128)(2,1)S(1)} fusion(bf16[2048,1024]{1,0:T(8,128)(2,1)} %get-tuple-element.168.hidden_ref, bf16[2048,2048]{1,0:T(8,128)(2,1)} %all-gather.4.cloned.1.call-done), kind=kOutput, calls=%fused_computation.8 | convolution fusion | flops 8592031744 | bytes 16777216 | tf_op jit(solution)/shard_map/dot_general | solution.py:30
  422.2 1.2 dynamic-slice_bitcast_fusion.2
  423.9 2.3 copy-done.10
  426.3 21.7 %multiply_convert_fusion = (bf16[2048,1024]{1,0:T(8,128)(2,1)}, bf16[2048,1024]{1,0:T(8,128)(2,1)}) fusion(f32[2048,1024]{1,0:T(8,128)} %fusion.6, f32[2048,1024]{1,0:T(8,128)} %get-tuple-element.169, bf16[2048,2048]{1,0:T(8,128)(2,1)} %all-gather.4.cloned.1.call-done, bf16[1024,2048]{1,0:T(8,128)(2,1)S(1)} %bitcast.71), kind=kOutput, calls=%fused_computation | convolution fusion | flops 8617197568 | bytes 37748736 | tf_op jit(solution)/shard_map/dot_general | solution.py:30
  448.5 2.6 fusion.5.refs_1_
  451.0 105.3 %ffn_back.1 = (f32[256,2048]{1,0:T(8,128)}, bf16[256,2048]{1,0:T(8,128)(2,1)}, bf16[2048,256]{1,0:T(8,128)(2,1)}, bf16[2048,1024]{1,0:T(8,128)(2,1)}, bf16[4,256...) custom-call(bf16[2048,1024]{1,0:T(8,128)(2,1)} %get-tuple-element.11, ...), custom_call_target="tpu_custom_call" | custom-call | flops 51539607552 | bytes 200000000 | tf_op jit(solution)/shard_map/ffn_back/pallas_call | solution.py:979
  556.5 3.2 add_convert_fusion
  559.8 38.7 %attend_backward.2 = (bf16[2048,384]{1,0:T(8,128)(2,1)}, bf16[2048,384]{1,0:T(8,128)(2,1)}) custom-call(bf16[2,2048,128]{2,1,0:T(8,128)(2,1)} %get-tuple-element.90.q_ref, bf16[2,2048,128]{2,1,0:T(8,128)(2,1)} %get-tuple-element.91.k_ref, bf16[2,2048,128]{2,1,0:T(8,128)(2,1)} %get-tuple-element.92.v_ref, bf16[2048,256]{1,0:T(8,128)(2,1)} %get-tuple-element.126.grad_ref, ...), custom_call_target="tpu_custom_call" | custom-call | flops 24696061952 | bytes 100000000 | tf_op jit(solution)/shard_map/attend_backward/pallas_call | solution.py:195
  598.6 9.3 %collective-permute-done.5 = bf16[2,2,2,64,1024]{4,3,2,1,0:T(8,128)(2,1)S(1)} collective-permute-done((bf16[2,2,2,64,1024]{4,3,2,1,0:T(8,128)(2,1)S(1)}, bf16[2,2,2,64,1024]{4,3,2,1,0:T(8,128)(2,1)S(1)}, u32[]{:S(2)}, u32[]{:S(2)}) %collective-permute-start.5) | collective-permute-done | bytes 1048608 | tf_op jit(solution)/shard_map/ppermute | solution.py:1179
  607.9 1.4 fusion.4
  609.6 1.8 dynamic-slice_bitcast_fusion
  611.5 1.2 collective-permute-start.6
  612.7 37.3 %attend_backward.3 = (bf16[2048,384]{1,0:T(8,128)(2,1)}, bf16[2048,384]{1,0:T(8,128)(2,1)}) custom-call(bf16[2,2048,128]{2,1,0:T(8,128)(2,1)} %get-tuple-element.90.q_ref, bf16[2,2048,128]{2,1,0:T(8,128)(2,1)} %get-tuple-element.91.k_ref, bf16[2,2048,128]{2,1,0:T(8,128)(2,1)} %get-tuple-element.92.v_ref, bf16[2048,256]{1,0:T(8,128)(2,1)} %get-tuple-element.126.grad_ref, ...), custom_call_target="tpu_custom_call" | custom-call | flops 24696061952 | bytes 100000000 | tf_op jit(solution)/shard_map/attend_backward/pallas_call | solution.py:195
  650.0 9.5 %collective-permute-done.6 = bf16[2,2,2,2,64,1024]{5,4,3,2,1,0:T(8,128)(2,1)} collective-permute-done((bf16[2,2,2,2,64,1024]{5,4,3,2,1,0:T(8,128)(2,1)S(1)}, bf16[2,2,2,2,64,1024]{5,4,3,2,1,0:T(8,128)(2,1)}, u32[]{:S(2)}, u32[]{:S(2)}) %collective-permute-start.6) | collective-permute-done | bytes 2097184 | tf_op jit(solution)/shard_map/ppermute | solution.py:1179
  659.5 2.7 fusion.1
  662.9 1.6 constant_dynamic-slice_fusion
  664.5 111.1 %last_sums.1 = (f32[256,2048]{1,0:T(8,128)}, bf16[256,2048]{1,0:T(8,128)(2,1)}, bf16[8,64,1024]{2,1,0:T(8,128)(2,1)}, bf16[8,64,1024]{2,1,0:T(8,128)(2,1)}) custom-call(bf16[2048,384]{1,0:T(8,128)(2,1)} %get-tuple-element.125.left_ref, bf16[2048,384]{1,0:T(8,128)(2,1)} %get-tuple-element.130.other_ref, bf16[2048,768]{1,0:T(8,128)(2,1)} %bitcast.81, ...), custom_call_target="tpu_custom_call" | custom-call | flops 805306368 | bytes 300000000 | tf_op jit(solution)/shard_map/last_sums/pallas_call | solution.py:1062
  775.6 6.8 convolution_convert_fusion.1
  783.3 1.2 divide_sqrt_fusion
  784.6 0.9 multiply_convert_fusion.3
  785.5 3.9 fusion.2
  789.4 2.9 fusion.3.refs_2_
  792.3 28.3 %exchange.1 = (bf16[8,64,384]{2,1,0:T(8,128)(2,1)}, bf16[8,64,384]{2,1,0:T(8,128)(2,1)}, bf16[8,64,1024]{2,1,0:T(8,128)(2,1)}) custom-call(bf16[8,64,384]{2,1,0:T(8,128)(2,1)} %bitcast.82, bf16[8,64,384]{2,1,0:T(8,128)(2,1)} %bitcast.83, bf16[8,64,1024]{2,1,0:T(8,128)(2,1)} %fusion.3.refs_2_), custom_call_target="tpu_custom_call" | custom-call | flops 1000000 | bytes 40000000 | tf_op jit(solution)/shard_map/exchange/pallas_call | solution.py:1108
  820.7 1.2 copy-done.5
  821.9 1.2 copy-done.6
  823.2 1.0 copy-done.7
  824.1 1.0 copy-done.8
  825.1 3.2 home.1
  828.4 1.9 convert_element_type.149
  830.3 2.3 copy.44
  832.6 1.3 copy.45
  (87 shorter events, 5.3 us)
Async XLA Ops:
  7.2 273.8 %all-gather.6.cloned.1.call-start = ((), (), s32[]{:S(2)}) async-start(), calls=%async_computation.4 | async-start | bytes 8650752 | tf_op jit(solution)/shard_map/all_gather | solution.py:1258
  110.4 299.0 %all-gather.4.cloned.1.call-start = ((), (), s32[]{:S(2)}) async-start(), calls=%async_computation.3 | async-start | bytes 9437184 | tf_op jit(solution)/shard_map/all_gather | solution.py:1304
  110.5 79.2 %collective-permute-start = (bf16[16,64,1024]{2,1,0:T(8,128)(2,1)}, bf16[16,64,1024]{2,1,0:T(8,128)(2,1)S(1)}, u32[]{:S(2)}, u32[]{:S(2)}) collective-permute-start(bf16[16,64,1024]{2,1,0:T(8,128)(2,1)} %get-tuple-element.93.refs_0_), channel_id=1, source_target_pairs={{0,4},{1,5},{2,6},{3,7},{4,0},{5,1},{6,2},{7,3},{8,12},{9,13},{10,... | collective-permute-start | bytes 6291464 | tf_op jit(solution)/shard_map/ppermute | solution.py:1179
  114.6 75.0 %collective-permute-start.1 = (bf16[12,64,1024]{2,1,0:T(8,128)(2,1)}, bf16[12,64,1024]{2,1,0:T(8,128)(2,1)}, u32[]{:S(2)}, u32[]{:S(2)}) collective-permute-start(bf16[12,64,1024]{2,1,0:T(8,128)(2,1)} %slice.19), channel_id=1, source_target_pairs={{0,16},{1,17},{2,18},{3,19},{4,20},{5,21},{6,22},{7,23},{8,24},{9,... | collective-permute-start | bytes 4718600 | tf_op jit(solution)/shard_map/ppermute | solution.py:1179
  115.5 1.4 copy-start.18
  116.8 72.9 %copy-start.14 = (bf16[256,2048]{1,0:T(8,128)(2,1)S(1)}, bf16[256,2048]{1,0:T(8,128)(2,1)}, u32[]{:S(2)}) copy-start(bf16[256,2048]{1,0:T(8,128)(2,1)} %refs_3_.1) | copy-start | bytes 3145732
  189.6 92.0 %copy-start.15 = (bf16[16,64,1024]{2,1,0:T(8,128)(2,1)}, bf16[16,64,1024]{2,1,0:T(8,128)(2,1)S(1)}, u32[]{:S(2)}) copy-start(bf16[16,64,1024]{2,1,0:T(8,128)(2,1)S(1)} %collective-permute-done.refs_1_) | copy-start | bytes 6291460
  189.6 419.9 %all-gather.8.cloned.1.call-start = ((), (), s32[]{:S(2)}) async-start(), calls=%async_computation.5 | async-start | bytes 9437184 | tf_op jit(solution)/shard_map/all_gather | solution.py:1340
  189.7 187.4 %collective-permute-start.2 = (bf16[256,2048]{1,0:T(8,128)(2,1)S(1)}, bf16[256,2048]{1,0:T(8,128)(2,1)}, u32[]{:S(2)}, u32[]{:S(2)}) collective-permute-start(bf16[256,2048]{1,0:T(8,128)(2,1)S(1)} %copy-done.14), channel_id=1, source_target_pairs={{0,16},{1,17},{2,18},{3,19},{4,20},{5,21},{6,22},{7,23},{8,24},{9,... | collective-permute-start | bytes 3145736 | tf_op jit(solution)/shard_map/ppermute | solution.py:1179
  377.1 46.8 %collective-permute-start.3 = (bf16[256,2048]{1,0:T(8,128)(2,1)}, bf16[256,2048]{1,0:T(8,128)(2,1)S(1)}, u32[]{:S(2)}, u32[]{:S(2)}) collective-permute-start(bf16[256,2048]{1,0:T(8,128)(2,1)} %collective-permute-done.2), channel_id=1, source_target_pairs={{0,4},{1,5},{2,6},{3,7},{4,0},{5,1},{6,2},{7,3},{8,12},{9,13},{10,... | collective-permute-start | bytes 3145736 | tf_op jit(solution)/shard_map/ppermute | solution.py:1179
  378.6 17.1 %slice-start = ((s8[8388608]{0:T(1024)(128)(4,1)}), s8[4194304]{0:T(1024)(128)(4,1)S(1)}, s32[]{:S(2)}) async-start(s8[8388608]{0:T(1024)(128)(4,1)} %bitcast.88), calls=%async_computation.9 | async-start | bytes 8388608
  381.1 14.6 %slice-start.1 = ((s8[8388608]{0:T(1024)(128)(4,1)}), s8[4194304]{0:T(1024)(128)(4,1)S(1)}, s32[]{:S(2)}) async-start(s8[8388608]{0:T(1024)(128)(4,1)} %bitcast.88), calls=%async_computation.10 | async-start | bytes 8388608
  381.1 14.6 %copy-start.19 = (bf16[32,64,1024]{2,1,0:T(8,128)(2,1)S(1)}, bf16[32,64,1024]{2,1,0:T(8,128)(2,1)}, u32[]{:S(2)}) copy-start(bf16[32,64,1024]{2,1,0:T(8,128)(2,1)} %get-tuple-element.106) | copy-start | bytes 12582916
  422.1 4.2 copy-start.13
  422.1 4.1 copy-start.10
  423.3 25.1 %collective-permute-start.4 = (bf16[256,2048]{1,0:T(8,128)(2,1)S(1)}, bf16[256,2048]{1,0:T(8,128)(2,1)S(1)}, u32[]{:S(2)}, u32[]{:S(2)}) collective-permute-start(bf16[256,2048]{1,0:T(8,128)(2,1)S(1)} %get-tuple-element.163), channel_id=1, source_target_pairs={{0,4},{1,5},{2,6},{3,7},{4,0},{5,1},{6,2},{7,3},{8,12},{9,13},{10,... | collective-permute-start | bytes 3145736 | tf_op jit(solution)/shard_map/ppermute | solution.py:1179
  426.3 21.7 %copy-start.11 = (bf16[4,256,2048]{2,1,0:T(8,128)(2,1)}, bf16[4,256,2048]{2,1,0:T(8,128)(2,1)S(1)}, u32[]{:S(2)}) copy-start(bf16[4,256,2048]{2,1,0:T(8,128)(2,1)S(1)} %bitcast_dynamic-update-slice_fusion) | copy-start | bytes 12582916
  556.4 108.1 %reduce-scatter.4.cloned.1.call-start = ((), (), s32[]{:S(2)}) async-start(), calls=%async_computation.6 | async-start | bytes 1966080 | tf_op jit(solution)/shard_map/reduce_scatter | solution.py:1185
  559.8 48.1 %collective-permute-start.5 = (bf16[2,2,2,64,1024]{4,3,2,1,0:T(8,128)(2,1)S(1)}, bf16[2,2,2,64,1024]{4,3,2,1,0:T(8,128)(2,1)S(1)}, u32[]{:S(2)}, u32[]{:S(2)}) collective-permute-start(bf16[2,2,2,64,1024]{4,3,2,1,0:T(8,128)(2,1)S(1)} %dynamic-slice_bitcast_fusion.1), channel_id=1, source_target_pairs={{0,16},{1,17},{2,18},{3,19},{4,20},{5,21},{6,22},{7,23},{8,24},{9,... | collective-permute-start | bytes 3145736 | tf_op jit(solution)/shard_map/ppermute | solution.py:1179
  609.6 182.7 %reduce-scatter.6.cloned.1.call-start = ((), (), s32[]{:S(2)}) async-start(), calls=%async_computation.7 | async-start | bytes 1966080 | tf_op jit(solution)/shard_map/reduce_scatter | solution.py:1185
  611.5 48.0 %copy-start.12 = (bf16[2048,1024]{1,0:T(8,128)(2,1)S(1)}, bf16[2048,1024]{1,0:T(8,128)(2,1)}, u32[]{:S(2)}) copy-start(bf16[2048,1024]{1,0:T(8,128)(2,1)} %get-tuple-element.129) | copy-start | bytes 12582916
  611.5 48.0 %collective-permute-start.6 = (bf16[2,2,2,2,64,1024]{5,4,3,2,1,0:T(8,128)(2,1)S(1)}, bf16[2,2,2,2,64,1024]{5,4,3,2,1,0:T(8,128)(2,1)}, u32[]{:S(2)}, u32[]{:S(2)}) collective-permute-start(bf16[2,2,2,2,64,1024]{5,4,3,2,1,0:T(8,128)(2,1)S(1)} %dynamic-slice_bitcast_fusion), channel_id=1, source_target_pairs={{0,4},{1,5},{2,6},{3,7},{4,0},{5,1},{6,2},{7,3},{8,12},{9,13},{10,... | collective-permute-start | bytes 6291464 | tf_op jit(solution)/shard_map/ppermute | solution.py:1179
  650.0 12.3 %copy-start.17 = (f32[32,64]{1,0:T(8,128)S(1)}, f32[32,64]{1,0:T(8,128)}, u32[]{:S(2)}) copy-start(f32[32,64]{1,0:T(8,128)} %get-tuple-element.156) | copy-start | bytes 24580
  662.2 166.2 %reduce-scatter.8.cloned.1.call-start = ((), (), s32[]{:S(2)}) async-start(), calls=%async_computation.8 | async-start | bytes 1310720 | tf_op jit(solution)/shard_map/reduce_scatter | solution.py:1185
  664.5 111.1 %copy-start.9 = (bf16[2048,256]{1,0:T(8,128)(2,1)S(1)}, bf16[2048,256]{1,0:T(8,128)(2,1)}, u32[]{:S(2)}) copy-start(bf16[2048,256]{1,0:T(8,128)(2,1)} %get-tuple-element.148.left_ref) | copy-start | bytes 3145732
  775.6 6.8 copy-start.20
  775.6 6.9 copy-start.21
  775.6 9.0 %copy-start.2 = (bf16[64,2048]{1,0:T(8,128)(2,1)S(1)}, bf16[64,2048]{1,0:T(8,128)(2,1)}, u32[]{:S(2)}) copy-start(bf16[64,2048]{1,0:T(8,128)(2,1)} %refs_4_.1) | copy-start | bytes 786436
  775.6 9.0 %copy-start.3 = (bf16[64,2048]{1,0:T(8,128)(2,1)S(1)}, bf16[64,2048]{1,0:T(8,128)(2,1)}, u32[]{:S(2)}) copy-start(bf16[64,2048]{1,0:T(8,128)(2,1)} %refs_5_.1) | copy-start | bytes 786436
  785.5 35.2 %copy-start = (bf16[64,8192]{1,0:T(8,128)(2,1)S(1)}, bf16[64,8192]{1,0:T(8,128)(2,1)}, u32[]{:S(2)}) copy-start(bf16[64,8192]{1,0:T(8,128)(2,1)} %refs_7_.1) | copy-start | bytes 3145732
  785.5 35.2 %copy-start.1 = (bf16[64,8192]{1,0:T(8,128)(2,1)S(1)}, bf16[64,8192]{1,0:T(8,128)(2,1)}, u32[]{:S(2)}) copy-start(bf16[64,8192]{1,0:T(8,128)(2,1)} %refs_8_.1) | copy-start | bytes 3145732
  785.5 35.2 %copy-start.4 = (bf16[64,2048]{1,0:T(8,128)(2,1)S(1)}, bf16[64,2048]{1,0:T(8,128)(2,1)}, u32[]{:S(2)}) copy-start(bf16[64,2048]{1,0:T(8,128)(2,1)} %refs_6_.1) | copy-start | bytes 786436
  820.7 1.2 copy-start.5
  821.9 1.2 copy-start.6
  823.2 1.0 copy-start.7
  824.1 1.0 copy-start.8
  828.4 4.2 copy-start.16
Sparse Core Ops, SparseCore 0:
  110.5 170.4 all-gather.5
  282.6 74.1 all-gather.3
  556.5 52.9 all-gather.7
  612.3 35.2 reduce-scatter.3
  662.3 64.6 reduce-scatter.5
  782.5 35.4 reduce-scatter.7

commit v8 on v7

--- a/solution.py
+++ b/solution.py
@@ -748,11 +748,9 @@
     if carry:
         for copy in early_yz:
             copy.start()
-    heads = landed.shape[2] // HEAD_DIM
+    share = landed.shape[2]
     for b in range(team):
-        for g in range(heads):
-            first = (g * team + b) * HEAD_DIM
-            together[:, first : first + HEAD_DIM] = landed[b, :, g * HEAD_DIM : (g + 1) * HEAD_DIM]
+        together[:, b * share : (b + 1) * share] = landed[b]
     tile = 512
 
     @pl.loop(0, own.shape[1] // tile)
@@ -926,12 +924,10 @@
     residual = cot_ref[...].astype(f32) + norm_back(h2_ref[...], gain_ref[...], total[...])
     residual_ref[...] = residual
     branch_ref[...] = residual.astype(bf16)
-    tile, share = team * HEAD_DIM, width // team
-    for g in range(width // tile):
-        heads = contract(branch_ref[...], out_w_ref[g * tile : (g + 1) * tile, :], 1, 1).astype(bf16)
-        for b in range(team):
-            first = b * share + g * HEAD_DIM
-            to_core[0, :, first : first + HEAD_DIM] = heads[:, b * HEAD_DIM : (b + 1) * HEAD_DIM]
+    share = width // team
+    for b in range(team):
+        part = slice(b * share, (b + 1) * share)
+        to_core[0, :, part] = contract(branch_ref[...], out_w_ref[part, :], 1, 1).astype(bf16)
     own_place = mates[0][1]
     own_rows = pl.ds(pl.multiple_of(own_place * block, block), block)
     def heads_of(place):
@@ -1254,8 +1250,12 @@
     blocks = lax.dynamic_slice_in_dim(gathered, device - mate, team, 0)
     blocks = blocks[:, 1 : 1 + tok_rows // 128].astype(jnp.int32).reshape(SEQ)
     row_blocks, col_blocks = blocks.reshape(1, SEQ), blocks.reshape(SEQ, 1)
-    both_mine, qkv_w, out_mine = tie(both_mine, qkv_w, w_out)
-    out_w = lax.all_gather(out_mine, AXIS, axis=0, tiled=True)
+    if weight_rows == HEAD_DIM:
+        both_mine, qkv_w, out_mine = tie(both_mine, qkv_w, gather_across(w_out))
+        out_w = lax.all_gather(out_mine, AXIS, axis=0, tiled=True, axis_index_groups=in_team)
+    else:
+        out_w = lax.all_gather(w_out, AXIS, axis=0, tiled=True)
+        out_w = out_w.reshape(heads, team, HEAD_DIM, width).transpose(1, 0, 2, 3).reshape(width, width)
 
     def whole_rows(mine):
         shape = row_shape + (weight_rows, ff_cols)

time: 845 us -> 793 us (0.938)
  waiting for transfers between devices: 137 us -> 60.1 us
  Pallas kernels: 563 us -> 588 us
    all_gather x1 -> x2, waiting for transfers between devices: 87.5 us -> 0.03 us  [the longest x1 0.02 us: gather_across(): return lax.all_gather(x, AXIS, axis=0, tiled=True, axis_index_groups=across)]
    pallas_call x1, Pallas kernels: 95.5 us -> 114 us  [branch(): pl.pallas_call(functools.partial(branch_kernel, bool(carry), swap_bits, s...]
    pallas_call x1, Pallas kernels: 101 us -> 111 us  [front(): pl.pallas_call(functools.partial(front_kernel, team, teams, qkv_moves, ff...]
  transfers between devices with their start and end apart: 13 -> 14, of which waited for: 6 -> 6; matrix products, arithmetic and copies ran while one was open for 12% -> 12% of each run, Pallas kernels for 42% -> 62%
where the time goes in v8:
time: 793 us; the launch traced here: 789 us
  Pallas kernels  588 us (74%)
  matrix products  69.9 us (9%)
  waiting for transfers between devices  60.1 us (8%)
  local copies, waits for them, and re-layouts  24.6 us (3%)
  other arithmetic  22.4 us (3%)
  between operations  15.4 us (2%)
  starting transfers between devices  9.39 us (1%)
    pallas_call x1, Pallas kernels, branch(): pl.pallas_call(functools.partial(branch_kernel, bool(carry), swap_bits, s...  114 us
    pallas_call x1, Pallas kernels, front(): pl.pallas_call(functools.partial(front_kernel, team, teams, qkv_moves, ff...  111 us
    pallas_call x1, Pallas kernels, last_sums(): pl.pallas_call(functools.partial(last_sums_kernel, carry_bits, sum_bits,...  111 us
    pallas_call x1, Pallas kernels, ffn_back(): pl.pallas_call(functools.partial(ffn_back_kernel, cross, sum_bits, swap_b...  101 us
    pallas_call x2, Pallas kernels, attend_backward(): pl.pallas_call(functools.partial(attend_backward_kernel, 2 * pair), grid=...  75.2 us
    dot_general x5, matrix products, contract(): lax.dot_general(left, right, (((left_dim,), (right_dim,)), ((), ())), pre...  69.9 us
    ppermute x7, waiting for transfers between devices, flip(): return lax.ppermute(x, AXIS, [(i, i ^ bit) for i in range(devices)])  53.9 us
    pallas_call x1, Pallas kernels, attend_forward(): pl.pallas_call(attend_forward_kernel, out_shape=(shape((pairs, length, PA...  42.9 us
  transfers between devices with their start and end apart: 14, of which 6 were waited for; matrix products, arithmetic and copies ran while one was open for 12% of the time, Pallas kernels for 62%

profile of v8, /device:TPU:0, one launch (start us, length us, event | category | flops | bytes accessed | tf_op | source)
XLA Modules:
  0.0 789.4 jit_solution(2530247049588157617)
XLA Ops:
  10.1 111.1 %front.1 = (bf16[2048,2048]{1,0:T(8,128)(2,1)}, bf16[4,512,768]{2,1,0:T(8,128)(2,1)}, bf16[16,64,1024]{2,1,0:T(8,128)(2,1)}, f32[32,8,128]{2,1,0:T(8,128)}, bf16[256,2048]{1,0:T(8,128)(2,1)}) custom-call(bf16[256,2048]{1,0:T(8,128)(2,1)} %tokens_ref.3, bf16[64,2048]{1,0:T(8,128)(2,1)} %refs_4_.1, bf16[64,2048]{1,0:T(8,128)(2,1)} %refs_5_.1, ...), custom_call_target="tpu_custom_call" | custom-call | bytes 200000000 | tf_op jit(solution)/shard_map/front/pallas_call | solution.py:640
  121.4 0.8 dynamic-slice_convert_fusion
  122.1 1.3 copy.32.col_ref
  123.5 1.4 collective-permute-start
  124.9 1.7 slice.19
  126.7 42.9 %attend_forward.1 = (bf16[2,2048,128]{2,1,0:T(8,128)(2,1)}, bf16[2,2048,128]{2,1,0:T(8,128)(2,1)}, bf16[2,2048,128]{2,1,0:T(8,128)(2,1)}, bf16[2048,256]{1,0:T(8...) custom-call(bf16[2048,2048]{1,0:T(8,128)(2,1)} %get-tuple-element.85.normed_ref, bf16[2048,768]{1,0:T(8,128)(2,1)} %bitcast.78, ...), custom_call_target="tpu_custom_call" | custom-call | flops 23622320128 | bytes 100000000 | tf_op jit(solution)/shard_map/attend_forward/pallas_call | solution.py:124
  169.6 25.3 %collective-permute-done.1.refs_2_ = bf16[12,64,1024]{2,1,0:T(8,128)(2,1)S(1)} collective-permute-done((bf16[12,64,1024]{2,1,0:T(8,128)(2,1)S(1)}, bf16[12,64,1024]{2,1,0:T(8,128)(2,1)S(1)}, u32[]{:S(2)}, u32[]{:S(2)}) %collective-permute-start.1) | collective-permute-done | bytes 1572896 | tf_op jit(solution)/shard_map/ppermute | solution.py:1175
  194.9 8.9 %collective-permute-done.refs_1_ = bf16[16,64,1024]{2,1,0:T(8,128)(2,1)S(1)} collective-permute-done((bf16[16,64,1024]{2,1,0:T(8,128)(2,1)}, bf16[16,64,1024]{2,1,0:T(8,128)(2,1)S(1)}, u32[]{:S(2)}, u32[]{:S(2)}) %collective-permute-start) | collective-permute-done | bytes 2097184 | tf_op jit(solution)/shard_map/ppermute | solution.py:1175
  204.0 2.0 slice_reduce_fusion
  208.2 114.4 %attention_branch.1 = (f32[256,2048]{1,0:T(8,128)}, bf16[2048,2048]{1,0:T(8,128)(2,1)}, f32[8,128]{1,0:T(8,128)}, bf16[32,64,1024]{2,1,0:T(8,128)(2,1)}, bf16[32...) custom-call(bf16[2048,256]{1,0:T(8,128)(2,1)} %get-tuple-element.148.left_ref, ...), custom_call_target="tpu_custom_call" | custom-call | flops 2147483648 | bytes 300000000 | tf_op jit(solution)/shard_map/attention_branch/pallas_call | solution.py:803
  322.6 1.7 collective-permute-start.3
  324.3 14.6 %fusion.6 = f32[2048,1024]{1,0:T(8,128)} fusion(bf16[2048,2048]{1,0:T(8,128)(2,1)} %get-tuple-element.104.normed_ref, bf16[2048,1024]{1,0:T(8,128)(2,1)} %bitcast.86), kind=kOutput, calls=%fused_computation.41 | convolution fusion | flops 8589934592 | bytes 20971520 | tf_op jit(solution)/shard_map/dot_general | solution.py:30
  338.8 13.7 %multiply_convert_fusion.2 = (bf16[2048,1024]{1,0:T(8,128)(2,1)}, f32[2048,1024]{1,0:T(8,128)}) fusion(f32[2048,1024]{1,0:T(8,128)} %fusion.6, bf16[2048,2048]{1,0:T(8,128)(2,1)S(1)} %copy-done.18, bf16[2048,1024]{1,0:T(8,128)(2,1)S(1)} %bitcast.89), kind=kOutput, calls=%fused_computation.2 | convolution fusion | flops 8602517504 | bytes 33554432 | tf_op jit(solution)/shard_map/dot_general | solution.py:30
  352.5 2.3 bitcast_dynamic-update-slice_fusion.1
  354.9 1.1 bitcast_dynamic-update-slice_fusion
  356.0 12.7 %convolution_convert_fusion = bf16[1024,2048]{1,0:T(8,128)(2,1)S(1)} fusion(bf16[2048,1024]{1,0:T(8,128)(2,1)} %get-tuple-element.168.hidden_ref, bf16[2048,2048]{1,0:T(8,128)(2,1)} %all-gather.7.cloned.1.call-done), kind=kOutput, calls=%fused_computation.8 | convolution fusion | flops 8592031744 | bytes 16777216 | tf_op jit(solution)/shard_map/dot_general | solution.py:30
  368.7 1.3 dynamic-slice_bitcast_fusion.2
  370.4 22.3 %multiply_convert_fusion = (bf16[2048,1024]{1,0:T(8,128)(2,1)}, bf16[2048,1024]{1,0:T(8,128)(2,1)}) fusion(f32[2048,1024]{1,0:T(8,128)} %fusion.6, f32[2048,1024]{1,0:T(8,128)} %get-tuple-element.169, bf16[2048,2048]{1,0:T(8,128)(2,1)} %all-gather.7.cloned.1.call-done, bf16[1024,2048]{1,0:T(8,128)(2,1)} %bitcast.12.down_ref), kind=kOutput, calls=%fused_computation | convolution fusion | flops 8617197568 | bytes 37748736 | tf_op jit(solution)/shard_map/dot_general | solution.py:30
  392.7 2.4 collective-permute-done.4
  395.1 1.4 fusion.5.refs_1_
  396.5 101.4 %ffn_back.1 = (f32[256,2048]{1,0:T(8,128)}, bf16[256,2048]{1,0:T(8,128)(2,1)}, bf16[2048,256]{1,0:T(8,128)(2,1)}, bf16[2048,1024]{1,0:T(8,128)(2,1)}, bf16[4,256...) custom-call(bf16[2048,1024]{1,0:T(8,128)(2,1)} %get-tuple-element.11, ...), custom_call_target="tpu_custom_call" | custom-call | flops 51539607552 | bytes 200000000 | tf_op jit(solution)/shard_map/ffn_back/pallas_call | solution.py:975
  497.9 3.2 add_convert_fusion
  501.2 4.2 collective-permute-start.5
  505.4 37.9 %attend_backward.2 = (bf16[2048,384]{1,0:T(8,128)(2,1)}, bf16[2048,384]{1,0:T(8,128)(2,1)}) custom-call(bf16[2,2048,128]{2,1,0:T(8,128)(2,1)} %get-tuple-element.90.q_ref, bf16[2,2048,128]{2,1,0:T(8,128)(2,1)} %get-tuple-element.91.k_ref, bf16[2,2048,128]{2,1,0:T(8,128)(2,1)} %get-tuple-element.92.v_ref, bf16[2048,256]{1,0:T(8,128)(2,1)} %get-tuple-element.126.grad_ref, ...), custom_call_target="tpu_custom_call" | custom-call | flops 24696061952 | bytes 100000000 | tf_op jit(solution)/shard_map/attend_backward/pallas_call | solution.py:195
  543.4 7.9 collective-permute-done.5
  551.2 1.4 fusion.4
  552.6 5.3 all-gather.11.cloned.1.call-done
  558.0 1.8 dynamic-slice_bitcast_fusion
  559.9 1.2 collective-permute-start.6
  561.1 37.3 %attend_backward.3 = (bf16[2048,384]{1,0:T(8,128)(2,1)}, bf16[2048,384]{1,0:T(8,128)(2,1)}) custom-call(bf16[2,2048,128]{2,1,0:T(8,128)(2,1)} %get-tuple-element.90.q_ref, bf16[2,2048,128]{2,1,0:T(8,128)(2,1)} %get-tuple-element.91.k_ref, bf16[2,2048,128]{2,1,0:T(8,128)(2,1)} %get-tuple-element.92.v_ref, bf16[2048,256]{1,0:T(8,128)(2,1)} %get-tuple-element.126.grad_ref, ...), custom_call_target="tpu_custom_call" | custom-call | flops 24696061952 | bytes 100000000 | tf_op jit(solution)/shard_map/attend_backward/pallas_call | solution.py:195
  598.4 9.5 %collective-permute-done.6 = bf16[2,2,2,2,64,1024]{5,4,3,2,1,0:T(8,128)(2,1)} collective-permute-done((bf16[2,2,2,2,64,1024]{5,4,3,2,1,0:T(8,128)(2,1)S(1)}, bf16[2,2,2,2,64,1024]{5,4,3,2,1,0:T(8,128)(2,1)}, u32[]{:S(2)}, u32[]{:S(2)}) %collective-permute-start.6) | collective-permute-done | bytes 2097184 | tf_op jit(solution)/shard_map/ppermute | solution.py:1175
  607.8 2.7 fusion.1
  611.3 1.6 constant_dynamic-slice_fusion
  612.9 111.0 %last_sums.1 = (f32[256,2048]{1,0:T(8,128)}, bf16[256,2048]{1,0:T(8,128)(2,1)}, bf16[8,64,1024]{2,1,0:T(8,128)(2,1)}, bf16[8,64,1024]{2,1,0:T(8,128)(2,1)}) custom-call(bf16[2048,384]{1,0:T(8,128)(2,1)} %get-tuple-element.125.left_ref, bf16[2048,384]{1,0:T(8,128)(2,1)} %get-tuple-element.130.other_ref, bf16[2048,768]{1,0:T(8,128)(2,1)} %bitcast.79, ...), custom_call_target="tpu_custom_call" | custom-call | flops 805306368 | bytes 300000000 | tf_op jit(solution)/shard_map/last_sums/pallas_call | solution.py:1058
  724.0 6.8 convolution_convert_fusion.1
  731.7 1.2 divide_sqrt_fusion
  733.0 0.9 multiply_convert_fusion.3
  733.9 3.9 fusion.2
  737.8 2.9 fusion.3.refs_2_
  740.7 28.4 %exchange.1 = (bf16[8,64,384]{2,1,0:T(8,128)(2,1)}, bf16[8,64,384]{2,1,0:T(8,128)(2,1)}, bf16[8,64,1024]{2,1,0:T(8,128)(2,1)}) custom-call(bf16[8,64,384]{2,1,0:T(8,128)(2,1)} %bitcast.80, bf16[8,64,384]{2,1,0:T(8,128)(2,1)} %bitcast.81, bf16[8,64,1024]{2,1,0:T(8,128)(2,1)} %fusion.3.refs_2_), custom_call_target="tpu_custom_call" | custom-call | flops 1000000 | bytes 40000000 | tf_op jit(solution)/shard_map/exchange/pallas_call | solution.py:1104
  769.1 1.2 copy-done.5
  770.3 1.2 copy-done.6
  771.6 1.0 copy-done.7
  772.5 1.0 copy-done.8
  773.5 3.2 home.1
  776.8 1.9 convert_element_type.149
  778.7 2.3 copy.44
  781.0 1.3 copy.45
  (85 shorter events, 7.2 us)
Async XLA Ops:
  7.2 114.1 %all-gather.5.cloned.1.call-start = ((), (), s32[]{:S(2)}) async-start(), calls=%async_computation.3 | async-start | bytes 1310720 | tf_op jit(solution)/shard_map/all_gather | solution.py:1178
  7.9 199.7 %all-gather.9.cloned.1.call-start = ((), (), s32[]{:S(2)}) async-start(), calls=%async_computation.5 | async-start | bytes 9437184 | tf_op jit(solution)/shard_map/all_gather | solution.py:1255
  121.3 234.7 %all-gather.7.cloned.1.call-start = ((), (), s32[]{:S(2)}) async-start(), calls=%async_computation.4 | async-start | bytes 9437184 | tf_op jit(solution)/shard_map/all_gather | solution.py:1304
  122.1 4.6 copy-start.17
  123.5 80.3 %collective-permute-start = (bf16[16,64,1024]{2,1,0:T(8,128)(2,1)}, bf16[16,64,1024]{2,1,0:T(8,128)(2,1)S(1)}, u32[]{:S(2)}, u32[]{:S(2)}) collective-permute-start(bf16[16,64,1024]{2,1,0:T(8,128)(2,1)} %get-tuple-element.93.refs_0_), channel_id=1, source_target_pairs={{0,4},{1,5},{2,6},{3,7},{4,0},{5,1},{6,2},{7,3},{8,12},{9,13},{10,... | collective-permute-start | bytes 6291464 | tf_op jit(solution)/shard_map/ppermute | solution.py:1175
  126.6 68.3 %collective-permute-start.1 = (bf16[12,64,1024]{2,1,0:T(8,128)(2,1)S(1)}, bf16[12,64,1024]{2,1,0:T(8,128)(2,1)S(1)}, u32[]{:S(2)}, u32[]{:S(2)}) collective-permute-start(bf16[12,64,1024]{2,1,0:T(8,128)(2,1)S(1)} %slice.19), channel_id=1, source_target_pairs={{0,16},{1,17},{2,18},{3,19},{4,20},{5,21},{6,22},{7,23},{8,24},{9,... | collective-permute-start | bytes 4718600 | tf_op jit(solution)/shard_map/ppermute | solution.py:1175
  126.7 77.1 %copy-start.12 = (bf16[256,2048]{1,0:T(8,128)(2,1)S(1)}, bf16[256,2048]{1,0:T(8,128)(2,1)}, u32[]{:S(2)}) copy-start(bf16[256,2048]{1,0:T(8,128)(2,1)} %refs_3_.1) | copy-start | bytes 3145732
  194.9 8.9 %copy-start.15 = (bf16[12,64,1024]{2,1,0:T(8,128)(2,1)}, bf16[12,64,1024]{2,1,0:T(8,128)(2,1)S(1)}, u32[]{:S(2)}) copy-start(bf16[12,64,1024]{2,1,0:T(8,128)(2,1)S(1)} %collective-permute-done.1.refs_2_) | copy-start | bytes 4718596
  203.8 4.4 copy-start.13
  203.8 354.2 %all-gather.11.cloned.1.call-start = ((), (), s32[]{:S(2)}) async-start(), calls=%async_computation.6 | async-start | bytes 9437184 | tf_op jit(solution)/shard_map/all_gather | solution.py:1340
  203.9 118.7 %collective-permute-start.2 = (bf16[256,2048]{1,0:T(8,128)(2,1)S(1)}, bf16[256,2048]{1,0:T(8,128)(2,1)}, u32[]{:S(2)}, u32[]{:S(2)}) collective-permute-start(bf16[256,2048]{1,0:T(8,128)(2,1)S(1)} %copy-done.12), channel_id=1, source_target_pairs={{0,16},{1,17},{2,18},{3,19},{4,20},{5,21},{6,22},{7,23},{8,24},{9,... | collective-permute-start | bytes 3145736 | tf_op jit(solution)/shard_map/ppermute | solution.py:1175
  322.6 32.2 %collective-permute-start.3 = (bf16[256,2048]{1,0:T(8,128)(2,1)}, bf16[256,2048]{1,0:T(8,128)(2,1)S(1)}, u32[]{:S(2)}, u32[]{:S(2)}) collective-permute-start(bf16[256,2048]{1,0:T(8,128)(2,1)} %collective-permute-done.2), channel_id=1, source_target_pairs={{0,4},{1,5},{2,6},{3,7},{4,0},{5,1},{6,2},{7,3},{8,12},{9,13},{10,... | collective-permute-start | bytes 3145736 | tf_op jit(solution)/shard_map/ppermute | solution.py:1175
  324.3 14.6 %copy-start.18 = (bf16[2048,2048]{1,0:T(8,128)(2,1)S(1)}, bf16[2048,2048]{1,0:T(8,128)(2,1)}, u32[]{:S(2)}) copy-start(bf16[2048,2048]{1,0:T(8,128)(2,1)} %get-tuple-element.104.normed_ref) | copy-start | bytes 25165828
  324.3 14.6 %copy-start.19 = (bf16[32,64,1024]{2,1,0:T(8,128)(2,1)S(1)}, bf16[32,64,1024]{2,1,0:T(8,128)(2,1)}, u32[]{:S(2)}) copy-start(bf16[32,64,1024]{2,1,0:T(8,128)(2,1)} %get-tuple-element.106) | copy-start | bytes 12582916
  368.7 26.5 %copy-start.11 = (bf16[1024,2048]{1,0:T(8,128)(2,1)}, bf16[1024,2048]{1,0:T(8,128)(2,1)S(1)}, u32[]{:S(2)}) copy-start(bf16[1024,2048]{1,0:T(8,128)(2,1)S(1)} %convolution_convert_fusion) | copy-start | bytes 12582916
  370.0 25.1 %collective-permute-start.4 = (bf16[256,2048]{1,0:T(8,128)(2,1)S(1)}, bf16[256,2048]{1,0:T(8,128)(2,1)S(1)}, u32[]{:S(2)}, u32[]{:S(2)}) collective-permute-start(bf16[256,2048]{1,0:T(8,128)(2,1)S(1)} %get-tuple-element.163), channel_id=1, source_target_pairs={{0,4},{1,5},{2,6},{3,7},{4,0},{5,1},{6,2},{7,3},{8,12},{9,13},{10,... | collective-permute-start | bytes 3145736 | tf_op jit(solution)/shard_map/ppermute | solution.py:1175
  497.9 115.0 %reduce-scatter.4.cloned.1.call-start = ((), (), s32[]{:S(2)}) async-start(), calls=%async_computation.7 | async-start | bytes 1966080 | tf_op jit(solution)/shard_map/reduce_scatter | solution.py:1181
  501.2 50.0 %collective-permute-start.5 = (bf16[2,2,2,64,1024]{4,3,2,1,0:T(8,128)(2,1)S(1)}, bf16[2,2,2,64,1024]{4,3,2,1,0:T(8,128)(2,1)S(1)}, u32[]{:S(2)}, u32[]{:S(2)}) collective-permute-start(bf16[2,2,2,64,1024]{4,3,2,1,0:T(8,128)(2,1)S(1)} %dynamic-slice_bitcast_fusion.1), channel_id=1, source_target_pairs={{0,16},{1,17},{2,18},{3,19},{4,20},{5,21},{6,22},{7,23},{8,24},{9,... | collective-permute-start | bytes 3145736 | tf_op jit(solution)/shard_map/ppermute | solution.py:1175
  558.0 182.7 %reduce-scatter.6.cloned.1.call-start = ((), (), s32[]{:S(2)}) async-start(), calls=%async_computation.8 | async-start | bytes 1966080 | tf_op jit(solution)/shard_map/reduce_scatter | solution.py:1181
  559.9 48.0 %copy-start.10 = (bf16[2048,1024]{1,0:T(8,128)(2,1)S(1)}, bf16[2048,1024]{1,0:T(8,128)(2,1)}, u32[]{:S(2)}) copy-start(bf16[2048,1024]{1,0:T(8,128)(2,1)} %get-tuple-element.129) | copy-start | bytes 12582916
  559.9 48.0 %collective-permute-start.6 = (bf16[2,2,2,2,64,1024]{5,4,3,2,1,0:T(8,128)(2,1)S(1)}, bf16[2,2,2,2,64,1024]{5,4,3,2,1,0:T(8,128)(2,1)}, u32[]{:S(2)}, u32[]{:S(2)}) collective-permute-start(bf16[2,2,2,2,64,1024]{5,4,3,2,1,0:T(8,128)(2,1)S(1)} %dynamic-slice_bitcast_fusion), channel_id=1, source_target_pairs={{0,4},{1,5},{2,6},{3,7},{4,0},{5,1},{6,2},{7,3},{8,12},{9,13},{10,... | collective-permute-start | bytes 6291464 | tf_op jit(solution)/shard_map/ppermute | solution.py:1175
  598.4 12.3 %copy-start.16 = (f32[32,64]{1,0:T(8,128)S(1)}, f32[32,64]{1,0:T(8,128)}, u32[]{:S(2)}) copy-start(f32[32,64]{1,0:T(8,128)} %get-tuple-element.156) | copy-start | bytes 24580
  610.6 166.2 %reduce-scatter.8.cloned.1.call-start = ((), (), s32[]{:S(2)}) async-start(), calls=%async_computation.9 | async-start | bytes 1310720 | tf_op jit(solution)/shard_map/reduce_scatter | solution.py:1181
  612.9 111.1 %copy-start.9 = (bf16[2048,256]{1,0:T(8,128)(2,1)S(1)}, bf16[2048,256]{1,0:T(8,128)(2,1)}, u32[]{:S(2)}) copy-start(bf16[2048,256]{1,0:T(8,128)(2,1)} %get-tuple-element.148.left_ref) | copy-start | bytes 3145732
  723.9 6.8 copy-start.20
  724.0 6.9 copy-start.21
  724.0 9.0 %copy-start.2 = (bf16[64,2048]{1,0:T(8,128)(2,1)S(1)}, bf16[64,2048]{1,0:T(8,128)(2,1)}, u32[]{:S(2)}) copy-start(bf16[64,2048]{1,0:T(8,128)(2,1)} %refs_4_.1) | copy-start | bytes 786436
  724.0 9.0 %copy-start.3 = (bf16[64,2048]{1,0:T(8,128)(2,1)S(1)}, bf16[64,2048]{1,0:T(8,128)(2,1)}, u32[]{:S(2)}) copy-start(bf16[64,2048]{1,0:T(8,128)(2,1)} %refs_5_.1) | copy-start | bytes 786436
  733.9 35.2 %copy-start = (bf16[64,8192]{1,0:T(8,128)(2,1)S(1)}, bf16[64,8192]{1,0:T(8,128)(2,1)}, u32[]{:S(2)}) copy-start(bf16[64,8192]{1,0:T(8,128)(2,1)} %refs_7_.1) | copy-start | bytes 3145732
  733.9 35.2 %copy-start.1 = (bf16[64,8192]{1,0:T(8,128)(2,1)S(1)}, bf16[64,8192]{1,0:T(8,128)(2,1)}, u32[]{:S(2)}) copy-start(bf16[64,8192]{1,0:T(8,128)(2,1)} %refs_8_.1) | copy-start | bytes 3145732
  733.9 35.2 %copy-start.4 = (bf16[64,2048]{1,0:T(8,128)(2,1)S(1)}, bf16[64,2048]{1,0:T(8,128)(2,1)}, u32[]{:S(2)}) copy-start(bf16[64,2048]{1,0:T(8,128)(2,1)} %refs_6_.1) | copy-start | bytes 786436
  769.1 1.2 copy-start.5
  770.3 1.2 copy-start.6
  771.5 1.0 copy-start.7
  772.5 1.0 copy-start.8
  776.8 4.2 copy-start.14
Sparse Core Ops, SparseCore 0:
  9.6 35.6 all-gather.4
  121.4 84.3 all-gather.8
  207.4 98.2 all-gather.6
  498.0 59.9 all-gather.10
  560.7 35.2 reduce-scatter.3
  610.7 64.6 reduce-scatter.5
  730.9 35.5 reduce-scatter.7

commit v9 on v8

--- a/solution.py
+++ b/solution.py
@@ -737,6 +737,7 @@
         up_yz = [
             carried.copy(4 + half, placed(half, (1, 0)), placed(half, (1, 0)), by_y) for half in range(early, 4)
         ]
+        down_z = carried.copy(8, down_own, down_full.at[unit(0, 0)], by_z)
         for copy in up_z + kept:
             copy.start()
 
@@ -768,6 +769,7 @@
         for over, on in zip(up_z, up_yz):
             over.wait_recv()
             on.start()
+        down_z.start()
     for k, phase in enumerate(spread[1:-1]):
         phase()
         if k < len(bits):
@@ -780,9 +782,9 @@
     if carry:
         for copy in kept:
             copy.wait()
-        for copy in early_yz + up_yz:
+        for copy in early_yz + up_yz + [down_z]:
             copy.wait_recv()
-        for copy in up_z + early_yz + up_yz:
+        for copy in up_z + early_yz + up_yz + [down_z]:
             copy.wait_send()
 
 
@@ -799,7 +801,7 @@
             shape((32,) + carry[0].shape[1:], bf16), shape((32,) + carry[0].shape[1:], bf16),
             shape((4,) + carry[3].shape, bf16),
         ]
-        scratch += [dma((8,)), dma((8,)), dma((14,))]
+        scratch += [dma((9,)), dma((9,)), dma((14,))]
     return pl.pallas_call(
         functools.partial(branch_kernel, bool(carry), swap_bits, spread_bits),
         out_shape=tuple(out_shape),
@@ -1275,20 +1277,17 @@
     )
     peaks = jnp.broadcast_to(jnp.pad(peaks, (0, 128 - head_total))[None], (8, 128))
     if carry:
-        carry[1], carry[2], attended, down_sent, cot_mine = tie(carry[1], carry[2], attended, w_down, cotangent)
-        over = flip(down_sent, 16)
+        carry[1], carry[2], attended, cot_mine = tie(carry[1], carry[2], attended, cotangent)
     after_attn, normed_ffn, peaks, *full = branch(
         attended, out_w, tokens, gain_ffn, peaks, carry, attn_bits, ffn_bits, bit_count
     )
     head_peak = peaks[0, :head_total]
-    if carry:
-        normed_ffn, over = tie(normed_ffn, over)
     if carry:
         gate_w, up_w = (w.reshape(width, ff_cols) for w in full[:2])
         z_side, y_side = (device // 16) % 2, (device // 4) % 2
-        full_down = lax.dynamic_update_slice(full[2], over[None], ((1 - z_side) * 2 + y_side, 0, 0))
+        passed = lax.dynamic_index_in_dim(full[2], (1 - z_side) * 2 + y_side, 0, True)
         down_w = lax.dynamic_update_slice(
-            full_down, flip(over, 4)[None], ((1 - z_side) * 2 + 1 - y_side, 0, 0)
+            full[2], flip(passed, 4), ((1 - z_side) * 2 + 1 - y_side, 0, 0)
         ).reshape(ff_cols, width)
     else:
         gate_w, up_w = whole_rows(both_mine[:team]), whole_rows(both_mine[team:])

time: 793 us -> 790 us (level)
    ppermute x7 -> x6, waiting for transfers between devices: 53.9 us -> 53.7 us  [flip(): return lax.ppermute(x, AXIS, [(i, i ^ bit) for i in range(devices)])]
  transfers between devices with their start and end apart: 14 -> 13, of which waited for: 6 -> 6; matrix products, arithmetic and copies ran while one was open for 12% -> 12% of each run, Pallas kernels for 62% -> 62%
where the time goes in v9:
time: 790 us; the launch traced here: 786 us
  Pallas kernels  593 us (75%)
  matrix products  70 us (9%)
  waiting for transfers between devices  54.9 us (7%)
  local copies, waits for them, and re-layouts  23.8 us (3%)
  other arithmetic  22.4 us (3%)
  between operations  15.4 us (2%)
    pallas_call x1, Pallas kernels, branch(): pl.pallas_call(functools.partial(branch_kernel, bool(carry), swap_bits, s...  115 us
    pallas_call x1, Pallas kernels, front(): pl.pallas_call(functools.partial(front_kernel, team, teams, qkv_moves, ff...  111 us
    pallas_call x1, Pallas kernels, last_sums(): pl.pallas_call(functools.partial(last_sums_kernel, carry_bits, sum_bits,...  111 us
    pallas_call x1, Pallas kernels, ffn_back(): pl.pallas_call(functools.partial(ffn_back_kernel, cross, sum_bits, swap_b...  106 us
    pallas_call x2, Pallas kernels, attend_backward(): pl.pallas_call(functools.partial(attend_backward_kernel, 2 * pair), grid=...  75.7 us
    dot_general x5, matrix products, contract(): lax.dot_general(left, right, (((left_dim,), (right_dim,)), ((), ())), pre...  70 us
    ppermute x6, waiting for transfers between devices, flip(): return lax.ppermute(x, AXIS, [(i, i ^ bit) for i in range(devices)])  53.7 us
    pallas_call x1, Pallas kernels, attend_forward(): pl.pallas_call(attend_forward_kernel, out_shape=(shape((pairs, length, PA...  42.9 us
  transfers between devices with their start and end apart: 13, of which 6 were waited for; matrix products, arithmetic and copies ran while one was open for 12% of the time, Pallas kernels for 62%

profile of v9, /device:TPU:0, one launch (start us, length us, event | category | flops | bytes accessed | tf_op | source)
XLA Modules:
  0.0 786.1 jit_solution(4414263307001510378)
XLA Ops:
  10.1 111.1 %front.1 = (bf16[2048,2048]{1,0:T(8,128)(2,1)}, bf16[4,512,768]{2,1,0:T(8,128)(2,1)}, bf16[16,64,1024]{2,1,0:T(8,128)(2,1)}, f32[32,8,128]{2,1,0:T(8,128)}, bf16[256,2048]{1,0:T(8,128)(2,1)}) custom-call(bf16[256,2048]{1,0:T(8,128)(2,1)} %tokens_ref.3, bf16[64,2048]{1,0:T(8,128)(2,1)} %refs_4_.1, bf16[64,2048]{1,0:T(8,128)(2,1)} %refs_5_.1, ...), custom_call_target="tpu_custom_call" | custom-call | bytes 200000000 | tf_op jit(solution)/shard_map/front/pallas_call | solution.py:640
  121.4 0.8 dynamic-slice_convert_fusion
  122.2 1.3 copy.32.col_ref
  123.5 1.4 collective-permute-start
  124.9 1.7 slice.19
  126.7 42.9 %attend_forward.1 = (bf16[2,2048,128]{2,1,0:T(8,128)(2,1)}, bf16[2,2048,128]{2,1,0:T(8,128)(2,1)}, bf16[2,2048,128]{2,1,0:T(8,128)(2,1)}, bf16[2048,256]{1,0:T(8...) custom-call(bf16[2048,2048]{1,0:T(8,128)(2,1)} %get-tuple-element.82.normed_ref, bf16[2048,768]{1,0:T(8,128)(2,1)} %bitcast.74, ...), custom_call_target="tpu_custom_call" | custom-call | flops 23622320128 | bytes 100000000 | tf_op jit(solution)/shard_map/attend_forward/pallas_call | solution.py:124
  169.6 25.3 %collective-permute-done.1.refs_2_ = bf16[12,64,1024]{2,1,0:T(8,128)(2,1)S(1)} collective-permute-done((bf16[12,64,1024]{2,1,0:T(8,128)(2,1)S(1)}, bf16[12,64,1024]{2,1,0:T(8,128)(2,1)S(1)}, u32[]{:S(2)}, u32[]{:S(2)}) %collective-permute-start.1) | collective-permute-done | bytes 1572896 | tf_op jit(solution)/shard_map/ppermute | solution.py:1177
  194.9 8.9 %collective-permute-done.refs_1_ = bf16[16,64,1024]{2,1,0:T(8,128)(2,1)S(1)} collective-permute-done((bf16[16,64,1024]{2,1,0:T(8,128)(2,1)}, bf16[16,64,1024]{2,1,0:T(8,128)(2,1)S(1)}, u32[]{:S(2)}, u32[]{:S(2)}) %collective-permute-start) | collective-permute-done | bytes 2097184 | tf_op jit(solution)/shard_map/ppermute | solution.py:1177
  203.9 2.0 slice_reduce_fusion
  208.1 115.0 %attention_branch.1 = (f32[256,2048]{1,0:T(8,128)}, bf16[2048,2048]{1,0:T(8,128)(2,1)}, f32[8,128]{1,0:T(8,128)}, bf16[32,64,1024]{2,1,0:T(8,128)(2,1)}, bf16[32...) custom-call(bf16[2048,256]{1,0:T(8,128)(2,1)} %get-tuple-element.142.left_ref, ...), custom_call_target="tpu_custom_call" | custom-call | flops 2147483648 | bytes 300000000 | tf_op jit(solution)/shard_map/attention_branch/pallas_call | solution.py:805
  323.2 1.4 constant_dynamic-slice_fusion.2
  324.6 1.3 collective-permute-start.2
  325.9 14.6 %fusion.6 = f32[2048,1024]{1,0:T(8,128)} fusion(bf16[2048,2048]{1,0:T(8,128)(2,1)} %get-tuple-element.99.normed_ref, bf16[2048,1024]{1,0:T(8,128)(2,1)} %bitcast.84), kind=kOutput, calls=%fused_computation.41 | convolution fusion | flops 8589934592 | bytes 20971520 | tf_op jit(solution)/shard_map/dot_general | solution.py:30
  340.5 13.7 %multiply_convert_fusion.2 = (bf16[2048,1024]{1,0:T(8,128)(2,1)}, f32[2048,1024]{1,0:T(8,128)}) fusion(f32[2048,1024]{1,0:T(8,128)} %fusion.6, bf16[2048,2048]{1,0:T(8,128)(2,1)S(1)} %bitcast.83, bf16[2048,1024]{1,0:T(8,128)(2,1)S(1)} %bitcast.87), kind=kOutput, calls=%fused_computation.2 | convolution fusion | flops 8602517504 | bytes 33554432 | tf_op jit(solution)/shard_map/dot_general | solution.py:30
  354.2 1.1 constant_dynamic-update-slice_fusion
  355.3 12.7 %convolution_convert_fusion = bf16[1024,2048]{1,0:T(8,128)(2,1)S(1)} fusion(bf16[2048,1024]{1,0:T(8,128)(2,1)} %get-tuple-element.162.hidden_ref, bf16[2048,2048]{1,0:T(8,128)(2,1)} %all-gather.7.cloned.1.call-done), kind=kOutput, calls=%fused_computation.8 | convolution fusion | flops 8592031744 | bytes 16777216 | tf_op jit(solution)/shard_map/dot_general | solution.py:30
  368.0 1.3 dynamic-slice_bitcast_fusion.2
  369.3 0.8 collective-permute-start.3
  370.1 22.3 %multiply_convert_fusion = (bf16[2048,1024]{1,0:T(8,128)(2,1)}, bf16[2048,1024]{1,0:T(8,128)(2,1)}) fusion(f32[2048,1024]{1,0:T(8,128)} %fusion.6, f32[2048,1024]{1,0:T(8,128)} %get-tuple-element.163, bf16[2048,2048]{1,0:T(8,128)(2,1)} %all-gather.7.cloned.1.call-done, bf16[1024,2048]{1,0:T(8,128)(2,1)} %bitcast.10.down_ref), kind=kOutput, calls=%fused_computation | convolution fusion | flops 8617197568 | bytes 37748736 | tf_op jit(solution)/shard_map/dot_general | solution.py:30
  392.4 2.1 collective-permute-done.3
  394.5 1.4 fusion.5.refs_1_
  395.8 105.9 %ffn_back.1 = (f32[256,2048]{1,0:T(8,128)}, bf16[256,2048]{1,0:T(8,128)(2,1)}, bf16[2048,256]{1,0:T(8,128)(2,1)}, bf16[2048,1024]{1,0:T(8,128)(2,1)}, bf16[4,256...) custom-call(bf16[2048,1024]{1,0:T(8,128)(2,1)} %get-tuple-element.10, ...), custom_call_target="tpu_custom_call" | custom-call | flops 51539607552 | bytes 200000000 | tf_op jit(solution)/shard_map/ffn_back/pallas_call | solution.py:977
  501.9 3.2 add_convert_fusion
  505.2 1.3 collective-permute-start.4
  506.5 38.5 %attend_backward.2 = (bf16[2048,384]{1,0:T(8,128)(2,1)}, bf16[2048,384]{1,0:T(8,128)(2,1)}) custom-call(bf16[2,2048,128]{2,1,0:T(8,128)(2,1)} %get-tuple-element.87.q_ref, bf16[2,2048,128]{2,1,0:T(8,128)(2,1)} %get-tuple-element.88.k_ref, bf16[2,2048,128]{2,1,0:T(8,128)(2,1)} %get-tuple-element.89.v_ref, bf16[2048,256]{1,0:T(8,128)(2,1)} %get-tuple-element.120.grad_ref, ...), custom_call_target="tpu_custom_call" | custom-call | flops 24696061952 | bytes 100000000 | tf_op jit(solution)/shard_map/attend_backward/pallas_call | solution.py:195
  545.0 7.9 %collective-permute-done.4 = bf16[2,2,2,64,1024]{4,3,2,1,0:T(8,128)(2,1)S(1)} collective-permute-done((bf16[2,2,2,64,1024]{4,3,2,1,0:T(8,128)(2,1)S(1)}, bf16[2,2,2,64,1024]{4,3,2,1,0:T(8,128)(2,1)S(1)}, u32[]{:S(2)}, u32[]{:S(2)}) %collective-permute-start.4) | collective-permute-done | bytes 1048608 | tf_op jit(solution)/shard_map/ppermute | solution.py:1177
  552.9 1.4 fusion.4
  554.7 1.8 dynamic-slice_bitcast_fusion
  556.5 1.2 collective-permute-start.5
  557.7 37.3 %attend_backward.3 = (bf16[2048,384]{1,0:T(8,128)(2,1)}, bf16[2048,384]{1,0:T(8,128)(2,1)}) custom-call(bf16[2,2048,128]{2,1,0:T(8,128)(2,1)} %get-tuple-element.87.q_ref, bf16[2,2048,128]{2,1,0:T(8,128)(2,1)} %get-tuple-element.88.k_ref, bf16[2,2048,128]{2,1,0:T(8,128)(2,1)} %get-tuple-element.89.v_ref, bf16[2048,256]{1,0:T(8,128)(2,1)} %get-tuple-element.120.grad_ref, ...), custom_call_target="tpu_custom_call" | custom-call | flops 24696061952 | bytes 100000000 | tf_op jit(solution)/shard_map/attend_backward/pallas_call | solution.py:195
  595.0 9.5 %collective-permute-done.5 = bf16[2,2,2,2,64,1024]{5,4,3,2,1,0:T(8,128)(2,1)} collective-permute-done((bf16[2,2,2,2,64,1024]{5,4,3,2,1,0:T(8,128)(2,1)S(1)}, bf16[2,2,2,2,64,1024]{5,4,3,2,1,0:T(8,128)(2,1)}, u32[]{:S(2)}, u32[]{:S(2)}) %collective-permute-start.5) | collective-permute-done | bytes 2097184 | tf_op jit(solution)/shard_map/ppermute | solution.py:1177
  604.5 2.7 fusion.1
  608.0 1.6 constant_dynamic-slice_fusion
  609.6 111.1 %last_sums.1 = (f32[256,2048]{1,0:T(8,128)}, bf16[256,2048]{1,0:T(8,128)(2,1)}, bf16[8,64,1024]{2,1,0:T(8,128)(2,1)}, bf16[8,64,1024]{2,1,0:T(8,128)(2,1)}) custom-call(bf16[2048,384]{1,0:T(8,128)(2,1)} %get-tuple-element.119.left_ref, bf16[2048,384]{1,0:T(8,128)(2,1)} %get-tuple-element.124.other_ref, bf16[2048,768]{1,0:T(8,128)(2,1)} %bitcast.75, ...), custom_call_target="tpu_custom_call" | custom-call | flops 805306368 | bytes 300000000 | tf_op jit(solution)/shard_map/last_sums/pallas_call | solution.py:1060
  720.7 6.8 convolution_convert_fusion.1
  728.3 1.2 divide_sqrt_fusion
  729.7 0.9 multiply_convert_fusion.3
  730.6 3.9 fusion.2
  734.4 2.9 fusion.3.refs_2_
  737.4 28.3 %exchange.1 = (bf16[8,64,384]{2,1,0:T(8,128)(2,1)}, bf16[8,64,384]{2,1,0:T(8,128)(2,1)}, bf16[8,64,1024]{2,1,0:T(8,128)(2,1)}) custom-call(bf16[8,64,384]{2,1,0:T(8,128)(2,1)} %bitcast.76, bf16[8,64,384]{2,1,0:T(8,128)(2,1)} %bitcast.77, bf16[8,64,1024]{2,1,0:T(8,128)(2,1)} %fusion.3.refs_2_), custom_call_target="tpu_custom_call" | custom-call | flops 1000000 | bytes 40000000 | tf_op jit(solution)/shard_map/exchange/pallas_call | solution.py:1106
  765.8 1.2 copy-done.5
  767.0 1.2 copy-done.6
  768.2 1.0 copy-done.7
  769.2 1.0 copy-done.8
  770.2 3.2 home.1
  773.4 1.9 convert_element_type.149
  775.4 2.3 copy.43
  777.7 1.3 copy.44
  (84 shorter events, 7.0 us)
Async XLA Ops:
  7.2 114.1 %all-gather.5.cloned.1.call-start = ((), (), s32[]{:S(2)}) async-start(), calls=%async_computation.3 | async-start | bytes 1310720 | tf_op jit(solution)/shard_map/all_gather | solution.py:1180
  7.9 199.6 %all-gather.9.cloned.1.call-start = ((), (), s32[]{:S(2)}) async-start(), calls=%async_computation.5 | async-start | bytes 9437184 | tf_op jit(solution)/shard_map/all_gather | solution.py:1257
  121.3 234.0 %all-gather.7.cloned.1.call-start = ((), (), s32[]{:S(2)}) async-start(), calls=%async_computation.4 | async-start | bytes 9437184 | tf_op jit(solution)/shard_map/all_gather | solution.py:1303
  122.2 4.6 copy-start.16
  123.5 80.3 %collective-permute-start = (bf16[16,64,1024]{2,1,0:T(8,128)(2,1)}, bf16[16,64,1024]{2,1,0:T(8,128)(2,1)S(1)}, u32[]{:S(2)}, u32[]{:S(2)}) collective-permute-start(bf16[16,64,1024]{2,1,0:T(8,128)(2,1)} %get-tuple-element.90.refs_0_), channel_id=1, source_target_pairs={{0,4},{1,5},{2,6},{3,7},{4,0},{5,1},{6,2},{7,3},{8,12},{9,13},{10,... | collective-permute-start | bytes 6291464 | tf_op jit(solution)/shard_map/ppermute | solution.py:1177
  126.6 68.3 %collective-permute-start.1 = (bf16[12,64,1024]{2,1,0:T(8,128)(2,1)S(1)}, bf16[12,64,1024]{2,1,0:T(8,128)(2,1)S(1)}, u32[]{:S(2)}, u32[]{:S(2)}) collective-permute-start(bf16[12,64,1024]{2,1,0:T(8,128)(2,1)S(1)} %slice.19), channel_id=1, source_target_pairs={{0,16},{1,17},{2,18},{3,19},{4,20},{5,21},{6,22},{7,23},{8,24},{9,... | collective-permute-start | bytes 4718600 | tf_op jit(solution)/shard_map/ppermute | solution.py:1177
  194.9 8.9 %copy-start.14 = (bf16[12,64,1024]{2,1,0:T(8,128)(2,1)}, bf16[12,64,1024]{2,1,0:T(8,128)(2,1)S(1)}, u32[]{:S(2)}) copy-start(bf16[12,64,1024]{2,1,0:T(8,128)(2,1)S(1)} %collective-permute-done.1.refs_2_) | copy-start | bytes 4718596
  203.8 4.3 copy-start.12
  203.8 350.8 %all-gather.11.cloned.1.call-start = ((), (), s32[]{:S(2)}) async-start(), calls=%async_computation.6 | async-start | bytes 9437184 | tf_op jit(solution)/shard_map/all_gather | solution.py:1339
  323.1 17.3 %slice-start = ((s8[8388608]{0:T(1024)(128)(4,1)}), s8[4194304]{0:T(1024)(128)(4,1)S(1)}, s32[]{:S(2)}) async-start(s8[8388608]{0:T(1024)(128)(4,1)} %bitcast.82), calls=%async_computation.10 | async-start | bytes 8388608
  324.6 29.6 %collective-permute-start.2 = (bf16[1,256,2048]{2,1,0:T(8,128)(2,1)S(1)}, bf16[1,256,2048]{2,1,0:T(8,128)(2,1)S(1)}, u32[]{:S(2)}, u32[]{:S(2)}) collective-permute-start(bf16[1,256,2048]{2,1,0:T(8,128)(2,1)S(1)} %constant_dynamic-slice_fusion.2), channel_id=1, source_target_pairs={{0,4},{1,5},{2,6},{3,7},{4,0},{5,1},{6,2},{7,3},{8,12},{9,13},{10,... | collective-permute-start | bytes 3145736 | tf_op jit(solution)/shard_map/ppermute | solution.py:1177
  325.9 14.6 %slice-start.1 = ((s8[8388608]{0:T(1024)(128)(4,1)}), s8[4194304]{0:T(1024)(128)(4,1)S(1)}, s32[]{:S(2)}) async-start(s8[8388608]{0:T(1024)(128)(4,1)} %bitcast.82), calls=%async_computation.11 | async-start | bytes 8388608
  325.9 14.6 %copy-start.17 = (bf16[32,64,1024]{2,1,0:T(8,128)(2,1)S(1)}, bf16[32,64,1024]{2,1,0:T(8,128)(2,1)}, u32[]{:S(2)}) copy-start(bf16[32,64,1024]{2,1,0:T(8,128)(2,1)} %get-tuple-element.101) | copy-start | bytes 12582916
  368.0 26.5 %copy-start.11 = (bf16[1024,2048]{1,0:T(8,128)(2,1)}, bf16[1024,2048]{1,0:T(8,128)(2,1)S(1)}, u32[]{:S(2)}) copy-start(bf16[1024,2048]{1,0:T(8,128)(2,1)S(1)} %convolution_convert_fusion) | copy-start | bytes 12582916
  369.3 25.1 %collective-permute-start.3 = (bf16[256,2048]{1,0:T(8,128)(2,1)S(1)}, bf16[256,2048]{1,0:T(8,128)(2,1)S(1)}, u32[]{:S(2)}, u32[]{:S(2)}) collective-permute-start(bf16[256,2048]{1,0:T(8,128)(2,1)S(1)} %get-tuple-element.157), channel_id=1, source_target_pairs={{0,4},{1,5},{2,6},{3,7},{4,0},{5,1},{6,2},{7,3},{8,12},{9,13},{10,... | collective-permute-start | bytes 3145736 | tf_op jit(solution)/shard_map/ppermute | solution.py:1177
  501.8 107.8 %reduce-scatter.4.cloned.1.call-start = ((), (), s32[]{:S(2)}) async-start(), calls=%async_computation.7 | async-start | bytes 1966080 | tf_op jit(solution)/shard_map/reduce_scatter | solution.py:1183
  505.2 47.7 %collective-permute-start.4 = (bf16[2,2,2,64,1024]{4,3,2,1,0:T(8,128)(2,1)S(1)}, bf16[2,2,2,64,1024]{4,3,2,1,0:T(8,128)(2,1)S(1)}, u32[]{:S(2)}, u32[]{:S(2)}) collective-permute-start(bf16[2,2,2,64,1024]{4,3,2,1,0:T(8,128)(2,1)S(1)} %dynamic-slice_bitcast_fusion.1), channel_id=1, source_target_pairs={{0,16},{1,17},{2,18},{3,19},{4,20},{5,21},{6,22},{7,23},{8,24},{9,... | collective-permute-start | bytes 3145736 | tf_op jit(solution)/shard_map/ppermute | solution.py:1177
  554.7 182.7 %reduce-scatter.6.cloned.1.call-start = ((), (), s32[]{:S(2)}) async-start(), calls=%async_computation.8 | async-start | bytes 1966080 | tf_op jit(solution)/shard_map/reduce_scatter | solution.py:1183
  556.5 48.0 %copy-start.10 = (bf16[2048,1024]{1,0:T(8,128)(2,1)S(1)}, bf16[2048,1024]{1,0:T(8,128)(2,1)}, u32[]{:S(2)}) copy-start(bf16[2048,1024]{1,0:T(8,128)(2,1)} %get-tuple-element.123) | copy-start | bytes 12582916
  556.5 48.0 %collective-permute-start.5 = (bf16[2,2,2,2,64,1024]{5,4,3,2,1,0:T(8,128)(2,1)S(1)}, bf16[2,2,2,2,64,1024]{5,4,3,2,1,0:T(8,128)(2,1)}, u32[]{:S(2)}, u32[]{:S(2)}) collective-permute-start(bf16[2,2,2,2,64,1024]{5,4,3,2,1,0:T(8,128)(2,1)S(1)} %dynamic-slice_bitcast_fusion), channel_id=1, source_target_pairs={{0,4},{1,5},{2,6},{3,7},{4,0},{5,1},{6,2},{7,3},{8,12},{9,13},{10,... | collective-permute-start | bytes 6291464 | tf_op jit(solution)/shard_map/ppermute | solution.py:1177
  595.0 12.3 %copy-start.15 = (f32[32,64]{1,0:T(8,128)S(1)}, f32[32,64]{1,0:T(8,128)}, u32[]{:S(2)}) copy-start(f32[32,64]{1,0:T(8,128)} %get-tuple-element.150) | copy-start | bytes 24580
  607.2 166.2 %reduce-scatter.8.cloned.1.call-start = ((), (), s32[]{:S(2)}) async-start(), calls=%async_computation.9 | async-start | bytes 1310720 | tf_op jit(solution)/shard_map/reduce_scatter | solution.py:1183
  609.6 111.1 %copy-start.9 = (bf16[2048,256]{1,0:T(8,128)(2,1)S(1)}, bf16[2048,256]{1,0:T(8,128)(2,1)}, u32[]{:S(2)}) copy-start(bf16[2048,256]{1,0:T(8,128)(2,1)} %get-tuple-element.142.left_ref) | copy-start | bytes 3145732
  720.6 6.8 copy-start.18
  720.6 6.9 copy-start.19
  720.7 9.0 %copy-start.2 = (bf16[64,2048]{1,0:T(8,128)(2,1)S(1)}, bf16[64,2048]{1,0:T(8,128)(2,1)}, u32[]{:S(2)}) copy-start(bf16[64,2048]{1,0:T(8,128)(2,1)} %refs_4_.1) | copy-start | bytes 786436
  720.7 9.0 %copy-start.3 = (bf16[64,2048]{1,0:T(8,128)(2,1)S(1)}, bf16[64,2048]{1,0:T(8,128)(2,1)}, u32[]{:S(2)}) copy-start(bf16[64,2048]{1,0:T(8,128)(2,1)} %refs_5_.1) | copy-start | bytes 786436
  730.6 35.2 %copy-start = (bf16[64,8192]{1,0:T(8,128)(2,1)S(1)}, bf16[64,8192]{1,0:T(8,128)(2,1)}, u32[]{:S(2)}) copy-start(bf16[64,8192]{1,0:T(8,128)(2,1)} %refs_7_.1) | copy-start | bytes 3145732
  730.6 35.2 %copy-start.1 = (bf16[64,8192]{1,0:T(8,128)(2,1)S(1)}, bf16[64,8192]{1,0:T(8,128)(2,1)}, u32[]{:S(2)}) copy-start(bf16[64,8192]{1,0:T(8,128)(2,1)} %refs_8_.1) | copy-start | bytes 3145732
  730.6 35.2 %copy-start.4 = (bf16[64,2048]{1,0:T(8,128)(2,1)S(1)}, bf16[64,2048]{1,0:T(8,128)(2,1)}, u32[]{:S(2)}) copy-start(bf16[64,2048]{1,0:T(8,128)(2,1)} %refs_6_.1) | copy-start | bytes 786436
  765.8 1.2 copy-start.5
  767.0 1.2 copy-start.6
  768.2 1.0 copy-start.7
  769.2 1.0 copy-start.8
  773.4 4.2 copy-start.13
Sparse Core Ops, SparseCore 0:
  9.6 35.6 all-gather.4
  121.4 84.2 all-gather.8
  207.4 97.0 all-gather.6
  501.9 52.6 all-gather.10
  557.4 35.2 reduce-scatter.3
  607.4 64.6 reduce-scatter.5
  727.6 35.4 reduce-scatter.7

commit v10 on v9

--- a/solution.py
+++ b/solution.py
@@ -14,7 +14,7 @@
 HALF = 128
 LAST_CUT = 0
 EARLY_HALVES = 3
-BRANCH_CUT = 128
+BRANCH_CUT = 64
 AXIS = "fsdp"
 MESH = pl.DeviceIdType.MESH
 

time: 790 us -> 786 us (level)
  transfers between devices with their start and end apart: 13 -> 13, of which waited for: 6 -> 5; matrix products, arithmetic and copies ran while one was open for 12% -> 12% of each run, Pallas kernels for 62% -> 62%
where the time goes in v10:
time: 786 us; the launch traced here: 782 us
  Pallas kernels  586 us (75%)
  matrix products  70 us (9%)
  waiting for transfers between devices  54.8 us (7%)
  local copies, waits for them, and re-layouts  23.8 us (3%)
  other arithmetic  22.4 us (3%)
  between operations  15.4 us (2%)
  starting transfers between devices  9.95 us (1%)
    pallas_call x1, Pallas kernels, branch(): pl.pallas_call(functools.partial(branch_kernel, bool(carry), swap_bits, s...  112 us
    pallas_call x1, Pallas kernels, front(): pl.pallas_call(functools.partial(front_kernel, team, teams, qkv_moves, ff...  111 us
    pallas_call x1, Pallas kernels, last_sums(): pl.pallas_call(functools.partial(last_sums_kernel, carry_bits, sum_bits,...  111 us
    pallas_call x1, Pallas kernels, ffn_back(): pl.pallas_call(functools.partial(ffn_back_kernel, cross, sum_bits, swap_b...  102 us
    pallas_call x2, Pallas kernels, attend_backward(): pl.pallas_call(functools.partial(attend_backward_kernel, 2 * pair), grid=...  75.7 us
    dot_general x5, matrix products, contract(): lax.dot_general(left, right, (((left_dim,), (right_dim,)), ((), ())), pre...  70 us
    ppermute x6, waiting for transfers between devices, flip(): return lax.ppermute(x, AXIS, [(i, i ^ bit) for i in range(devices)])  53.9 us
    pallas_call x1, Pallas kernels, attend_forward(): pl.pallas_call(attend_forward_kernel, out_shape=(shape((pairs, length, PA...  42.9 us
  transfers between devices with their start and end apart: 13, of which 5 were waited for; matrix products, arithmetic and copies ran while one was open for 12% of the time, Pallas kernels for 62%

profile of v10, /device:TPU:0, one launch (start us, length us, event | category | flops | bytes accessed | tf_op | source)
XLA Modules:
  0.0 781.9 jit_solution(16228606766879507468)
XLA Ops:
  8.0 0.7 maximum_convert_fusion
  10.1 111.1 %front.1 = (bf16[2048,2048]{1,0:T(8,128)(2,1)}, bf16[4,512,768]{2,1,0:T(8,128)(2,1)}, bf16[16,64,1024]{2,1,0:T(8,128)(2,1)}, f32[32,8,128]{2,1,0:T(8,128)}, bf16[256,2048]{1,0:T(8,128)(2,1)}) custom-call(bf16[256,2048]{1,0:T(8,128)(2,1)} %tokens_ref.3, bf16[64,2048]{1,0:T(8,128)(2,1)} %refs_4_.1, bf16[64,2048]{1,0:T(8,128)(2,1)} %refs_5_.1, ...), custom_call_target="tpu_custom_call" | custom-call | bytes 200000000 | tf_op jit(solution)/shard_map/front/pallas_call | solution.py:640
  121.4 0.8 dynamic-slice_convert_fusion
  122.2 1.3 copy.32.col_ref
  123.5 1.4 collective-permute-start
  124.9 1.7 slice.19
  126.7 42.9 %attend_forward.1 = (bf16[2,2048,128]{2,1,0:T(8,128)(2,1)}, bf16[2,2048,128]{2,1,0:T(8,128)(2,1)}, bf16[2,2048,128]{2,1,0:T(8,128)(2,1)}, bf16[2048,256]{1,0:T(8...) custom-call(bf16[2048,2048]{1,0:T(8,128)(2,1)} %get-tuple-element.82.normed_ref, bf16[2048,768]{1,0:T(8,128)(2,1)} %bitcast.74, ...), custom_call_target="tpu_custom_call" | custom-call | flops 23622320128 | bytes 100000000 | tf_op jit(solution)/shard_map/attend_forward/pallas_call | solution.py:124
  169.6 25.3 %collective-permute-done.1.refs_2_ = bf16[12,64,1024]{2,1,0:T(8,128)(2,1)S(1)} collective-permute-done((bf16[12,64,1024]{2,1,0:T(8,128)(2,1)S(1)}, bf16[12,64,1024]{2,1,0:T(8,128)(2,1)S(1)}, u32[]{:S(2)}, u32[]{:S(2)}) %collective-permute-start.1) | collective-permute-done | bytes 1572896 | tf_op jit(solution)/shard_map/ppermute | solution.py:1177
  194.9 8.9 %collective-permute-done.refs_1_ = bf16[16,64,1024]{2,1,0:T(8,128)(2,1)S(1)} collective-permute-done((bf16[16,64,1024]{2,1,0:T(8,128)(2,1)}, bf16[16,64,1024]{2,1,0:T(8,128)(2,1)S(1)}, u32[]{:S(2)}, u32[]{:S(2)}) %collective-permute-start) | collective-permute-done | bytes 2097184 | tf_op jit(solution)/shard_map/ppermute | solution.py:1177
  203.9 2.0 slice_reduce_fusion
  208.1 111.8 %attention_branch.1 = (f32[256,2048]{1,0:T(8,128)}, bf16[2048,2048]{1,0:T(8,128)(2,1)}, f32[8,128]{1,0:T(8,128)}, bf16[32,64,1024]{2,1,0:T(8,128)(2,1)}, bf16[32...) custom-call(bf16[2048,256]{1,0:T(8,128)(2,1)} %get-tuple-element.142.left_ref, ...), custom_call_target="tpu_custom_call" | custom-call | flops 2147483648 | bytes 300000000 | tf_op jit(solution)/shard_map/attention_branch/pallas_call | solution.py:805
  319.9 1.4 constant_dynamic-slice_fusion.2
  321.4 1.8 collective-permute-start.2
  323.1 14.6 %fusion.6 = f32[2048,1024]{1,0:T(8,128)} fusion(bf16[2048,2048]{1,0:T(8,128)(2,1)} %get-tuple-element.99.normed_ref, bf16[2048,1024]{1,0:T(8,128)(2,1)} %bitcast.84), kind=kOutput, calls=%fused_computation.41 | convolution fusion | flops 8589934592 | bytes 20971520 | tf_op jit(solution)/shard_map/dot_general | solution.py:30
  337.7 13.7 %multiply_convert_fusion.2 = (bf16[2048,1024]{1,0:T(8,128)(2,1)}, f32[2048,1024]{1,0:T(8,128)}) fusion(f32[2048,1024]{1,0:T(8,128)} %fusion.6, bf16[2048,2048]{1,0:T(8,128)(2,1)S(1)} %bitcast.83, bf16[2048,1024]{1,0:T(8,128)(2,1)S(1)} %bitcast.87), kind=kOutput, calls=%fused_computation.2 | convolution fusion | flops 8602517504 | bytes 33554432 | tf_op jit(solution)/shard_map/dot_general | solution.py:30
  351.4 1.1 constant_dynamic-update-slice_fusion
  352.6 12.7 %convolution_convert_fusion = bf16[1024,2048]{1,0:T(8,128)(2,1)S(1)} fusion(bf16[2048,1024]{1,0:T(8,128)(2,1)} %get-tuple-element.162.hidden_ref, bf16[2048,2048]{1,0:T(8,128)(2,1)} %all-gather.7.cloned.1.call-done), kind=kOutput, calls=%fused_computation.8 | convolution fusion | flops 8592031744 | bytes 16777216 | tf_op jit(solution)/shard_map/dot_general | solution.py:30
  365.3 1.3 dynamic-slice_bitcast_fusion.2
  366.8 22.3 %multiply_convert_fusion = (bf16[2048,1024]{1,0:T(8,128)(2,1)}, bf16[2048,1024]{1,0:T(8,128)(2,1)}) fusion(f32[2048,1024]{1,0:T(8,128)} %fusion.6, f32[2048,1024]{1,0:T(8,128)} %get-tuple-element.163, bf16[2048,2048]{1,0:T(8,128)(2,1)} %all-gather.7.cloned.1.call-done, bf16[1024,2048]{1,0:T(8,128)(2,1)} %bitcast.10.down_ref), kind=kOutput, calls=%fused_computation | convolution fusion | flops 8617197568 | bytes 37748736 | tf_op jit(solution)/shard_map/dot_general | solution.py:30
  389.1 2.4 collective-permute-done.3
  391.5 1.4 fusion.5.refs_1_
  392.8 101.6 %ffn_back.1 = (f32[256,2048]{1,0:T(8,128)}, bf16[256,2048]{1,0:T(8,128)(2,1)}, bf16[2048,256]{1,0:T(8,128)(2,1)}, bf16[2048,1024]{1,0:T(8,128)(2,1)}, bf16[4,256...) custom-call(bf16[2048,1024]{1,0:T(8,128)(2,1)} %get-tuple-element.10, ...), custom_call_target="tpu_custom_call" | custom-call | flops 51539607552 | bytes 200000000 | tf_op jit(solution)/shard_map/ffn_back/pallas_call | solution.py:977
  494.5 3.2 add_convert_fusion
  497.8 5.1 collective-permute-start.4
  503.0 38.3 %attend_backward.2 = (bf16[2048,384]{1,0:T(8,128)(2,1)}, bf16[2048,384]{1,0:T(8,128)(2,1)}) custom-call(bf16[2,2048,128]{2,1,0:T(8,128)(2,1)} %get-tuple-element.87.q_ref, bf16[2,2048,128]{2,1,0:T(8,128)(2,1)} %get-tuple-element.88.k_ref, bf16[2,2048,128]{2,1,0:T(8,128)(2,1)} %get-tuple-element.89.v_ref, bf16[2048,256]{1,0:T(8,128)(2,1)} %get-tuple-element.120.grad_ref, ...), custom_call_target="tpu_custom_call" | custom-call | flops 24696061952 | bytes 100000000 | tf_op jit(solution)/shard_map/attend_backward/pallas_call | solution.py:195
  541.2 8.0 %collective-permute-done.4 = bf16[2,2,2,64,1024]{4,3,2,1,0:T(8,128)(2,1)S(1)} collective-permute-done((bf16[2,2,2,64,1024]{4,3,2,1,0:T(8,128)(2,1)S(1)}, bf16[2,2,2,64,1024]{4,3,2,1,0:T(8,128)(2,1)S(1)}, u32[]{:S(2)}, u32[]{:S(2)}) %collective-permute-start.4) | collective-permute-done | bytes 1048608 | tf_op jit(solution)/shard_map/ppermute | solution.py:1177
  549.3 1.4 fusion.4
  550.7 1.8 dynamic-slice_bitcast_fusion
  552.6 1.0 collective-permute-start.5
  553.6 37.5 %attend_backward.3 = (bf16[2048,384]{1,0:T(8,128)(2,1)}, bf16[2048,384]{1,0:T(8,128)(2,1)}) custom-call(bf16[2,2048,128]{2,1,0:T(8,128)(2,1)} %get-tuple-element.87.q_ref, bf16[2,2048,128]{2,1,0:T(8,128)(2,1)} %get-tuple-element.88.k_ref, bf16[2,2048,128]{2,1,0:T(8,128)(2,1)} %get-tuple-element.89.v_ref, bf16[2048,256]{1,0:T(8,128)(2,1)} %get-tuple-element.120.grad_ref, ...), custom_call_target="tpu_custom_call" | custom-call | flops 24696061952 | bytes 100000000 | tf_op jit(solution)/shard_map/attend_backward/pallas_call | solution.py:195
  591.1 9.4 %collective-permute-done.5 = bf16[2,2,2,2,64,1024]{5,4,3,2,1,0:T(8,128)(2,1)} collective-permute-done((bf16[2,2,2,2,64,1024]{5,4,3,2,1,0:T(8,128)(2,1)S(1)}, bf16[2,2,2,2,64,1024]{5,4,3,2,1,0:T(8,128)(2,1)}, u32[]{:S(2)}, u32[]{:S(2)}) %collective-permute-start.5) | collective-permute-done | bytes 2097184 | tf_op jit(solution)/shard_map/ppermute | solution.py:1177
  600.4 2.7 fusion.1
  603.9 1.6 constant_dynamic-slice_fusion
  605.5 111.0 %last_sums.1 = (f32[256,2048]{1,0:T(8,128)}, bf16[256,2048]{1,0:T(8,128)(2,1)}, bf16[8,64,1024]{2,1,0:T(8,128)(2,1)}, bf16[8,64,1024]{2,1,0:T(8,128)(2,1)}) custom-call(bf16[2048,384]{1,0:T(8,128)(2,1)} %get-tuple-element.119.left_ref, bf16[2048,384]{1,0:T(8,128)(2,1)} %get-tuple-element.124.other_ref, bf16[2048,768]{1,0:T(8,128)(2,1)} %bitcast.75, ...), custom_call_target="tpu_custom_call" | custom-call | flops 805306368 | bytes 300000000 | tf_op jit(solution)/shard_map/last_sums/pallas_call | solution.py:1060
  716.5 6.8 convolution_convert_fusion.1
  724.2 1.2 divide_sqrt_fusion
  725.5 0.9 multiply_convert_fusion.3
  726.4 3.9 fusion.2
  730.3 2.9 fusion.3.refs_2_
  733.3 28.3 %exchange.1 = (bf16[8,64,384]{2,1,0:T(8,128)(2,1)}, bf16[8,64,384]{2,1,0:T(8,128)(2,1)}, bf16[8,64,1024]{2,1,0:T(8,128)(2,1)}) custom-call(bf16[8,64,384]{2,1,0:T(8,128)(2,1)} %bitcast.76, bf16[8,64,384]{2,1,0:T(8,128)(2,1)} %bitcast.77, bf16[8,64,1024]{2,1,0:T(8,128)(2,1)} %fusion.3.refs_2_), custom_call_target="tpu_custom_call" | custom-call | flops 1000000 | bytes 40000000 | tf_op jit(solution)/shard_map/exchange/pallas_call | solution.py:1106
  761.6 1.2 copy-done.5
  762.9 1.2 copy-done.6
  764.1 1.0 copy-done.7
  765.1 1.0 copy-done.8
  766.1 3.2 home.1
  769.3 1.9 convert_element_type.149
  771.2 2.3 copy.43
  773.5 1.3 copy.44
  (84 shorter events, 6.2 us)
Async XLA Ops:
  7.2 114.1 %all-gather.5.cloned.1.call-start = ((), (), s32[]{:S(2)}) async-start(), calls=%async_computation.3 | async-start | bytes 1310720 | tf_op jit(solution)/shard_map/all_gather | solution.py:1180
  7.9 199.6 %all-gather.9.cloned.1.call-start = ((), (), s32[]{:S(2)}) async-start(), calls=%async_computation.5 | async-start | bytes 9437184 | tf_op jit(solution)/shard_map/all_gather | solution.py:1257
  121.3 231.3 %all-gather.7.cloned.1.call-start = ((), (), s32[]{:S(2)}) async-start(), calls=%async_computation.4 | async-start | bytes 9437184 | tf_op jit(solution)/shard_map/all_gather | solution.py:1303
  122.2 4.6 copy-start.16
  123.5 80.3 %collective-permute-start = (bf16[16,64,1024]{2,1,0:T(8,128)(2,1)}, bf16[16,64,1024]{2,1,0:T(8,128)(2,1)S(1)}, u32[]{:S(2)}, u32[]{:S(2)}) collective-permute-start(bf16[16,64,1024]{2,1,0:T(8,128)(2,1)} %get-tuple-element.90.refs_0_), channel_id=1, source_target_pairs={{0,4},{1,5},{2,6},{3,7},{4,0},{5,1},{6,2},{7,3},{8,12},{9,13},{10,... | collective-permute-start | bytes 6291464 | tf_op jit(solution)/shard_map/ppermute | solution.py:1177
  126.6 68.3 %collective-permute-start.1 = (bf16[12,64,1024]{2,1,0:T(8,128)(2,1)S(1)}, bf16[12,64,1024]{2,1,0:T(8,128)(2,1)S(1)}, u32[]{:S(2)}, u32[]{:S(2)}) collective-permute-start(bf16[12,64,1024]{2,1,0:T(8,128)(2,1)S(1)} %slice.19), channel_id=1, source_target_pairs={{0,16},{1,17},{2,18},{3,19},{4,20},{5,21},{6,22},{7,23},{8,24},{9,... | collective-permute-start | bytes 4718600 | tf_op jit(solution)/shard_map/ppermute | solution.py:1177
  194.9 8.9 %copy-start.14 = (bf16[12,64,1024]{2,1,0:T(8,128)(2,1)}, bf16[12,64,1024]{2,1,0:T(8,128)(2,1)S(1)}, u32[]{:S(2)}) copy-start(bf16[12,64,1024]{2,1,0:T(8,128)(2,1)S(1)} %collective-permute-done.1.refs_2_) | copy-start | bytes 4718596
  203.8 4.3 copy-start.12
  203.8 346.9 %all-gather.11.cloned.1.call-start = ((), (), s32[]{:S(2)}) async-start(), calls=%async_computation.6 | async-start | bytes 9437184 | tf_op jit(solution)/shard_map/all_gather | solution.py:1339
  319.9 17.8 %slice-start = ((s8[8388608]{0:T(1024)(128)(4,1)}), s8[4194304]{0:T(1024)(128)(4,1)S(1)}, s32[]{:S(2)}) async-start(s8[8388608]{0:T(1024)(128)(4,1)} %bitcast.82), calls=%async_computation.10 | async-start | bytes 8388608
  321.4 30.1 %collective-permute-start.2 = (bf16[1,256,2048]{2,1,0:T(8,128)(2,1)S(1)}, bf16[1,256,2048]{2,1,0:T(8,128)(2,1)S(1)}, u32[]{:S(2)}, u32[]{:S(2)}) collective-permute-start(bf16[1,256,2048]{2,1,0:T(8,128)(2,1)S(1)} %constant_dynamic-slice_fusion.2), channel_id=1, source_target_pairs={{0,4},{1,5},{2,6},{3,7},{4,0},{5,1},{6,2},{7,3},{8,12},{9,13},{10,... | collective-permute-start | bytes 3145736 | tf_op jit(solution)/shard_map/ppermute | solution.py:1177
  323.1 14.6 %slice-start.1 = ((s8[8388608]{0:T(1024)(128)(4,1)}), s8[4194304]{0:T(1024)(128)(4,1)S(1)}, s32[]{:S(2)}) async-start(s8[8388608]{0:T(1024)(128)(4,1)} %bitcast.82), calls=%async_computation.11 | async-start | bytes 8388608
  323.1 14.6 %copy-start.17 = (bf16[32,64,1024]{2,1,0:T(8,128)(2,1)S(1)}, bf16[32,64,1024]{2,1,0:T(8,128)(2,1)}, u32[]{:S(2)}) copy-start(bf16[32,64,1024]{2,1,0:T(8,128)(2,1)} %get-tuple-element.101) | copy-start | bytes 12582916
  365.3 26.2 %copy-start.11 = (bf16[1024,2048]{1,0:T(8,128)(2,1)}, bf16[1024,2048]{1,0:T(8,128)(2,1)S(1)}, u32[]{:S(2)}) copy-start(bf16[1024,2048]{1,0:T(8,128)(2,1)S(1)} %convolution_convert_fusion) | copy-start | bytes 12582916
  366.6 24.9 %collective-permute-start.3 = (bf16[256,2048]{1,0:T(8,128)(2,1)S(1)}, bf16[256,2048]{1,0:T(8,128)(2,1)S(1)}, u32[]{:S(2)}, u32[]{:S(2)}) collective-permute-start(bf16[256,2048]{1,0:T(8,128)(2,1)S(1)} %get-tuple-element.157), channel_id=1, source_target_pairs={{0,4},{1,5},{2,6},{3,7},{4,0},{5,1},{6,2},{7,3},{8,12},{9,13},{10,... | collective-permute-start | bytes 3145736 | tf_op jit(solution)/shard_map/ppermute | solution.py:1177
  494.5 111.0 %reduce-scatter.4.cloned.1.call-start = ((), (), s32[]{:S(2)}) async-start(), calls=%async_computation.7 | async-start | bytes 1966080 | tf_op jit(solution)/shard_map/reduce_scatter | solution.py:1183
  497.8 51.4 %collective-permute-start.4 = (bf16[2,2,2,64,1024]{4,3,2,1,0:T(8,128)(2,1)S(1)}, bf16[2,2,2,64,1024]{4,3,2,1,0:T(8,128)(2,1)S(1)}, u32[]{:S(2)}, u32[]{:S(2)}) collective-permute-start(bf16[2,2,2,64,1024]{4,3,2,1,0:T(8,128)(2,1)S(1)} %dynamic-slice_bitcast_fusion.1), channel_id=1, source_target_pairs={{0,16},{1,17},{2,18},{3,19},{4,20},{5,21},{6,22},{7,23},{8,24},{9,... | collective-permute-start | bytes 3145736 | tf_op jit(solution)/shard_map/ppermute | solution.py:1177
  550.7 182.6 %reduce-scatter.6.cloned.1.call-start = ((), (), s32[]{:S(2)}) async-start(), calls=%async_computation.8 | async-start | bytes 1966080 | tf_op jit(solution)/shard_map/reduce_scatter | solution.py:1183
  552.6 47.9 %copy-start.10 = (bf16[2048,1024]{1,0:T(8,128)(2,1)S(1)}, bf16[2048,1024]{1,0:T(8,128)(2,1)}, u32[]{:S(2)}) copy-start(bf16[2048,1024]{1,0:T(8,128)(2,1)} %get-tuple-element.123) | copy-start | bytes 12582916
  552.6 47.8 %collective-permute-start.5 = (bf16[2,2,2,2,64,1024]{5,4,3,2,1,0:T(8,128)(2,1)S(1)}, bf16[2,2,2,2,64,1024]{5,4,3,2,1,0:T(8,128)(2,1)}, u32[]{:S(2)}, u32[]{:S(2)}) collective-permute-start(bf16[2,2,2,2,64,1024]{5,4,3,2,1,0:T(8,128)(2,1)S(1)} %dynamic-slice_bitcast_fusion), channel_id=1, source_target_pairs={{0,4},{1,5},{2,6},{3,7},{4,0},{5,1},{6,2},{7,3},{8,12},{9,13},{10,... | collective-permute-start | bytes 6291464 | tf_op jit(solution)/shard_map/ppermute | solution.py:1177
  591.1 12.1 %copy-start.15 = (f32[32,64]{1,0:T(8,128)S(1)}, f32[32,64]{1,0:T(8,128)}, u32[]{:S(2)}) copy-start(f32[32,64]{1,0:T(8,128)} %get-tuple-element.150) | copy-start | bytes 24580
  603.2 166.1 %reduce-scatter.8.cloned.1.call-start = ((), (), s32[]{:S(2)}) async-start(), calls=%async_computation.9 | async-start | bytes 1310720 | tf_op jit(solution)/shard_map/reduce_scatter | solution.py:1183
  605.5 111.0 %copy-start.9 = (bf16[2048,256]{1,0:T(8,128)(2,1)S(1)}, bf16[2048,256]{1,0:T(8,128)(2,1)}, u32[]{:S(2)}) copy-start(bf16[2048,256]{1,0:T(8,128)(2,1)} %get-tuple-element.142.left_ref) | copy-start | bytes 3145732
  716.5 6.8 copy-start.18
  716.5 6.9 copy-start.19
  716.5 9.0 %copy-start.2 = (bf16[64,2048]{1,0:T(8,128)(2,1)S(1)}, bf16[64,2048]{1,0:T(8,128)(2,1)}, u32[]{:S(2)}) copy-start(bf16[64,2048]{1,0:T(8,128)(2,1)} %refs_4_.1) | copy-start | bytes 786436
  716.5 9.0 %copy-start.3 = (bf16[64,2048]{1,0:T(8,128)(2,1)S(1)}, bf16[64,2048]{1,0:T(8,128)(2,1)}, u32[]{:S(2)}) copy-start(bf16[64,2048]{1,0:T(8,128)(2,1)} %refs_5_.1) | copy-start | bytes 786436
  726.4 35.2 %copy-start = (bf16[64,8192]{1,0:T(8,128)(2,1)S(1)}, bf16[64,8192]{1,0:T(8,128)(2,1)}, u32[]{:S(2)}) copy-start(bf16[64,8192]{1,0:T(8,128)(2,1)} %refs_7_.1) | copy-start | bytes 3145732
  726.4 35.2 %copy-start.1 = (bf16[64,8192]{1,0:T(8,128)(2,1)S(1)}, bf16[64,8192]{1,0:T(8,128)(2,1)}, u32[]{:S(2)}) copy-start(bf16[64,8192]{1,0:T(8,128)(2,1)} %refs_8_.1) | copy-start | bytes 3145732
  726.4 35.2 %copy-start.4 = (bf16[64,2048]{1,0:T(8,128)(2,1)S(1)}, bf16[64,2048]{1,0:T(8,128)(2,1)}, u32[]{:S(2)}) copy-start(bf16[64,2048]{1,0:T(8,128)(2,1)} %refs_6_.1) | copy-start | bytes 786436
  761.6 1.2 copy-start.5
  762.9 1.2 copy-start.6
  764.1 1.0 copy-start.7
  765.1 1.0 copy-start.8
  769.3 4.2 copy-start.13
Sparse Core Ops, SparseCore 0:
  9.6 35.6 all-gather.4
  121.4 84.2 all-gather.8
  207.4 97.0 all-gather.6
  494.6 55.9 all-gather.10
  553.3 35.2 reduce-scatter.3
  603.3 64.6 reduce-scatter.5
  723.5 35.4 reduce-scatter.7
